TPU v7x, 512 devices: a whole 4x8x8 slice. The times are simulated.
512 devices in a mesh: side: 4 (over z_lo), rep: 8 (over x, core), tp: 16 (over z_hi, y).
Axes of the slice: x: 4, y: 8, z: 8 (z_hi: 2, z_lo: 4; z = z_hi * 4 + z_lo), core: 2. Of those that a mesh axis runs over, the one named last changes fastest.
Arguments:
- learn_inputs: bfloat16 [4, 8192, 8192], P('side', 'rep', 'tp'), may hold values from -6 to 6
- learn_grads: bfloat16 [4, 8192, 2048], P('side', ('rep', 'tp')), may hold values from -0.5 to 0.5
- kv_master: float32 [8192, 2048], P('tp', 'rep'), may hold values from -0.0625 to 0.0625
- first_moment: bfloat16 [8192, 2048], P('tp', 'rep'), may hold values from -12 to 12
- second_moment: bfloat16 [8192, 2048], P('tp', 'rep'), may hold values from 0.0099487305 to 0.29882812
- decode_inputs: bfloat16 [512, 8192], P(('side', 'rep'), 'tp'), may hold values from -6 to 6
- queries: bfloat16 [512, 8192], P(('side', 'rep', 'tp')), may hold values from -6 to 6
- key_cache_slots: bfloat16 [512, 128, 1024], P(('side', 'rep', 'tp')), may hold values from -6 to 6
- value_cache_slots: bfloat16 [512, 128, 1024], P(('side', 'rep', 'tp')), may hold values from -6 to 6
- cache_lengths: int32 [512], P(('side', 'rep', 'tp')), may hold values from 1 to 128, 8320 in all
Outputs:
- new_master: float32 [8192, 2048], P('tp', 'rep')
- new_first: bfloat16 [8192, 2048], P('tp', 'rep')
- new_second: bfloat16 [8192, 2048], P('tp', 'rep')
- attended: bfloat16 [512, 8192], P(('side', 'rep', 'tp'))
Inputs may be any that keep to these rules, and one draw needn't show every extreme that they name: `cache_lengths`: the largest length is 128.
All inputs are finite; a program needn't handle non-finite values. No bound on the sum of `cache_lengths` on one device may be relied on, other than what follows from the above.
Results may differ from a plain program's by a relative error of at most 0.009.
Values may be sent and summed in bfloat16 or wider, within the bound.
No kernel may reach another device: no remote copies, remote signals or barrier semaphores. Data moves between devices by JAX's collectives and lax.ppermute only.
A program may use at most 64 MiB of HBM per device.

v0:
```python
import jax
import jax.numpy as jnp
from jax import lax
from jax.sharding import PartitionSpec as P

QUERY_HEADS = 64
KEY_VALUE_HEADS = 8
HEAD_SIZE = 128
STEP = 10


BETA_FIRST = 0.9
BETA_SECOND = 0.95
ADAM_EPSILON = 1e-08
LEARN_RATE = 0.001
DECAY_RATE = 0.1


def adamw(master, first_moment, second_moment, gradient):
    first_full = BETA_FIRST * first_moment.astype(jnp.float32) + (1.0 - BETA_FIRST) * gradient
    second_full = (
        BETA_SECOND * second_moment.astype(jnp.float32) + (1.0 - BETA_SECOND) * gradient * gradient
    )
    first_fix = 1.0 - BETA_FIRST**STEP
    second_fix = 1.0 - BETA_SECOND**STEP
    update = first_full / first_fix / (jnp.sqrt(second_full / second_fix) + ADAM_EPSILON)
    master_new = master - LEARN_RATE * (update + DECAY_RATE * master)
    return (master_new, first_full.astype(jnp.bfloat16), second_full.astype(jnp.bfloat16))


def attend(queries, key_cache_slots, value_cache_slots, cache_lengths, fresh_output):
    decode_row_count = queries.shape[0]
    slot_length = key_cache_slots.shape[1]
    query_groups = QUERY_HEADS // KEY_VALUE_HEADS
    query_head_rows = queries.reshape(decode_row_count, KEY_VALUE_HEADS, query_groups, HEAD_SIZE)
    stored_keys = key_cache_slots.reshape(decode_row_count, slot_length, KEY_VALUE_HEADS, HEAD_SIZE)
    stored_values = value_cache_slots.reshape(
        decode_row_count, slot_length, KEY_VALUE_HEADS, HEAD_SIZE
    )
    newest_keys = fresh_output[:, : KEY_VALUE_HEADS * HEAD_SIZE].reshape(
        decode_row_count, KEY_VALUE_HEADS, HEAD_SIZE
    )
    newest_values = fresh_output[:, KEY_VALUE_HEADS * HEAD_SIZE :].reshape(
        decode_row_count, KEY_VALUE_HEADS, HEAD_SIZE
    )
    score_scale = HEAD_SIZE ** (-0.5)
    scores = (
        jnp.einsum(
            "bkgd,blkd->bkgl", query_head_rows, stored_keys, preferred_element_type=jnp.float32
        )
        * score_scale
    )
    visible = jnp.arange(slot_length, dtype=jnp.int32)[None, :] < cache_lengths[:, None]
    scores = jnp.where(visible[:, None, None, :], scores, -1e30)
    self_score = (
        jnp.einsum(
            "zwai,zwi->zwa", query_head_rows, newest_keys, preferred_element_type=jnp.float32
        )
        * score_scale
    )
    highest = jnp.maximum(jnp.max(scores, axis=-1), self_score)
    weights = jnp.exp(scores - highest[..., None])
    own_weight = jnp.exp(self_score - highest)
    denominator = jnp.sum(weights, axis=-1) + own_weight
    probabilities = (weights / denominator[..., None]).astype(jnp.bfloat16)
    own_prob = (own_weight / denominator).astype(jnp.bfloat16)
    mixed = jnp.einsum(
        "bkgl,blkd->bkgd", probabilities, stored_values, preferred_element_type=jnp.float32
    )
    mixed = (
        mixed
        + own_prob.astype(jnp.float32)[..., None] * newest_values.astype(jnp.float32)[:, :, None, :]
    )
    return mixed.reshape(decode_row_count, QUERY_HEADS * HEAD_SIZE).astype(jnp.bfloat16)


def contract_rows(left, right):
    return lax.dot_general(
        left, right, (((0,), (0,)), ((), ())), preferred_element_type=jnp.float32
    )


def local(
    learn_inputs,
    learn_grads,
    kv_master,
    first_moment,
    second_moment,
    decode_inputs,
    queries,
    key_cache_slots,
    value_cache_slots,
    cache_lengths,
):
    inputs_own = learn_inputs[0]
    grads_own = learn_grads[0]
    group_term = contract_rows(inputs_own, lax.all_gather(grads_own, "tp", axis=0, tiled=True))
    own_term = lax.psum_scatter(group_term, "rep", scatter_dimension=1, tiled=True)
    gradient = lax.psum(own_term, "side")
    master_new, first_new, second_new = adamw(kv_master, first_moment, second_moment, gradient)
    rounded_weights = master_new.astype(jnp.bfloat16)
    partial_sums = jnp.dot(
        decode_inputs,
        lax.all_gather(rounded_weights, "rep", axis=1, tiled=True),
        preferred_element_type=jnp.float32,
    )
    fresh_all = lax.psum(partial_sums, "tp").astype(jnp.bfloat16)
    local_count = queries.shape[0]
    fresh_output = lax.dynamic_slice_in_dim(
        fresh_all, lax.axis_index("tp") * local_count, local_count, 0
    )
    attended = attend(queries, key_cache_slots, value_cache_slots, cache_lengths, fresh_output)
    return (master_new, first_new, second_new, attended)


def solution(mesh):
    placed = (
        P("side", "rep", "tp"),
        P("side", ("rep", "tp"), None),
        P("tp", "rep"),
        P("tp", "rep"),
        P("tp", "rep"),
        P(("side", "rep"), "tp"),
        P(("side", "rep", "tp"), None),
        P(("side", "rep", "tp"), None, None),
        P(("side", "rep", "tp"), None, None),
        P(("side", "rep", "tp")),
    )
    return jax.shard_map(
        local,
        mesh=mesh,
        in_specs=placed,
        out_specs=(P("tp", "rep"), P("tp", "rep"), P("tp", "rep"), P(("side", "rep", "tp"), None)),
        check_vma=False,
    )
```

profile of v0, /device:TPU:4, one launch (start us, length us, event | category | flops | bytes accessed | tf_op | source)
XLA Modules:
  0.0 397.3 jit_solution(9312091367250627962)
XLA Ops:
  7.2 0.0 copy-start
  7.2 0.0 all-gather.6.cloned.1.call-start
  7.2 0.7 all-gather.6.cloned.1.call-update
  7.9 0.0 reduce-scatter.2.cloned.1.call-start
  8.0 141.0 %all-gather.6.cloned.1.call-done = bf16[1,1024,2048]{2,1,0:T(8,128)(2,1)} async-done(((bf16[1,64,2048]{2,1,0:T(8,128)(2,1)}), bf16[1,1024,2048]{2,1,0:T(8,128)(2,1)}) %all-gather.6.cloned.1.call-update) | async-done | bytes 4194320 | tf_op jit(solution)/shard_map/all_gather | solution.py:97
  149.0 6.5 %fusion = f32[512,2048]{1,0:T(8,128)} fusion(bf16[1,1024,2048]{2,1,0:T(8,128)(2,1)} %all-gather.6.cloned.1.call-done, bf16[1,1024,512]{2,1,0:T(8,128)(2,1)S(1)} %copy-done), kind=kOutput, calls=%fused_computation | convolution fusion | flops 2147483648 | bytes 9437184 | tf_op jit(solution)/shard_map/dot_general | solution.py:78
  155.5 0.0 copy-start.7
  155.5 0.0 reduce-scatter.2.cloned.1.call-update
  155.6 0.0 all-reduce.3.cloned.1.call-start
  155.6 32.6 %reduce-scatter.2.cloned.1.call-done = f32[512,256]{1,0:T(8,128)} async-done(((f32[512,2048]{1,0:T(8,128)}), f32[512,256]{1,0:T(8,128)}) %reduce-scatter.2.cloned.1.call-update) | async-done | bytes 524304 | tf_op jit(solution)/shard_map/reduce_scatter | solution.py:98
  188.3 0.0 all-reduce.3.cloned.1.call-update
  188.3 0.0 all-gather.4.cloned.1.call-start
  188.3 64.8 %all-reduce.3.cloned.1.call-done = f32[512,256]{1,0:T(8,128)} async-done(((f32[512,256]{1,0:T(8,128)}), f32[512,256]{1,0:T(8,128)}) %all-reduce.3.cloned.1.call-update) | async-done | bytes 524304 | tf_op jit(solution)/shard_map/psum | solution.py:99
  253.1 2.7 fusion.18
  255.8 0.0 all-gather.4.cloned.1.call-update
  256.6 0.1 reduce.4
  256.7 0.3 fusion.19
  257.1 30.0 %all-gather.4.cloned.1.call-done = bf16[512,2048]{1,0:T(8,128)(2,1)} async-done(((bf16[512,256]{1,0:T(8,128)(2,1)}), bf16[512,2048]{1,0:T(8,128)(2,1)}) %all-gather.4.cloned.1.call-update) | async-done | bytes 2097168 | tf_op jit(solution)/shard_map/all_gather | solution.py:104
  287.1 2.0 convolution_bitcast_fusion
  289.1 100.4 %all-reduce.4 = bf16[16,2048]{1,0:T(8,128)(2,1)S(1)} all-reduce(f32[16,2048]{1,0:T(8,128)S(1)} %convolution_bitcast_fusion), channel_id=1, replica_groups=mesh['side'=4,'rep'=8,'tp'=16] {'tp'}, use_global_device_ids=true, to_apply=%region_3.4 | all-reduce | flops 32768 | bytes 196608 | tf_op jit(solution)/shard_map/psum | solution.py:107
  389.5 0.1 fusion.11
  389.7 0.2 fusion.10
  389.8 0.2 fusion.3
  390.1 0.6 convert_element_type.68
  (21 shorter events, 0.2 us)
Async XLA Ops:
  7.2 141.8 %copy-start = (bf16[1,1024,512]{2,1,0:T(8,128)(2,1)S(1)}, bf16[1,1024,512]{2,1,0:T(8,128)(2,1)}, u32[]{:S(2)}) copy-start(bf16[1,1024,512]{2,1,0:T(8,128)(2,1)} %param.10) | copy-start | bytes 3145732
  7.2 141.8 %all-gather.6.cloned.1.call-start = ((), (), s32[]{:S(2)}) async-start(), calls=%async_computation.4 | async-start | bytes 4456448 | tf_op jit(solution)/shard_map/all_gather | solution.py:97
  7.9 180.3 %reduce-scatter.2.cloned.1.call-start = ((), (), s32[]{:S(2)}) async-start(), calls=%async_computation.1 | async-start | bytes 4718592 | tf_op jit(solution)/shard_map/reduce_scatter | solution.py:98
  155.5 97.6 %copy-start.1 = (f32[512,256]{1,0:T(8,128)S(1)}, f32[512,256]{1,0:T(8,128)}, u32[]{:S(2)}) copy-start(f32[512,256]{1,0:T(8,128)} %param.12) | copy-start | bytes 1572868
  155.5 97.6 %copy-start.4 = (bf16[512,256]{1,0:T(8,128)(2,1)S(1)}, bf16[512,256]{1,0:T(8,128)(2,1)}, u32[]{:S(2)}) copy-start(bf16[512,256]{1,0:T(8,128)(2,1)} %param.14) | copy-start | bytes 786436
  155.5 97.6 %copy-start.5 = (bf16[512,256]{1,0:T(8,128)(2,1)S(1)}, bf16[512,256]{1,0:T(8,128)(2,1)}, u32[]{:S(2)}) copy-start(bf16[512,256]{1,0:T(8,128)(2,1)} %param.13) | copy-start | bytes 786436
  155.5 100.4 %copy-start.2 = (bf16[1,128,1024]{2,1,0:T(8,128)(2,1)S(1)}, bf16[1,128,1024]{2,1,0:T(8,128)(2,1)}, u32[]{:S(2)}) copy-start(bf16[1,128,1024]{2,1,0:T(8,128)(2,1)} %param.18) | copy-start | bytes 786436
  155.5 100.4 %copy-start.3 = (bf16[1,128,1024]{2,1,0:T(8,128)(2,1)S(1)}, bf16[1,128,1024]{2,1,0:T(8,128)(2,1)}, u32[]{:S(2)}) copy-start(bf16[1,128,1024]{2,1,0:T(8,128)(2,1)} %param.17) | copy-start | bytes 786436
  155.5 101.1 %copy-start.6 = (bf16[1,8192]{1,0:T(2,128)(2,1)S(1)}, bf16[1,8192]{1,0:T(2,128)(2,1)}, u32[]{:S(2)}) copy-start(bf16[1,8192]{1,0:T(2,128)(2,1)} %param.16) | copy-start | bytes 49156
  155.5 131.6 %copy-start.7 = (bf16[16,512]{1,0:T(8,128)(2,1)S(1)}, bf16[16,512]{1,0:T(8,128)(2,1)}, u32[]{:S(2)}) copy-start(bf16[16,512]{1,0:T(8,128)(2,1)} %param.15) | copy-start | bytes 49156
  155.6 97.5 %all-reduce.3.cloned.1.call-start = ((), (), s32[]{:S(2)}) async-start(), calls=%async_computation.2 | async-start | bytes 1048576 | tf_op jit(solution)/shard_map/psum | solution.py:99
  188.3 98.8 %all-gather.4.cloned.1.call-start = ((), (), s32[]{:S(2)}) async-start(), calls=%async_computation.3 | async-start | bytes 2359296 | tf_op jit(solution)/shard_map/all_gather | solution.py:104
Sparse Core Ops, SparseCore 0:
  11.2 137.7 all-gather.5
  155.7 32.5 reduce-scatter.1
  191.2 61.8 all-reduce.2
  256.0 31.0 all-gather.3
where the time goes:
time: 398 us; the launch traced here: 397 us
  waiting for transfers between devices  269 us (68%)
  blocking collectives  100 us (25%)
  between operations  14.5 us (4%)
  matrix products  9.15 us (2%)
    all_gather x1, waiting for transfers between devices, local(): lax.all_gather(grads_own, 'tp', axis=0, tiled=True)  141 us
    psum x1, blocking collectives, local(): fresh_all = lax.psum(partial_sums, 'tp').astype(jnp.bfloat16)  100 us
    psum x1, waiting for transfers between devices, local(): gradient = lax.psum(own_term, 'side')  64.8 us
    reduce_scatter x1, waiting for transfers between devices, local(): lax.psum_scatter(group_term, 'rep', scatter_dimension=1, tiled=True)  32.6 us
    all_gather x1, waiting for transfers between devices, local(): lax.all_gather(rounded_weights, 'rep', axis=1, tiled=True)  30 us
  transfers between devices with their start and end apart: 4, of which 4 were waited for; matrix products, arithmetic and copies ran while one was open for 0% of the time, Pallas kernels for 0%

commit v1 on v0

--- a/solution.py
+++ b/solution.py
@@ -1,6 +1,7 @@
 import jax
 import jax.numpy as jnp
 from jax import lax
+from jax.sharding import Mesh
 from jax.sharding import PartitionSpec as P
 
 QUERY_HEADS = 64
@@ -74,10 +75,18 @@
     return mixed.reshape(decode_row_count, QUERY_HEADS * HEAD_SIZE).astype(jnp.bfloat16)
 
 
-def contract_rows(left, right):
-    return lax.dot_general(
-        left, right, (((0,), (0,)), ((), ())), preferred_element_type=jnp.float32
-    )
+FINE_AXES = ("side", "x", "core", "zhi", "y")
+REP = ("x", "core")
+TP = ("zhi", "y")
+
+
+def pick_core(columns, core):
+    return lax.dynamic_index_in_dim(columns, core, axis=2, keepdims=False)
+
+
+def gather_cotangents(pieces):
+    pairs = lax.all_gather(pieces, "zhi", axis=1)
+    return lax.all_gather(pairs, "y", axis=2)
 
 
 def local(
@@ -92,44 +101,60 @@
     value_cache_slots,
     cache_lengths,
 ):
+    core = lax.axis_index("core")
+    swap = [(0, 1), (1, 0)]
     inputs_own = learn_inputs[0]
-    grads_own = learn_grads[0]
-    group_term = contract_rows(inputs_own, lax.all_gather(grads_own, "tp", axis=0, tiled=True))
-    own_term = lax.psum_scatter(group_term, "rep", scatter_dimension=1, tiled=True)
-    gradient = lax.psum(own_term, "side")
+    row_count, feature_count = inputs_own.shape
+    x_count, side_count = lax.axis_size("x"), lax.axis_size("side")
+    block_width = kv_master.shape[1]
+    columns = learn_grads[0].reshape(-1, x_count, 2, block_width)
+    grads_other = lax.ppermute(pick_core(columns, 1 - core), "core", swap)
+    pieces = jnp.stack([pick_core(columns, core), grads_other])
+    inputs_other = lax.ppermute(inputs_own, "core", swap)
+    gathered = gather_cotangents(pieces)
+    grads_all = gathered.reshape(2, row_count, x_count, block_width)
+    inputs_all = jnp.stack([inputs_own, inputs_other])
+    partial = jnp.einsum(
+        "prf,prxc->xfc", inputs_all, grads_all, preferred_element_type=jnp.float32
+    ).astype(jnp.bfloat16)
+    quarter = feature_count // side_count
+    partial = partial.reshape(x_count * side_count, quarter, block_width)
+    terms = lax.all_to_all(partial, ("x", "side"), 0, 0, tiled=True)
+    own_quarter = jnp.sum(terms.astype(jnp.float32), axis=0).astype(jnp.bfloat16)
+    spread = jnp.broadcast_to(own_quarter[None], (side_count, quarter, block_width))
+    gradient = lax.all_to_all(spread, "side", 0, 0, tiled=True)
+    gradient = gradient.reshape(feature_count, block_width).astype(jnp.float32)
     master_new, first_new, second_new = adamw(kv_master, first_moment, second_moment, gradient)
     rounded_weights = master_new.astype(jnp.bfloat16)
-    partial_sums = jnp.dot(
-        decode_inputs,
-        lax.all_gather(rounded_weights, "rep", axis=1, tiled=True),
-        preferred_element_type=jnp.float32,
-    )
-    fresh_all = lax.psum(partial_sums, "tp").astype(jnp.bfloat16)
-    local_count = queries.shape[0]
-    fresh_output = lax.dynamic_slice_in_dim(
-        fresh_all, lax.axis_index("tp") * local_count, local_count, 0
-    )
+    decode_rows = lax.all_gather(decode_inputs, REP, axis=0, tiled=True)
+    partial_fresh = jnp.dot(decode_rows, rounded_weights, preferred_element_type=jnp.float32)
+    rep_count, tp_count = lax.axis_size(REP), lax.axis_size(TP)
+    partial_fresh = partial_fresh.reshape(rep_count, tp_count, block_width)
+    fresh_terms = lax.all_to_all(partial_fresh, TP, 1, 1, tiled=True)
+    fresh_block = jnp.sum(fresh_terms, axis=1).astype(jnp.bfloat16)
+    fresh_output = lax.all_to_all(fresh_block, REP, 0, 0, tiled=True).reshape(1, -1)
     attended = attend(queries, key_cache_slots, value_cache_slots, cache_lengths, fresh_output)
     return (master_new, first_new, second_new, attended)
 
 
 def solution(mesh):
+    fine = Mesh(mesh.devices.reshape(mesh.devices.shape[0], -1, 2, 2, 8), FINE_AXES)
     placed = (
-        P("side", "rep", "tp"),
-        P("side", ("rep", "tp"), None),
-        P("tp", "rep"),
-        P("tp", "rep"),
-        P("tp", "rep"),
-        P(("side", "rep"), "tp"),
-        P(("side", "rep", "tp"), None),
-        P(("side", "rep", "tp"), None, None),
-        P(("side", "rep", "tp"), None, None),
-        P(("side", "rep", "tp")),
+        P("side", REP, TP),
+        P("side", REP + TP, None),
+        P(TP, REP),
+        P(TP, REP),
+        P(TP, REP),
+        P(("side",) + REP, TP),
+        P(("side",) + REP + TP, None),
+        P(("side",) + REP + TP, None, None),
+        P(("side",) + REP + TP, None, None),
+        P(("side",) + REP + TP),
     )
     return jax.shard_map(
         local,
-        mesh=mesh,
+        mesh=fine,
         in_specs=placed,
-        out_specs=(P("tp", "rep"), P("tp", "rep"), P("tp", "rep"), P(("side", "rep", "tp"), None)),
+        out_specs=(P(TP, REP), P(TP, REP), P(TP, REP), P(("side",) + REP + TP, None)),
         check_vma=False,
     )

time: 398 us -> 192 us (0.48)
  the two profiles are of different devices: /device:TPU:4 before, /device:TPU:1 now
where the time goes in v1:
time: 192 us
  waiting for transfers between devices  73.2 us (38%)
  blocking collectives  62.7 us (33%)
  starting transfers between devices  27.6 us (14%)
  between operations  14.9 us (8%)
  local copies, waits for them, and re-layouts  5.76 us (3%)
  matrix products  5.41 us (3%)
  other arithmetic  2.43 us (1%)
    all_gather x1, waiting for transfers between devices, gather_cotangents(): return lax.all_gather(pairs, 'y', axis=2)  55.3 us
    all_to_all x1, blocking collectives, local(): terms = lax.all_to_all(partial, ('x', 'side'), 0, 0, tiled=True)  34.2 us
    all_gather x1, blocking collectives, local(): decode_rows = lax.all_gather(decode_inputs, REP, axis=0, tiled=True)  14.3 us
    all_gather x1, blocking collectives, gather_cotangents(): pairs = lax.all_gather(pieces, 'zhi', axis=1)  14.1 us
    all_to_all x1, waiting for transfers between devices, local(): fresh_terms = lax.all_to_all(partial_fresh, TP, 1, 1, tiled=True)  10.5 us
    ppermute x1, starting transfers between devices, local(): grads_other = lax.ppermute(pick_core(columns, 1 - core), 'core', swap)  8.79 us
    all_to_all x1, starting transfers between devices, local(): fresh_terms = lax.all_to_all(partial_fresh, TP, 1, 1, tiled=True)  7.14 us
    all_to_all x1, starting transfers between devices, local(): lax.all_to_all(fresh_block, REP, 0, 0, tiled=True).reshape(1, -1)  4.95 us
  transfers between devices with their start and end apart: 6, of which 5 were waited for; matrix products, arithmetic and copies ran while one was open for 0% of the time, Pallas kernels for 0%

profile of v1, /device:TPU:1, one launch (start us, length us, event | category | flops | bytes accessed | tf_op | source)
XLA Modules:
  0.0 192.0 jit_solution(7206271749576300181)
XLA Ops:
  7.2 1.2 reshape_squeeze.3
  8.5 0.6 constant_dynamic-slice_fusion.1
  9.1 8.8 %collective-permute-start = (bf16[64,4,256]{2,0,1:T(8,128)(2,1)S(1)}, bf16[64,4,256]{2,0,1:T(8,128)(2,1)S(1)}, u32[]{:S(2)}, u32[]{:S(2)}) collective-permute-start(bf16[64,4,256]{2,0,1:T(8,128)(2,1)S(1)} %bitcast.73), channel_id=1, source_target_pairs={{0,16},{16,0},{1,17},{17,1},{2,18},{18,2},{3,19},{19,3},{4,20},{20... | collective-permute-start | bytes 393224 | tf_op jit(solution)/shard_map/ppermute | solution.py:111
  17.9 0.9 collective-permute-done
  18.9 14.1 %all-gather = bf16[2,128,4,256]{3,1,2,0:T(8,128)(2,1)} all-gather(bf16[2,64,4,256]{3,1,2,0:T(8,128)(2,1)S(1)} %pad_maximum_fusion), channel_id=2, replica_groups=mesh['side'=4,'x'=4,'core'=2,'zhi'=2,'y'=8] {'zhi'}, dimensions={1}, use_global_device_ids=true | all-gather | bytes 786432 | tf_op jit(solution)/shard_map/all_gather | solution.py:88
  33.0 3.1 %collective-permute-start.1 = (bf16[1024,512]{1,0:T(8,128)(2,1)S(1)}, bf16[1024,512]{1,0:T(8,128)(2,1)S(1)}, u32[]{:S(2)}, u32[]{:S(2)}) collective-permute-start(bf16[1024,512]{1,0:T(8,128)(2,1)S(1)} %bitcast.82), channel_id=1, source_target_pairs={{0,16},{16,0},{1,17},{17,1},{2,18},{18,2},{3,19},{19,3},{4,20},{20... | collective-permute-start | bytes 3145736 | tf_op jit(solution)/shard_map/ppermute | solution.py:113
  36.2 2.3 %collective-permute-done.1 = bf16[1024,512]{1,0:T(8,128)(2,1)S(1)} collective-permute-done((bf16[1024,512]{1,0:T(8,128)(2,1)S(1)}, bf16[1024,512]{1,0:T(8,128)(2,1)S(1)}, u32[]{:S(2)}, u32[]{:S(2)}) %collective-permute-start.1) | collective-permute-done | bytes 1048608 | tf_op jit(solution)/shard_map/ppermute | solution.py:113
  38.5 55.3 %all-gather.4.cloned.1.call-done = bf16[2,2,512,4,256]{4,2,1,3,0:T(8,128)(2,1)} async-done(((bf16[2,2,64,4,256]{4,2,1,3,0:T(8,128)(2,1)}), bf16[2,2,512,4,256]{4,2,1,3,0:T(8,128)(2,1)}) %all-gather.4.cloned.1.call-update) | async-done | bytes 4194320 | tf_op jit(solution)/shard_map/all_gather | solution.py:89
  93.8 4.5 %fusion.7 = bf16[4,512,256]{1,2,0:T(8,128)(2,1)S(1)} fusion(bf16[2,1024,4,256]{3,1,2,0:T(8,128)(2,1)} %bitcast.81, bf16[1,1024,512]{2,1,0:T(8,128)(2,1)S(1)} %bitcast.83, bf16[1,1024,512]{2,1,0:T(8,128)(2,1)S(1)} %copy-done.8), kind=kOutput, calls=%fused_computation.6 | convolution fusion | flops 2149056512 | bytes 7340032 | tf_op jit(solution)/shard_map/prf,prxc->xfc/dot_general | solution.py:117
  98.3 0.5 copy.36
  98.9 34.2 %all_to_all.21 = bf16[16,128,256]{2,1,0:T(8,128)(2,1)S(1)} all-to-all(bf16[16,128,256]{2,1,0:T(8,128)(2,1)S(1)} %bitcast.65), channel_id=1, replica_groups=mesh['side'=4,'x'=4,'core'=2,'zhi'=2,'y'=8] {'x','side'}, dimensions={0} | all-to-all | bytes 2097152 | tf_op jit(solution)/shard_map/all_to_all | solution.py:122
  133.3 0.7 broadcast_in_dim.10
  134.0 3.5 %all-to-all-start.1 = ((bf16[4,128,256]{2,1,0:T(8,128)(2,1)}), bf16[4,128,256]{2,1,0:T(8,128)(2,1)S(1)}, u32[]{:S(2)}, u32[]{:S(2)}) async-start(bf16[4,128,256]{2,1,0:T(8,128)(2,1)} %broadcast_in_dim.10), calls=%async_computation.1 | async-start | bytes 524288 | tf_op jit(solution)/shard_map/all_to_all | solution.py:125
  137.6 14.3 %all_gather.19 = bf16[128,512]{1,0:T(8,128)(2,1)S(1)} all-gather(bf16[16,512]{1,0:T(8,128)(2,1)S(1)} %copy-done.7), channel_id=1, replica_groups=mesh['side'=4,'x'=4,'core'=2,'zhi'=2,'y'=8] {'x','core'}, dimensions={0}, use_global_device_ids=true | all-gather | bytes 147456 | tf_op jit(solution)/shard_map/all_gather | solution.py:129
  151.9 1.3 fusion.15
  153.4 0.7 copy.38
  154.2 7.1 %all-to-all-start.2 = ((f32[8,16,256]{2,0,1:T(8,128)}), f32[8,16,256]{2,0,1:T(8,128)S(1)}, u32[]{:S(2)}, u32[]{:S(2)}) async-start(f32[8,16,256]{2,0,1:T(8,128)} %copy.38), calls=%async_computation.2 | async-start | bytes 262144 | tf_op jit(solution)/shard_map/all_to_all | solution.py:133
  162.1 10.5 %all-to-all-done.2 = f32[8,16,256]{2,0,1:T(8,128)S(1)} async-done(((f32[8,16,256]{2,0,1:T(8,128)}), f32[8,16,256]{2,0,1:T(8,128)S(1)}, u32[]{:S(2)}, u32[]{:S(2)}) %all-to-all-start.2) | async-done | bytes 131104 | tf_op jit(solution)/shard_map/all_to_all | solution.py:133
  172.7 0.5 broadcast.33
  173.2 0.6 reduce.6
  173.8 0.6 reshape.155
  174.4 5.0 %all-to-all-start.3 = ((bf16[8,2,128]{2,1,0:T(2,128)(2,1)}), bf16[8,2,128]{2,1,0:T(2,128)(2,1)S(1)}, u32[]{:S(2)}, u32[]{:S(2)}) async-start(bf16[8,2,128]{2,1,0:T(2,128)(2,1)} %reshape.155), calls=%async_computation.3 | async-start | bytes 8192 | tf_op jit(solution)/shard_map/all_to_all | solution.py:135
  179.8 4.1 %all-to-all-done.3 = bf16[8,2,128]{2,1,0:T(2,128)(2,1)S(1)} async-done(((bf16[8,2,128]{2,1,0:T(2,128)(2,1)}), bf16[8,2,128]{2,1,0:T(2,128)(2,1)S(1)}, u32[]{:S(2)}, u32[]{:S(2)}) %all-to-all-start.3) | async-done | bytes 4128 | tf_op jit(solution)/shard_map/all_to_all | solution.py:135
  184.5 0.6 convert_element_type.97
  (39 shorter events, 1.6 us)
Async XLA Ops:
  7.2 154.9 %copy-start = (bf16[1,8192]{1,0:T(2,128)(2,1)S(1)}, bf16[1,8192]{1,0:T(2,128)(2,1)}, u32[]{:S(2)}) copy-start(bf16[1,8192]{1,0:T(2,128)(2,1)} %param.16) | copy-start | bytes 49156
  7.2 86.6 %all-gather.4.cloned.1.call-start = ((), (), s32[]{:S(2)}) async-start(), calls=%async_computation.4 | async-start | bytes 4718592 | tf_op jit(solution)/shard_map/all_gather | solution.py:89
  7.2 25.8 %copy-start.8 = (bf16[1,1024,512]{2,1,0:T(8,128)(2,1)S(1)}, bf16[1,1024,512]{2,1,0:T(8,128)(2,1)}, u32[]{:S(2)}) copy-start(bf16[1,1024,512]{2,1,0:T(8,128)(2,1)} %param.10) | copy-start | bytes 3145732
  9.1 9.8 %collective-permute-start = (bf16[64,4,256]{2,0,1:T(8,128)(2,1)S(1)}, bf16[64,4,256]{2,0,1:T(8,128)(2,1)S(1)}, u32[]{:S(2)}, u32[]{:S(2)}) collective-permute-start(bf16[64,4,256]{2,0,1:T(8,128)(2,1)S(1)} %bitcast.73), channel_id=1, source_target_pairs={{0,16},{16,0},{1,17},{17,1},{2,18},{18,2},{3,19},{19,3},{4,20},{20... | collective-permute-start | bytes 393224 | tf_op jit(solution)/shard_map/ppermute | solution.py:111
  33.0 5.4 %collective-permute-start.1 = (bf16[1024,512]{1,0:T(8,128)(2,1)S(1)}, bf16[1024,512]{1,0:T(8,128)(2,1)S(1)}, u32[]{:S(2)}, u32[]{:S(2)}) collective-permute-start(bf16[1024,512]{1,0:T(8,128)(2,1)S(1)} %bitcast.82), channel_id=1, source_target_pairs={{0,16},{16,0},{1,17},{17,1},{2,18},{18,2},{3,19},{19,3},{4,20},{20... | collective-permute-start | bytes 3145736 | tf_op jit(solution)/shard_map/ppermute | solution.py:113
  98.9 38.7 %copy-start.7 = (bf16[16,512]{1,0:T(8,128)(2,1)S(1)}, bf16[16,512]{1,0:T(8,128)(2,1)}, u32[]{:S(2)}) copy-start(bf16[16,512]{1,0:T(8,128)(2,1)} %param.15) | copy-start | bytes 49156
  98.9 53.0 %copy-start.2 = (f32[512,256]{1,0:T(8,128)S(1)}, f32[512,256]{1,0:T(8,128)}, u32[]{:S(2)}) copy-start(f32[512,256]{1,0:T(8,128)} %param.12) | copy-start | bytes 1572868
  98.9 53.0 %copy-start.3 = (bf16[512,256]{1,0:T(8,128)(2,1)S(1)}, bf16[512,256]{1,0:T(8,128)(2,1)}, u32[]{:S(2)}) copy-start(bf16[512,256]{1,0:T(8,128)(2,1)} %param.14) | copy-start | bytes 786436
  98.9 53.0 %copy-start.4 = (bf16[512,256]{1,0:T(8,128)(2,1)S(1)}, bf16[512,256]{1,0:T(8,128)(2,1)}, u32[]{:S(2)}) copy-start(bf16[512,256]{1,0:T(8,128)(2,1)} %param.13) | copy-start | bytes 786436
  134.0 27.3 %copy-start.5 = (bf16[1,128,1024]{2,1,0:T(8,128)(2,1)S(1)}, bf16[1,128,1024]{2,1,0:T(8,128)(2,1)}, u32[]{:S(2)}) copy-start(bf16[1,128,1024]{2,1,0:T(8,128)(2,1)} %param.17) | copy-start | bytes 786436
  134.0 17.9 %all-to-all-start.1 = ((bf16[4,128,256]{2,1,0:T(8,128)(2,1)}), bf16[4,128,256]{2,1,0:T(8,128)(2,1)S(1)}, u32[]{:S(2)}, u32[]{:S(2)}) async-start(bf16[4,128,256]{2,1,0:T(8,128)(2,1)} %broadcast_in_dim.10), calls=%async_computation.1 | async-start | bytes 524288 | tf_op jit(solution)/shard_map/all_to_all | solution.py:125
  151.9 27.8 %copy-start.6 = (bf16[1,128,1024]{2,1,0:T(8,128)(2,1)S(1)}, bf16[1,128,1024]{2,1,0:T(8,128)(2,1)}, u32[]{:S(2)}) copy-start(bf16[1,128,1024]{2,1,0:T(8,128)(2,1)} %param.18) | copy-start | bytes 786436
  153.2 31.9 %copy-start.1 = (f32[512,256]{1,0:T(8,128)}, f32[512,256]{1,0:T(8,128)S(1)}, u32[]{:S(2)}) copy-start(f32[512,256]{1,0:T(8,128)S(1)} %get-tuple-element.5) | copy-start | bytes 1572868
  154.2 18.5 %all-to-all-start.2 = ((f32[8,16,256]{2,0,1:T(8,128)}), f32[8,16,256]{2,0,1:T(8,128)S(1)}, u32[]{:S(2)}, u32[]{:S(2)}) async-start(f32[8,16,256]{2,0,1:T(8,128)} %copy.38), calls=%async_computation.2 | async-start | bytes 262144 | tf_op jit(solution)/shard_map/all_to_all | solution.py:133
  174.4 9.5 %all-to-all-start.3 = ((bf16[8,2,128]{2,1,0:T(2,128)(2,1)}), bf16[8,2,128]{2,1,0:T(2,128)(2,1)S(1)}, u32[]{:S(2)}, u32[]{:S(2)}) async-start(bf16[8,2,128]{2,1,0:T(2,128)(2,1)} %reshape.155), calls=%async_computation.3 | async-start | bytes 8192 | tf_op jit(solution)/shard_map/all_to_all | solution.py:135
Sparse Core Ops, SparseCore 0:
  33.2 60.5 all-gather.3

commit v2 on v1

--- a/solution.py
+++ b/solution.py
@@ -78,15 +78,28 @@
 FINE_AXES = ("side", "x", "core", "zhi", "y")
 REP = ("x", "core")
 TP = ("zhi", "y")
+CHUNKS = 2
 
 
-def pick_core(columns, core):
-    return lax.dynamic_index_in_dim(columns, core, axis=2, keepdims=False)
+def swap_over(array, axis):
+    return lax.ppermute(array, axis, [(0, 1), (1, 0)])
 
 
-def gather_cotangents(pieces):
-    pairs = lax.all_gather(pieces, "zhi", axis=1)
-    return lax.all_gather(pairs, "y", axis=2)
+def other_features(inputs_own):
+    half = lax.axis_index("zhi")
+    halves = inputs_own.reshape(2, -1, inputs_own.shape[1])
+    kept = lax.dynamic_index_in_dim(halves, half, 0, keepdims=False)
+    received = swap_over(lax.dynamic_index_in_dim(halves, 1 - half, 0, keepdims=False), "zhi")
+    return kept, received
+
+
+def ordered(kept, received, axis):
+    first = lax.axis_index("zhi") == 0
+    return jnp.stack([jnp.where(first, kept, received), jnp.where(first, received, kept)], axis)
+
+
+def summed(terms):
+    return jnp.sum(terms.astype(jnp.float32), axis=0).astype(jnp.bfloat16)
 
 
 def local(
@@ -102,37 +115,47 @@
     cache_lengths,
 ):
     core = lax.axis_index("core")
-    swap = [(0, 1), (1, 0)]
     inputs_own = learn_inputs[0]
-    row_count, feature_count = inputs_own.shape
+    feature_count = inputs_own.shape[1]
     x_count, side_count = lax.axis_size("x"), lax.axis_size("side")
     block_width = kv_master.shape[1]
-    columns = learn_grads[0].reshape(-1, x_count, 2, block_width)
-    grads_other = lax.ppermute(pick_core(columns, 1 - core), "core", swap)
-    pieces = jnp.stack([pick_core(columns, core), grads_other])
-    inputs_other = lax.ppermute(inputs_own, "core", swap)
-    gathered = gather_cotangents(pieces)
-    grads_all = gathered.reshape(2, row_count, x_count, block_width)
-    inputs_all = jnp.stack([inputs_own, inputs_other])
-    partial = jnp.einsum(
-        "prf,prxc->xfc", inputs_all, grads_all, preferred_element_type=jnp.float32
-    ).astype(jnp.bfloat16)
+    chunk_width = block_width // CHUNKS
     quarter = feature_count // side_count
-    partial = partial.reshape(x_count * side_count, quarter, block_width)
-    terms = lax.all_to_all(partial, ("x", "side"), 0, 0, tiled=True)
-    own_quarter = jnp.sum(terms.astype(jnp.float32), axis=0).astype(jnp.bfloat16)
-    spread = jnp.broadcast_to(own_quarter[None], (side_count, quarter, block_width))
-    gradient = lax.all_to_all(spread, "side", 0, 0, tiled=True)
-    gradient = gradient.reshape(feature_count, block_width).astype(jnp.float32)
+
+    columns = learn_grads[0].reshape(-1, x_count, 2, CHUNKS, chunk_width)
+    grads_other = swap_over(
+        lax.dynamic_index_in_dim(columns, 1 - core, axis=2, keepdims=False), "core"
+    )
+    grads_own = lax.dynamic_index_in_dim(columns, core, axis=2, keepdims=False)
+    kept, received = other_features(inputs_own)
+    kept_pair = jnp.stack([kept, swap_over(kept, "core")])
+    received_pair = jnp.stack([received, swap_over(received, "core")])
+    inputs_all = ordered(kept_pair, received_pair, 2)
+    decode_rows = lax.all_gather(decode_inputs, REP, axis=0, tiled=True)
+    inputs_all, decode_rows = lax.optimization_barrier((inputs_all, decode_rows))
+
+    gradients = []
+    for chunk in range(CHUNKS):
+        piece = jnp.stack([grads_own[:, :, chunk], grads_other[:, :, chunk]])
+        grads_all = lax.all_gather(piece, "y", axis=1, tiled=True)
+        partial = jnp.einsum(
+            "prhf,prxn->xhfn", inputs_all, grads_all, preferred_element_type=jnp.float32
+        ).astype(jnp.bfloat16)
+        partial = partial.reshape(x_count, 2 * feature_count, chunk_width)
+        over_x = summed(lax.all_to_all(partial, "x", 0, 0, tiled=True))
+        over_x = over_x.reshape(2 * side_count, quarter, chunk_width)
+        own_quarter = summed(lax.all_to_all(over_x, ("zhi", "side"), 0, 0, tiled=True))
+        spread = jnp.broadcast_to(own_quarter[None], (side_count, quarter, chunk_width))
+        gradients.append(lax.all_to_all(spread, "side", 0, 0, tiled=True).reshape(feature_count, chunk_width))
+    gradient = jnp.concatenate(gradients, axis=1).astype(jnp.float32)
     master_new, first_new, second_new = adamw(kv_master, first_moment, second_moment, gradient)
     rounded_weights = master_new.astype(jnp.bfloat16)
-    decode_rows = lax.all_gather(decode_inputs, REP, axis=0, tiled=True)
     partial_fresh = jnp.dot(decode_rows, rounded_weights, preferred_element_type=jnp.float32)
-    rep_count, tp_count = lax.axis_size(REP), lax.axis_size(TP)
-    partial_fresh = partial_fresh.reshape(rep_count, tp_count, block_width)
-    fresh_terms = lax.all_to_all(partial_fresh, TP, 1, 1, tiled=True)
-    fresh_block = jnp.sum(fresh_terms, axis=1).astype(jnp.bfloat16)
-    fresh_output = lax.all_to_all(fresh_block, REP, 0, 0, tiled=True).reshape(1, -1)
+    partial_fresh = partial_fresh.astype(jnp.bfloat16).reshape(-1, 2, block_width // 2)
+    fresh_terms = lax.all_to_all(partial_fresh, REP + TP, 0, 0, tiled=True)
+    fresh_terms = fresh_terms.reshape(lax.axis_size(REP), lax.axis_size(TP), block_width)
+    fresh_output = jnp.sum(fresh_terms.astype(jnp.float32), axis=1).astype(jnp.bfloat16)
+    fresh_output = fresh_output.reshape(1, -1)
     attended = attend(queries, key_cache_slots, value_cache_slots, cache_lengths, fresh_output)
     return (master_new, first_new, second_new, attended)
 

time: 192 us -> 208 us (1.083)
  blocking collectives: 62.7 us -> 12.6 us
  starting transfers between devices: 27.6 us -> 63.5 us
  waiting for transfers between devices: 73.2 us -> 96.2 us
  other arithmetic: 2.43 us -> 5.24 us
  local copies, waits for them, and re-layouts: 5.76 us -> 8.02 us
    all_to_all x3 -> x7, waiting for transfers between devices: 14.6 us -> 49.4 us  [the longest x2 17.6 us: local(): lax.all_to_all(over_x, ('zhi', 'side'), 0, 0, tiled=True)]
    all_to_all x1 -> x0, blocking collectives: 34.2 us -> none  [local(): terms = lax.all_to_all(partial, ('x', 'side'), 0, 0, tiled=True)]
    all_to_all x3 -> x7, starting transfers between devices: 15.6 us -> 43.6 us  [the longest x1 18.3 us: local(): fresh_terms = lax.all_to_all(partial_fresh, REP + TP, 0, 0, tiled=True)]
    all_gather x1 -> x2, waiting for transfers between devices: 55.3 us -> 29.6 us  [local(): grads_all = lax.all_gather(piece, 'y', axis=1, tiled=True)]
    all_gather x1 -> x0, blocking collectives: 14.1 us -> none  [gather_cotangents(): pairs = lax.all_gather(pieces, 'zhi', axis=1)]
    ppermute x2 -> x4, waiting for transfers between devices: 3.18 us -> 17.1 us  [swap_over(): return lax.ppermute(array, axis, [(0, 1), (1, 0)])]
    ppermute x2 -> x4, starting transfers between devices: 11.9 us -> 19.8 us  [swap_over(): return lax.ppermute(array, axis, [(0, 1), (1, 0)])]
    convert_element_type x2, local copies, waits for them, and re-layouts: 1.04 us -> 3.61 us  [local(): partial = jnp.einsum('prhf,prxn->xhfn', inputs_all, grads_all, preferred_...]
  transfers between devices with their start and end apart: 6 -> 13, of which waited for: 5 -> 9; matrix products, arithmetic and copies ran while one was open for 0% -> 6% of each run, Pallas kernels for 0% -> 0%
where the time goes in v2:
time: 208 us; the launch traced here: 207 us
  waiting for transfers between devices  96.2 us (46%)
  starting transfers between devices  63.5 us (31%)
  between operations  15 us (7%)
  blocking collectives  12.6 us (6%)
  local copies, waits for them, and re-layouts  8.02 us (4%)
  matrix products  6.81 us (3%)
  other arithmetic  5.24 us (3%)
    all_gather x2, waiting for transfers between devices, local(): grads_all = lax.all_gather(piece, 'y', axis=1, tiled=True)  29.6 us
    ppermute x4, starting transfers between devices, swap_over(): return lax.ppermute(array, axis, [(0, 1), (1, 0)])  19.8 us
    all_to_all x1, starting transfers between devices, local(): fresh_terms = lax.all_to_all(partial_fresh, REP + TP, 0, 0, tiled=True)  18.3 us
    all_to_all x2, waiting for transfers between devices, local(): lax.all_to_all(over_x, ('zhi', 'side'), 0, 0, tiled=True)  17.6 us
    ppermute x4, waiting for transfers between devices, swap_over(): return lax.ppermute(array, axis, [(0, 1), (1, 0)])  17.1 us
    all_to_all x1, waiting for transfers between devices, local(): fresh_terms = lax.all_to_all(partial_fresh, REP + TP, 0, 0, tiled=True)  13.9 us
    all_gather x1, blocking collectives, local(): decode_rows = lax.all_gather(decode_inputs, REP, axis=0, tiled=True)  12.6 us
    all_to_all x2, starting transfers between devices, local(): lax.all_to_all(over_x, ('zhi', 'side'), 0, 0, tiled=True)  10.4 us
  transfers between devices with their start and end apart: 13, of which 9 were waited for; matrix products, arithmetic and copies ran while one was open for 6% of the time, Pallas kernels for 0%

profile of v2, /device:TPU:1, one launch (start us, length us, event | category | flops | bytes accessed | tf_op | source)
XLA Modules:
  0.0 207.3 jit_solution(17496301983239665811)
XLA Ops:
  8.7 8.8 %collective-permute-start = (bf16[64,4,2,128]{3,0,1,2:T(8,128)(2,1)S(1)}, bf16[64,4,2,128]{3,0,1,2:T(8,128)(2,1)S(1)}, u32[]{:S(2)}, u32[]{:S(2)}) collective-permute-start(bf16[64,4,2,128]{3,0,1,2:T(8,128)(2,1)S(1)} %bitcast.107), channel_id=1, source_target_pairs={{0,16},{16,0},{1,17},{17,1},{2,18},{18,2},{3,19},{19,3},{4,20},{20... | collective-permute-start | bytes 393224 | tf_op jit(solution)/shard_map/ppermute | solution.py:85
  19.3 5.3 %collective-permute-start.2 = (bf16[512,512]{1,0:T(8,128)(2,1)S(1)}, bf16[512,512]{1,0:T(8,128)(2,1)S(1)}, u32[]{:S(2)}, u32[]{:S(2)}) collective-permute-start(bf16[512,512]{1,0:T(8,128)(2,1)S(1)} %get-tuple-element.12), channel_id=1, source_target_pairs={{0,8},{8,0},{1,9},{9,1},{2,10},{10,2},{3,11},{11,3},{4,12},{12,4},... | collective-permute-start | bytes 1572872 | tf_op jit(solution)/shard_map/ppermute | solution.py:85
  25.3 2.6 %collective-permute-start.1 = (bf16[512,512]{1,0:T(8,128)(2,1)S(1)}, bf16[512,512]{1,0:T(8,128)(2,1)S(1)}, u32[]{:S(2)}, u32[]{:S(2)}) collective-permute-start(bf16[512,512]{1,0:T(8,128)(2,1)S(1)} %get-tuple-element.11), channel_id=1, source_target_pairs={{0,16},{16,0},{1,17},{17,1},{2,18},{18,2},{3,19},{19,3},{4,20},{20... | collective-permute-start | bytes 1572872 | tf_op jit(solution)/shard_map/ppermute | solution.py:85
  27.9 16.2 %collective-permute-done.2 = bf16[512,512]{1,0:T(8,128)(2,1)S(1)} collective-permute-done((bf16[512,512]{1,0:T(8,128)(2,1)S(1)}, bf16[512,512]{1,0:T(8,128)(2,1)S(1)}, u32[]{:S(2)}, u32[]{:S(2)}) %collective-permute-start.2) | collective-permute-done | bytes 524320 | tf_op jit(solution)/shard_map/ppermute | solution.py:85
  44.1 3.2 %collective-permute-start.3 = (bf16[512,512]{1,0:T(8,128)(2,1)S(1)}, bf16[512,512]{1,0:T(8,128)(2,1)S(1)}, u32[]{:S(2)}, u32[]{:S(2)}) collective-permute-start(bf16[512,512]{1,0:T(8,128)(2,1)S(1)} %collective-permute-done.2), channel_id=1, source_target_pairs={{0,16},{16,0},{1,17},{17,1},{2,18},{18,2},{3,19},{19,3},{4,20},{20... | collective-permute-start | bytes 1572872 | tf_op jit(solution)/shard_map/ppermute | solution.py:85
  47.4 12.6 %all_gather.10 = bf16[128,512]{1,0:T(8,128)(2,1)S(1)} all-gather(bf16[16,512]{1,0:T(8,128)(2,1)S(1)} %copy-done.8), channel_id=1, replica_groups=mesh['side'=4,'x'=4,'core'=2,'zhi'=2,'y'=8] {'x','core'}, dimensions={0}, use_global_device_ids=true | all-gather | bytes 147456 | tf_op jit(solution)/shard_map/all_gather | solution.py:134
  60.4 2.5 %fusion.8 = bf16[4,2,512,128]{2,3,1,0:T(8,128)(2,1)S(1)} fusion(bf16[2,512,2,512]{3,1,0,2:T(8,128)(2,1)S(1)} %pad_maximum_fusion, bf16[2,512,4,128]{3,1,0,2:T(8,128)(2,1)} %all-gather.3.cloned.1.call-done), kind=kOutput, calls=%fused_computation.7 | convolution fusion | flops 1074266112 | bytes 4194304 | tf_op jit(solution)/shard_map/prhf,prxn->xhfn/dot_general | solution.py:141
  62.9 1.3 copy.34
  64.2 3.5 %all-to-all-start = ((bf16[4,1024,128]{2,1,0:T(8,128)(2,1)}), bf16[4,1024,128]{2,1,0:T(8,128)(2,1)S(1)}, u32[]{:S(2)}, u32[]{:S(2)}) async-start(bf16[4,1024,128]{2,1,0:T(8,128)(2,1)} %bitcast.95), calls=%async_computation | async-start | bytes 2097152 | tf_op jit(solution)/shard_map/all_to_all | solution.py:145
  67.7 29.6 %all-gather.5.cloned.1.call-done = bf16[2,512,4,128]{3,1,2,0:T(8,128)(2,1)} async-done(((bf16[2,64,4,128]{3,1,2,0:T(8,128)(2,1)}), bf16[2,512,4,128]{3,1,2,0:T(8,128)(2,1)}) %all-gather.5.cloned.1.call-update) | async-done | bytes 1048592 | tf_op jit(solution)/shard_map/all_gather | solution.py:140
  97.3 3.5 %fusion.11 = bf16[4,2,512,128]{2,3,1,0:T(8,128)(2,1)} fusion(bf16[2,512,2,512]{3,1,0,2:T(8,128)(2,1)S(1)} %pad_maximum_fusion, bf16[2,512,4,128]{3,1,2,0:T(8,128)(2,1)} %all-gather.5.cloned.1.call-done), kind=kOutput, calls=%fused_computation.8 | convolution fusion | flops 1074266112 | bytes 4194304 | tf_op jit(solution)/shard_map/prhf,prxn->xhfn/dot_general | solution.py:141
  100.7 2.3 %copy.36 = bf16[4,2,512,128]{3,2,1,0:T(8,128)(2,1)} copy(bf16[4,2,512,128]{2,3,1,0:T(8,128)(2,1)} %fusion.11) | data formatting | bytes 2097152 | tf_op jit(solution)/shard_map/convert_element_type | solution.py:143
  103.0 4.7 %all-to-all-start.3 = ((bf16[4,1024,128]{2,1,0:T(8,128)(2,1)}), bf16[4,1024,128]{2,1,0:T(8,128)(2,1)S(1)}, u32[]{:S(2)}, u32[]{:S(2)}) async-start(bf16[4,1024,128]{2,1,0:T(8,128)(2,1)} %bitcast.28), calls=%async_computation.3 | async-start | bytes 2097152 | tf_op jit(solution)/shard_map/all_to_all | solution.py:145
  108.7 9.0 %all-to-all-done.3 = bf16[4,1024,128]{2,1,0:T(8,128)(2,1)S(1)} async-done(((bf16[4,1024,128]{2,1,0:T(8,128)(2,1)}), bf16[4,1024,128]{2,1,0:T(8,128)(2,1)S(1)}, u32[]{:S(2)}, u32[]{:S(2)}) %all-to-all-start.3) | async-done | bytes 1048608 | tf_op jit(solution)/shard_map/all_to_all | solution.py:145
  117.7 7.0 %all-to-all-start.1 = ((bf16[8,128,128]{2,1,0:T(8,128)(2,1)}), bf16[8,128,128]{2,1,0:T(8,128)(2,1)S(1)}, u32[]{:S(2)}, u32[]{:S(2)}) async-start(bf16[8,128,128]{2,1,0:T(8,128)(2,1)} %bitcast.20), calls=%async_computation.1 | async-start | bytes 524288 | tf_op jit(solution)/shard_map/all_to_all | solution.py:147
  125.6 8.4 %all-to-all-done.1 = bf16[8,128,128]{2,1,0:T(8,128)(2,1)S(1)} async-done(((bf16[8,128,128]{2,1,0:T(8,128)(2,1)}), bf16[8,128,128]{2,1,0:T(8,128)(2,1)S(1)}, u32[]{:S(2)}, u32[]{:S(2)}) %all-to-all-start.1) | async-done | bytes 262176 | tf_op jit(solution)/shard_map/all_to_all | solution.py:147
  134.0 3.4 %all-to-all-start.4 = ((bf16[8,128,128]{2,1,0:T(8,128)(2,1)}), bf16[8,128,128]{2,1,0:T(8,128)(2,1)S(1)}, u32[]{:S(2)}, u32[]{:S(2)}) async-start(bf16[8,128,128]{2,1,0:T(8,128)(2,1)} %bitcast.29), calls=%async_computation.4 | async-start | bytes 524288 | tf_op jit(solution)/shard_map/all_to_all | solution.py:147
  137.5 9.2 %all-to-all-done.4 = bf16[8,128,128]{2,1,0:T(8,128)(2,1)S(1)} async-done(((bf16[8,128,128]{2,1,0:T(8,128)(2,1)}), bf16[8,128,128]{2,1,0:T(8,128)(2,1)S(1)}, u32[]{:S(2)}, u32[]{:S(2)}) %all-to-all-start.4) | async-done | bytes 262176 | tf_op jit(solution)/shard_map/all_to_all | solution.py:147
  147.4 3.3 %all-to-all-start.2 = ((bf16[4,128,128]{2,1,0:T(8,128)(2,1)}), bf16[4,128,128]{2,1,0:T(8,128)(2,1)S(1)}, u32[]{:S(2)}, u32[]{:S(2)}) async-start(bf16[4,128,128]{2,1,0:T(8,128)(2,1)} %broadcast_in_dim.12), calls=%async_computation.2 | async-start | bytes 262144 | tf_op jit(solution)/shard_map/all_to_all | solution.py:149
  150.7 5.0 %all-to-all-done.2 = bf16[4,128,128]{2,1,0:T(8,128)(2,1)S(1)} async-done(((bf16[4,128,128]{2,1,0:T(8,128)(2,1)}), bf16[4,128,128]{2,1,0:T(8,128)(2,1)S(1)}, u32[]{:S(2)}, u32[]{:S(2)}) %all-to-all-start.2) | async-done | bytes 131104 | tf_op jit(solution)/shard_map/all_to_all | solution.py:149
  156.4 3.3 %all-to-all-start.5 = ((bf16[4,128,128]{2,1,0:T(8,128)(2,1)}), bf16[4,128,128]{2,1,0:T(8,128)(2,1)S(1)}, u32[]{:S(2)}, u32[]{:S(2)}) async-start(bf16[4,128,128]{2,1,0:T(8,128)(2,1)} %broadcast_in_dim.13), calls=%async_computation.5 | async-start | bytes 262144 | tf_op jit(solution)/shard_map/all_to_all | solution.py:149
  160.6 3.9 %all-to-all-done.5 = bf16[4,128,128]{2,1,0:T(8,128)(2,1)S(1)} async-done(((bf16[4,128,128]{2,1,0:T(8,128)(2,1)}), bf16[4,128,128]{2,1,0:T(8,128)(2,1)S(1)}, u32[]{:S(2)}, u32[]{:S(2)}) %all-to-all-start.5) | async-done | bytes 131104 | tf_op jit(solution)/shard_map/all_to_all | solution.py:149
  166.7 18.3 %all-to-all-start.6 = ((bf16[128,2,128]{2,1,0:T(2,128)(2,1)}), bf16[128,2,128]{2,1,0:T(2,128)(2,1)S(1)}, u32[]{:S(2)}, u32[]{:S(2)}) async-start(bf16[128,2,128]{2,1,0:T(2,128)(2,1)} %reshape.261), calls=%async_computation.6 | async-start | bytes 131072 | tf_op jit(solution)/shard_map/all_to_all | solution.py:155
  185.3 13.9 %all-to-all-done.6 = bf16[128,2,128]{2,1,0:T(2,128)(2,1)S(1)} async-done(((bf16[128,2,128]{2,1,0:T(2,128)(2,1)}), bf16[128,2,128]{2,1,0:T(2,128)(2,1)S(1)}, u32[]{:S(2)}, u32[]{:S(2)}) %all-to-all-start.6) | async-done | bytes 65568 | tf_op jit(solution)/shard_map/all_to_all | solution.py:155
  (62 shorter events, 11.6 us)
Async XLA Ops:
  7.2 153.4 %copy-start = (bf16[1,8192]{1,0:T(2,128)(2,1)S(1)}, bf16[1,8192]{1,0:T(2,128)(2,1)}, u32[]{:S(2)}) copy-start(bf16[1,8192]{1,0:T(2,128)(2,1)} %param.16) | copy-start | bytes 49156
  7.2 12.0 %copy-start.2 = (bf16[1,1024,512]{2,1,0:T(8,128)(2,1)S(1)}, bf16[1,1024,512]{2,1,0:T(8,128)(2,1)}, u32[]{:S(2)}) copy-start(bf16[1,1024,512]{2,1,0:T(8,128)(2,1)} %param.10) | copy-start | bytes 3145732
  7.2 53.2 %all-gather.3.cloned.1.call-start = ((), (), s32[]{:S(2)}) async-start(), calls=%async_computation.7 | async-start | bytes 1179648 | tf_op jit(solution)/shard_map/all_gather | solution.py:140
  8.7 9.8 %collective-permute-start = (bf16[64,4,2,128]{3,0,1,2:T(8,128)(2,1)S(1)}, bf16[64,4,2,128]{3,0,1,2:T(8,128)(2,1)S(1)}, u32[]{:S(2)}, u32[]{:S(2)}) collective-permute-start(bf16[64,4,2,128]{3,0,1,2:T(8,128)(2,1)S(1)} %bitcast.107), channel_id=1, source_target_pairs={{0,16},{16,0},{1,17},{17,1},{2,18},{18,2},{3,19},{19,3},{4,20},{20... | collective-permute-start | bytes 393224 | tf_op jit(solution)/shard_map/ppermute | solution.py:85
  17.5 29.9 %copy-start.8 = (bf16[16,512]{1,0:T(8,128)(2,1)S(1)}, bf16[16,512]{1,0:T(8,128)(2,1)}, u32[]{:S(2)}) copy-start(bf16[16,512]{1,0:T(8,128)(2,1)} %param.15) | copy-start | bytes 49156
  19.1 78.2 %all-gather.5.cloned.1.call-start = ((), (), s32[]{:S(2)}) async-start(), calls=%async_computation.8 | async-start | bytes 1179648 | tf_op jit(solution)/shard_map/all_gather | solution.py:140
  19.3 24.7 %collective-permute-start.2 = (bf16[512,512]{1,0:T(8,128)(2,1)S(1)}, bf16[512,512]{1,0:T(8,128)(2,1)S(1)}, u32[]{:S(2)}, u32[]{:S(2)}) collective-permute-start(bf16[512,512]{1,0:T(8,128)(2,1)S(1)} %get-tuple-element.12), channel_id=1, source_target_pairs={{0,8},{8,0},{1,9},{9,1},{2,10},{10,2},{3,11},{11,3},{4,12},{12,4},... | collective-permute-start | bytes 1572872 | tf_op jit(solution)/shard_map/ppermute | solution.py:85
  25.3 34.6 %collective-permute-start.1 = (bf16[512,512]{1,0:T(8,128)(2,1)S(1)}, bf16[512,512]{1,0:T(8,128)(2,1)S(1)}, u32[]{:S(2)}, u32[]{:S(2)}) collective-permute-start(bf16[512,512]{1,0:T(8,128)(2,1)S(1)} %get-tuple-element.11), channel_id=1, source_target_pairs={{0,16},{16,0},{1,17},{17,1},{2,18},{18,2},{3,19},{19,3},{4,20},{20... | collective-permute-start | bytes 1572872 | tf_op jit(solution)/shard_map/ppermute | solution.py:85
  44.1 15.9 %collective-permute-start.3 = (bf16[512,512]{1,0:T(8,128)(2,1)S(1)}, bf16[512,512]{1,0:T(8,128)(2,1)S(1)}, u32[]{:S(2)}, u32[]{:S(2)}) collective-permute-start(bf16[512,512]{1,0:T(8,128)(2,1)S(1)} %collective-permute-done.2), channel_id=1, source_target_pairs={{0,16},{16,0},{1,17},{17,1},{2,18},{18,2},{3,19},{19,3},{4,20},{20... | collective-permute-start | bytes 1572872 | tf_op jit(solution)/shard_map/ppermute | solution.py:85
  64.2 38.8 %all-to-all-start = ((bf16[4,1024,128]{2,1,0:T(8,128)(2,1)}), bf16[4,1024,128]{2,1,0:T(8,128)(2,1)S(1)}, u32[]{:S(2)}, u32[]{:S(2)}) async-start(bf16[4,1024,128]{2,1,0:T(8,128)(2,1)} %bitcast.95), calls=%async_computation | async-start | bytes 2097152 | tf_op jit(solution)/shard_map/all_to_all | solution.py:145
  103.0 14.7 %all-to-all-start.3 = ((bf16[4,1024,128]{2,1,0:T(8,128)(2,1)}), bf16[4,1024,128]{2,1,0:T(8,128)(2,1)S(1)}, u32[]{:S(2)}, u32[]{:S(2)}) async-start(bf16[4,1024,128]{2,1,0:T(8,128)(2,1)} %bitcast.28), calls=%async_computation.3 | async-start | bytes 2097152 | tf_op jit(solution)/shard_map/all_to_all | solution.py:145
  108.7 51.1 %copy-start.6 = (bf16[1,128,1024]{2,1,0:T(8,128)(2,1)S(1)}, bf16[1,128,1024]{2,1,0:T(8,128)(2,1)}, u32[]{:S(2)}) copy-start(bf16[1,128,1024]{2,1,0:T(8,128)(2,1)} %param.17) | copy-start | bytes 786436
  117.7 42.8 %copy-start.7 = (bf16[1,128,1024]{2,1,0:T(8,128)(2,1)S(1)}, bf16[1,128,1024]{2,1,0:T(8,128)(2,1)}, u32[]{:S(2)}) copy-start(bf16[1,128,1024]{2,1,0:T(8,128)(2,1)} %param.18) | copy-start | bytes 786436
  117.7 16.3 %all-to-all-start.1 = ((bf16[8,128,128]{2,1,0:T(8,128)(2,1)}), bf16[8,128,128]{2,1,0:T(8,128)(2,1)S(1)}, u32[]{:S(2)}, u32[]{:S(2)}) async-start(bf16[8,128,128]{2,1,0:T(8,128)(2,1)} %bitcast.20), calls=%async_computation.1 | async-start | bytes 524288 | tf_op jit(solution)/shard_map/all_to_all | solution.py:147
  124.7 39.8 %copy-start.3 = (f32[512,256]{1,0:T(8,128)S(1)}, f32[512,256]{1,0:T(8,128)}, u32[]{:S(2)}) copy-start(f32[512,256]{1,0:T(8,128)} %param.12) | copy-start | bytes 1572868
  124.7 39.8 %copy-start.4 = (bf16[512,256]{1,0:T(8,128)(2,1)S(1)}, bf16[512,256]{1,0:T(8,128)(2,1)}, u32[]{:S(2)}) copy-start(bf16[512,256]{1,0:T(8,128)(2,1)} %param.14) | copy-start | bytes 786436
  124.7 39.8 %copy-start.5 = (bf16[512,256]{1,0:T(8,128)(2,1)S(1)}, bf16[512,256]{1,0:T(8,128)(2,1)}, u32[]{:S(2)}) copy-start(bf16[512,256]{1,0:T(8,128)(2,1)} %param.13) | copy-start | bytes 786436
  134.0 12.7 %all-to-all-start.4 = ((bf16[8,128,128]{2,1,0:T(8,128)(2,1)}), bf16[8,128,128]{2,1,0:T(8,128)(2,1)S(1)}, u32[]{:S(2)}, u32[]{:S(2)}) async-start(bf16[8,128,128]{2,1,0:T(8,128)(2,1)} %bitcast.29), calls=%async_computation.4 | async-start | bytes 524288 | tf_op jit(solution)/shard_map/all_to_all | solution.py:147
  147.4 8.4 %all-to-all-start.2 = ((bf16[4,128,128]{2,1,0:T(8,128)(2,1)}), bf16[4,128,128]{2,1,0:T(8,128)(2,1)S(1)}, u32[]{:S(2)}, u32[]{:S(2)}) async-start(bf16[4,128,128]{2,1,0:T(8,128)(2,1)} %broadcast_in_dim.12), calls=%async_computation.2 | async-start | bytes 262144 | tf_op jit(solution)/shard_map/all_to_all | solution.py:149
  156.4 8.1 %all-to-all-start.5 = ((bf16[4,128,128]{2,1,0:T(8,128)(2,1)}), bf16[4,128,128]{2,1,0:T(8,128)(2,1)S(1)}, u32[]{:S(2)}, u32[]{:S(2)}) async-start(bf16[4,128,128]{2,1,0:T(8,128)(2,1)} %broadcast_in_dim.13), calls=%async_computation.5 | async-start | bytes 262144 | tf_op jit(solution)/shard_map/all_to_all | solution.py:149
  165.8 34.7 %copy-start.1 = (f32[512,256]{1,0:T(8,128)}, f32[512,256]{1,0:T(8,128)S(1)}, u32[]{:S(2)}) copy-start(f32[512,256]{1,0:T(8,128)S(1)} %get-tuple-element.14) | copy-start | bytes 1572868
  166.7 32.5 %all-to-all-start.6 = ((bf16[128,2,128]{2,1,0:T(2,128)(2,1)}), bf16[128,2,128]{2,1,0:T(2,128)(2,1)S(1)}, u32[]{:S(2)}, u32[]{:S(2)}) async-start(bf16[128,2,128]{2,1,0:T(2,128)(2,1)} %reshape.261), calls=%async_computation.6 | async-start | bytes 131072 | tf_op jit(solution)/shard_map/all_to_all | solution.py:155
Sparse Core Ops, SparseCore 0:
  19.3 35.7 all-gather.2
  57.7 39.5 all-gather.4

commit v3 on v1

--- a/solution.py
+++ b/solution.py
@@ -1,6 +1,8 @@
 import jax
 import jax.numpy as jnp
 from jax import lax
+from jax.experimental import pallas as pl
+from jax.experimental.pallas import tpu as pltpu
 from jax.sharding import Mesh
 from jax.sharding import PartitionSpec as P
 
@@ -80,13 +82,86 @@
 TP = ("zhi", "y")
 
 
-def pick_core(columns, core):
-    return lax.dynamic_index_in_dim(columns, core, axis=2, keepdims=False)
-
-
-def gather_cotangents(pieces):
-    pairs = lax.all_gather(pieces, "zhi", axis=1)
-    return lax.all_gather(pairs, "y", axis=2)
+def swap_over(array, axis):
+    return lax.ppermute(array, axis, [(0, 1), (1, 0)])
+
+
+def shifted(array, axis, by):
+    count = lax.axis_size(axis)
+    return lax.ppermute(array, axis, [(i, (i + by) % count) for i in range(count)])
+
+
+def gathered_round(piece):
+    half = piece.shape[0] // 2
+    behind1, ahead1 = shifted(piece, "y", 1), shifted(piece, "y", -1)
+    behind2, ahead2 = shifted(piece, "y", 2), shifted(piece, "y", -2)
+    behind3, ahead3 = shifted(behind2, "y", 1), shifted(ahead2, "y", -1)
+    across = [shifted(behind3[:half], "y", 1), shifted(ahead3[half:], "y", -1)]
+    return [piece, behind1, behind2, behind3, *across, ahead3, ahead2, ahead1]
+
+
+def own_columns(columns, width, core):
+    blocks = [columns[:, i : i + width] for i in range(0, columns.shape[1], width)]
+    even, odd = jnp.concatenate(blocks[::2], axis=1), jnp.concatenate(blocks[1::2], axis=1)
+    return jnp.where(core == 0, even, odd), jnp.where(core == 0, odd, even)
+
+
+def product_kernel(position, inputs, kept_other, received_own, received_other, *refs):
+    *pieces, out = refs
+    half, along = position[0], position[1]
+    count = lax.axis_size("y")
+    feature_count = inputs.shape[1]
+    rows = received_own.shape[0] // count
+    x_count, _, width = out.shape
+    starts = [
+        pl.multiple_of(lax.rem(along - behind + count, count) * rows, rows)
+        for behind in range(count)
+    ]
+    half_start = pl.multiple_of(half * received_own.shape[0], rows)
+    sides = (
+        (inputs, half_start, kept_other, half),
+        (received_own, 0, received_other, 1 - half),
+    )
+    for own, offset, other, place in sides:
+        left = jnp.concatenate(
+            [
+                block
+                for start in starts
+                for block in (own[pl.ds(offset + start, rows), :], other[pl.ds(start, rows), :])
+            ]
+        )
+        target = pl.ds(pl.multiple_of(place * feature_count, feature_count), feature_count)
+        for x in range(x_count):
+            right = jnp.concatenate([piece[:, x * width : (x + 1) * width] for piece in pieces])
+            out[x, target, :] = lax.dot_general(
+                left, right, (((0,), (0,)), ((), ())), preferred_element_type=jnp.float32
+            ).astype(out.dtype)
+
+
+def products(half, inputs, kept_other, received_own, received_other, pieces, x_count):
+    feature_count = inputs.shape[1]
+    width = pieces[0].shape[1] // x_count
+    position = jnp.stack([half, lax.axis_index("y")]).astype(jnp.int32)
+    operands = (inputs, kept_other, received_own, received_other, *pieces)
+    out_shape = jax.ShapeDtypeStruct((x_count, 2 * feature_count, width), jnp.bfloat16)
+    return pl.pallas_call(
+        product_kernel,
+        out_shape=out_shape,
+        in_specs=[pl.BlockSpec(memory_space=pltpu.SMEM)]
+        + [pl.BlockSpec(memory_space=pltpu.VMEM)] * len(operands),
+        out_specs=pl.BlockSpec(memory_space=pltpu.VMEM),
+        compiler_params=pltpu.CompilerParams(vmem_limit_bytes=24 * 2**20),
+        cost_estimate=pl.CostEstimate(
+            flops=4 * feature_count * received_own.shape[0] * 2 * x_count * width,
+            bytes_accessed=8 * 2**20,
+            transcendentals=0,
+        ),
+        name="products",
+    )(position, *operands)
+
+
+def summed(terms):
+    return jnp.sum(terms.astype(jnp.float32), axis=0).astype(jnp.bfloat16)
 
 
 def local(
@@ -101,38 +176,39 @@
     value_cache_slots,
     cache_lengths,
 ):
-    core = lax.axis_index("core")
-    swap = [(0, 1), (1, 0)]
-    inputs_own = learn_inputs[0]
-    row_count, feature_count = inputs_own.shape
+    core, half = lax.axis_index("core"), lax.axis_index("zhi")
     x_count, side_count = lax.axis_size("x"), lax.axis_size("side")
+    feature_count = learn_inputs.shape[2]
     block_width = kv_master.shape[1]
-    columns = learn_grads[0].reshape(-1, x_count, 2, block_width)
-    grads_other = lax.ppermute(pick_core(columns, 1 - core), "core", swap)
-    pieces = jnp.stack([pick_core(columns, core), grads_other])
-    inputs_other = lax.ppermute(inputs_own, "core", swap)
-    gathered = gather_cotangents(pieces)
-    grads_all = gathered.reshape(2, row_count, x_count, block_width)
-    inputs_all = jnp.stack([inputs_own, inputs_other])
-    partial = jnp.einsum(
-        "prf,prxc->xfc", inputs_all, grads_all, preferred_element_type=jnp.float32
-    ).astype(jnp.bfloat16)
     quarter = feature_count // side_count
-    partial = partial.reshape(x_count * side_count, quarter, block_width)
-    terms = lax.all_to_all(partial, ("x", "side"), 0, 0, tiled=True)
-    own_quarter = jnp.sum(terms.astype(jnp.float32), axis=0).astype(jnp.bfloat16)
+
+    grads_own, grads_sent = own_columns(learn_grads[0], block_width, core)
+    piece = jnp.concatenate([grads_own, swap_over(grads_sent, "core")])
+    pieces = gathered_round(piece)
+
+    inputs = learn_inputs[0]
+    row_halves = inputs.reshape(2, -1, feature_count)
+    kept = lax.dynamic_index_in_dim(row_halves, half, 0, keepdims=False)
+    received = swap_over(lax.dynamic_index_in_dim(row_halves, 1 - half, 0, keepdims=False), "zhi")
+    kept_other, received_other = swap_over(kept, "core"), swap_over(received, "core")
+    decode_rows = lax.all_gather(decode_inputs, REP, axis=0, tiled=True)
+    received_other, decode_rows = lax.optimization_barrier((received_other, decode_rows))
+
+    partial = products(half, inputs, kept_other, received, received_other, pieces, x_count)
+    over_x = summed(lax.all_to_all(partial, "x", 0, 0, tiled=True))
+    over_x = over_x.reshape(2 * side_count, quarter, block_width)
+    own_quarter = summed(lax.all_to_all(over_x, ("zhi", "side"), 0, 0, tiled=True))
     spread = jnp.broadcast_to(own_quarter[None], (side_count, quarter, block_width))
     gradient = lax.all_to_all(spread, "side", 0, 0, tiled=True)
     gradient = gradient.reshape(feature_count, block_width).astype(jnp.float32)
     master_new, first_new, second_new = adamw(kv_master, first_moment, second_moment, gradient)
     rounded_weights = master_new.astype(jnp.bfloat16)
-    decode_rows = lax.all_gather(decode_inputs, REP, axis=0, tiled=True)
     partial_fresh = jnp.dot(decode_rows, rounded_weights, preferred_element_type=jnp.float32)
-    rep_count, tp_count = lax.axis_size(REP), lax.axis_size(TP)
-    partial_fresh = partial_fresh.reshape(rep_count, tp_count, block_width)
-    fresh_terms = lax.all_to_all(partial_fresh, TP, 1, 1, tiled=True)
-    fresh_block = jnp.sum(fresh_terms, axis=1).astype(jnp.bfloat16)
-    fresh_output = lax.all_to_all(fresh_block, REP, 0, 0, tiled=True).reshape(1, -1)
+    partial_fresh = partial_fresh.astype(jnp.bfloat16).reshape(-1, 2, block_width // 2)
+    fresh_terms = lax.all_to_all(partial_fresh, REP + TP, 0, 0, tiled=True)
+    fresh_terms = fresh_terms.reshape(lax.axis_size(REP), lax.axis_size(TP), block_width)
+    fresh_output = jnp.sum(fresh_terms.astype(jnp.float32), axis=1).astype(jnp.bfloat16)
+    fresh_output = fresh_output.reshape(1, -1)
     attended = attend(queries, key_cache_slots, value_cache_slots, cache_lengths, fresh_output)
     return (master_new, first_new, second_new, attended)
 

time: 192 us -> 178 us (0.927)
  waiting for transfers between devices: 73.2 us -> 27.8 us
  starting transfers between devices: 27.6 us -> 61.6 us
  between operations: 14.9 us -> 1.7 us
  blocking collectives: 62.7 us -> 71 us
  matrix products: 5.41 us -> 0.87 us
  Pallas kernels: 0 us -> 3.55 us
  local copies, waits for them, and re-layouts: 5.76 us -> 8.31 us
    all_gather x1 -> x0, waiting for transfers between devices: 55.3 us -> none  [gather_cotangents(): return lax.all_gather(pairs, 'y', axis=2)]
    ppermute x2 -> x12, starting transfers between devices: 11.9 us -> 46.4 us  [the longest x8 25.4 us: shifted(): lax.ppermute(array, axis, [(i, (i + by) % count) for i in range(count)])]
    all_to_all x1 -> x2, blocking collectives: 34.2 us -> 55.6 us  [the longest x1 29.2 us: local(): over_x = summed(lax.all_to_all(partial, 'x', 0, 0, tiled=True))]
    all_gather x1 -> x0, blocking collectives: 14.1 us -> none  [gather_cotangents(): pairs = lax.all_gather(pieces, 'zhi', axis=1)]
    ppermute x2 -> x12, waiting for transfers between devices: 3.18 us -> 9.2 us  [the longest x8 8.23 us: shifted(): lax.ppermute(array, axis, [(i, (i + by) % count) for i in range(count)])]
    all_to_all x1, waiting for transfers between devices: 0.01 us -> 4.7 us  [local(): gradient = lax.all_to_all(spread, 'side', 0, 0, tiled=True)]
    dot_general x1 -> x0, matrix products: 4.54 us -> none  [local(): jnp.einsum('prf,prxc->xfc', inputs_all, grads_all, preferred_element_type...]
    pallas_call x0 -> x1, Pallas kernels: none -> 3.55 us  [products(): pl.pallas_call(product_kernel, out_shape=out_shape, in_specs=[pl.BlockSpe...]
  transfers between devices with their start and end apart: 6 -> 14, of which waited for: 5 -> 5; matrix products, arithmetic and copies ran while one was open for 0% -> 1% of each run, Pallas kernels for 0% -> 0%
where the time goes in v3:
time: 178 us; the launch traced here: 177 us
  blocking collectives  71 us (40%)
  starting transfers between devices  61.6 us (35%)
  waiting for transfers between devices  27.8 us (16%)
  local copies, waits for them, and re-layouts  8.31 us (5%)
  Pallas kernels  3.55 us (2%)
  other arithmetic  2.48 us (1%)
    all_to_all x1, blocking collectives, local(): over_x = summed(lax.all_to_all(partial, 'x', 0, 0, tiled=True))  29.2 us
    all_to_all x1, blocking collectives, local(): lax.all_to_all(over_x, ('zhi', 'side'), 0, 0, tiled=True)  26.4 us
    ppermute x8, starting transfers between devices, shifted(): lax.ppermute(array, axis, [(i, (i + by) % count) for i in range(count)])  25.4 us
    ppermute x4, starting transfers between devices, swap_over(): return lax.ppermute(array, axis, [(0, 1), (1, 0)])  20.9 us
    all_gather x1, blocking collectives, local(): decode_rows = lax.all_gather(decode_inputs, REP, axis=0, tiled=True)  15.4 us
    all_to_all x1, waiting for transfers between devices, local(): fresh_terms = lax.all_to_all(partial_fresh, REP + TP, 0, 0, tiled=True)  13.9 us
    all_to_all x1, starting transfers between devices, local(): fresh_terms = lax.all_to_all(partial_fresh, REP + TP, 0, 0, tiled=True)  11.9 us
    ppermute x8, waiting for transfers between devices, shifted(): lax.ppermute(array, axis, [(i, (i + by) % count) for i in range(count)])  8.23 us
  transfers between devices with their start and end apart: 14, of which 5 were waited for; matrix products, arithmetic and copies ran while one was open for 1% of the time, Pallas kernels for 0%

profile of v3, /device:TPU:1, one launch (start us, length us, event | category | flops | bytes accessed | tf_op | source)
XLA Modules:
  0.0 177.3 jit_solution(18187457355458335927)
XLA Ops:
  0.7 2.2 %dynamic-slice_bitcast_fusion = (bf16[512,512]{1,0:T(8,128)(2,1)S(1)}, bf16[512,512]{1,0:T(8,128)(2,1)}) fusion(bf16[2,512,512]{2,1,0:T(8,128)(2,1)} %bitcast.40, s32[]{:T(128)S(6)} %select_n.25, s32[]{:T(128)S(6)} %select_n.24), kind=kLoop, calls=%fused_computation.11 | loop fusion | bytes 2097160 | tf_op jit(solution)/shard_map/jit(dynamic_index_in_dim)/squeeze | solution.py:192
  2.8 11.5 %collective-permute-start.1 = (bf16[512,512]{1,0:T(8,128)(2,1)S(1)}, bf16[512,512]{1,0:T(8,128)(2,1)S(1)}, u32[]{:S(2)}, u32[]{:S(2)}) collective-permute-start(bf16[512,512]{1,0:T(8,128)(2,1)S(1)} %get-tuple-element.8), channel_id=1, source_target_pairs={{0,8},{8,0},{1,9},{9,1},{2,10},{10,2},{3,11},{11,3},{4,12},{12,4},... | collective-permute-start | bytes 1572872 | tf_op jit(solution)/shard_map/ppermute | solution.py:86
  14.4 2.9 %collective-permute-start.3 = (bf16[64,1024]{1,0:T(8,128)(2,1)S(1)}, bf16[64,1024]{1,0:T(8,128)(2,1)S(1)}, u32[]{:S(2)}, u32[]{:S(2)}) collective-permute-start(bf16[64,1024]{1,0:T(8,128)(2,1)S(1)} %get-tuple-element.14), channel_id=1, source_target_pairs={{0,16},{16,0},{1,17},{17,1},{2,18},{18,2},{3,19},{19,3},{4,20},{20... | collective-permute-start | bytes 393224 | tf_op jit(solution)/shard_map/ppermute | solution.py:86
  18.3 5.9 %collective-permute-start.8 = (bf16[128,1024]{1,0:T(8,128)(2,1)S(1)}, bf16[128,1024]{1,0:T(8,128)(2,1)S(1)}, u32[]{:S(2)}, u32[]{:S(2)}) collective-permute-start(bf16[128,1024]{1,0:T(8,128)(2,1)S(1)} %pad_maximum_fusion.refs_0_), channel_id=1, source_target_pairs={{0,6},{1,7},{2,0},{3,1},{4,2},{5,3},{6,4},{7,5},{8,14},{9,15},{10,... | collective-permute-start | bytes 786440 | tf_op jit(solution)/shard_map/ppermute | solution.py:91
  24.2 1.9 %collective-permute-start.5 = (bf16[128,1024]{1,0:T(8,128)(2,1)S(1)}, bf16[128,1024]{1,0:T(8,128)(2,1)S(1)}, u32[]{:S(2)}, u32[]{:S(2)}) collective-permute-start(bf16[128,1024]{1,0:T(8,128)(2,1)S(1)} %pad_maximum_fusion.refs_0_), channel_id=1, source_target_pairs={{0,2},{1,3},{2,4},{3,5},{4,6},{5,7},{6,0},{7,1},{8,10},{9,11},{10,... | collective-permute-start | bytes 786440 | tf_op jit(solution)/shard_map/ppermute | solution.py:91
  26.1 3.1 %collective-permute-start.2 = (bf16[512,512]{1,0:T(8,128)(2,1)S(1)}, bf16[512,512]{1,0:T(8,128)(2,1)S(1)}, u32[]{:S(2)}, u32[]{:S(2)}) collective-permute-start(bf16[512,512]{1,0:T(8,128)(2,1)S(1)} %collective-permute-done.1.received_own), channel_id=1, source_target_pairs={{0,16},{16,0},{1,17},{17,1},{2,18},{18,2},{3,19},{19,3},{4,20},{20... | collective-permute-start | bytes 1572872 | tf_op jit(solution)/shard_map/ppermute | solution.py:86
  29.2 6.3 %collective-permute-done.8.refs_7_ = bf16[128,1024]{1,0:T(8,128)(2,1)S(1)} collective-permute-done((bf16[128,1024]{1,0:T(8,128)(2,1)S(1)}, bf16[128,1024]{1,0:T(8,128)(2,1)S(1)}, u32[]{:S(2)}, u32[]{:S(2)}) %collective-permute-start.8) | collective-permute-done | bytes 262176 | tf_op jit(solution)/shard_map/ppermute | solution.py:91
  35.5 4.0 %collective-permute-start.9 = (bf16[128,1024]{1,0:T(8,128)(2,1)S(1)}, bf16[128,1024]{1,0:T(8,128)(2,1)S(1)}, u32[]{:S(2)}, u32[]{:S(2)}) collective-permute-start(bf16[128,1024]{1,0:T(8,128)(2,1)S(1)} %collective-permute-done.8.refs_7_), channel_id=1, source_target_pairs={{0,7},{1,0},{2,1},{3,2},{4,3},{5,4},{6,5},{7,6},{8,15},{9,8},{10,9... | collective-permute-start | bytes 786440 | tf_op jit(solution)/shard_map/ppermute | solution.py:91
  40.2 3.5 %collective-permute-start = (bf16[512,512]{1,0:T(8,128)(2,1)}, bf16[512,512]{1,0:T(8,128)(2,1)S(1)}, u32[]{:S(2)}, u32[]{:S(2)}) collective-permute-start(bf16[512,512]{1,0:T(8,128)(2,1)} %get-tuple-element.9), channel_id=1, source_target_pairs={{0,16},{16,0},{1,17},{17,1},{2,18},{18,2},{3,19},{19,3},{4,20},{20... | collective-permute-start | bytes 1572872 | tf_op jit(solution)/shard_map/ppermute | solution.py:86
  43.7 1.9 %collective-permute-start.6 = (bf16[128,1024]{1,0:T(8,128)(2,1)S(1)}, bf16[128,1024]{1,0:T(8,128)(2,1)S(1)}, u32[]{:S(2)}, u32[]{:S(2)}) collective-permute-start(bf16[128,1024]{1,0:T(8,128)(2,1)S(1)} %collective-permute-done.5.refs_2_), channel_id=1, source_target_pairs={{0,1},{1,2},{2,3},{3,4},{4,5},{5,6},{6,7},{7,0},{8,9},{9,10},{10,1... | collective-permute-start | bytes 786440 | tf_op jit(solution)/shard_map/ppermute | solution.py:91
  45.6 4.6 %collective-permute-start.11 = (bf16[128,1024]{1,0:T(8,128)(2,1)S(1)}, bf16[128,1024]{1,0:T(8,128)(2,1)}, u32[]{:S(2)}, u32[]{:S(2)}) collective-permute-start(bf16[128,1024]{1,0:T(8,128)(2,1)S(1)} %pad_maximum_fusion.refs_0_), channel_id=1, source_target_pairs={{0,7},{1,0},{2,1},{3,2},{4,3},{5,4},{6,5},{7,6},{8,15},{9,8},{10,9... | collective-permute-start | bytes 786440 | tf_op jit(solution)/shard_map/ppermute | solution.py:91
  50.2 1.9 %collective-permute-start.4 = (bf16[128,1024]{1,0:T(8,128)(2,1)S(1)}, bf16[128,1024]{1,0:T(8,128)(2,1)}, u32[]{:S(2)}, u32[]{:S(2)}) collective-permute-start(bf16[128,1024]{1,0:T(8,128)(2,1)S(1)} %pad_maximum_fusion.refs_0_), channel_id=1, source_target_pairs={{0,1},{1,2},{2,3},{3,4},{4,5},{5,6},{6,7},{7,0},{8,9},{9,10},{10,1... | collective-permute-start | bytes 786440 | tf_op jit(solution)/shard_map/ppermute | solution.py:91
  52.8 1.9 %collective-permute-done.6.refs_3_ = bf16[128,1024]{1,0:T(8,128)(2,1)S(1)} collective-permute-done((bf16[128,1024]{1,0:T(8,128)(2,1)S(1)}, bf16[128,1024]{1,0:T(8,128)(2,1)S(1)}, u32[]{:S(2)}, u32[]{:S(2)}) %collective-permute-start.6) | collective-permute-done | bytes 262176 | tf_op jit(solution)/shard_map/ppermute | solution.py:91
  54.7 2.8 %collective-permute-start.10 = (bf16[64,1024]{1,0:T(8,128)(2,1)}, bf16[64,1024]{1,0:T(8,128)(2,1)}, u32[]{:S(2)}, u32[]{:S(2)}) collective-permute-start(bf16[64,1024]{1,0:T(8,128)(2,1)} %slice.57), channel_id=1, source_target_pairs={{0,7},{1,0},{2,1},{3,2},{4,3},{5,4},{6,5},{7,6},{8,15},{9,8},{10,9... | collective-permute-start | bytes 393224 | tf_op jit(solution)/shard_map/ppermute | solution.py:91
  58.2 2.5 %collective-permute-start.7 = (bf16[64,1024]{1,0:T(8,128)(2,1)}, bf16[64,1024]{1,0:T(8,128)(2,1)}, u32[]{:S(2)}, u32[]{:S(2)}) collective-permute-start(bf16[64,1024]{1,0:T(8,128)(2,1)} %slice.56), channel_id=1, source_target_pairs={{0,1},{1,2},{2,3},{3,4},{4,5},{5,6},{6,7},{7,0},{8,9},{9,10},{10,1... | collective-permute-start | bytes 393224 | tf_op jit(solution)/shard_map/ppermute | solution.py:91
  60.7 15.4 %all_gather.3 = bf16[128,512]{1,0:T(8,128)(2,1)} all-gather(bf16[16,512]{1,0:T(8,128)(2,1)S(1)} %copy-done.14), channel_id=1, replica_groups=mesh['side'=4,'x'=4,'core'=2,'zhi'=2,'y'=8] {'x','core'}, dimensions={0}, use_global_device_ids=true | all-gather | bytes 147456 | tf_op jit(solution)/shard_map/all_gather | solution.py:194
  78.1 3.5 %products.1 = bf16[4,1024,256]{2,1,0:T(8,128)(2,1)S(1)} custom-call(s32[2]{0:T(128)S(1)} %pad_add_fusion.position, bf16[1024,512]{1,0:T(8,128)(2,1)S(1)} %bitcast.41, bf16[512,512]{1,0:T(8,128)(2,1)S(1)} %collective-permute-done.kept_other, bf16[512,512]{1,0:T(8,128)(2,1)S(1)} %collective-permute-done.1.received_own, ...), custom_call_target="tpu_custom_call" | custom-call | flops 2147483648 | bytes 8388608 | tf_op jit(solution)/shard_map/products/pallas_call | solution.py:147
  81.6 29.2 %all_to_all.20 = bf16[4,1024,256]{2,1,0:T(8,128)(2,1)S(1)} all-to-all(bf16[4,1024,256]{2,1,0:T(8,128)(2,1)S(1)} %products.1), channel_id=1, replica_groups=mesh['side'=4,'x'=4,'core'=2,'zhi'=2,'y'=8] {'x'}, dimensions={0} | all-to-all | bytes 4194304 | tf_op jit(solution)/shard_map/all_to_all | solution.py:198
  111.5 26.4 %all_to_all.21 = bf16[8,128,256]{2,1,0:T(8,128)(2,1)S(1)} all-to-all(bf16[8,128,256]{2,1,0:T(8,128)(2,1)S(1)} %bitcast.42), channel_id=1, replica_groups=mesh['side'=4,'x'=4,'core'=2,'zhi'=2,'y'=8] {'zhi','side'}, dimensions={0} | all-to-all | bytes 1048576 | tf_op jit(solution)/shard_map/all_to_all | solution.py:200
  138.8 3.4 %all-to-all-start.2 = ((bf16[4,128,256]{2,1,0:T(8,128)(2,1)}), bf16[4,128,256]{2,1,0:T(8,128)(2,1)S(1)}, u32[]{:S(2)}, u32[]{:S(2)}) async-start(bf16[4,128,256]{2,1,0:T(8,128)(2,1)} %broadcast_in_dim.10), calls=%async_computation.2 | async-start | bytes 524288 | tf_op jit(solution)/shard_map/all_to_all | solution.py:202
  143.1 4.7 %all-to-all-done.2 = bf16[4,128,256]{2,1,0:T(8,128)(2,1)S(1)} async-done(((bf16[4,128,256]{2,1,0:T(8,128)(2,1)}), bf16[4,128,256]{2,1,0:T(8,128)(2,1)S(1)}, u32[]{:S(2)}, u32[]{:S(2)}) %all-to-all-start.2) | async-done | bytes 262176 | tf_op jit(solution)/shard_map/all_to_all | solution.py:202
  147.8 1.3 fusion.5
  149.9 11.9 %all-to-all-start.3 = ((bf16[128,2,128]{2,1,0:T(2,128)(2,1)}), bf16[128,2,128]{2,1,0:T(2,128)(2,1)S(1)}, u32[]{:S(2)}, u32[]{:S(2)}) async-start(bf16[128,2,128]{2,1,0:T(2,128)(2,1)} %reshape.127), calls=%async_computation.3 | async-start | bytes 131072 | tf_op jit(solution)/shard_map/all_to_all | solution.py:208
  162.1 13.9 %all-to-all-done.3 = bf16[128,2,128]{2,1,0:T(2,128)(2,1)S(1)} async-done(((bf16[128,2,128]{2,1,0:T(2,128)(2,1)}), bf16[128,2,128]{2,1,0:T(2,128)(2,1)S(1)}, u32[]{:S(2)}, u32[]{:S(2)}) %all-to-all-start.3) | async-done | bytes 65568 | tf_op jit(solution)/shard_map/all_to_all | solution.py:208
  (66 shorter events, 9.2 us)
Async XLA Ops:
  0.6 142.3 %copy-start = (bf16[1,8192]{1,0:T(2,128)(2,1)S(1)}, bf16[1,8192]{1,0:T(2,128)(2,1)}, u32[]{:S(2)}) copy-start(bf16[1,8192]{1,0:T(2,128)(2,1)} %param.16) | copy-start | bytes 49156
  0.7 60.0 %copy-start.14 = (bf16[16,512]{1,0:T(8,128)(2,1)S(1)}, bf16[16,512]{1,0:T(8,128)(2,1)}, u32[]{:S(2)}) copy-start(bf16[16,512]{1,0:T(8,128)(2,1)} %param.15) | copy-start | bytes 49156
  0.7 75.5 %copy-start.1 = (bf16[1,1024,512]{2,1,0:T(8,128)(2,1)S(1)}, bf16[1,1024,512]{2,1,0:T(8,128)(2,1)}, u32[]{:S(2)}) copy-start(bf16[1,1024,512]{2,1,0:T(8,128)(2,1)} %param.10) | copy-start | bytes 3145732
  2.8 23.2 %collective-permute-start.1 = (bf16[512,512]{1,0:T(8,128)(2,1)S(1)}, bf16[512,512]{1,0:T(8,128)(2,1)S(1)}, u32[]{:S(2)}, u32[]{:S(2)}) collective-permute-start(bf16[512,512]{1,0:T(8,128)(2,1)S(1)} %get-tuple-element.8), channel_id=1, source_target_pairs={{0,8},{8,0},{1,9},{9,1},{2,10},{10,2},{3,11},{11,3},{4,12},{12,4},... | collective-permute-start | bytes 1572872 | tf_op jit(solution)/shard_map/ppermute | solution.py:86
  14.4 3.8 %collective-permute-start.3 = (bf16[64,1024]{1,0:T(8,128)(2,1)S(1)}, bf16[64,1024]{1,0:T(8,128)(2,1)S(1)}, u32[]{:S(2)}, u32[]{:S(2)}) collective-permute-start(bf16[64,1024]{1,0:T(8,128)(2,1)S(1)} %get-tuple-element.14), channel_id=1, source_target_pairs={{0,16},{16,0},{1,17},{17,1},{2,18},{18,2},{3,19},{19,3},{4,20},{20... | collective-permute-start | bytes 393224 | tf_op jit(solution)/shard_map/ppermute | solution.py:86
  18.3 17.3 %collective-permute-start.8 = (bf16[128,1024]{1,0:T(8,128)(2,1)S(1)}, bf16[128,1024]{1,0:T(8,128)(2,1)S(1)}, u32[]{:S(2)}, u32[]{:S(2)}) collective-permute-start(bf16[128,1024]{1,0:T(8,128)(2,1)S(1)} %pad_maximum_fusion.refs_0_), channel_id=1, source_target_pairs={{0,6},{1,7},{2,0},{3,1},{4,2},{5,3},{6,4},{7,5},{8,14},{9,15},{10,... | collective-permute-start | bytes 786440 | tf_op jit(solution)/shard_map/ppermute | solution.py:91
  24.2 19.5 %collective-permute-start.5 = (bf16[128,1024]{1,0:T(8,128)(2,1)S(1)}, bf16[128,1024]{1,0:T(8,128)(2,1)S(1)}, u32[]{:S(2)}, u32[]{:S(2)}) collective-permute-start(bf16[128,1024]{1,0:T(8,128)(2,1)S(1)} %pad_maximum_fusion.refs_0_), channel_id=1, source_target_pairs={{0,2},{1,3},{2,4},{3,5},{4,6},{5,7},{6,0},{7,1},{8,10},{9,11},{10,... | collective-permute-start | bytes 786440 | tf_op jit(solution)/shard_map/ppermute | solution.py:91
  26.1 32.1 %collective-permute-start.2 = (bf16[512,512]{1,0:T(8,128)(2,1)S(1)}, bf16[512,512]{1,0:T(8,128)(2,1)S(1)}, u32[]{:S(2)}, u32[]{:S(2)}) collective-permute-start(bf16[512,512]{1,0:T(8,128)(2,1)S(1)} %collective-permute-done.1.received_own), channel_id=1, source_target_pairs={{0,16},{16,0},{1,17},{17,1},{2,18},{18,2},{3,19},{19,3},{4,20},{20... | collective-permute-start | bytes 1572872 | tf_op jit(solution)/shard_map/ppermute | solution.py:86
  35.5 14.7 %collective-permute-start.9 = (bf16[128,1024]{1,0:T(8,128)(2,1)S(1)}, bf16[128,1024]{1,0:T(8,128)(2,1)S(1)}, u32[]{:S(2)}, u32[]{:S(2)}) collective-permute-start(bf16[128,1024]{1,0:T(8,128)(2,1)S(1)} %collective-permute-done.8.refs_7_), channel_id=1, source_target_pairs={{0,7},{1,0},{2,1},{3,2},{4,3},{5,4},{6,5},{7,6},{8,15},{9,8},{10,9... | collective-permute-start | bytes 786440 | tf_op jit(solution)/shard_map/ppermute | solution.py:91
  40.2 35.9 %collective-permute-start = (bf16[512,512]{1,0:T(8,128)(2,1)}, bf16[512,512]{1,0:T(8,128)(2,1)S(1)}, u32[]{:S(2)}, u32[]{:S(2)}) collective-permute-start(bf16[512,512]{1,0:T(8,128)(2,1)} %get-tuple-element.9), channel_id=1, source_target_pairs={{0,16},{16,0},{1,17},{17,1},{2,18},{18,2},{3,19},{19,3},{4,20},{20... | collective-permute-start | bytes 1572872 | tf_op jit(solution)/shard_map/ppermute | solution.py:86
  43.7 14.5 %copy-start.4 = (bf16[128,1024]{1,0:T(8,128)(2,1)}, bf16[128,1024]{1,0:T(8,128)(2,1)S(1)}, u32[]{:S(2)}) copy-start(bf16[128,1024]{1,0:T(8,128)(2,1)S(1)} %collective-permute-done.5.refs_2_) | copy-start | bytes 786436
  43.7 11.0 %collective-permute-start.6 = (bf16[128,1024]{1,0:T(8,128)(2,1)S(1)}, bf16[128,1024]{1,0:T(8,128)(2,1)S(1)}, u32[]{:S(2)}, u32[]{:S(2)}) collective-permute-start(bf16[128,1024]{1,0:T(8,128)(2,1)S(1)} %collective-permute-done.5.refs_2_), channel_id=1, source_target_pairs={{0,1},{1,2},{2,3},{3,4},{4,5},{5,6},{6,7},{7,0},{8,9},{9,10},{10,1... | collective-permute-start | bytes 786440 | tf_op jit(solution)/shard_map/ppermute | solution.py:91
  45.6 30.5 %collective-permute-start.11 = (bf16[128,1024]{1,0:T(8,128)(2,1)S(1)}, bf16[128,1024]{1,0:T(8,128)(2,1)}, u32[]{:S(2)}, u32[]{:S(2)}) collective-permute-start(bf16[128,1024]{1,0:T(8,128)(2,1)S(1)} %pad_maximum_fusion.refs_0_), channel_id=1, source_target_pairs={{0,7},{1,0},{2,1},{3,2},{4,3},{5,4},{6,5},{7,6},{8,15},{9,8},{10,9... | collective-permute-start | bytes 786440 | tf_op jit(solution)/shard_map/ppermute | solution.py:91
  50.2 25.9 %collective-permute-start.4 = (bf16[128,1024]{1,0:T(8,128)(2,1)S(1)}, bf16[128,1024]{1,0:T(8,128)(2,1)}, u32[]{:S(2)}, u32[]{:S(2)}) collective-permute-start(bf16[128,1024]{1,0:T(8,128)(2,1)S(1)} %pad_maximum_fusion.refs_0_), channel_id=1, source_target_pairs={{0,1},{1,2},{2,3},{3,4},{4,5},{5,6},{6,7},{7,0},{8,9},{9,10},{10,1... | collective-permute-start | bytes 786440 | tf_op jit(solution)/shard_map/ppermute | solution.py:91
  54.7 21.4 %collective-permute-start.10 = (bf16[64,1024]{1,0:T(8,128)(2,1)}, bf16[64,1024]{1,0:T(8,128)(2,1)}, u32[]{:S(2)}, u32[]{:S(2)}) collective-permute-start(bf16[64,1024]{1,0:T(8,128)(2,1)} %slice.57), channel_id=1, source_target_pairs={{0,7},{1,0},{2,1},{3,2},{4,3},{5,4},{6,5},{7,6},{8,15},{9,8},{10,9... | collective-permute-start | bytes 393224 | tf_op jit(solution)/shard_map/ppermute | solution.py:91
  58.2 18.0 %collective-permute-start.7 = (bf16[64,1024]{1,0:T(8,128)(2,1)}, bf16[64,1024]{1,0:T(8,128)(2,1)}, u32[]{:S(2)}, u32[]{:S(2)}) collective-permute-start(bf16[64,1024]{1,0:T(8,128)(2,1)} %slice.56), channel_id=1, source_target_pairs={{0,1},{1,2},{2,3},{3,4},{4,5},{5,6},{6,7},{7,0},{8,9},{9,10},{10,1... | collective-permute-start | bytes 393224 | tf_op jit(solution)/shard_map/ppermute | solution.py:91
  110.8 31.4 %copy-start.12 = (bf16[1,128,1024]{2,1,0:T(8,128)(2,1)S(1)}, bf16[1,128,1024]{2,1,0:T(8,128)(2,1)}, u32[]{:S(2)}) copy-start(bf16[1,128,1024]{2,1,0:T(8,128)(2,1)} %param.17) | copy-start | bytes 786436
  111.5 31.4 %copy-start.13 = (bf16[1,128,1024]{2,1,0:T(8,128)(2,1)S(1)}, bf16[1,128,1024]{2,1,0:T(8,128)(2,1)}, u32[]{:S(2)}) copy-start(bf16[1,128,1024]{2,1,0:T(8,128)(2,1)} %param.18) | copy-start | bytes 786436
  111.5 36.3 %copy-start.8 = (f32[512,256]{1,0:T(8,128)S(1)}, f32[512,256]{1,0:T(8,128)}, u32[]{:S(2)}) copy-start(f32[512,256]{1,0:T(8,128)} %param.12) | copy-start | bytes 1572868
  111.5 36.3 %copy-start.9 = (bf16[512,256]{1,0:T(8,128)(2,1)S(1)}, bf16[512,256]{1,0:T(8,128)(2,1)}, u32[]{:S(2)}) copy-start(bf16[512,256]{1,0:T(8,128)(2,1)} %param.14) | copy-start | bytes 786436
  111.5 36.3 %copy-start.10 = (bf16[512,256]{1,0:T(8,128)(2,1)S(1)}, bf16[512,256]{1,0:T(8,128)(2,1)}, u32[]{:S(2)}) copy-start(bf16[512,256]{1,0:T(8,128)(2,1)} %param.13) | copy-start | bytes 786436
  138.8 9.0 %all-to-all-start.2 = ((bf16[4,128,256]{2,1,0:T(8,128)(2,1)}), bf16[4,128,256]{2,1,0:T(8,128)(2,1)S(1)}, u32[]{:S(2)}, u32[]{:S(2)}) async-start(bf16[4,128,256]{2,1,0:T(8,128)(2,1)} %broadcast_in_dim.10), calls=%async_computation.2 | async-start | bytes 524288 | tf_op jit(solution)/shard_map/all_to_all | solution.py:202
  149.1 28.2 %copy-start.6 = (f32[512,256]{1,0:T(8,128)}, f32[512,256]{1,0:T(8,128)S(1)}, u32[]{:S(2)}) copy-start(f32[512,256]{1,0:T(8,128)S(1)} %get-tuple-element.11) | copy-start | bytes 1572868
  149.9 26.1 %all-to-all-start.3 = ((bf16[128,2,128]{2,1,0:T(2,128)(2,1)}), bf16[128,2,128]{2,1,0:T(2,128)(2,1)S(1)}, u32[]{:S(2)}, u32[]{:S(2)}) async-start(bf16[128,2,128]{2,1,0:T(2,128)(2,1)} %reshape.127), calls=%async_computation.3 | async-start | bytes 131072 | tf_op jit(solution)/shard_map/all_to_all | solution.py:208
  (5 other events, 27.3 us)

commit v4 on v3

--- a/solution.py
+++ b/solution.py
@@ -91,13 +91,16 @@
     return lax.ppermute(array, axis, [(i, (i + by) % count) for i in range(count)])
 
 
-def gathered_round(piece):
+def gathered_round(piece, inputs_sent):
     half = piece.shape[0] // 2
+    piece, inputs_sent = lax.optimization_barrier((piece, inputs_sent))
+    received = swap_over(inputs_sent, "zhi")
     behind1, ahead1 = shifted(piece, "y", 1), shifted(piece, "y", -1)
     behind2, ahead2 = shifted(piece, "y", 2), shifted(piece, "y", -2)
     behind3, ahead3 = shifted(behind2, "y", 1), shifted(ahead2, "y", -1)
+    behind3, ahead3, received = lax.optimization_barrier((behind3, ahead3, received))
     across = [shifted(behind3[:half], "y", 1), shifted(ahead3[half:], "y", -1)]
-    return [piece, behind1, behind2, behind3, *across, ahead3, ahead2, ahead1]
+    return [piece, behind1, behind2, behind3, *across, ahead3, ahead2, ahead1], received
 
 
 def own_columns(columns, width, core):
@@ -106,28 +109,31 @@
     return jnp.where(core == 0, even, odd), jnp.where(core == 0, odd, even)
 
 
-def product_kernel(position, inputs, kept_other, received_own, received_other, *refs):
+def product_kernel(position, inputs, received, others, decode_own, *refs):
     *pieces, out = refs
-    half, along = position[0], position[1]
+    half, along, core = position[0], position[1], position[2]
     count = lax.axis_size("y")
     feature_count = inputs.shape[1]
-    rows = received_own.shape[0] // count
+    half_rows = received.shape[0]
+    rows = half_rows // count
     x_count, _, width = out.shape
     starts = [
         pl.multiple_of(lax.rem(along - behind + count, count) * rows, rows)
         for behind in range(count)
     ]
-    half_start = pl.multiple_of(half * received_own.shape[0], rows)
-    sides = (
-        (inputs, half_start, kept_other, half),
-        (received_own, 0, received_other, 1 - half),
-    )
-    for own, offset, other, place in sides:
+    half_start = pl.multiple_of(half * half_rows, half_rows)
+    for own, offset, other_offset, place in (
+        (inputs, half_start, 0, half),
+        (received, 0, half_rows, 1 - half),
+    ):
         left = jnp.concatenate(
             [
                 block
                 for start in starts
-                for block in (own[pl.ds(offset + start, rows), :], other[pl.ds(start, rows), :])
+                for block in (
+                    own[pl.ds(offset + start, rows), :],
+                    others[pl.ds(other_offset + start, rows), :],
+                )
             ]
         )
         target = pl.ds(pl.multiple_of(place * feature_count, feature_count), feature_count)
@@ -136,14 +142,27 @@
             out[x, target, :] = lax.dot_general(
                 left, right, (((0,), (0,)), ((), ())), preferred_element_type=jnp.float32
             ).astype(out.dtype)
-
-
-def products(half, inputs, kept_other, received_own, received_other, pieces, x_count):
+    decode_rows, decode_parts = decode_own.shape[0], feature_count // width
+    for rows_of_core, place in (
+        (decode_own[...], core),
+        (others[2 * half_rows :, :], 1 - core),
+    ):
+        for part in range(decode_parts):
+            start = 2 * feature_count + (place * decode_parts + part) * decode_rows
+            target = pl.ds(pl.multiple_of(start, decode_rows), decode_rows)
+            for x in range(x_count):
+                out[x, target, :] = rows_of_core[:, part * width : (part + 1) * width]
+
+
+def products(inputs, received, others, decode_own, pieces, x_count):
     feature_count = inputs.shape[1]
     width = pieces[0].shape[1] // x_count
-    position = jnp.stack([half, lax.axis_index("y")]).astype(jnp.int32)
-    operands = (inputs, kept_other, received_own, received_other, *pieces)
-    out_shape = jax.ShapeDtypeStruct((x_count, 2 * feature_count, width), jnp.bfloat16)
+    position = jnp.stack([lax.axis_index(axis) for axis in ("zhi", "y", "core")]).astype(jnp.int32)
+    operands = (inputs, received, others, decode_own, *pieces)
+    extra_rows = 2 * decode_own.size // width
+    out_shape = jax.ShapeDtypeStruct(
+        (x_count, 2 * feature_count + extra_rows, width), jnp.bfloat16
+    )
     return pl.pallas_call(
         product_kernel,
         out_shape=out_shape,
@@ -152,7 +171,7 @@
         out_specs=pl.BlockSpec(memory_space=pltpu.VMEM),
         compiler_params=pltpu.CompilerParams(vmem_limit_bytes=24 * 2**20),
         cost_estimate=pl.CostEstimate(
-            flops=4 * feature_count * received_own.shape[0] * 2 * x_count * width,
+            flops=8 * feature_count * received.shape[0] * x_count * width,
             bytes_accessed=8 * 2**20,
             transcendentals=0,
         ),
@@ -184,19 +203,22 @@
 
     grads_own, grads_sent = own_columns(learn_grads[0], block_width, core)
     piece = jnp.concatenate([grads_own, swap_over(grads_sent, "core")])
-    pieces = gathered_round(piece)
 
     inputs = learn_inputs[0]
     row_halves = inputs.reshape(2, -1, feature_count)
-    kept = lax.dynamic_index_in_dim(row_halves, half, 0, keepdims=False)
-    received = swap_over(lax.dynamic_index_in_dim(row_halves, 1 - half, 0, keepdims=False), "zhi")
-    kept_other, received_other = swap_over(kept, "core"), swap_over(received, "core")
-    decode_rows = lax.all_gather(decode_inputs, REP, axis=0, tiled=True)
-    received_other, decode_rows = lax.optimization_barrier((received_other, decode_rows))
-
-    partial = products(half, inputs, kept_other, received, received_other, pieces, x_count)
-    over_x = summed(lax.all_to_all(partial, "x", 0, 0, tiled=True))
+    kept = jnp.where(half == 0, row_halves[0], row_halves[1])
+    inputs_sent = jnp.where(half == 0, row_halves[1], row_halves[0])
+    pieces, received = gathered_round(piece, inputs_sent)
+    others = swap_over(jnp.concatenate([kept, received, decode_inputs]), "core")
+
+    partial = products(inputs, received, others, decode_inputs, pieces, x_count)
+    terms = lax.all_to_all(partial, "x", 0, 0, tiled=True)
+    over_x = summed(terms[:, : 2 * feature_count])
     over_x = over_x.reshape(2 * side_count, quarter, block_width)
+    decode_rows = terms[:, 2 * feature_count :].reshape(
+        x_count, 2, feature_count // block_width, -1, block_width
+    )
+    decode_rows = decode_rows.transpose(0, 1, 3, 2, 4).reshape(-1, feature_count)
     own_quarter = summed(lax.all_to_all(over_x, ("zhi", "side"), 0, 0, tiled=True))
     spread = jnp.broadcast_to(own_quarter[None], (side_count, quarter, block_width))
     gradient = lax.all_to_all(spread, "side", 0, 0, tiled=True)

time: 178 us -> 168 us (0.944)
  blocking collectives: 71 us -> 55.7 us
  other arithmetic: 2.48 us -> 5.55 us
  local copies, waits for them, and re-layouts: 8.31 us -> 10.4 us
    all_gather x1 -> x0, blocking collectives: 15.4 us -> none  [local(): decode_rows = lax.all_gather(decode_inputs, REP, axis=0, tiled=True)]
    unnamed x33 -> x24, local copies, waits for them, and re-layouts: 2.75 us -> 6.04 us
    all_to_all x1, waiting for transfers between devices: 4.7 us -> 1.97 us  [local(): gradient = lax.all_to_all(spread, 'side', 0, 0, tiled=True)]
    ppermute x8, waiting for transfers between devices: 8.23 us -> 10.8 us  [shifted(): lax.ppermute(array, axis, [(i, (i + by) % count) for i in range(count)])]
    squeeze x1 -> x0, local copies, waits for them, and re-layouts: 2.16 us -> none  [local(): lax.dynamic_index_in_dim(row_halves, 1 - half, 0, keepdims=False)]
    ppermute x4 -> x3, starting transfers between devices: 20.9 us -> 19.5 us  [swap_over(): return lax.ppermute(array, axis, [(0, 1), (1, 0)])]
  transfers between devices with their start and end apart: 14 -> 13, of which waited for: 5 -> 8; matrix products, arithmetic and copies ran while one was open for 1% -> 4% of each run, Pallas kernels for 0% -> 0%
where the time goes in v4:
time: 168 us; the launch traced here: 167 us
  starting transfers between devices  61.9 us (37%)
  blocking collectives  55.7 us (33%)
  waiting for transfers between devices  27.5 us (16%)
  local copies, waits for them, and re-layouts  10.4 us (6%)
  other arithmetic  5.55 us (3%)
  Pallas kernels  3.56 us (2%)
    all_to_all x1, blocking collectives, local(): terms = lax.all_to_all(partial, 'x', 0, 0, tiled=True)  29.1 us
    all_to_all x1, blocking collectives, local(): lax.all_to_all(over_x, ('zhi', 'side'), 0, 0, tiled=True)  26.6 us
    ppermute x8, starting transfers between devices, shifted(): lax.ppermute(array, axis, [(i, (i + by) % count) for i in range(count)])  25.6 us
    ppermute x3, starting transfers between devices, swap_over(): return lax.ppermute(array, axis, [(0, 1), (1, 0)])  19.5 us
    all_to_all x1, waiting for transfers between devices, local(): fresh_terms = lax.all_to_all(partial_fresh, REP + TP, 0, 0, tiled=True)  13.9 us
    all_to_all x1, starting transfers between devices, local(): fresh_terms = lax.all_to_all(partial_fresh, REP + TP, 0, 0, tiled=True)  13.4 us
    ppermute x8, waiting for transfers between devices, shifted(): lax.ppermute(array, axis, [(i, (i + by) % count) for i in range(count)])  10.8 us
    unnamed x24, local copies, waits for them, and re-layouts  6.04 us
  transfers between devices with their start and end apart: 13, of which 8 were waited for; matrix products, arithmetic and copies ran while one was open for 4% of the time, Pallas kernels for 0%

profile of v4, /device:TPU:1, one launch (start us, length us, event | category | flops | bytes accessed | tf_op | source)
XLA Modules:
  0.0 167.1 jit_solution(16418084417513605175)
XLA Ops:
  1.6 8.8 %collective-permute-start = (bf16[64,1024]{1,0:T(8,128)(2,1)S(1)}, bf16[64,1024]{1,0:T(8,128)(2,1)S(1)}, u32[]{:S(2)}, u32[]{:S(2)}) collective-permute-start(bf16[64,1024]{1,0:T(8,128)(2,1)S(1)} %get-tuple-element.20), channel_id=1, source_target_pairs={{0,16},{16,0},{1,17},{17,1},{2,18},{18,2},{3,19},{19,3},{4,20},{20... | collective-permute-start | bytes 393224 | tf_op jit(solution)/shard_map/ppermute | solution.py:86
  11.8 1.9 %collective-permute-start.1 = (bf16[128,1024]{1,0:T(8,128)(2,1)S(1)}, bf16[128,1024]{1,0:T(8,128)(2,1)S(1)}, u32[]{:S(2)}, u32[]{:S(2)}) collective-permute-start(bf16[128,1024]{1,0:T(8,128)(2,1)S(1)} %pad_maximum_fusion.1.refs_0_), channel_id=1, source_target_pairs={{0,2},{1,3},{2,4},{3,5},{4,6},{5,7},{6,0},{7,1},{8,10},{9,11},{10,... | collective-permute-start | bytes 786440 | tf_op jit(solution)/shard_map/ppermute | solution.py:91
  13.8 5.5 %collective-permute-start.3 = (bf16[128,1024]{1,0:T(8,128)(2,1)S(1)}, bf16[128,1024]{1,0:T(8,128)(2,1)S(1)}, u32[]{:S(2)}, u32[]{:S(2)}) collective-permute-start(bf16[128,1024]{1,0:T(8,128)(2,1)S(1)} %pad_maximum_fusion.1.refs_0_), channel_id=1, source_target_pairs={{0,6},{1,7},{2,0},{3,1},{4,2},{5,3},{6,4},{7,5},{8,14},{9,15},{10,... | collective-permute-start | bytes 786440 | tf_op jit(solution)/shard_map/ppermute | solution.py:91
  19.2 5.7 %collective-permute-start.5 = (bf16[512,512]{1,0:T(8,128)(2,1)S(1)}, bf16[512,512]{1,0:T(8,128)(2,1)S(1)}, u32[]{:S(2)}, u32[]{:S(2)}) collective-permute-start(bf16[512,512]{1,0:T(8,128)(2,1)S(1)} %get-tuple-element.10), channel_id=1, source_target_pairs={{0,8},{8,0},{1,9},{9,1},{2,10},{10,2},{3,11},{11,3},{4,12},{12,4},... | collective-permute-start | bytes 1572872 | tf_op jit(solution)/shard_map/ppermute | solution.py:86
  24.9 3.2 %collective-permute-done.1.refs_2_ = bf16[128,1024]{1,0:T(8,128)(2,1)S(1)} collective-permute-done((bf16[128,1024]{1,0:T(8,128)(2,1)S(1)}, bf16[128,1024]{1,0:T(8,128)(2,1)S(1)}, u32[]{:S(2)}, u32[]{:S(2)}) %collective-permute-start.1) | collective-permute-done | bytes 262176 | tf_op jit(solution)/shard_map/ppermute | solution.py:91
  28.1 1.9 %collective-permute-start.2 = (bf16[128,1024]{1,0:T(8,128)(2,1)S(1)}, bf16[128,1024]{1,0:T(8,128)(2,1)S(1)}, u32[]{:S(2)}, u32[]{:S(2)}) collective-permute-start(bf16[128,1024]{1,0:T(8,128)(2,1)S(1)} %collective-permute-done.1.refs_2_), channel_id=1, source_target_pairs={{0,1},{1,2},{2,3},{3,4},{4,5},{5,6},{6,7},{7,0},{8,9},{9,10},{10,1... | collective-permute-start | bytes 786440 | tf_op jit(solution)/shard_map/ppermute | solution.py:91
  30.7 4.6 %collective-permute-start.4 = (bf16[128,1024]{1,0:T(8,128)(2,1)S(1)}, bf16[128,1024]{1,0:T(8,128)(2,1)S(1)}, u32[]{:S(2)}, u32[]{:S(2)}) collective-permute-start(bf16[128,1024]{1,0:T(8,128)(2,1)S(1)} %collective-permute-done.3.refs_7_), channel_id=1, source_target_pairs={{0,7},{1,0},{2,1},{3,2},{4,3},{5,4},{6,5},{7,6},{8,15},{9,8},{10,9... | collective-permute-start | bytes 786440 | tf_op jit(solution)/shard_map/ppermute | solution.py:91
  36.0 2.6 %collective-permute-done.2.refs_3_ = bf16[128,1024]{1,0:T(8,128)(2,1)S(1)} collective-permute-done((bf16[128,1024]{1,0:T(8,128)(2,1)S(1)}, bf16[128,1024]{1,0:T(8,128)(2,1)S(1)}, u32[]{:S(2)}, u32[]{:S(2)}) %collective-permute-start.2) | collective-permute-done | bytes 262176 | tf_op jit(solution)/shard_map/ppermute | solution.py:91
  38.7 1.6 collective-permute-done.4.refs_6_
  42.1 5.0 %collective-permute-start.6 = (bf16[1040,512]{1,0:T(8,128)(2,1)}, bf16[1040,512]{1,0:T(8,128)(2,1)S(1)}, u32[]{:S(2)}, u32[]{:S(2)}) collective-permute-start(bf16[1040,512]{1,0:T(8,128)(2,1)} %pad_maximum_fusion), channel_id=1, source_target_pairs={{0,16},{16,0},{1,17},{17,1},{2,18},{18,2},{3,19},{19,3},{4,20},{20... | collective-permute-start | bytes 3194888 | tf_op jit(solution)/shard_map/ppermute | solution.py:86
  47.1 3.0 %collective-permute-start.10 = (bf16[128,1024]{1,0:T(8,128)(2,1)S(1)}, bf16[128,1024]{1,0:T(8,128)(2,1)}, u32[]{:S(2)}, u32[]{:S(2)}) collective-permute-start(bf16[128,1024]{1,0:T(8,128)(2,1)S(1)} %pad_maximum_fusion.1.refs_0_), channel_id=1, source_target_pairs={{0,7},{1,0},{2,1},{3,2},{4,3},{5,4},{6,5},{7,6},{8,15},{9,8},{10,9... | collective-permute-start | bytes 786440 | tf_op jit(solution)/shard_map/ppermute | solution.py:91
  50.1 2.3 %collective-permute-start.7 = (bf16[128,1024]{1,0:T(8,128)(2,1)S(1)}, bf16[128,1024]{1,0:T(8,128)(2,1)}, u32[]{:S(2)}, u32[]{:S(2)}) collective-permute-start(bf16[128,1024]{1,0:T(8,128)(2,1)S(1)} %pad_maximum_fusion.1.refs_0_), channel_id=1, source_target_pairs={{0,1},{1,2},{2,3},{3,4},{4,5},{5,6},{6,7},{7,0},{8,9},{9,10},{10,1... | collective-permute-start | bytes 786440 | tf_op jit(solution)/shard_map/ppermute | solution.py:91
  53.1 1.9 %collective-permute-start.8 = (bf16[64,1024]{1,0:T(8,128)(2,1)}, bf16[64,1024]{1,0:T(8,128)(2,1)}, u32[]{:S(2)}, u32[]{:S(2)}) collective-permute-start(bf16[64,1024]{1,0:T(8,128)(2,1)} %slice.62), channel_id=1, source_target_pairs={{0,1},{1,2},{2,3},{3,4},{4,5},{5,6},{6,7},{7,0},{8,9},{9,10},{10,1... | collective-permute-start | bytes 393224 | tf_op jit(solution)/shard_map/ppermute | solution.py:91
  55.7 4.6 %collective-permute-start.9 = (bf16[64,1024]{1,0:T(8,128)(2,1)}, bf16[64,1024]{1,0:T(8,128)(2,1)}, u32[]{:S(2)}, u32[]{:S(2)}) collective-permute-start(bf16[64,1024]{1,0:T(8,128)(2,1)} %slice.63), channel_id=1, source_target_pairs={{0,7},{1,0},{2,1},{3,2},{4,3},{5,4},{6,5},{7,6},{8,15},{9,8},{10,9... | collective-permute-start | bytes 393224 | tf_op jit(solution)/shard_map/ppermute | solution.py:91
  60.9 2.8 %collective-permute-done.8.refs_4_ = bf16[64,1024]{1,0:T(8,128)(2,1)} collective-permute-done((bf16[64,1024]{1,0:T(8,128)(2,1)}, bf16[64,1024]{1,0:T(8,128)(2,1)}, u32[]{:S(2)}, u32[]{:S(2)}) %collective-permute-start.8) | collective-permute-done | bytes 131104 | tf_op jit(solution)/shard_map/ppermute | solution.py:91
  65.7 3.6 %products.1 = bf16[4,1088,256]{2,1,0:T(8,128)(2,1)S(1)} custom-call(s32[3]{0:T(128)S(1)} %pad_add_fusion.position, bf16[1024,512]{1,0:T(8,128)(2,1)S(1)} %bitcast.45, bf16[512,512]{1,0:T(8,128)(2,1)S(1)} %collective-permute-done.5.received, bf16[1040,512]{1,0:T(8,128)(2,1)S(1)} %collective-permute-done.6.others, bf16[16,512]{1,0:T(8,128)(2,1)S(1)} %copy-done.2, ...), custom_call_target="tpu_custom_call" | custom-call | flops 2147483648 | bytes 8388608 | tf_op jit(solution)/shard_map/products/pallas_call | solution.py:166
  69.2 29.1 %all_to_all.20 = bf16[4,1088,256]{2,1,0:T(8,128)(2,1)S(1)} all-to-all(bf16[4,1088,256]{2,1,0:T(8,128)(2,1)S(1)} %products.1), channel_id=1, replica_groups=mesh['side'=4,'x'=4,'core'=2,'zhi'=2,'y'=8] {'x'}, dimensions={0} | all-to-all | bytes 4456448 | tf_op jit(solution)/shard_map/all_to_all | solution.py:215
  98.6 26.6 %all_to_all.21 = bf16[8,128,256]{2,1,0:T(8,128)(2,1)S(1)} all-to-all(bf16[8,128,256]{2,1,0:T(8,128)(2,1)S(1)} %bitcast.46), channel_id=1, replica_groups=mesh['side'=4,'x'=4,'core'=2,'zhi'=2,'y'=8] {'zhi','side'}, dimensions={0} | all-to-all | bytes 1048576 | tf_op jit(solution)/shard_map/all_to_all | solution.py:222
  126.0 3.4 %all-to-all-start.2 = ((bf16[4,128,256]{2,1,0:T(8,128)(2,1)}), bf16[4,128,256]{2,1,0:T(8,128)(2,1)S(1)}, u32[]{:S(2)}, u32[]{:S(2)}) async-start(bf16[4,128,256]{2,1,0:T(8,128)(2,1)} %broadcast_in_dim.10), calls=%async_computation.2 | async-start | bytes 524288 | tf_op jit(solution)/shard_map/all_to_all | solution.py:224
  131.1 1.7 %copy.27 = bf16[16,8,8,128]{3,2,1,0:T(8,128)(2,1)} copy(bf16[16,8,8,128]{3,1,2,0:T(8,128)(2,1)} %bitcast.53) | data formatting | bytes 524288
  133.1 2.0 %all-to-all-done.2 = bf16[4,128,256]{2,1,0:T(8,128)(2,1)S(1)} async-done(((bf16[4,128,256]{2,1,0:T(8,128)(2,1)}), bf16[4,128,256]{2,1,0:T(8,128)(2,1)S(1)}, u32[]{:S(2)}, u32[]{:S(2)}) %all-to-all-start.2) | async-done | bytes 262176 | tf_op jit(solution)/shard_map/all_to_all | solution.py:224
  135.0 2.3 %fusion.5 = (bf16[512,256]{1,0:T(8,128)(2,1)}, f32[512,256]{1,0:T(8,128)S(1)}, bf16[512,256]{1,0:T(8,128)(2,1)}) fusion(bf16[512,256]{1,0:T(8,128)(2,1)} %param.14, bf16[4,128,256]{2,1,0:T(8,128)(2,1)S(1)} %all-to-all-done.2, f32[512,256]{1,0:T(8,128)S(1)} %copy-done.8, bf16[512,256]{1,0:T(8,128)(2,1)} %param.13), kind=kLoop, calls=%fused_computation.16 | loop fusion | flops 2621440 | bytes 2359296 | tf_op jit(solution)/shard_map/convert_element_type | solution.py:31
  138.2 13.4 %all-to-all-start.3 = ((bf16[128,2,128]{2,1,0:T(2,128)(2,1)}), bf16[128,2,128]{2,1,0:T(2,128)(2,1)S(1)}, u32[]{:S(2)}, u32[]{:S(2)}) async-start(bf16[128,2,128]{2,1,0:T(2,128)(2,1)} %reshape.143), calls=%async_computation.3 | async-start | bytes 131072 | tf_op jit(solution)/shard_map/all_to_all | solution.py:230
  151.9 13.9 %all-to-all-done.3 = bf16[128,2,128]{2,1,0:T(2,128)(2,1)S(1)} async-done(((bf16[128,2,128]{2,1,0:T(2,128)(2,1)}), bf16[128,2,128]{2,1,0:T(2,128)(2,1)S(1)}, u32[]{:S(2)}, u32[]{:S(2)}) %all-to-all-start.3) | async-done | bytes 65568 | tf_op jit(solution)/shard_map/all_to_all | solution.py:230
  (57 shorter events, 14.2 us)
Async XLA Ops:
  0.6 132.2 %copy-start = (bf16[1,8192]{1,0:T(2,128)(2,1)S(1)}, bf16[1,8192]{1,0:T(2,128)(2,1)}, u32[]{:S(2)}) copy-start(bf16[1,8192]{1,0:T(2,128)(2,1)} %param.16) | copy-start | bytes 49156
  0.6 40.4 %copy-start.2 = (bf16[16,512]{1,0:T(8,128)(2,1)S(1)}, bf16[16,512]{1,0:T(8,128)(2,1)}, u32[]{:S(2)}) copy-start(bf16[16,512]{1,0:T(8,128)(2,1)} %decode_own.1) | copy-start | bytes 49156
  1.6 10.2 %collective-permute-start = (bf16[64,1024]{1,0:T(8,128)(2,1)S(1)}, bf16[64,1024]{1,0:T(8,128)(2,1)S(1)}, u32[]{:S(2)}, u32[]{:S(2)}) collective-permute-start(bf16[64,1024]{1,0:T(8,128)(2,1)S(1)} %get-tuple-element.20), channel_id=1, source_target_pairs={{0,16},{16,0},{1,17},{17,1},{2,18},{18,2},{3,19},{19,3},{4,20},{20... | collective-permute-start | bytes 393224 | tf_op jit(solution)/shard_map/ppermute | solution.py:86
  10.4 53.3 %copy-start.1 = (bf16[1,1024,512]{2,1,0:T(8,128)(2,1)S(1)}, bf16[1,1024,512]{2,1,0:T(8,128)(2,1)}, u32[]{:S(2)}) copy-start(bf16[1,1024,512]{2,1,0:T(8,128)(2,1)} %param.10) | copy-start | bytes 3145732
  11.8 16.3 %collective-permute-start.1 = (bf16[128,1024]{1,0:T(8,128)(2,1)S(1)}, bf16[128,1024]{1,0:T(8,128)(2,1)S(1)}, u32[]{:S(2)}, u32[]{:S(2)}) collective-permute-start(bf16[128,1024]{1,0:T(8,128)(2,1)S(1)} %pad_maximum_fusion.1.refs_0_), channel_id=1, source_target_pairs={{0,2},{1,3},{2,4},{3,5},{4,6},{5,7},{6,0},{7,1},{8,10},{9,11},{10,... | collective-permute-start | bytes 786440 | tf_op jit(solution)/shard_map/ppermute | solution.py:91
  13.8 17.0 %collective-permute-start.3 = (bf16[128,1024]{1,0:T(8,128)(2,1)S(1)}, bf16[128,1024]{1,0:T(8,128)(2,1)S(1)}, u32[]{:S(2)}, u32[]{:S(2)}) collective-permute-start(bf16[128,1024]{1,0:T(8,128)(2,1)S(1)} %pad_maximum_fusion.1.refs_0_), channel_id=1, source_target_pairs={{0,6},{1,7},{2,0},{3,1},{4,2},{5,3},{6,4},{7,5},{8,14},{9,15},{10,... | collective-permute-start | bytes 786440 | tf_op jit(solution)/shard_map/ppermute | solution.py:91
  19.2 21.8 %collective-permute-start.5 = (bf16[512,512]{1,0:T(8,128)(2,1)S(1)}, bf16[512,512]{1,0:T(8,128)(2,1)S(1)}, u32[]{:S(2)}, u32[]{:S(2)}) collective-permute-start(bf16[512,512]{1,0:T(8,128)(2,1)S(1)} %get-tuple-element.10), channel_id=1, source_target_pairs={{0,8},{8,0},{1,9},{9,1},{2,10},{10,2},{3,11},{11,3},{4,12},{12,4},... | collective-permute-start | bytes 1572872 | tf_op jit(solution)/shard_map/ppermute | solution.py:86
  28.1 10.5 %collective-permute-start.2 = (bf16[128,1024]{1,0:T(8,128)(2,1)S(1)}, bf16[128,1024]{1,0:T(8,128)(2,1)S(1)}, u32[]{:S(2)}, u32[]{:S(2)}) collective-permute-start(bf16[128,1024]{1,0:T(8,128)(2,1)S(1)} %collective-permute-done.1.refs_2_), channel_id=1, source_target_pairs={{0,1},{1,2},{2,3},{3,4},{4,5},{5,6},{6,7},{7,0},{8,9},{9,10},{10,1... | collective-permute-start | bytes 786440 | tf_op jit(solution)/shard_map/ppermute | solution.py:91
  30.0 0.7 copy-start.3
  30.7 9.5 %collective-permute-start.4 = (bf16[128,1024]{1,0:T(8,128)(2,1)S(1)}, bf16[128,1024]{1,0:T(8,128)(2,1)S(1)}, u32[]{:S(2)}, u32[]{:S(2)}) collective-permute-start(bf16[128,1024]{1,0:T(8,128)(2,1)S(1)} %collective-permute-done.3.refs_7_), channel_id=1, source_target_pairs={{0,7},{1,0},{2,1},{3,2},{4,3},{5,4},{6,5},{7,6},{8,15},{9,8},{10,9... | collective-permute-start | bytes 786440 | tf_op jit(solution)/shard_map/ppermute | solution.py:91
  35.3 0.7 copy-start.5
  42.1 21.7 %collective-permute-start.6 = (bf16[1040,512]{1,0:T(8,128)(2,1)}, bf16[1040,512]{1,0:T(8,128)(2,1)S(1)}, u32[]{:S(2)}, u32[]{:S(2)}) collective-permute-start(bf16[1040,512]{1,0:T(8,128)(2,1)} %pad_maximum_fusion), channel_id=1, source_target_pairs={{0,16},{16,0},{1,17},{17,1},{2,18},{18,2},{3,19},{19,3},{4,20},{20... | collective-permute-start | bytes 3194888 | tf_op jit(solution)/shard_map/ppermute | solution.py:86
  47.1 13.2 %collective-permute-start.10 = (bf16[128,1024]{1,0:T(8,128)(2,1)S(1)}, bf16[128,1024]{1,0:T(8,128)(2,1)}, u32[]{:S(2)}, u32[]{:S(2)}) collective-permute-start(bf16[128,1024]{1,0:T(8,128)(2,1)S(1)} %pad_maximum_fusion.1.refs_0_), channel_id=1, source_target_pairs={{0,7},{1,0},{2,1},{3,2},{4,3},{5,4},{6,5},{7,6},{8,15},{9,8},{10,9... | collective-permute-start | bytes 786440 | tf_op jit(solution)/shard_map/ppermute | solution.py:91
  50.1 10.8 %collective-permute-start.7 = (bf16[128,1024]{1,0:T(8,128)(2,1)S(1)}, bf16[128,1024]{1,0:T(8,128)(2,1)}, u32[]{:S(2)}, u32[]{:S(2)}) collective-permute-start(bf16[128,1024]{1,0:T(8,128)(2,1)S(1)} %pad_maximum_fusion.1.refs_0_), channel_id=1, source_target_pairs={{0,1},{1,2},{2,3},{3,4},{4,5},{5,6},{6,7},{7,0},{8,9},{9,10},{10,1... | collective-permute-start | bytes 786440 | tf_op jit(solution)/shard_map/ppermute | solution.py:91
  53.1 10.7 %collective-permute-start.8 = (bf16[64,1024]{1,0:T(8,128)(2,1)}, bf16[64,1024]{1,0:T(8,128)(2,1)}, u32[]{:S(2)}, u32[]{:S(2)}) collective-permute-start(bf16[64,1024]{1,0:T(8,128)(2,1)} %slice.62), channel_id=1, source_target_pairs={{0,1},{1,2},{2,3},{3,4},{4,5},{5,6},{6,7},{7,0},{8,9},{9,10},{10,1... | collective-permute-start | bytes 393224 | tf_op jit(solution)/shard_map/ppermute | solution.py:91
  55.7 8.1 %collective-permute-start.9 = (bf16[64,1024]{1,0:T(8,128)(2,1)}, bf16[64,1024]{1,0:T(8,128)(2,1)}, u32[]{:S(2)}, u32[]{:S(2)}) collective-permute-start(bf16[64,1024]{1,0:T(8,128)(2,1)} %slice.63), channel_id=1, source_target_pairs={{0,7},{1,0},{2,1},{3,2},{4,3},{5,4},{6,5},{7,6},{8,15},{9,8},{10,9... | collective-permute-start | bytes 393224 | tf_op jit(solution)/shard_map/ppermute | solution.py:91
  63.7 1.0 copy-start.4
  64.7 0.9 copy-start.6
  98.6 36.4 %copy-start.8 = (f32[512,256]{1,0:T(8,128)S(1)}, f32[512,256]{1,0:T(8,128)}, u32[]{:S(2)}) copy-start(f32[512,256]{1,0:T(8,128)} %param.12) | copy-start | bytes 1572868
  126.0 9.0 %all-to-all-start.2 = ((bf16[4,128,256]{2,1,0:T(8,128)(2,1)}), bf16[4,128,256]{2,1,0:T(8,128)(2,1)S(1)}, u32[]{:S(2)}, u32[]{:S(2)}) async-start(bf16[4,128,256]{2,1,0:T(8,128)(2,1)} %broadcast_in_dim.10), calls=%async_computation.2 | async-start | bytes 524288 | tf_op jit(solution)/shard_map/all_to_all | solution.py:224
  133.0 33.2 %copy-start.9 = (bf16[16,8,8,128]{3,2,1,0:T(8,128)(2,1)S(1)}, bf16[16,8,8,128]{3,2,1,0:T(8,128)(2,1)}, u32[]{:S(2)}) copy-start(bf16[16,8,8,128]{3,2,1,0:T(8,128)(2,1)} %copy.27) | copy-start | bytes 786436
  137.4 29.7 %copy-start.7 = (f32[512,256]{1,0:T(8,128)}, f32[512,256]{1,0:T(8,128)S(1)}, u32[]{:S(2)}) copy-start(f32[512,256]{1,0:T(8,128)S(1)} %get-tuple-element.17) | copy-start | bytes 1572868
  138.2 27.6 %all-to-all-start.3 = ((bf16[128,2,128]{2,1,0:T(2,128)(2,1)}), bf16[128,2,128]{2,1,0:T(2,128)(2,1)S(1)}, u32[]{:S(2)}, u32[]{:S(2)}) async-start(bf16[128,2,128]{2,1,0:T(2,128)(2,1)} %reshape.143), calls=%async_computation.3 | async-start | bytes 131072 | tf_op jit(solution)/shard_map/all_to_all | solution.py:230

commit v5 on v1

--- a/solution.py
+++ b/solution.py
@@ -1,6 +1,10 @@
+import functools
+
 import jax
 import jax.numpy as jnp
 from jax import lax
+from jax.experimental import pallas as pl
+from jax.experimental.pallas import tpu as pltpu
 from jax.sharding import Mesh
 from jax.sharding import PartitionSpec as P
 
@@ -80,13 +84,73 @@
 TP = ("zhi", "y")
 
 
-def pick_core(columns, core):
-    return lax.dynamic_index_in_dim(columns, core, axis=2, keepdims=False)
-
-
-def gather_cotangents(pieces):
-    pairs = lax.all_gather(pieces, "zhi", axis=1)
-    return lax.all_gather(pairs, "y", axis=2)
+def swap_over(array, axis):
+    return lax.ppermute(array, axis, [(0, 1), (1, 0)])
+
+
+def shifted(array, axis, by):
+    count = lax.axis_size(axis)
+    return lax.ppermute(array, axis, [(i, (i + by) % count) for i in range(count)])
+
+
+def from_behind(array, axis):
+    return [array] + [shifted(array, axis, by) for by in range(1, lax.axis_size(axis))]
+
+
+def product_kernel(for_other, position, *refs):
+    *inputs, grads, out = refs
+    half, along, core = position[0], position[1], position[2]
+    y_count, x_count, rows, _ = grads.shape
+    half_rows = y_count * rows
+    feature_count = inputs[0].shape[1]
+    width = out.shape[1]
+    column = 1 - core if for_other else core
+    columns = pl.ds(pl.multiple_of(column * width, width), width)
+    sources = [lax.rem(along - behind + x_count, x_count) for behind in range(x_count)]
+    right = jnp.concatenate(
+        [grads[y, source, :, columns] for source in sources for y in range(y_count)]
+    )
+    for blocks, place in ((inputs[:x_count], half), (inputs[x_count:], 1 - half)):
+        left = jnp.concatenate([block[:half_rows, :] for block in blocks])
+        target = pl.ds(pl.multiple_of(place * feature_count, feature_count), feature_count)
+        out[target, :] = lax.dot_general(
+            left, right, (((0,), (0,)), ((), ())), preferred_element_type=jnp.float32
+        ).astype(out.dtype)
+    if for_other:
+        decode_rows = inputs[0].shape[0] - half_rows
+        for part in range(feature_count // width):
+            for block, source in zip(inputs[:x_count], sources):
+                start = 2 * feature_count + (part * x_count + source) * decode_rows
+                target = pl.ds(pl.multiple_of(start, decode_rows), decode_rows)
+                out[target, :] = block[half_rows:, part * width : (part + 1) * width]
+
+
+def products(for_other, inputs, grads, width):
+    feature_count = inputs[0].shape[1]
+    position = jnp.stack([lax.axis_index(axis) for axis in ("zhi", "x", "core")]).astype(jnp.int32)
+    y_count, x_count, rows, _ = grads.shape
+    extra = 0
+    if for_other:
+        extra = (inputs[0].shape[0] - y_count * rows) * x_count * feature_count // width
+    dtype = jnp.bfloat16 if for_other else jnp.float32
+    return pl.pallas_call(
+        functools.partial(product_kernel, for_other),
+        out_shape=jax.ShapeDtypeStruct((2 * feature_count + extra, width), dtype),
+        in_specs=[pl.BlockSpec(memory_space=pltpu.SMEM)]
+        + [pl.BlockSpec(memory_space=pltpu.VMEM)] * (len(inputs) + 1),
+        out_specs=pl.BlockSpec(memory_space=pltpu.VMEM),
+        compiler_params=pltpu.CompilerParams(vmem_limit_bytes=32 * 2**20),
+        cost_estimate=pl.CostEstimate(
+            flops=4 * feature_count * y_count * x_count * rows * width,
+            bytes_accessed=7 * 2**20,
+            transcendentals=0,
+        ),
+        name="products_other" if for_other else "products_own",
+    )(position, *inputs, grads)
+
+
+def summed(terms):
+    return jnp.sum(terms.astype(jnp.float32), axis=0).astype(jnp.bfloat16)
 
 
 def local(
@@ -101,38 +165,47 @@
     value_cache_slots,
     cache_lengths,
 ):
-    core = lax.axis_index("core")
-    swap = [(0, 1), (1, 0)]
-    inputs_own = learn_inputs[0]
-    row_count, feature_count = inputs_own.shape
+    core, half = lax.axis_index("core"), lax.axis_index("zhi")
     x_count, side_count = lax.axis_size("x"), lax.axis_size("side")
+    feature_count = learn_inputs.shape[2]
     block_width = kv_master.shape[1]
-    columns = learn_grads[0].reshape(-1, x_count, 2, block_width)
-    grads_other = lax.ppermute(pick_core(columns, 1 - core), "core", swap)
-    pieces = jnp.stack([pick_core(columns, core), grads_other])
-    inputs_other = lax.ppermute(inputs_own, "core", swap)
-    gathered = gather_cotangents(pieces)
-    grads_all = gathered.reshape(2, row_count, x_count, block_width)
-    inputs_all = jnp.stack([inputs_own, inputs_other])
-    partial = jnp.einsum(
-        "prf,prxc->xfc", inputs_all, grads_all, preferred_element_type=jnp.float32
-    ).astype(jnp.bfloat16)
     quarter = feature_count // side_count
-    partial = partial.reshape(x_count * side_count, quarter, block_width)
-    terms = lax.all_to_all(partial, ("x", "side"), 0, 0, tiled=True)
-    own_quarter = jnp.sum(terms.astype(jnp.float32), axis=0).astype(jnp.bfloat16)
+
+    row_halves = learn_inputs[0].reshape(2, -1, feature_count)
+    received = swap_over(jnp.where(half == 0, row_halves[1], row_halves[0]), "zhi")
+    kept = jnp.concatenate([jnp.where(half == 0, row_halves[0], row_halves[1]), decode_inputs])
+
+    columns = learn_grads[0].reshape(-1, x_count, 2 * block_width).transpose(1, 0, 2)
+    piece = lax.all_to_all(columns, "x", 0, 0, tiled=True)
+    piece, kept = lax.optimization_barrier((piece, kept))
+    grads_all = lax.all_gather(piece, "y", axis=0)
+    inputs = from_behind(kept, "x") + from_behind(received, "x")
+
+    sent = products(True, inputs, grads_all, block_width)
+    sent_back = swap_over(sent, "core")
+    kept_sum = products(False, inputs, grads_all, block_width)
+    over_rep = (kept_sum + sent_back[: 2 * feature_count].astype(jnp.float32)).astype(jnp.bfloat16)
+    over_x = over_rep.reshape(2 * side_count, quarter, block_width)
+    decode_of_core = [
+        jnp.concatenate(jnp.split(array[2 * feature_count :], feature_count // block_width), axis=1)
+        for array in (sent, sent_back)
+    ]
+    decode_of_core = [array.reshape(x_count, -1, feature_count) for array in decode_of_core]
+    decode_rows = jnp.where(
+        core == 0, jnp.stack(decode_of_core, 1), jnp.stack(decode_of_core[::-1], 1)
+    ).reshape(-1, feature_count)
+    own_quarter = summed(lax.all_to_all(over_x, ("zhi", "side"), 0, 0, tiled=True))
     spread = jnp.broadcast_to(own_quarter[None], (side_count, quarter, block_width))
     gradient = lax.all_to_all(spread, "side", 0, 0, tiled=True)
     gradient = gradient.reshape(feature_count, block_width).astype(jnp.float32)
     master_new, first_new, second_new = adamw(kv_master, first_moment, second_moment, gradient)
     rounded_weights = master_new.astype(jnp.bfloat16)
-    decode_rows = lax.all_gather(decode_inputs, REP, axis=0, tiled=True)
     partial_fresh = jnp.dot(decode_rows, rounded_weights, preferred_element_type=jnp.float32)
-    rep_count, tp_count = lax.axis_size(REP), lax.axis_size(TP)
-    partial_fresh = partial_fresh.reshape(rep_count, tp_count, block_width)
-    fresh_terms = lax.all_to_all(partial_fresh, TP, 1, 1, tiled=True)
-    fresh_block = jnp.sum(fresh_terms, axis=1).astype(jnp.bfloat16)
-    fresh_output = lax.all_to_all(fresh_block, REP, 0, 0, tiled=True).reshape(1, -1)
+    partial_fresh = partial_fresh.astype(jnp.bfloat16).reshape(-1, 2, block_width // 2)
+    fresh_terms = lax.all_to_all(partial_fresh, REP + TP, 0, 0, tiled=True)
+    fresh_terms = fresh_terms.reshape(lax.axis_size(REP), lax.axis_size(TP), block_width)
+    fresh_output = jnp.sum(fresh_terms.astype(jnp.float32), axis=1).astype(jnp.bfloat16)
+    fresh_output = fresh_output.reshape(1, -1)
     attended = attend(queries, key_cache_slots, value_cache_slots, cache_lengths, fresh_output)
     return (master_new, first_new, second_new, attended)
 

time: 192 us -> 172 us (0.90)
  blocking collectives: 62.7 us -> 0 us
  starting transfers between devices: 27.6 us -> 62.7 us
  Pallas kernels: 0 us -> 5.01 us
  matrix products: 5.41 us -> 0.87 us
  waiting for transfers between devices: 73.2 us -> 76.3 us
  local copies, waits for them, and re-layouts: 5.76 us -> 8.73 us
    all_gather x1, waiting for transfers between devices: 55.3 us -> 0.01 us  [local(): grads_all = lax.all_gather(piece, 'y', axis=0)]
    all_to_all x1 -> x0, blocking collectives: 34.2 us -> none  [local(): terms = lax.all_to_all(partial, ('x', 'side'), 0, 0, tiled=True)]
    ppermute x2 -> x8, waiting for transfers between devices: 3.18 us -> 34.8 us  [the longest x6 32 us: shifted(): lax.ppermute(array, axis, [(i, (i + by) % count) for i in range(count)])]
    all_gather x2 -> x0, blocking collectives: 28.5 us -> none  [the longest x1 14.3 us: local(): decode_rows = lax.all_gather(decode_inputs, REP, axis=0, tiled=True)]
    all_to_all x2 -> x3, waiting for transfers between devices: 14.6 us -> 35 us  [the longest x1 16.3 us: local(): lax.all_to_all(over_x, ('zhi', 'side'), 0, 0, tiled=True)]
    ppermute x2 -> x8, starting transfers between devices: 11.9 us -> 32.2 us  [the longest x6 17.9 us: shifted(): lax.ppermute(array, axis, [(i, (i + by) % count) for i in range(count)])]
    all_to_all x2 -> x3, starting transfers between devices: 12.1 us -> 27.1 us  [the longest x1 13 us: local(): fresh_terms = lax.all_to_all(partial_fresh, REP + TP, 0, 0, tiled=True)]
    all_to_all x1, waiting for transfers between devices: 0.01 us -> 6.48 us  [local(): gradient = lax.all_to_all(spread, 'side', 0, 0, tiled=True)]
  transfers between devices with their start and end apart: 6 -> 13, of which waited for: 5 -> 8; matrix products, arithmetic and copies ran while one was open for 0% -> 1% of each run, Pallas kernels for 0% -> 1%
where the time goes in v5:
time: 172 us; the launch traced here: 171 us
  waiting for transfers between devices  76.3 us (44%)
  starting transfers between devices  62.7 us (36%)
  between operations  15 us (9%)
  local copies, waits for them, and re-layouts  8.73 us (5%)
  Pallas kernels  5.01 us (3%)
  other arithmetic  2.85 us (2%)
    ppermute x6, waiting for transfers between devices, shifted(): lax.ppermute(array, axis, [(i, (i + by) % count) for i in range(count)])  32 us
    ppermute x6, starting transfers between devices, shifted(): lax.ppermute(array, axis, [(i, (i + by) % count) for i in range(count)])  17.9 us
    all_to_all x1, waiting for transfers between devices, local(): lax.all_to_all(over_x, ('zhi', 'side'), 0, 0, tiled=True)  16.3 us
    ppermute x2, starting transfers between devices, swap_over(): return lax.ppermute(array, axis, [(0, 1), (1, 0)])  14.3 us
    all_to_all x1, waiting for transfers between devices, local(): fresh_terms = lax.all_to_all(partial_fresh, REP + TP, 0, 0, tiled=True)  13.9 us
    all_to_all x1, starting transfers between devices, local(): fresh_terms = lax.all_to_all(partial_fresh, REP + TP, 0, 0, tiled=True)  13 us
    all_to_all x1, starting transfers between devices, local(): lax.all_to_all(over_x, ('zhi', 'side'), 0, 0, tiled=True)  9.23 us
    all_to_all x1, waiting for transfers between devices, local(): gradient = lax.all_to_all(spread, 'side', 0, 0, tiled=True)  6.48 us
  transfers between devices with their start and end apart: 13, of which 8 were waited for; matrix products, arithmetic and copies ran while one was open for 1% of the time, Pallas kernels for 1%

profile of v5, /device:TPU:1, one launch (start us, length us, event | category | flops | bytes accessed | tf_op | source)
XLA Modules:
  0.0 171.4 jit_solution(4075846087364064720)
XLA Ops:
  9.2 4.8 %all-to-all-start = ((bf16[4,64,512]{2,1,0:T(8,128)(2,1)}), bf16[4,64,512]{2,1,0:T(8,128)(2,1)S(1)}, u32[]{:S(2)}, u32[]{:S(2)}) async-start(bf16[4,64,512]{2,1,0:T(8,128)(2,1)} %copy.37), calls=%async_computation | async-start | bytes 524288 | tf_op jit(solution)/shard_map/all_to_all | solution.py:179
  14.8 4.8 %all-to-all-done = bf16[4,64,512]{2,1,0:T(8,128)(2,1)S(1)} async-done(((bf16[4,64,512]{2,1,0:T(8,128)(2,1)}), bf16[4,64,512]{2,1,0:T(8,128)(2,1)S(1)}, u32[]{:S(2)}, u32[]{:S(2)}) %all-to-all-start) | async-done | bytes 262176 | tf_op jit(solution)/shard_map/all_to_all | solution.py:179
  20.3 2.2 %collective-permute-start = (bf16[528,512]{1,0:T(8,128)(2,1)S(1)}, bf16[528,512]{1,0:T(8,128)(2,1)S(1)}, u32[]{:S(2)}, u32[]{:S(2)}) collective-permute-start(bf16[528,512]{1,0:T(8,128)(2,1)S(1)} %pad_maximum_fusion.refs_0_), channel_id=1, source_target_pairs={{0,32},{32,64},{64,96},{96,0},{1,33},{33,65},{65,97},{97,1},{2,34}... | collective-permute-start | bytes 1622024 | tf_op jit(solution)/shard_map/ppermute | solution.py:93
  22.5 10.7 %collective-permute-start.3 = (bf16[512,512]{1,0:T(8,128)(2,1)S(1)}, bf16[512,512]{1,0:T(8,128)(2,1)S(1)}, u32[]{:S(2)}, u32[]{:S(2)}) collective-permute-start(bf16[512,512]{1,0:T(8,128)(2,1)S(1)} %get-tuple-element.8), channel_id=1, source_target_pairs={{0,8},{8,0},{1,9},{9,1},{2,10},{10,2},{3,11},{11,3},{4,12},{12,4},... | collective-permute-start | bytes 1572872 | tf_op jit(solution)/shard_map/ppermute | solution.py:88
  33.2 3.6 %collective-permute-start.1 = (bf16[528,512]{1,0:T(8,128)(2,1)S(1)}, bf16[528,512]{1,0:T(8,128)(2,1)S(1)}, u32[]{:S(2)}, u32[]{:S(2)}) collective-permute-start(bf16[528,512]{1,0:T(8,128)(2,1)S(1)} %pad_maximum_fusion.refs_0_), channel_id=1, source_target_pairs={{0,64},{32,96},{64,0},{96,32},{1,65},{33,97},{65,1},{97,33},{2,66}... | collective-permute-start | bytes 1622024 | tf_op jit(solution)/shard_map/ppermute | solution.py:93
  36.8 2.6 %collective-permute-start.2 = (bf16[528,512]{1,0:T(8,128)(2,1)S(1)}, bf16[528,512]{1,0:T(8,128)(2,1)S(1)}, u32[]{:S(2)}, u32[]{:S(2)}) collective-permute-start(bf16[528,512]{1,0:T(8,128)(2,1)S(1)} %pad_maximum_fusion.refs_0_), channel_id=1, source_target_pairs={{0,96},{32,0},{64,32},{96,64},{1,97},{33,1},{65,33},{97,65},{2,98}... | collective-permute-start | bytes 1622024 | tf_op jit(solution)/shard_map/ppermute | solution.py:93
  39.4 2.8 %collective-permute-done.3.refs_4_ = bf16[512,512]{1,0:T(8,128)(2,1)S(1)} collective-permute-done((bf16[512,512]{1,0:T(8,128)(2,1)S(1)}, bf16[512,512]{1,0:T(8,128)(2,1)S(1)}, u32[]{:S(2)}, u32[]{:S(2)}) %collective-permute-start.3) | collective-permute-done | bytes 524320 | tf_op jit(solution)/shard_map/ppermute | solution.py:88
  42.2 2.2 %collective-permute-start.4 = (bf16[512,512]{1,0:T(8,128)(2,1)S(1)}, bf16[512,512]{1,0:T(8,128)(2,1)S(1)}, u32[]{:S(2)}, u32[]{:S(2)}) collective-permute-start(bf16[512,512]{1,0:T(8,128)(2,1)S(1)} %collective-permute-done.3.refs_4_), channel_id=1, source_target_pairs={{0,32},{32,64},{64,96},{96,0},{1,33},{33,65},{65,97},{97,1},{2,34}... | collective-permute-start | bytes 1572872 | tf_op jit(solution)/shard_map/ppermute | solution.py:93
  44.4 5.1 %collective-permute-start.5 = (bf16[512,512]{1,0:T(8,128)(2,1)S(1)}, bf16[512,512]{1,0:T(8,128)(2,1)}, u32[]{:S(2)}, u32[]{:S(2)}) collective-permute-start(bf16[512,512]{1,0:T(8,128)(2,1)S(1)} %collective-permute-done.3.refs_4_), channel_id=1, source_target_pairs={{0,64},{32,96},{64,0},{96,32},{1,65},{33,97},{65,1},{97,33},{2,66}... | collective-permute-start | bytes 1572872 | tf_op jit(solution)/shard_map/ppermute | solution.py:93
  49.6 2.1 %collective-permute-start.6 = (bf16[512,512]{1,0:T(8,128)(2,1)S(1)}, bf16[512,512]{1,0:T(8,128)(2,1)}, u32[]{:S(2)}, u32[]{:S(2)}) collective-permute-start(bf16[512,512]{1,0:T(8,128)(2,1)S(1)} %collective-permute-done.3.refs_4_), channel_id=1, source_target_pairs={{0,96},{32,0},{64,32},{96,64},{1,97},{33,1},{65,33},{97,65},{2,98}... | collective-permute-start | bytes 1572872 | tf_op jit(solution)/shard_map/ppermute | solution.py:93
  51.8 12.0 %collective-permute-done.2.refs_3_ = bf16[528,512]{1,0:T(8,128)(2,1)S(1)} collective-permute-done((bf16[528,512]{1,0:T(8,128)(2,1)S(1)}, bf16[528,512]{1,0:T(8,128)(2,1)S(1)}, u32[]{:S(2)}, u32[]{:S(2)}) %collective-permute-start.2) | collective-permute-done | bytes 540704 | tf_op jit(solution)/shard_map/ppermute | solution.py:93
  63.8 7.1 %collective-permute-done.5.refs_6_ = bf16[512,512]{1,0:T(8,128)(2,1)} collective-permute-done((bf16[512,512]{1,0:T(8,128)(2,1)S(1)}, bf16[512,512]{1,0:T(8,128)(2,1)}, u32[]{:S(2)}, u32[]{:S(2)}) %collective-permute-start.5) | collective-permute-done | bytes 524320 | tf_op jit(solution)/shard_map/ppermute | solution.py:93
  70.9 12.9 %collective-permute-done.6.refs_7_ = bf16[512,512]{1,0:T(8,128)(2,1)} collective-permute-done((bf16[512,512]{1,0:T(8,128)(2,1)S(1)}, bf16[512,512]{1,0:T(8,128)(2,1)}, u32[]{:S(2)}, u32[]{:S(2)}) %collective-permute-start.6) | collective-permute-done | bytes 524320 | tf_op jit(solution)/shard_map/ppermute | solution.py:93
  83.8 1.6 copy-done.1
  85.4 2.5 %products_other.1 = bf16[1152,256]{1,0:T(8,128)(2,1)S(1)} custom-call(s32[3]{0:T(128)S(1)} %pad_add_fusion.position, bf16[528,512]{1,0:T(8,128)(2,1)S(1)} %pad_maximum_fusion.refs_0_, bf16[528,512]{1,0:T(8,128)(2,1)S(1)} %collective-permute-done.refs_1_, bf16[528,512]{1,0:T(8,128)(2,1)S(1)} %collective-permute-done.1.refs_2_, ...), custom_call_target="tpu_custom_call" | custom-call | flops 1073741824 | bytes 7340032 | tf_op jit(solution)/shard_map/products_other/pallas_call | solution.py:136
  87.9 3.6 %collective-permute-start.7 = (bf16[1152,256]{1,0:T(8,128)(2,1)S(1)}, bf16[1152,256]{1,0:T(8,128)(2,1)S(1)}, u32[]{:S(2)}, u32[]{:S(2)}) collective-permute-start(bf16[1152,256]{1,0:T(8,128)(2,1)S(1)} %products_other.1), channel_id=1, source_target_pairs={{0,16},{16,0},{1,17},{17,1},{2,18},{18,2},{3,19},{19,3},{4,20},{20... | collective-permute-start | bytes 1769480 | tf_op jit(solution)/shard_map/ppermute | solution.py:88
  91.5 2.5 %products_own.1 = f32[1024,256]{1,0:T(8,128)S(1)} custom-call(s32[3]{0:T(128)S(1)} %pad_add_fusion.position, bf16[528,512]{1,0:T(8,128)(2,1)S(1)} %pad_maximum_fusion.refs_0_, bf16[528,512]{1,0:T(8,128)(2,1)S(1)} %collective-permute-done.refs_1_, bf16[528,512]{1,0:T(8,128)(2,1)S(1)} %collective-permute-done.1.refs_2_, ...), custom_call_target="tpu_custom_call" | custom-call | flops 1073741824 | bytes 7340032 | tf_op jit(solution)/shard_map/products_own/pallas_call | solution.py:136
  95.1 9.2 %all-to-all-start.1 = ((bf16[8,128,256]{2,1,0:T(8,128)(2,1)}), bf16[8,128,256]{2,1,0:T(8,128)(2,1)S(1)}, u32[]{:S(2)}, u32[]{:S(2)}) async-start(bf16[8,128,256]{2,1,0:T(8,128)(2,1)} %bitcast.7), calls=%async_computation.1 | async-start | bytes 1048576 | tf_op jit(solution)/shard_map/all_to_all | solution.py:197
  106.0 16.3 %all-to-all-done.1 = bf16[8,128,256]{2,1,0:T(8,128)(2,1)S(1)} async-done(((bf16[8,128,256]{2,1,0:T(8,128)(2,1)}), bf16[8,128,256]{2,1,0:T(8,128)(2,1)S(1)}, u32[]{:S(2)}, u32[]{:S(2)}) %all-to-all-start.1) | async-done | bytes 524320 | tf_op jit(solution)/shard_map/all_to_all | solution.py:197
  123.1 3.4 %all-to-all-start.2 = ((bf16[4,128,256]{2,1,0:T(8,128)(2,1)}), bf16[4,128,256]{2,1,0:T(8,128)(2,1)S(1)}, u32[]{:S(2)}, u32[]{:S(2)}) async-start(bf16[4,128,256]{2,1,0:T(8,128)(2,1)} %broadcast_in_dim.10), calls=%async_computation.2 | async-start | bytes 524288 | tf_op jit(solution)/shard_map/all_to_all | solution.py:199
  127.4 6.5 %all-to-all-done.2 = bf16[4,128,256]{2,1,0:T(8,128)(2,1)S(1)} async-done(((bf16[4,128,256]{2,1,0:T(8,128)(2,1)}), bf16[4,128,256]{2,1,0:T(8,128)(2,1)S(1)}, u32[]{:S(2)}, u32[]{:S(2)}) %all-to-all-start.2) | async-done | bytes 262176 | tf_op jit(solution)/shard_map/all_to_all | solution.py:199
  133.8 1.3 fusion.5
  136.0 13.0 %all-to-all-start.3 = ((bf16[128,2,128]{2,1,0:T(2,128)(2,1)}), bf16[128,2,128]{2,1,0:T(2,128)(2,1)S(1)}, u32[]{:S(2)}, u32[]{:S(2)}) async-start(bf16[128,2,128]{2,1,0:T(2,128)(2,1)} %reshape.140), calls=%async_computation.3 | async-start | bytes 131072 | tf_op jit(solution)/shard_map/all_to_all | solution.py:205
  149.3 13.9 %all-to-all-done.3 = bf16[128,2,128]{2,1,0:T(2,128)(2,1)S(1)} async-done(((bf16[128,2,128]{2,1,0:T(2,128)(2,1)}), bf16[128,2,128]{2,1,0:T(2,128)(2,1)S(1)}, u32[]{:S(2)}, u32[]{:S(2)}) %all-to-all-start.3) | async-done | bytes 65568 | tf_op jit(solution)/shard_map/all_to_all | solution.py:205
  (62 shorter events, 9.6 us)
Async XLA Ops:
  7.2 97.9 %copy-start = (bf16[1,8192]{1,0:T(2,128)(2,1)S(1)}, bf16[1,8192]{1,0:T(2,128)(2,1)}, u32[]{:S(2)}) copy-start(bf16[1,8192]{1,0:T(2,128)(2,1)} %param.16) | copy-start | bytes 49156
  7.2 6.8 %copy-start.4 = (bf16[1,1024,512]{2,1,0:T(8,128)(2,1)S(1)}, bf16[1,1024,512]{2,1,0:T(8,128)(2,1)}, u32[]{:S(2)}) copy-start(bf16[1,1024,512]{2,1,0:T(8,128)(2,1)} %param.10) | copy-start | bytes 3145732
  9.2 10.4 %all-to-all-start = ((bf16[4,64,512]{2,1,0:T(8,128)(2,1)}), bf16[4,64,512]{2,1,0:T(8,128)(2,1)S(1)}, u32[]{:S(2)}, u32[]{:S(2)}) async-start(bf16[4,64,512]{2,1,0:T(8,128)(2,1)} %copy.37), calls=%async_computation | async-start | bytes 524288 | tf_op jit(solution)/shard_map/all_to_all | solution.py:179
  14.0 69.8 %all-gather.3.cloned.1.call-start = ((), (), s32[]{:S(2)}) async-start(), calls=%async_computation.4 | async-start | bytes 2359296 | tf_op jit(solution)/shard_map/all_gather | solution.py:181
  20.3 29.3 %collective-permute-start = (bf16[528,512]{1,0:T(8,128)(2,1)S(1)}, bf16[528,512]{1,0:T(8,128)(2,1)S(1)}, u32[]{:S(2)}, u32[]{:S(2)}) collective-permute-start(bf16[528,512]{1,0:T(8,128)(2,1)S(1)} %pad_maximum_fusion.refs_0_), channel_id=1, source_target_pairs={{0,32},{32,64},{64,96},{96,0},{1,33},{33,65},{65,97},{97,1},{2,34}... | collective-permute-start | bytes 1622024 | tf_op jit(solution)/shard_map/ppermute | solution.py:93
  22.5 19.8 %collective-permute-start.3 = (bf16[512,512]{1,0:T(8,128)(2,1)S(1)}, bf16[512,512]{1,0:T(8,128)(2,1)S(1)}, u32[]{:S(2)}, u32[]{:S(2)}) collective-permute-start(bf16[512,512]{1,0:T(8,128)(2,1)S(1)} %get-tuple-element.8), channel_id=1, source_target_pairs={{0,8},{8,0},{1,9},{9,1},{2,10},{10,2},{3,11},{11,3},{4,12},{12,4},... | collective-permute-start | bytes 1572872 | tf_op jit(solution)/shard_map/ppermute | solution.py:88
  33.2 18.6 %collective-permute-start.1 = (bf16[528,512]{1,0:T(8,128)(2,1)S(1)}, bf16[528,512]{1,0:T(8,128)(2,1)S(1)}, u32[]{:S(2)}, u32[]{:S(2)}) collective-permute-start(bf16[528,512]{1,0:T(8,128)(2,1)S(1)} %pad_maximum_fusion.refs_0_), channel_id=1, source_target_pairs={{0,64},{32,96},{64,0},{96,32},{1,65},{33,97},{65,1},{97,33},{2,66}... | collective-permute-start | bytes 1622024 | tf_op jit(solution)/shard_map/ppermute | solution.py:93
  36.8 27.0 %collective-permute-start.2 = (bf16[528,512]{1,0:T(8,128)(2,1)S(1)}, bf16[528,512]{1,0:T(8,128)(2,1)S(1)}, u32[]{:S(2)}, u32[]{:S(2)}) collective-permute-start(bf16[528,512]{1,0:T(8,128)(2,1)S(1)} %pad_maximum_fusion.refs_0_), channel_id=1, source_target_pairs={{0,96},{32,0},{64,32},{96,64},{1,97},{33,1},{65,33},{97,65},{2,98}... | collective-permute-start | bytes 1622024 | tf_op jit(solution)/shard_map/ppermute | solution.py:93
  42.2 21.6 %collective-permute-start.4 = (bf16[512,512]{1,0:T(8,128)(2,1)S(1)}, bf16[512,512]{1,0:T(8,128)(2,1)S(1)}, u32[]{:S(2)}, u32[]{:S(2)}) collective-permute-start(bf16[512,512]{1,0:T(8,128)(2,1)S(1)} %collective-permute-done.3.refs_4_), channel_id=1, source_target_pairs={{0,32},{32,64},{64,96},{96,0},{1,33},{33,65},{65,97},{97,1},{2,34}... | collective-permute-start | bytes 1572872 | tf_op jit(solution)/shard_map/ppermute | solution.py:93
  44.4 26.5 %collective-permute-start.5 = (bf16[512,512]{1,0:T(8,128)(2,1)S(1)}, bf16[512,512]{1,0:T(8,128)(2,1)}, u32[]{:S(2)}, u32[]{:S(2)}) collective-permute-start(bf16[512,512]{1,0:T(8,128)(2,1)S(1)} %collective-permute-done.3.refs_4_), channel_id=1, source_target_pairs={{0,64},{32,96},{64,0},{96,32},{1,65},{33,97},{65,1},{97,33},{2,66}... | collective-permute-start | bytes 1572872 | tf_op jit(solution)/shard_map/ppermute | solution.py:93
  49.6 34.2 %collective-permute-start.6 = (bf16[512,512]{1,0:T(8,128)(2,1)S(1)}, bf16[512,512]{1,0:T(8,128)(2,1)}, u32[]{:S(2)}, u32[]{:S(2)}) collective-permute-start(bf16[512,512]{1,0:T(8,128)(2,1)S(1)} %collective-permute-done.3.refs_4_), channel_id=1, source_target_pairs={{0,96},{32,0},{64,32},{96,64},{1,97},{33,1},{65,33},{97,65},{2,98}... | collective-permute-start | bytes 1572872 | tf_op jit(solution)/shard_map/ppermute | solution.py:93
  83.8 1.6 copy-start.1
  87.9 6.1 %copy-start.2 = (bf16[1152,256]{1,0:T(8,128)(2,1)}, bf16[1152,256]{1,0:T(8,128)(2,1)S(1)}, u32[]{:S(2)}) copy-start(bf16[1152,256]{1,0:T(8,128)(2,1)S(1)} %products_other.1) | copy-start | bytes 1769476
  87.9 6.2 %collective-permute-start.7 = (bf16[1152,256]{1,0:T(8,128)(2,1)S(1)}, bf16[1152,256]{1,0:T(8,128)(2,1)S(1)}, u32[]{:S(2)}, u32[]{:S(2)}) collective-permute-start(bf16[1152,256]{1,0:T(8,128)(2,1)S(1)} %products_other.1), channel_id=1, source_target_pairs={{0,16},{16,0},{1,17},{17,1},{2,18},{18,2},{3,19},{19,3},{4,20},{20... | collective-permute-start | bytes 1769480 | tf_op jit(solution)/shard_map/ppermute | solution.py:88
  94.0 10.3 %copy-start.10 = (bf16[1,128,1024]{2,1,0:T(8,128)(2,1)S(1)}, bf16[1,128,1024]{2,1,0:T(8,128)(2,1)}, u32[]{:S(2)}) copy-start(bf16[1,128,1024]{2,1,0:T(8,128)(2,1)} %param.18) | copy-start | bytes 786436
  94.1 1.0 copy-start.6
  95.1 9.3 %copy-start.11 = (bf16[1,128,1024]{2,1,0:T(8,128)(2,1)S(1)}, bf16[1,128,1024]{2,1,0:T(8,128)(2,1)}, u32[]{:S(2)}) copy-start(bf16[1,128,1024]{2,1,0:T(8,128)(2,1)} %param.17) | copy-start | bytes 786436
  95.1 27.3 %all-to-all-start.1 = ((bf16[8,128,256]{2,1,0:T(8,128)(2,1)}), bf16[8,128,256]{2,1,0:T(8,128)(2,1)S(1)}, u32[]{:S(2)}, u32[]{:S(2)}) async-start(bf16[8,128,256]{2,1,0:T(8,128)(2,1)} %bitcast.7), calls=%async_computation.1 | async-start | bytes 1048576 | tf_op jit(solution)/shard_map/all_to_all | solution.py:197
  106.0 27.9 %copy-start.7 = (f32[512,256]{1,0:T(8,128)S(1)}, f32[512,256]{1,0:T(8,128)}, u32[]{:S(2)}) copy-start(f32[512,256]{1,0:T(8,128)} %param.12) | copy-start | bytes 1572868
  106.0 27.9 %copy-start.8 = (bf16[512,256]{1,0:T(8,128)(2,1)S(1)}, bf16[512,256]{1,0:T(8,128)(2,1)}, u32[]{:S(2)}) copy-start(bf16[512,256]{1,0:T(8,128)(2,1)} %param.14) | copy-start | bytes 786436
  106.0 27.9 %copy-start.9 = (bf16[512,256]{1,0:T(8,128)(2,1)S(1)}, bf16[512,256]{1,0:T(8,128)(2,1)}, u32[]{:S(2)}) copy-start(bf16[512,256]{1,0:T(8,128)(2,1)} %param.13) | copy-start | bytes 786436
  123.1 10.7 %all-to-all-start.2 = ((bf16[4,128,256]{2,1,0:T(8,128)(2,1)}), bf16[4,128,256]{2,1,0:T(8,128)(2,1)S(1)}, u32[]{:S(2)}, u32[]{:S(2)}) async-start(bf16[4,128,256]{2,1,0:T(8,128)(2,1)} %broadcast_in_dim.10), calls=%async_computation.2 | async-start | bytes 524288 | tf_op jit(solution)/shard_map/all_to_all | solution.py:199
  135.2 29.4 %copy-start.3 = (f32[512,256]{1,0:T(8,128)}, f32[512,256]{1,0:T(8,128)S(1)}, u32[]{:S(2)}) copy-start(f32[512,256]{1,0:T(8,128)S(1)} %get-tuple-element.15) | copy-start | bytes 1572868
  136.0 27.2 %all-to-all-start.3 = ((bf16[128,2,128]{2,1,0:T(2,128)(2,1)}), bf16[128,2,128]{2,1,0:T(2,128)(2,1)S(1)}, u32[]{:S(2)}, u32[]{:S(2)}) async-start(bf16[128,2,128]{2,1,0:T(2,128)(2,1)} %reshape.140), calls=%async_computation.3 | async-start | bytes 131072 | tf_op jit(solution)/shard_map/all_to_all | solution.py:205
  (2 other events, 1.4 us)
Sparse Core Ops, SparseCore 0:
  20.4 44.1 all-gather.2

commit v6 on v5

--- a/solution.py
+++ b/solution.py
@@ -93,8 +93,19 @@
     return lax.ppermute(array, axis, [(i, (i + by) % count) for i in range(count)])
 
 
-def from_behind(array, axis):
-    return [array] + [shifted(array, axis, by) for by in range(1, lax.axis_size(axis))]
+def around_x(kept, received):
+    half = received.shape[0] // 2
+    upper, lower = [received[:half]], [received[half:]]
+    for step in range(lax.axis_size("x") - 1):
+        if step == 1:
+            kept, *ends = lax.optimization_barrier((kept, upper[-1], lower[-1]))
+            upper[-1], lower[-1] = ends
+        upper.append(shifted(upper[-1], "x", 1))
+        lower.append(shifted(lower[-1], "x", -1))
+    behind, ahead = shifted(kept, "x", 1), shifted(kept, "x", -1)
+    across = jnp.concatenate([shifted(behind[:half], "x", 1), shifted(ahead[half:], "x", -1)])
+    parts = [part for pair in zip(upper[1:], lower[:0:-1]) for part in pair]
+    return [kept, behind, across, ahead], [received, *parts]
 
 
 def product_kernel(for_other, position, *refs):
@@ -179,7 +190,7 @@
     piece = lax.all_to_all(columns, "x", 0, 0, tiled=True)
     piece, kept = lax.optimization_barrier((piece, kept))
     grads_all = lax.all_gather(piece, "y", axis=0)
-    inputs = from_behind(kept, "x") + from_behind(received, "x")
+    inputs = sum(around_x(kept, received), [])
 
     sent = products(True, inputs, grads_all, block_width)
     sent_back = swap_over(sent, "core")

time: 172 us -> 192 us (1.12)
  starting transfers between devices: 62.7 us -> 94 us
  waiting for transfers between devices: 76.3 us -> 58.7 us
  local copies, waits for them, and re-layouts: 8.73 us -> 14.8 us
    ppermute x6 -> x10, waiting for transfers between devices: 32 us -> 7.87 us  [shifted(): lax.ppermute(array, axis, [(i, (i + by) % count) for i in range(count)])]
    ppermute x6 -> x10, starting transfers between devices: 17.9 us -> 32 us  [shifted(): lax.ppermute(array, axis, [(i, (i + by) % count) for i in range(count)])]
    all_to_all x1, starting transfers between devices: 9.23 us -> 19.4 us  [local(): lax.all_to_all(over_x, ('zhi', 'side'), 0, 0, tiled=True)]
    ppermute x2, starting transfers between devices: 14.3 us -> 23.3 us  [swap_over(): return lax.ppermute(array, axis, [(0, 1), (1, 0)])]
    ppermute x2, waiting for transfers between devices: 2.84 us -> 9.32 us  [swap_over(): return lax.ppermute(array, axis, [(0, 1), (1, 0)])]
    unnamed x29 -> x38, local copies, waits for them, and re-layouts: 3.15 us -> 7.4 us
  transfers between devices with their start and end apart: 13 -> 17, of which waited for: 8 -> 10; matrix products, arithmetic and copies ran while one was open for 1% -> 3% of each run, Pallas kernels for 1% -> 1%
where the time goes in v6:
time: 192 us; the launch traced here: 191 us
  starting transfers between devices  94 us (49%)
  waiting for transfers between devices  58.7 us (31%)
  between operations  15.1 us (8%)
  local copies, waits for them, and re-layouts  14.8 us (8%)
  Pallas kernels  4.51 us (2%)
  other arithmetic  2.85 us (1%)
    ppermute x10, starting transfers between devices, shifted(): lax.ppermute(array, axis, [(i, (i + by) % count) for i in range(count)])  32 us
    ppermute x2, starting transfers between devices, swap_over(): return lax.ppermute(array, axis, [(0, 1), (1, 0)])  23.3 us
    all_to_all x1, starting transfers between devices, local(): lax.all_to_all(over_x, ('zhi', 'side'), 0, 0, tiled=True)  19.4 us
    all_to_all x1, waiting for transfers between devices, local(): lax.all_to_all(over_x, ('zhi', 'side'), 0, 0, tiled=True)  16.3 us
    all_to_all x1, waiting for transfers between devices, local(): fresh_terms = lax.all_to_all(partial_fresh, REP + TP, 0, 0, tiled=True)  13.9 us
    all_to_all x1, starting transfers between devices, local(): fresh_terms = lax.all_to_all(partial_fresh, REP + TP, 0, 0, tiled=True)  11.1 us
    ppermute x2, waiting for transfers between devices, swap_over(): return lax.ppermute(array, axis, [(0, 1), (1, 0)])  9.32 us
    ppermute x10, waiting for transfers between devices, shifted(): lax.ppermute(array, axis, [(i, (i + by) % count) for i in range(count)])  7.87 us
  transfers between devices with their start and end apart: 17, of which 10 were waited for; matrix products, arithmetic and copies ran while one was open for 3% of the time, Pallas kernels for 1%

profile of v6, /device:TPU:1, one launch (start us, length us, event | category | flops | bytes accessed | tf_op | source)
XLA Modules:
  0.0 190.7 jit_solution(3635517992824680817)
XLA Ops:
  9.2 4.8 %all-to-all-start = ((bf16[4,64,512]{2,1,0:T(8,128)(2,1)}), bf16[4,64,512]{2,1,0:T(8,128)(2,1)S(1)}, u32[]{:S(2)}, u32[]{:S(2)}) async-start(bf16[4,64,512]{2,1,0:T(8,128)(2,1)} %copy.37), calls=%async_computation | async-start | bytes 524288 | tf_op jit(solution)/shard_map/all_to_all | solution.py:190
  14.8 4.8 %all-to-all-done = bf16[4,64,512]{2,1,0:T(8,128)(2,1)S(1)} async-done(((bf16[4,64,512]{2,1,0:T(8,128)(2,1)}), bf16[4,64,512]{2,1,0:T(8,128)(2,1)S(1)}, u32[]{:S(2)}, u32[]{:S(2)}) %all-to-all-start) | async-done | bytes 262176 | tf_op jit(solution)/shard_map/all_to_all | solution.py:190
  20.3 10.7 %collective-permute-start = (bf16[512,512]{1,0:T(8,128)(2,1)S(1)}, bf16[512,512]{1,0:T(8,128)(2,1)S(1)}, u32[]{:S(2)}, u32[]{:S(2)}) collective-permute-start(bf16[512,512]{1,0:T(8,128)(2,1)S(1)} %get-tuple-element.14), channel_id=1, source_target_pairs={{0,8},{8,0},{1,9},{9,1},{2,10},{10,2},{3,11},{11,3},{4,12},{12,4},... | collective-permute-start | bytes 1572872 | tf_op jit(solution)/shard_map/ppermute | solution.py:88
  30.9 9.3 %collective-permute-done.refs_4_ = bf16[512,512]{1,0:T(8,128)(2,1)S(1)} collective-permute-done((bf16[512,512]{1,0:T(8,128)(2,1)S(1)}, bf16[512,512]{1,0:T(8,128)(2,1)S(1)}, u32[]{:S(2)}, u32[]{:S(2)}) %collective-permute-start) | collective-permute-done | bytes 524320 | tf_op jit(solution)/shard_map/ppermute | solution.py:88
  40.3 2.3 %collective-permute-start.1 = (bf16[256,512]{1,0:T(8,128)(2,1)S(1)}, bf16[256,512]{1,0:T(8,128)(2,1)S(1)}, u32[]{:S(2)}, u32[]{:S(2)}) collective-permute-start(bf16[256,512]{1,0:T(8,128)(2,1)S(1)} %get-tuple-element.24), channel_id=1, source_target_pairs={{0,32},{32,64},{64,96},{96,0},{1,33},{33,65},{65,97},{97,1},{2,34}... | collective-permute-start | bytes 786440 | tf_op jit(solution)/shard_map/ppermute | solution.py:93
  42.6 4.2 %collective-permute-start.2 = (bf16[256,512]{1,0:T(8,128)(2,1)S(1)}, bf16[256,512]{1,0:T(8,128)(2,1)S(1)}, u32[]{:S(2)}, u32[]{:S(2)}) collective-permute-start(bf16[256,512]{1,0:T(8,128)(2,1)S(1)} %get-tuple-element.23), channel_id=1, source_target_pairs={{0,96},{32,0},{64,32},{96,64},{1,97},{33,1},{65,33},{97,65},{2,98}... | collective-permute-start | bytes 786440 | tf_op jit(solution)/shard_map/ppermute | solution.py:93
  46.8 2.2 %collective-permute-done.1.refs_5_ = bf16[256,512]{1,0:T(8,128)(2,1)S(1)} collective-permute-done((bf16[256,512]{1,0:T(8,128)(2,1)S(1)}, bf16[256,512]{1,0:T(8,128)(2,1)S(1)}, u32[]{:S(2)}, u32[]{:S(2)}) %collective-permute-start.1) | collective-permute-done | bytes 262176 | tf_op jit(solution)/shard_map/ppermute | solution.py:93
  52.0 5.4 %collective-permute-start.5 = (bf16[528,512]{1,0:T(8,128)(2,1)S(1)}, bf16[528,512]{1,0:T(8,128)(2,1)S(1)}, u32[]{:S(2)}, u32[]{:S(2)}) collective-permute-start(bf16[528,512]{1,0:T(8,128)(2,1)S(1)} %pad_maximum_fusion.refs_0_), channel_id=1, source_target_pairs={{0,96},{32,0},{64,32},{96,64},{1,97},{33,1},{65,33},{97,65},{2,98}... | collective-permute-start | bytes 1622024 | tf_op jit(solution)/shard_map/ppermute | solution.py:93
  57.4 3.4 %collective-permute-start.7 = (bf16[256,512]{1,0:T(8,128)(2,1)S(1)}, bf16[256,512]{1,0:T(8,128)(2,1)S(1)}, u32[]{:S(2)}, u32[]{:S(2)}) collective-permute-start(bf16[256,512]{1,0:T(8,128)(2,1)S(1)} %collective-permute-done.2.refs_10_), channel_id=1, source_target_pairs={{0,96},{32,0},{64,32},{96,64},{1,97},{33,1},{65,33},{97,65},{2,98}... | collective-permute-start | bytes 786440 | tf_op jit(solution)/shard_map/ppermute | solution.py:93
  60.8 1.9 %collective-permute-start.9 = (bf16[256,512]{1,0:T(8,128)(2,1)S(1)}, bf16[256,512]{1,0:T(8,128)(2,1)}, u32[]{:S(2)}, u32[]{:S(2)}) collective-permute-start(bf16[256,512]{1,0:T(8,128)(2,1)S(1)} %collective-permute-done.1.refs_5_), channel_id=1, source_target_pairs={{0,32},{32,64},{64,96},{96,0},{1,33},{33,65},{65,97},{97,1},{2,34}... | collective-permute-start | bytes 786440 | tf_op jit(solution)/shard_map/ppermute | solution.py:93
  63.5 1.9 %collective-permute-start.4 = (bf16[256,512]{1,0:T(8,128)(2,1)S(1)}, bf16[256,512]{1,0:T(8,128)(2,1)}, u32[]{:S(2)}, u32[]{:S(2)}) collective-permute-start(bf16[256,512]{1,0:T(8,128)(2,1)S(1)} %slice.48), channel_id=1, source_target_pairs={{0,32},{32,64},{64,96},{96,0},{1,33},{33,65},{65,97},{97,1},{2,34}... | collective-permute-start | bytes 786440 | tf_op jit(solution)/shard_map/ppermute | solution.py:93
  66.1 4.6 %collective-permute-start.6 = (bf16[272,512]{1,0:T(8,128)(2,1)}, bf16[272,512]{1,0:T(8,128)(2,1)}, u32[]{:S(2)}, u32[]{:S(2)}) collective-permute-start(bf16[272,512]{1,0:T(8,128)(2,1)} %slice.49), channel_id=1, source_target_pairs={{0,96},{32,0},{64,32},{96,64},{1,97},{33,1},{65,33},{97,65},{2,98}... | collective-permute-start | bytes 835592 | tf_op jit(solution)/shard_map/ppermute | solution.py:93
  70.7 4.4 %collective-permute-start.8 = (bf16[256,512]{1,0:T(8,128)(2,1)S(1)}, bf16[256,512]{1,0:T(8,128)(2,1)S(1)}, u32[]{:S(2)}, u32[]{:S(2)}) collective-permute-start(bf16[256,512]{1,0:T(8,128)(2,1)S(1)} %collective-permute-done.7.refs_8_), channel_id=1, source_target_pairs={{0,96},{32,0},{64,32},{96,64},{1,97},{33,1},{65,33},{97,65},{2,98}... | collective-permute-start | bytes 786440 | tf_op jit(solution)/shard_map/ppermute | solution.py:93
  75.2 1.9 %collective-permute-start.10 = (bf16[256,512]{1,0:T(8,128)(2,1)}, bf16[256,512]{1,0:T(8,128)(2,1)S(1)}, u32[]{:S(2)}, u32[]{:S(2)}) collective-permute-start(bf16[256,512]{1,0:T(8,128)(2,1)} %collective-permute-done.9.refs_7_), channel_id=1, source_target_pairs={{0,32},{32,64},{64,96},{96,0},{1,33},{33,65},{65,97},{97,1},{2,34}... | collective-permute-start | bytes 786440 | tf_op jit(solution)/shard_map/ppermute | solution.py:93
  81.6 2.1 %collective-permute-done.10.refs_9_ = bf16[256,512]{1,0:T(8,128)(2,1)S(1)} collective-permute-done((bf16[256,512]{1,0:T(8,128)(2,1)}, bf16[256,512]{1,0:T(8,128)(2,1)S(1)}, u32[]{:S(2)}, u32[]{:S(2)}) %collective-permute-start.10) | collective-permute-done | bytes 262176 | tf_op jit(solution)/shard_map/ppermute | solution.py:93
  87.9 2.2 %products_other.1 = bf16[1152,256]{1,0:T(8,128)(2,1)S(1)} custom-call(s32[3]{0:T(128)S(1)} %pad_add_fusion.position, bf16[528,512]{1,0:T(8,128)(2,1)S(1)} %pad_maximum_fusion.refs_0_, bf16[528,512]{1,0:T(8,128)(2,1)S(1)} %collective-permute-done.3.refs_1_, bf16[528,512]{1,0:T(8,128)(2,1)S(1)} %constant_dynamic-update-slice_fusion.refs_2_, ...), custom_call_target="tpu_custom_call" | custom-call | flops 1073741824 | bytes 7340032 | tf_op jit(solution)/shard_map/products_other/pallas_call | solution.py:147
  90.2 12.7 %collective-permute-start.11 = (bf16[1152,256]{1,0:T(8,128)(2,1)S(1)}, bf16[1152,256]{1,0:T(8,128)(2,1)S(1)}, u32[]{:S(2)}, u32[]{:S(2)}) collective-permute-start(bf16[1152,256]{1,0:T(8,128)(2,1)S(1)} %products_other.1), channel_id=1, source_target_pairs={{0,16},{16,0},{1,17},{17,1},{2,18},{18,2},{3,19},{19,3},{4,20},{20... | collective-permute-start | bytes 1769480 | tf_op jit(solution)/shard_map/ppermute | solution.py:88
  102.9 2.3 %products_own.1 = f32[1024,256]{1,0:T(8,128)S(1)} custom-call(s32[3]{0:T(128)S(1)} %pad_add_fusion.position, bf16[528,512]{1,0:T(8,128)(2,1)S(1)} %pad_maximum_fusion.refs_0_, bf16[528,512]{1,0:T(8,128)(2,1)S(1)} %collective-permute-done.3.refs_1_, bf16[528,512]{1,0:T(8,128)(2,1)S(1)} %constant_dynamic-update-slice_fusion.refs_2_, ...), custom_call_target="tpu_custom_call" | custom-call | flops 1073741824 | bytes 7340032 | tf_op jit(solution)/shard_map/products_own/pallas_call | solution.py:147
  106.2 19.4 %all-to-all-start.1 = ((bf16[8,128,256]{2,1,0:T(8,128)(2,1)}), bf16[8,128,256]{2,1,0:T(8,128)(2,1)S(1)}, u32[]{:S(2)}, u32[]{:S(2)}) async-start(bf16[8,128,256]{2,1,0:T(8,128)(2,1)} %bitcast.7), calls=%async_computation.1 | async-start | bytes 1048576 | tf_op jit(solution)/shard_map/all_to_all | solution.py:208
  127.2 16.3 %all-to-all-done.1 = bf16[8,128,256]{2,1,0:T(8,128)(2,1)S(1)} async-done(((bf16[8,128,256]{2,1,0:T(8,128)(2,1)}), bf16[8,128,256]{2,1,0:T(8,128)(2,1)S(1)}, u32[]{:S(2)}, u32[]{:S(2)}) %all-to-all-start.1) | async-done | bytes 524320 | tf_op jit(solution)/shard_map/all_to_all | solution.py:208
  144.4 3.4 %all-to-all-start.2 = ((bf16[4,128,256]{2,1,0:T(8,128)(2,1)}), bf16[4,128,256]{2,1,0:T(8,128)(2,1)S(1)}, u32[]{:S(2)}, u32[]{:S(2)}) async-start(bf16[4,128,256]{2,1,0:T(8,128)(2,1)} %broadcast_in_dim.10), calls=%async_computation.2 | async-start | bytes 524288 | tf_op jit(solution)/shard_map/all_to_all | solution.py:210
  148.6 6.5 %all-to-all-done.2 = bf16[4,128,256]{2,1,0:T(8,128)(2,1)S(1)} async-done(((bf16[4,128,256]{2,1,0:T(8,128)(2,1)}), bf16[4,128,256]{2,1,0:T(8,128)(2,1)S(1)}, u32[]{:S(2)}, u32[]{:S(2)}) %all-to-all-start.2) | async-done | bytes 262176 | tf_op jit(solution)/shard_map/all_to_all | solution.py:210
  157.3 11.1 %all-to-all-start.3 = ((bf16[128,2,128]{2,1,0:T(2,128)(2,1)}), bf16[128,2,128]{2,1,0:T(2,128)(2,1)S(1)}, u32[]{:S(2)}, u32[]{:S(2)}) async-start(bf16[128,2,128]{2,1,0:T(2,128)(2,1)} %reshape.140), calls=%async_computation.3 | async-start | bytes 131072 | tf_op jit(solution)/shard_map/all_to_all | solution.py:216
  168.7 13.9 %all-to-all-done.3 = bf16[128,2,128]{2,1,0:T(2,128)(2,1)S(1)} async-done(((bf16[128,2,128]{2,1,0:T(2,128)(2,1)}), bf16[128,2,128]{2,1,0:T(2,128)(2,1)S(1)}, u32[]{:S(2)}, u32[]{:S(2)}) %all-to-all-start.3) | async-done | bytes 65568 | tf_op jit(solution)/shard_map/all_to_all | solution.py:216
  (83 shorter events, 24.0 us)
Async XLA Ops:
  7.2 119.1 %copy-start = (bf16[1,8192]{1,0:T(2,128)(2,1)S(1)}, bf16[1,8192]{1,0:T(2,128)(2,1)}, u32[]{:S(2)}) copy-start(bf16[1,8192]{1,0:T(2,128)(2,1)} %param.16) | copy-start | bytes 49156
  9.2 10.4 %all-to-all-start = ((bf16[4,64,512]{2,1,0:T(8,128)(2,1)}), bf16[4,64,512]{2,1,0:T(8,128)(2,1)S(1)}, u32[]{:S(2)}, u32[]{:S(2)}) async-start(bf16[4,64,512]{2,1,0:T(8,128)(2,1)} %copy.37), calls=%async_computation | async-start | bytes 524288 | tf_op jit(solution)/shard_map/all_to_all | solution.py:190
  14.0 70.4 %all-gather.3.cloned.1.call-start = ((), (), s32[]{:S(2)}) async-start(), calls=%async_computation.4 | async-start | bytes 2359296 | tf_op jit(solution)/shard_map/all_gather | solution.py:192
  20.3 20.0 %collective-permute-start = (bf16[512,512]{1,0:T(8,128)(2,1)S(1)}, bf16[512,512]{1,0:T(8,128)(2,1)S(1)}, u32[]{:S(2)}, u32[]{:S(2)}) collective-permute-start(bf16[512,512]{1,0:T(8,128)(2,1)S(1)} %get-tuple-element.14), channel_id=1, source_target_pairs={{0,8},{8,0},{1,9},{9,1},{2,10},{10,2},{3,11},{11,3},{4,12},{12,4},... | collective-permute-start | bytes 1572872 | tf_op jit(solution)/shard_map/ppermute | solution.py:88
  40.3 8.7 %collective-permute-start.1 = (bf16[256,512]{1,0:T(8,128)(2,1)S(1)}, bf16[256,512]{1,0:T(8,128)(2,1)S(1)}, u32[]{:S(2)}, u32[]{:S(2)}) collective-permute-start(bf16[256,512]{1,0:T(8,128)(2,1)S(1)} %get-tuple-element.24), channel_id=1, source_target_pairs={{0,32},{32,64},{64,96},{96,0},{1,33},{33,65},{65,97},{97,1},{2,34}... | collective-permute-start | bytes 786440 | tf_op jit(solution)/shard_map/ppermute | solution.py:93
  42.6 7.5 %collective-permute-start.2 = (bf16[256,512]{1,0:T(8,128)(2,1)S(1)}, bf16[256,512]{1,0:T(8,128)(2,1)S(1)}, u32[]{:S(2)}, u32[]{:S(2)}) collective-permute-start(bf16[256,512]{1,0:T(8,128)(2,1)S(1)} %get-tuple-element.23), channel_id=1, source_target_pairs={{0,96},{32,0},{64,32},{96,64},{1,97},{33,1},{65,33},{97,65},{2,98}... | collective-permute-start | bytes 786440 | tf_op jit(solution)/shard_map/ppermute | solution.py:93
  50.1 13.4 %collective-permute-start.3 = (bf16[528,512]{1,0:T(8,128)(2,1)S(1)}, bf16[528,512]{1,0:T(8,128)(2,1)S(1)}, u32[]{:S(2)}, u32[]{:S(2)}) collective-permute-start(bf16[528,512]{1,0:T(8,128)(2,1)S(1)} %pad_maximum_fusion.refs_0_), channel_id=1, source_target_pairs={{0,32},{32,64},{64,96},{96,0},{1,33},{33,65},{65,97},{97,1},{2,34}... | collective-permute-start | bytes 1622024 | tf_op jit(solution)/shard_map/ppermute | solution.py:93
  52.0 13.4 %collective-permute-start.5 = (bf16[528,512]{1,0:T(8,128)(2,1)S(1)}, bf16[528,512]{1,0:T(8,128)(2,1)S(1)}, u32[]{:S(2)}, u32[]{:S(2)}) collective-permute-start(bf16[528,512]{1,0:T(8,128)(2,1)S(1)} %pad_maximum_fusion.refs_0_), channel_id=1, source_target_pairs={{0,96},{32,0},{64,32},{96,64},{1,97},{33,1},{65,33},{97,65},{2,98}... | collective-permute-start | bytes 1622024 | tf_op jit(solution)/shard_map/ppermute | solution.py:93
  57.4 13.3 %collective-permute-start.7 = (bf16[256,512]{1,0:T(8,128)(2,1)S(1)}, bf16[256,512]{1,0:T(8,128)(2,1)S(1)}, u32[]{:S(2)}, u32[]{:S(2)}) collective-permute-start(bf16[256,512]{1,0:T(8,128)(2,1)S(1)} %collective-permute-done.2.refs_10_), channel_id=1, source_target_pairs={{0,96},{32,0},{64,32},{96,64},{1,97},{33,1},{65,33},{97,65},{2,98}... | collective-permute-start | bytes 786440 | tf_op jit(solution)/shard_map/ppermute | solution.py:93
  60.8 14.4 %collective-permute-start.9 = (bf16[256,512]{1,0:T(8,128)(2,1)S(1)}, bf16[256,512]{1,0:T(8,128)(2,1)}, u32[]{:S(2)}, u32[]{:S(2)}) collective-permute-start(bf16[256,512]{1,0:T(8,128)(2,1)S(1)} %collective-permute-done.1.refs_5_), channel_id=1, source_target_pairs={{0,32},{32,64},{64,96},{96,0},{1,33},{33,65},{65,97},{97,1},{2,34}... | collective-permute-start | bytes 786440 | tf_op jit(solution)/shard_map/ppermute | solution.py:93
  63.5 13.7 %collective-permute-start.4 = (bf16[256,512]{1,0:T(8,128)(2,1)S(1)}, bf16[256,512]{1,0:T(8,128)(2,1)}, u32[]{:S(2)}, u32[]{:S(2)}) collective-permute-start(bf16[256,512]{1,0:T(8,128)(2,1)S(1)} %slice.48), channel_id=1, source_target_pairs={{0,32},{32,64},{64,96},{96,0},{1,33},{33,65},{65,97},{97,1},{2,34}... | collective-permute-start | bytes 786440 | tf_op jit(solution)/shard_map/ppermute | solution.py:93
  66.1 12.0 %collective-permute-start.6 = (bf16[272,512]{1,0:T(8,128)(2,1)}, bf16[272,512]{1,0:T(8,128)(2,1)}, u32[]{:S(2)}, u32[]{:S(2)}) collective-permute-start(bf16[272,512]{1,0:T(8,128)(2,1)} %slice.49), channel_id=1, source_target_pairs={{0,96},{32,0},{64,32},{96,64},{1,97},{33,1},{65,33},{97,65},{2,98}... | collective-permute-start | bytes 835592 | tf_op jit(solution)/shard_map/ppermute | solution.py:93
  70.7 10.2 %collective-permute-start.8 = (bf16[256,512]{1,0:T(8,128)(2,1)S(1)}, bf16[256,512]{1,0:T(8,128)(2,1)S(1)}, u32[]{:S(2)}, u32[]{:S(2)}) collective-permute-start(bf16[256,512]{1,0:T(8,128)(2,1)S(1)} %collective-permute-done.7.refs_8_), channel_id=1, source_target_pairs={{0,96},{32,0},{64,32},{96,64},{1,97},{33,1},{65,33},{97,65},{2,98}... | collective-permute-start | bytes 786440 | tf_op jit(solution)/shard_map/ppermute | solution.py:93
  75.2 8.5 %collective-permute-start.10 = (bf16[256,512]{1,0:T(8,128)(2,1)}, bf16[256,512]{1,0:T(8,128)(2,1)S(1)}, u32[]{:S(2)}, u32[]{:S(2)}) collective-permute-start(bf16[256,512]{1,0:T(8,128)(2,1)} %collective-permute-done.9.refs_7_), channel_id=1, source_target_pairs={{0,32},{32,64},{64,96},{96,0},{1,33},{33,65},{65,97},{97,1},{2,34}... | collective-permute-start | bytes 786440 | tf_op jit(solution)/shard_map/ppermute | solution.py:93
  90.2 15.0 %collective-permute-start.11 = (bf16[1152,256]{1,0:T(8,128)(2,1)S(1)}, bf16[1152,256]{1,0:T(8,128)(2,1)S(1)}, u32[]{:S(2)}, u32[]{:S(2)}) collective-permute-start(bf16[1152,256]{1,0:T(8,128)(2,1)S(1)} %products_other.1), channel_id=1, source_target_pairs={{0,16},{16,0},{1,17},{17,1},{2,18},{18,2},{3,19},{19,3},{4,20},{20... | collective-permute-start | bytes 1769480 | tf_op jit(solution)/shard_map/ppermute | solution.py:88
  105.1 20.4 %copy-start.14 = (bf16[1,128,1024]{2,1,0:T(8,128)(2,1)S(1)}, bf16[1,128,1024]{2,1,0:T(8,128)(2,1)}, u32[]{:S(2)}) copy-start(bf16[1,128,1024]{2,1,0:T(8,128)(2,1)} %param.18) | copy-start | bytes 786436
  106.2 19.4 %copy-start.15 = (bf16[1,128,1024]{2,1,0:T(8,128)(2,1)S(1)}, bf16[1,128,1024]{2,1,0:T(8,128)(2,1)}, u32[]{:S(2)}) copy-start(bf16[1,128,1024]{2,1,0:T(8,128)(2,1)} %param.17) | copy-start | bytes 786436
  106.2 37.4 %all-to-all-start.1 = ((bf16[8,128,256]{2,1,0:T(8,128)(2,1)}), bf16[8,128,256]{2,1,0:T(8,128)(2,1)S(1)}, u32[]{:S(2)}, u32[]{:S(2)}) async-start(bf16[8,128,256]{2,1,0:T(8,128)(2,1)} %bitcast.7), calls=%async_computation.1 | async-start | bytes 1048576 | tf_op jit(solution)/shard_map/all_to_all | solution.py:208
  127.2 27.9 %copy-start.11 = (f32[512,256]{1,0:T(8,128)S(1)}, f32[512,256]{1,0:T(8,128)}, u32[]{:S(2)}) copy-start(f32[512,256]{1,0:T(8,128)} %param.12) | copy-start | bytes 1572868
  127.2 27.9 %copy-start.12 = (bf16[512,256]{1,0:T(8,128)(2,1)S(1)}, bf16[512,256]{1,0:T(8,128)(2,1)}, u32[]{:S(2)}) copy-start(bf16[512,256]{1,0:T(8,128)(2,1)} %param.14) | copy-start | bytes 786436
  127.2 27.9 %copy-start.13 = (bf16[512,256]{1,0:T(8,128)(2,1)S(1)}, bf16[512,256]{1,0:T(8,128)(2,1)}, u32[]{:S(2)}) copy-start(bf16[512,256]{1,0:T(8,128)(2,1)} %param.13) | copy-start | bytes 786436
  144.4 10.7 %all-to-all-start.2 = ((bf16[4,128,256]{2,1,0:T(8,128)(2,1)}), bf16[4,128,256]{2,1,0:T(8,128)(2,1)S(1)}, u32[]{:S(2)}, u32[]{:S(2)}) async-start(bf16[4,128,256]{2,1,0:T(8,128)(2,1)} %broadcast_in_dim.10), calls=%async_computation.2 | async-start | bytes 524288 | tf_op jit(solution)/shard_map/all_to_all | solution.py:210
  156.4 27.5 %copy-start.7 = (f32[512,256]{1,0:T(8,128)}, f32[512,256]{1,0:T(8,128)S(1)}, u32[]{:S(2)}) copy-start(f32[512,256]{1,0:T(8,128)S(1)} %get-tuple-element.21) | copy-start | bytes 1572868
  157.3 25.3 %all-to-all-start.3 = ((bf16[128,2,128]{2,1,0:T(2,128)(2,1)}), bf16[128,2,128]{2,1,0:T(2,128)(2,1)S(1)}, u32[]{:S(2)}, u32[]{:S(2)}) async-start(bf16[128,2,128]{2,1,0:T(2,128)(2,1)} %reshape.140), calls=%async_computation.3 | async-start | bytes 131072 | tf_op jit(solution)/shard_map/all_to_all | solution.py:216
  (10 other events, 29.1 us)
Sparse Core Ops, SparseCore 0:
  20.4 44.1 all-gather.2

commit v7 on v5

--- a/solution.py
+++ b/solution.py
@@ -95,6 +95,22 @@
 
 def from_behind(array, axis):
     return [array] + [shifted(array, axis, by) for by in range(1, lax.axis_size(axis))]
+
+
+def same_kernel(array, out):
+    pass
+
+
+def held(array):
+    return pl.pallas_call(
+        same_kernel,
+        out_shape=jax.ShapeDtypeStruct(array.shape, array.dtype),
+        in_specs=[pl.BlockSpec(memory_space=pl.ANY)],
+        out_specs=pl.BlockSpec(memory_space=pl.ANY),
+        input_output_aliases={0: 0},
+        cost_estimate=pl.CostEstimate(flops=50 * 10**9, bytes_accessed=0, transcendentals=0),
+        name="held",
+    )(array)
 
 
 def product_kernel(for_other, position, *refs):
@@ -175,11 +191,16 @@
     received = swap_over(jnp.where(half == 0, row_halves[1], row_halves[0]), "zhi")
     kept = jnp.concatenate([jnp.where(half == 0, row_halves[0], row_halves[1]), decode_inputs])
 
-    columns = learn_grads[0].reshape(-1, x_count, 2 * block_width).transpose(1, 0, 2)
+    width = 2 * block_width
+    columns = jnp.stack([learn_grads[0, :, i * width : (i + 1) * width] for i in range(x_count)])
     piece = lax.all_to_all(columns, "x", 0, 0, tiled=True)
     piece, kept = lax.optimization_barrier((piece, kept))
-    grads_all = lax.all_gather(piece, "y", axis=0)
-    inputs = from_behind(kept, "x") + from_behind(received, "x")
+    y_count = lax.axis_size("y")
+    grads_all = lax.all_to_all(jnp.broadcast_to(piece[None], (y_count, *piece.shape)), "y", 0, 0)
+    behind = shifted(kept, "x", 1)
+    kept, received = lax.optimization_barrier((kept, held(received)))
+    inputs = [kept, behind, shifted(kept, "x", 2), shifted(kept, "x", 3)]
+    inputs += from_behind(received, "x")
 
     sent = products(True, inputs, grads_all, block_width)
     sent_back = swap_over(sent, "core")

time: 172 us -> 168 us (0.977)
  between operations: 15 us -> 1.61 us
  starting transfers between devices: 62.7 us -> 69.3 us
  local copies, waits for them, and re-layouts: 8.73 us -> 5.44 us
  other arithmetic: 2.85 us -> 5.6 us
    all_to_all x0 -> x1, starting transfers between devices: none -> 6.82 us  [local(): lax.all_to_all(jnp.broadcast_to(piece[None], (y_count, *piece.shape)), 'y...]
    unnamed x29 -> x25, local copies, waits for them, and re-layouts: 3.15 us -> 0.23 us
    ppermute x2, waiting for transfers between devices: 2.84 us -> 0.01 us  [swap_over(): return lax.ppermute(array, axis, [(0, 1), (1, 0)])]
    ppermute x6, waiting for transfers between devices: 32 us -> 34.2 us  [shifted(): lax.ppermute(array, axis, [(i, (i + by) % count) for i in range(count)])]
    select_n x1, other arithmetic: 0.07 us -> 2.11 us  [local(): jnp.where(half == 0, row_halves[1], row_halves[0])]
  transfers between devices with their start and end apart: 13 -> 13, of which waited for: 8 -> 7; matrix products, arithmetic and copies ran while one was open for 1% -> 3% of each run, Pallas kernels for 1% -> 2%
where the time goes in v7:
time: 168 us; the launch traced here: 167 us
  waiting for transfers between devices  77.7 us (46%)
  starting transfers between devices  69.3 us (41%)
  Pallas kernels  6.29 us (4%)
  other arithmetic  5.6 us (3%)
  local copies, waits for them, and re-layouts  5.44 us (3%)
    ppermute x6, waiting for transfers between devices, shifted(): lax.ppermute(array, axis, [(i, (i + by) % count) for i in range(count)])  34.2 us
    ppermute x6, starting transfers between devices, shifted(): lax.ppermute(array, axis, [(i, (i + by) % count) for i in range(count)])  18.6 us
    all_to_all x1, waiting for transfers between devices, local(): lax.all_to_all(over_x, ('zhi', 'side'), 0, 0, tiled=True)  16.3 us
    ppermute x2, starting transfers between devices, swap_over(): return lax.ppermute(array, axis, [(0, 1), (1, 0)])  14.2 us
    all_to_all x1, waiting for transfers between devices, local(): fresh_terms = lax.all_to_all(partial_fresh, REP + TP, 0, 0, tiled=True)  13.9 us
    all_to_all x1, starting transfers between devices, local(): fresh_terms = lax.all_to_all(partial_fresh, REP + TP, 0, 0, tiled=True)  13 us
    all_to_all x1, starting transfers between devices, local(): lax.all_to_all(over_x, ('zhi', 'side'), 0, 0, tiled=True)  9.29 us
    all_to_all x1, starting transfers between devices, local(): lax.all_to_all(jnp.broadcast_to(piece[None], (y_count, *piece.shape)), 'y...  6.82 us
  transfers between devices with their start and end apart: 13, of which 7 were waited for; matrix products, arithmetic and copies ran while one was open for 3% of the time, Pallas kernels for 2%

profile of v7, /device:TPU:1, one launch (start us, length us, event | category | flops | bytes accessed | tf_op | source)
XLA Modules:
  0.0 166.8 jit_solution(4821694680258598227)
XLA Ops:
  0.7 2.1 %select_bitcast_fusion = (bf16[512,512]{1,0:T(8,128)(2,1)}, bf16[512,512]{1,0:T(8,128)(2,1)S(1)}) fusion(pred[]{:T(512)S(6)} %eq.7, bf16[1,1024,512]{2,1,0:T(8,128)(2,1)} %param.10), kind=kLoop, calls=%fused_computation.13 | loop fusion | flops 524288 | bytes 2097153 | tf_op jit(solution)/shard_map/jit(_where)/select_n | solution.py:191
  2.8 11.6 %collective-permute-start = (bf16[512,512]{1,0:T(8,128)(2,1)}, bf16[512,512]{1,0:T(8,128)(2,1)}, u32[]{:S(2)}, u32[]{:S(2)}) collective-permute-start(bf16[512,512]{1,0:T(8,128)(2,1)} %get-tuple-element.12), channel_id=1, source_target_pairs={{0,8},{8,0},{1,9},{9,1},{2,10},{10,2},{3,11},{11,3},{4,12},{12,4},... | collective-permute-start | bytes 1572872 | tf_op jit(solution)/shard_map/ppermute | solution.py:88
  15.1 4.0 %all-to-all-start = ((bf16[4,64,512]{2,1,0:T(8,128)(2,1)}), bf16[4,64,512]{2,1,0:T(8,128)(2,1)S(1)}, u32[]{:S(2)}, u32[]{:S(2)}) async-start(bf16[4,64,512]{2,1,0:T(8,128)(2,1)} %pad_maximum_fusion.1), calls=%async_computation | async-start | bytes 524288 | tf_op jit(solution)/shard_map/all_to_all | solution.py:196
  19.2 5.9 %all-to-all-done = bf16[4,64,512]{2,1,0:T(8,128)(2,1)S(1)} async-done(((bf16[4,64,512]{2,1,0:T(8,128)(2,1)}), bf16[4,64,512]{2,1,0:T(8,128)(2,1)S(1)}, u32[]{:S(2)}, u32[]{:S(2)}) %all-to-all-start) | async-done | bytes 262176 | tf_op jit(solution)/shard_map/all_to_all | solution.py:196
  25.1 2.2 %collective-permute-start.1 = (bf16[528,512]{1,0:T(8,128)(2,1)S(1)}, bf16[528,512]{1,0:T(8,128)(2,1)S(1)}, u32[]{:S(2)}, u32[]{:S(2)}) collective-permute-start(bf16[528,512]{1,0:T(8,128)(2,1)S(1)} %pad_maximum_fusion.refs_0_), channel_id=1, source_target_pairs={{0,32},{32,64},{64,96},{96,0},{1,33},{33,65},{65,97},{97,1},{2,34}... | collective-permute-start | bytes 1622024 | tf_op jit(solution)/shard_map/ppermute | solution.py:93
  27.3 1.6 broadcast_in_dim.12
  28.9 6.8 %all-to-all-start.1 = ((bf16[8,4,64,512]{3,2,1,0:T(8,128)(2,1)}), bf16[8,4,64,512]{3,2,1,0:T(8,128)(2,1)S(1)}, u32[]{:S(2)}, u32[]{:S(2)}) async-start(bf16[8,4,64,512]{3,2,1,0:T(8,128)(2,1)} %broadcast_in_dim.12), calls=%async_computation.1 | async-start | bytes 4194304 | tf_op jit(solution)/shard_map/all_to_all | solution.py:199
  35.7 3.7 %collective-permute-start.2 = (bf16[528,512]{1,0:T(8,128)(2,1)S(1)}, bf16[528,512]{1,0:T(8,128)(2,1)}, u32[]{:S(2)}, u32[]{:S(2)}) collective-permute-start(bf16[528,512]{1,0:T(8,128)(2,1)S(1)} %pad_maximum_fusion.refs_0_), channel_id=1, source_target_pairs={{0,64},{32,96},{64,0},{96,32},{1,65},{33,97},{65,1},{97,33},{2,66}... | collective-permute-start | bytes 1622024 | tf_op jit(solution)/shard_map/ppermute | solution.py:93
  39.4 2.5 %collective-permute-start.3 = (bf16[528,512]{1,0:T(8,128)(2,1)S(1)}, bf16[528,512]{1,0:T(8,128)(2,1)}, u32[]{:S(2)}, u32[]{:S(2)}) collective-permute-start(bf16[528,512]{1,0:T(8,128)(2,1)S(1)} %pad_maximum_fusion.refs_0_), channel_id=1, source_target_pairs={{0,96},{32,0},{64,32},{96,64},{1,97},{33,1},{65,33},{97,65},{2,98}... | collective-permute-start | bytes 1622024 | tf_op jit(solution)/shard_map/ppermute | solution.py:93
  41.9 2.8 %collective-permute-start.4 = (bf16[512,512]{1,0:T(8,128)(2,1)}, bf16[512,512]{1,0:T(8,128)(2,1)}, u32[]{:S(2)}, u32[]{:S(2)}) collective-permute-start(bf16[512,512]{1,0:T(8,128)(2,1)} %held.1.refs_4_), channel_id=1, source_target_pairs={{0,32},{32,64},{64,96},{96,0},{1,33},{33,65},{65,97},{97,1},{2,34}... | collective-permute-start | bytes 1572872 | tf_op jit(solution)/shard_map/ppermute | solution.py:93
  44.7 3.4 %collective-permute-start.5 = (bf16[512,512]{1,0:T(8,128)(2,1)}, bf16[512,512]{1,0:T(8,128)(2,1)}, u32[]{:S(2)}, u32[]{:S(2)}) collective-permute-start(bf16[512,512]{1,0:T(8,128)(2,1)} %held.1.refs_4_), channel_id=1, source_target_pairs={{0,64},{32,96},{64,0},{96,32},{1,65},{33,97},{65,1},{97,33},{2,66}... | collective-permute-start | bytes 1572872 | tf_op jit(solution)/shard_map/ppermute | solution.py:93
  48.1 4.0 %collective-permute-start.6 = (bf16[512,512]{1,0:T(8,128)(2,1)}, bf16[512,512]{1,0:T(8,128)(2,1)}, u32[]{:S(2)}, u32[]{:S(2)}) collective-permute-start(bf16[512,512]{1,0:T(8,128)(2,1)} %held.1.refs_4_), channel_id=1, source_target_pairs={{0,96},{32,0},{64,32},{96,64},{1,97},{33,1},{65,33},{97,65},{2,98}... | collective-permute-start | bytes 1572872 | tf_op jit(solution)/shard_map/ppermute | solution.py:93
  52.2 24.0 %collective-permute-done.4.refs_5_ = bf16[512,512]{1,0:T(8,128)(2,1)} collective-permute-done((bf16[512,512]{1,0:T(8,128)(2,1)}, bf16[512,512]{1,0:T(8,128)(2,1)}, u32[]{:S(2)}, u32[]{:S(2)}) %collective-permute-start.4) | collective-permute-done | bytes 524320 | tf_op jit(solution)/shard_map/ppermute | solution.py:93
  76.2 10.2 %collective-permute-done.6.refs_7_ = bf16[512,512]{1,0:T(8,128)(2,1)} collective-permute-done((bf16[512,512]{1,0:T(8,128)(2,1)}, bf16[512,512]{1,0:T(8,128)(2,1)}, u32[]{:S(2)}, u32[]{:S(2)}) %collective-permute-start.6) | collective-permute-done | bytes 524320 | tf_op jit(solution)/shard_map/ppermute | solution.py:93
  87.3 3.1 %products_other.1 = bf16[1152,256]{1,0:T(8,128)(2,1)S(1)} custom-call(s32[3]{0:T(128)S(1)} %pad_add_fusion.position, bf16[528,512]{1,0:T(8,128)(2,1)S(1)} %pad_maximum_fusion.refs_0_, bf16[528,512]{1,0:T(8,128)(2,1)S(1)} %collective-permute-done.1.refs_1_, bf16[528,512]{1,0:T(8,128)(2,1)} %collective-permute-done.2.refs_2_, ...), custom_call_target="tpu_custom_call" | custom-call | flops 1073741824 | bytes 7340032 | tf_op jit(solution)/shard_map/products_other/pallas_call | solution.py:152
  90.5 2.6 %collective-permute-start.7 = (bf16[1152,256]{1,0:T(8,128)(2,1)S(1)}, bf16[1152,256]{1,0:T(8,128)(2,1)S(1)}, u32[]{:S(2)}, u32[]{:S(2)}) collective-permute-start(bf16[1152,256]{1,0:T(8,128)(2,1)S(1)} %products_other.1), channel_id=1, source_target_pairs={{0,16},{16,0},{1,17},{17,1},{2,18},{18,2},{3,19},{19,3},{4,20},{20... | collective-permute-start | bytes 1769480 | tf_op jit(solution)/shard_map/ppermute | solution.py:88
  93.1 3.2 %products_own.1 = f32[1024,256]{1,0:T(8,128)S(1)} custom-call(s32[3]{0:T(128)S(1)} %pad_add_fusion.position, bf16[528,512]{1,0:T(8,128)(2,1)S(1)} %pad_maximum_fusion.refs_0_, bf16[528,512]{1,0:T(8,128)(2,1)S(1)} %collective-permute-done.1.refs_1_, bf16[528,512]{1,0:T(8,128)(2,1)} %collective-permute-done.2.refs_2_, ...), custom_call_target="tpu_custom_call" | custom-call | flops 1073741824 | bytes 7340032 | tf_op jit(solution)/shard_map/products_own/pallas_call | solution.py:152
  97.3 9.3 %all-to-all-start.2 = ((bf16[8,128,256]{2,1,0:T(8,128)(2,1)}), bf16[8,128,256]{2,1,0:T(8,128)(2,1)S(1)}, u32[]{:S(2)}, u32[]{:S(2)}) async-start(bf16[8,128,256]{2,1,0:T(8,128)(2,1)} %bitcast.5), calls=%async_computation.2 | async-start | bytes 1048576 | tf_op jit(solution)/shard_map/all_to_all | solution.py:218
  108.3 16.3 %all-to-all-done.2 = bf16[8,128,256]{2,1,0:T(8,128)(2,1)S(1)} async-done(((bf16[8,128,256]{2,1,0:T(8,128)(2,1)}), bf16[8,128,256]{2,1,0:T(8,128)(2,1)S(1)}, u32[]{:S(2)}, u32[]{:S(2)}) %all-to-all-start.2) | async-done | bytes 524320 | tf_op jit(solution)/shard_map/all_to_all | solution.py:218
  125.4 3.4 %all-to-all-start.3 = ((bf16[4,128,256]{2,1,0:T(8,128)(2,1)}), bf16[4,128,256]{2,1,0:T(8,128)(2,1)S(1)}, u32[]{:S(2)}, u32[]{:S(2)}) async-start(bf16[4,128,256]{2,1,0:T(8,128)(2,1)} %broadcast_in_dim.13), calls=%async_computation.3 | async-start | bytes 524288 | tf_op jit(solution)/shard_map/all_to_all | solution.py:220
  129.7 6.5 %all-to-all-done.3 = bf16[4,128,256]{2,1,0:T(8,128)(2,1)S(1)} async-done(((bf16[4,128,256]{2,1,0:T(8,128)(2,1)}), bf16[4,128,256]{2,1,0:T(8,128)(2,1)S(1)}, u32[]{:S(2)}, u32[]{:S(2)}) %all-to-all-start.3) | async-done | bytes 262176 | tf_op jit(solution)/shard_map/all_to_all | solution.py:220
  136.2 1.3 fusion.5
  138.3 13.0 %all-to-all-start.4 = ((bf16[128,2,128]{2,1,0:T(2,128)(2,1)}), bf16[128,2,128]{2,1,0:T(2,128)(2,1)S(1)}, u32[]{:S(2)}, u32[]{:S(2)}) async-start(bf16[128,2,128]{2,1,0:T(2,128)(2,1)} %reshape.141), calls=%async_computation.4 | async-start | bytes 131072 | tf_op jit(solution)/shard_map/all_to_all | solution.py:226
  151.6 13.9 %all-to-all-done.4 = bf16[128,2,128]{2,1,0:T(2,128)(2,1)S(1)} async-done(((bf16[128,2,128]{2,1,0:T(2,128)(2,1)}), bf16[128,2,128]{2,1,0:T(2,128)(2,1)S(1)}, u32[]{:S(2)}, u32[]{:S(2)}) %all-to-all-start.4) | async-done | bytes 65568 | tf_op jit(solution)/shard_map/all_to_all | solution.py:226
  (59 shorter events, 7.8 us)
Async XLA Ops:
  0.6 106.8 %copy-start = (bf16[1,8192]{1,0:T(2,128)(2,1)S(1)}, bf16[1,8192]{1,0:T(2,128)(2,1)}, u32[]{:S(2)}) copy-start(bf16[1,8192]{1,0:T(2,128)(2,1)} %param.16) | copy-start | bytes 49156
  0.6 13.7 %copy-start.7 = (bf16[1,64,2048]{2,1,0:T(8,128)(2,1)S(1)}, bf16[1,64,2048]{2,1,0:T(8,128)(2,1)}, u32[]{:S(2)}) copy-start(bf16[1,64,2048]{2,1,0:T(8,128)(2,1)} %param.11) | copy-start | bytes 786436
  2.8 16.4 %copy-start.10 = (bf16[16,512]{1,0:T(8,128)(2,1)S(1)}, bf16[16,512]{1,0:T(8,128)(2,1)}, u32[]{:S(2)}) copy-start(bf16[16,512]{1,0:T(8,128)(2,1)} %param.15) | copy-start | bytes 49156
  2.8 32.9 %collective-permute-start = (bf16[512,512]{1,0:T(8,128)(2,1)}, bf16[512,512]{1,0:T(8,128)(2,1)}, u32[]{:S(2)}, u32[]{:S(2)}) collective-permute-start(bf16[512,512]{1,0:T(8,128)(2,1)} %get-tuple-element.12), channel_id=1, source_target_pairs={{0,8},{8,0},{1,9},{9,1},{2,10},{10,2},{3,11},{11,3},{4,12},{12,4},... | collective-permute-start | bytes 1572872 | tf_op jit(solution)/shard_map/ppermute | solution.py:88
  15.1 9.9 %all-to-all-start = ((bf16[4,64,512]{2,1,0:T(8,128)(2,1)}), bf16[4,64,512]{2,1,0:T(8,128)(2,1)S(1)}, u32[]{:S(2)}, u32[]{:S(2)}) async-start(bf16[4,64,512]{2,1,0:T(8,128)(2,1)} %pad_maximum_fusion.1), calls=%async_computation | async-start | bytes 524288 | tf_op jit(solution)/shard_map/all_to_all | solution.py:196
  25.1 23.0 %collective-permute-start.1 = (bf16[528,512]{1,0:T(8,128)(2,1)S(1)}, bf16[528,512]{1,0:T(8,128)(2,1)S(1)}, u32[]{:S(2)}, u32[]{:S(2)}) collective-permute-start(bf16[528,512]{1,0:T(8,128)(2,1)S(1)} %pad_maximum_fusion.refs_0_), channel_id=1, source_target_pairs={{0,32},{32,64},{64,96},{96,0},{1,33},{33,65},{65,97},{97,1},{2,34}... | collective-permute-start | bytes 1622024 | tf_op jit(solution)/shard_map/ppermute | solution.py:93
  28.9 58.5 %all-to-all-start.1 = ((bf16[8,4,64,512]{3,2,1,0:T(8,128)(2,1)}), bf16[8,4,64,512]{3,2,1,0:T(8,128)(2,1)S(1)}, u32[]{:S(2)}, u32[]{:S(2)}) async-start(bf16[8,4,64,512]{3,2,1,0:T(8,128)(2,1)} %broadcast_in_dim.12), calls=%async_computation.1 | async-start | bytes 4194304 | tf_op jit(solution)/shard_map/all_to_all | solution.py:199
  35.7 50.7 %collective-permute-start.2 = (bf16[528,512]{1,0:T(8,128)(2,1)S(1)}, bf16[528,512]{1,0:T(8,128)(2,1)}, u32[]{:S(2)}, u32[]{:S(2)}) collective-permute-start(bf16[528,512]{1,0:T(8,128)(2,1)S(1)} %pad_maximum_fusion.refs_0_), channel_id=1, source_target_pairs={{0,64},{32,96},{64,0},{96,32},{1,65},{33,97},{65,1},{97,33},{2,66}... | collective-permute-start | bytes 1622024 | tf_op jit(solution)/shard_map/ppermute | solution.py:93
  39.4 47.0 %collective-permute-start.3 = (bf16[528,512]{1,0:T(8,128)(2,1)S(1)}, bf16[528,512]{1,0:T(8,128)(2,1)}, u32[]{:S(2)}, u32[]{:S(2)}) collective-permute-start(bf16[528,512]{1,0:T(8,128)(2,1)S(1)} %pad_maximum_fusion.refs_0_), channel_id=1, source_target_pairs={{0,96},{32,0},{64,32},{96,64},{1,97},{33,1},{65,33},{97,65},{2,98}... | collective-permute-start | bytes 1622024 | tf_op jit(solution)/shard_map/ppermute | solution.py:93
  41.9 34.3 %collective-permute-start.4 = (bf16[512,512]{1,0:T(8,128)(2,1)}, bf16[512,512]{1,0:T(8,128)(2,1)}, u32[]{:S(2)}, u32[]{:S(2)}) collective-permute-start(bf16[512,512]{1,0:T(8,128)(2,1)} %held.1.refs_4_), channel_id=1, source_target_pairs={{0,32},{32,64},{64,96},{96,0},{1,33},{33,65},{65,97},{97,1},{2,34}... | collective-permute-start | bytes 1572872 | tf_op jit(solution)/shard_map/ppermute | solution.py:93
  44.7 31.5 %collective-permute-start.5 = (bf16[512,512]{1,0:T(8,128)(2,1)}, bf16[512,512]{1,0:T(8,128)(2,1)}, u32[]{:S(2)}, u32[]{:S(2)}) collective-permute-start(bf16[512,512]{1,0:T(8,128)(2,1)} %held.1.refs_4_), channel_id=1, source_target_pairs={{0,64},{32,96},{64,0},{96,32},{1,65},{33,97},{65,1},{97,33},{2,66}... | collective-permute-start | bytes 1572872 | tf_op jit(solution)/shard_map/ppermute | solution.py:93
  48.1 38.3 %collective-permute-start.6 = (bf16[512,512]{1,0:T(8,128)(2,1)}, bf16[512,512]{1,0:T(8,128)(2,1)}, u32[]{:S(2)}, u32[]{:S(2)}) collective-permute-start(bf16[512,512]{1,0:T(8,128)(2,1)} %held.1.refs_4_), channel_id=1, source_target_pairs={{0,96},{32,0},{64,32},{96,64},{1,97},{33,1},{65,33},{97,65},{2,98}... | collective-permute-start | bytes 1572872 | tf_op jit(solution)/shard_map/ppermute | solution.py:93
  90.5 5.8 %copy-start.1 = (bf16[1152,256]{1,0:T(8,128)(2,1)}, bf16[1152,256]{1,0:T(8,128)(2,1)S(1)}, u32[]{:S(2)}) copy-start(bf16[1152,256]{1,0:T(8,128)(2,1)S(1)} %products_other.1) | copy-start | bytes 1769476
  90.5 5.8 %collective-permute-start.7 = (bf16[1152,256]{1,0:T(8,128)(2,1)S(1)}, bf16[1152,256]{1,0:T(8,128)(2,1)S(1)}, u32[]{:S(2)}, u32[]{:S(2)}) collective-permute-start(bf16[1152,256]{1,0:T(8,128)(2,1)S(1)} %products_other.1), channel_id=1, source_target_pairs={{0,16},{16,0},{1,17},{17,1},{2,18},{18,2},{3,19},{19,3},{4,20},{20... | collective-permute-start | bytes 1769480 | tf_op jit(solution)/shard_map/ppermute | solution.py:88
  96.3 10.3 %copy-start.8 = (bf16[1,128,1024]{2,1,0:T(8,128)(2,1)S(1)}, bf16[1,128,1024]{2,1,0:T(8,128)(2,1)}, u32[]{:S(2)}) copy-start(bf16[1,128,1024]{2,1,0:T(8,128)(2,1)} %param.17) | copy-start | bytes 786436
  96.3 1.0 copy-start.3
  97.3 10.0 %copy-start.9 = (bf16[1,128,1024]{2,1,0:T(8,128)(2,1)S(1)}, bf16[1,128,1024]{2,1,0:T(8,128)(2,1)}, u32[]{:S(2)}) copy-start(bf16[1,128,1024]{2,1,0:T(8,128)(2,1)} %param.18) | copy-start | bytes 786436
  97.3 27.3 %all-to-all-start.2 = ((bf16[8,128,256]{2,1,0:T(8,128)(2,1)}), bf16[8,128,256]{2,1,0:T(8,128)(2,1)S(1)}, u32[]{:S(2)}, u32[]{:S(2)}) async-start(bf16[8,128,256]{2,1,0:T(8,128)(2,1)} %bitcast.5), calls=%async_computation.2 | async-start | bytes 1048576 | tf_op jit(solution)/shard_map/all_to_all | solution.py:218
  108.3 27.9 %copy-start.4 = (f32[512,256]{1,0:T(8,128)S(1)}, f32[512,256]{1,0:T(8,128)}, u32[]{:S(2)}) copy-start(f32[512,256]{1,0:T(8,128)} %param.12) | copy-start | bytes 1572868
  108.3 27.9 %copy-start.5 = (bf16[512,256]{1,0:T(8,128)(2,1)S(1)}, bf16[512,256]{1,0:T(8,128)(2,1)}, u32[]{:S(2)}) copy-start(bf16[512,256]{1,0:T(8,128)(2,1)} %param.14) | copy-start | bytes 786436
  108.3 27.9 %copy-start.6 = (bf16[512,256]{1,0:T(8,128)(2,1)S(1)}, bf16[512,256]{1,0:T(8,128)(2,1)}, u32[]{:S(2)}) copy-start(bf16[512,256]{1,0:T(8,128)(2,1)} %param.13) | copy-start | bytes 786436
  125.4 10.7 %all-to-all-start.3 = ((bf16[4,128,256]{2,1,0:T(8,128)(2,1)}), bf16[4,128,256]{2,1,0:T(8,128)(2,1)S(1)}, u32[]{:S(2)}, u32[]{:S(2)}) async-start(bf16[4,128,256]{2,1,0:T(8,128)(2,1)} %broadcast_in_dim.13), calls=%async_computation.3 | async-start | bytes 524288 | tf_op jit(solution)/shard_map/all_to_all | solution.py:220
  137.5 29.3 %copy-start.2 = (f32[512,256]{1,0:T(8,128)}, f32[512,256]{1,0:T(8,128)S(1)}, u32[]{:S(2)}) copy-start(f32[512,256]{1,0:T(8,128)S(1)} %get-tuple-element.19) | copy-start | bytes 1572868
  138.3 27.2 %all-to-all-start.4 = ((bf16[128,2,128]{2,1,0:T(2,128)(2,1)}), bf16[128,2,128]{2,1,0:T(2,128)(2,1)S(1)}, u32[]{:S(2)}, u32[]{:S(2)}) async-start(bf16[128,2,128]{2,1,0:T(2,128)(2,1)} %reshape.141), calls=%async_computation.4 | async-start | bytes 131072 | tf_op jit(solution)/shard_map/all_to_all | solution.py:226

commit v8 on v5

--- a/solution.py
+++ b/solution.py
@@ -93,8 +93,10 @@
     return lax.ppermute(array, axis, [(i, (i + by) % count) for i in range(count)])
 
 
-def from_behind(array, axis):
-    return [array] + [shifted(array, axis, by) for by in range(1, lax.axis_size(axis))]
+def around(array, axis):
+    half = array.shape[0] // 32 * 16
+    behind, ahead = shifted(array, axis, 1), shifted(array, axis, -1)
+    return [array, behind, shifted(behind[:half], axis, 1), shifted(ahead[half:], axis, -1), ahead]
 
 
 def product_kernel(for_other, position, *refs):
@@ -110,19 +112,24 @@
     right = jnp.concatenate(
         [grads[y, source, :, columns] for source in sources for y in range(y_count)]
     )
-    for blocks, place in ((inputs[:x_count], half), (inputs[x_count:], 1 - half)):
-        left = jnp.concatenate([block[:half_rows, :] for block in blocks])
+    unit = half_rows // 2
+    parts = len(inputs) // 2
+    for blocks, place in ((inputs[:parts], half), (inputs[parts:], 1 - half)):
+        left = jnp.concatenate([block[: block.shape[0] // unit * unit, :] for block in blocks])
         target = pl.ds(pl.multiple_of(place * feature_count, feature_count), feature_count)
         out[target, :] = lax.dot_general(
             left, right, (((0,), (0,)), ((), ())), preferred_element_type=jnp.float32
         ).astype(out.dtype)
     if for_other:
         decode_rows = inputs[0].shape[0] - half_rows
+        below = [block for block in inputs[:parts] if block.shape[0] % unit]
         for part in range(feature_count // width):
-            for block, source in zip(inputs[:x_count], sources):
+            for block, source in zip(below, sources):
                 start = 2 * feature_count + (part * x_count + source) * decode_rows
                 target = pl.ds(pl.multiple_of(start, decode_rows), decode_rows)
-                out[target, :] = block[half_rows:, part * width : (part + 1) * width]
+                out[target, :] = block[
+                    block.shape[0] - decode_rows :, part * width : (part + 1) * width
+                ]
 
 
 def products(for_other, inputs, grads, width):
@@ -175,11 +182,13 @@
     received = swap_over(jnp.where(half == 0, row_halves[1], row_halves[0]), "zhi")
     kept = jnp.concatenate([jnp.where(half == 0, row_halves[0], row_halves[1]), decode_inputs])
 
-    columns = learn_grads[0].reshape(-1, x_count, 2 * block_width).transpose(1, 0, 2)
+    width = 2 * block_width
+    columns = jnp.stack([learn_grads[0, :, i * width : (i + 1) * width] for i in range(x_count)])
     piece = lax.all_to_all(columns, "x", 0, 0, tiled=True)
     piece, kept = lax.optimization_barrier((piece, kept))
-    grads_all = lax.all_gather(piece, "y", axis=0)
-    inputs = from_behind(kept, "x") + from_behind(received, "x")
+    y_count = lax.axis_size("y")
+    grads_all = lax.all_to_all(jnp.broadcast_to(piece[None], (y_count, *piece.shape)), "y", 0, 0)
+    inputs = around(kept, "x") + around(received, "x")
 
     sent = products(True, inputs, grads_all, block_width)
     sent_back = swap_over(sent, "core")

time: 172 us -> 169 us (0.983)
  starting transfers between devices: 62.7 us -> 86.8 us
  waiting for transfers between devices: 76.3 us -> 53.4 us
  between operations: 15 us -> 1.62 us
  local copies, waits for them, and re-layouts: 8.73 us -> 15.9 us
    ppermute x6 -> x8, waiting for transfers between devices: 32 us -> 7.25 us  [shifted(): lax.ppermute(array, axis, [(i, (i + by) % count) for i in range(count)])]
    all_to_all x0 -> x1, starting transfers between devices: none -> 6.85 us  [local(): lax.all_to_all(jnp.broadcast_to(piece[None], (y_count, *piece.shape)), 'y...]
    ppermute x2, starting transfers between devices: 14.3 us -> 20.3 us  [swap_over(): return lax.ppermute(array, axis, [(0, 1), (1, 0)])]
    ppermute x6 -> x8, starting transfers between devices: 17.9 us -> 23.5 us  [shifted(): lax.ppermute(array, axis, [(i, (i + by) % count) for i in range(count)])]
    all_to_all x1, starting transfers between devices: 9.23 us -> 14 us  [local(): lax.all_to_all(over_x, ('zhi', 'side'), 0, 0, tiled=True)]
    slice x0 -> x5, local copies, waits for them, and re-layouts: none -> 3.93 us  [the longest x2 1.44 us: around(): ahead[half:]]
    unnamed x29 -> x41, local copies, waits for them, and re-layouts: 3.15 us -> 6.81 us
    ppermute x2, waiting for transfers between devices: 2.84 us -> 4.88 us  [swap_over(): return lax.ppermute(array, axis, [(0, 1), (1, 0)])]
  transfers between devices with their start and end apart: 13 -> 15, of which waited for: 8 -> 8; matrix products, arithmetic and copies ran while one was open for 1% -> 4% of each run, Pallas kernels for 1% -> 1%
where the time goes in v8:
time: 169 us; the launch traced here: 168 us
  starting transfers between devices  86.8 us (51%)
  waiting for transfers between devices  53.4 us (32%)
  local copies, waits for them, and re-layouts  15.9 us (9%)
  Pallas kernels  4.82 us (3%)
  other arithmetic  4.36 us (3%)
    ppermute x8, starting transfers between devices, shifted(): lax.ppermute(array, axis, [(i, (i + by) % count) for i in range(count)])  23.5 us
    ppermute x2, starting transfers between devices, swap_over(): return lax.ppermute(array, axis, [(0, 1), (1, 0)])  20.3 us
    all_to_all x1, waiting for transfers between devices, local(): lax.all_to_all(over_x, ('zhi', 'side'), 0, 0, tiled=True)  16.3 us
    all_to_all x1, starting transfers between devices, local(): lax.all_to_all(over_x, ('zhi', 'side'), 0, 0, tiled=True)  14 us
    all_to_all x1, starting transfers between devices, local(): fresh_terms = lax.all_to_all(partial_fresh, REP + TP, 0, 0, tiled=True)  13.9 us
    all_to_all x1, waiting for transfers between devices, local(): fresh_terms = lax.all_to_all(partial_fresh, REP + TP, 0, 0, tiled=True)  13.9 us
    ppermute x8, waiting for transfers between devices, shifted(): lax.ppermute(array, axis, [(i, (i + by) % count) for i in range(count)])  7.25 us
    all_to_all x1, starting transfers between devices, local(): lax.all_to_all(jnp.broadcast_to(piece[None], (y_count, *piece.shape)), 'y...  6.85 us
  transfers between devices with their start and end apart: 15, of which 8 were waited for; matrix products, arithmetic and copies ran while one was open for 4% of the time, Pallas kernels for 1%

profile of v8, /device:TPU:1, one launch (start us, length us, event | category | flops | bytes accessed | tf_op | source)
XLA Modules:
  0.0 167.8 jit_solution(17107276274206135997)
XLA Ops:
  2.4 4.8 %all-to-all-start = ((bf16[4,64,512]{2,1,0:T(8,128)(2,1)}), bf16[4,64,512]{2,1,0:T(8,128)(2,1)S(1)}, u32[]{:S(2)}, u32[]{:S(2)}) async-start(bf16[4,64,512]{2,1,0:T(8,128)(2,1)} %pad_maximum_fusion.1), calls=%async_computation | async-start | bytes 524288 | tf_op jit(solution)/shard_map/all_to_all | solution.py:187
  8.2 4.6 %all-to-all-done = bf16[4,64,512]{2,1,0:T(8,128)(2,1)S(1)} async-done(((bf16[4,64,512]{2,1,0:T(8,128)(2,1)}), bf16[4,64,512]{2,1,0:T(8,128)(2,1)S(1)}, u32[]{:S(2)}, u32[]{:S(2)}) %all-to-all-start) | async-done | bytes 262176 | tf_op jit(solution)/shard_map/all_to_all | solution.py:187
  14.4 6.8 %all-to-all-start.1 = ((bf16[8,4,64,512]{3,2,1,0:T(8,128)(2,1)}), bf16[8,4,64,512]{3,2,1,0:T(8,128)(2,1)S(1)}, u32[]{:S(2)}, u32[]{:S(2)}) async-start(bf16[8,4,64,512]{3,2,1,0:T(8,128)(2,1)} %broadcast_in_dim.12), calls=%async_computation.1 | async-start | bytes 4194304 | tf_op jit(solution)/shard_map/all_to_all | solution.py:190
  21.3 10.6 %collective-permute-start.4 = (bf16[512,512]{1,0:T(8,128)(2,1)}, bf16[512,512]{1,0:T(8,128)(2,1)S(1)}, u32[]{:S(2)}, u32[]{:S(2)}) collective-permute-start(bf16[512,512]{1,0:T(8,128)(2,1)} %get-tuple-element.8), channel_id=1, source_target_pairs={{0,8},{8,0},{1,9},{9,1},{2,10},{10,2},{3,11},{11,3},{4,12},{12,4},... | collective-permute-start | bytes 1572872 | tf_op jit(solution)/shard_map/ppermute | solution.py:88
  31.9 2.8 %collective-permute-start.2 = (bf16[528,512]{1,0:T(8,128)(2,1)S(1)}, bf16[528,512]{1,0:T(8,128)(2,1)S(1)}, u32[]{:S(2)}, u32[]{:S(2)}) collective-permute-start(bf16[528,512]{1,0:T(8,128)(2,1)S(1)} %pad_maximum_fusion.refs_0_), channel_id=1, source_target_pairs={{0,96},{32,0},{64,32},{96,64},{1,97},{33,1},{65,33},{97,65},{2,98}... | collective-permute-start | bytes 1622024 | tf_op jit(solution)/shard_map/ppermute | solution.py:93
  34.7 2.5 %collective-permute-start = (bf16[528,512]{1,0:T(8,128)(2,1)S(1)}, bf16[528,512]{1,0:T(8,128)(2,1)S(1)}, u32[]{:S(2)}, u32[]{:S(2)}) collective-permute-start(bf16[528,512]{1,0:T(8,128)(2,1)S(1)} %pad_maximum_fusion.refs_0_), channel_id=1, source_target_pairs={{0,32},{32,64},{64,96},{96,0},{1,33},{33,65},{65,97},{97,1},{2,34}... | collective-permute-start | bytes 1622024 | tf_op jit(solution)/shard_map/ppermute | solution.py:93
  37.2 4.9 %collective-permute-done.4.refs_5_ = bf16[512,512]{1,0:T(8,128)(2,1)S(1)} collective-permute-done((bf16[512,512]{1,0:T(8,128)(2,1)}, bf16[512,512]{1,0:T(8,128)(2,1)S(1)}, u32[]{:S(2)}, u32[]{:S(2)}) %collective-permute-start.4) | collective-permute-done | bytes 524320 | tf_op jit(solution)/shard_map/ppermute | solution.py:88
  42.1 2.2 %collective-permute-start.5 = (bf16[512,512]{1,0:T(8,128)(2,1)S(1)}, bf16[512,512]{1,0:T(8,128)(2,1)S(1)}, u32[]{:S(2)}, u32[]{:S(2)}) collective-permute-start(bf16[512,512]{1,0:T(8,128)(2,1)S(1)} %collective-permute-done.4.refs_5_), channel_id=1, source_target_pairs={{0,32},{32,64},{64,96},{96,0},{1,33},{33,65},{65,97},{97,1},{2,34}... | collective-permute-start | bytes 1572872 | tf_op jit(solution)/shard_map/ppermute | solution.py:93
  44.3 4.2 %collective-permute-start.7 = (bf16[512,512]{1,0:T(8,128)(2,1)S(1)}, bf16[512,512]{1,0:T(8,128)(2,1)S(1)}, u32[]{:S(2)}, u32[]{:S(2)}) collective-permute-start(bf16[512,512]{1,0:T(8,128)(2,1)S(1)} %collective-permute-done.4.refs_5_), channel_id=1, source_target_pairs={{0,96},{32,0},{64,32},{96,64},{1,97},{33,1},{65,33},{97,65},{2,98}... | collective-permute-start | bytes 1572872 | tf_op jit(solution)/shard_map/ppermute | solution.py:93
  49.3 1.9 %collective-permute-start.3 = (bf16[272,512]{1,0:T(8,128)(2,1)}, bf16[272,512]{1,0:T(8,128)(2,1)S(1)}, u32[]{:S(2)}, u32[]{:S(2)}) collective-permute-start(bf16[272,512]{1,0:T(8,128)(2,1)} %slice.63), channel_id=1, source_target_pairs={{0,96},{32,0},{64,32},{96,64},{1,97},{33,1},{65,33},{97,65},{2,98}... | collective-permute-start | bytes 835592 | tf_op jit(solution)/shard_map/ppermute | solution.py:93
  52.8 3.4 %collective-permute-start.1 = (bf16[256,512]{1,0:T(8,128)(2,1)}, bf16[256,512]{1,0:T(8,128)(2,1)}, u32[]{:S(2)}, u32[]{:S(2)}) collective-permute-start(bf16[256,512]{1,0:T(8,128)(2,1)} %slice.62), channel_id=1, source_target_pairs={{0,32},{32,64},{64,96},{96,0},{1,33},{33,65},{65,97},{97,1},{2,34}... | collective-permute-start | bytes 786440 | tf_op jit(solution)/shard_map/ppermute | solution.py:93
  56.1 3.7 %collective-permute-done.5.refs_6_ = bf16[512,512]{1,0:T(8,128)(2,1)S(1)} collective-permute-done((bf16[512,512]{1,0:T(8,128)(2,1)S(1)}, bf16[512,512]{1,0:T(8,128)(2,1)S(1)}, u32[]{:S(2)}, u32[]{:S(2)}) %collective-permute-start.5) | collective-permute-done | bytes 524320 | tf_op jit(solution)/shard_map/ppermute | solution.py:93
  61.3 1.9 %collective-permute-start.6 = (bf16[256,512]{1,0:T(8,128)(2,1)}, bf16[256,512]{1,0:T(8,128)(2,1)}, u32[]{:S(2)}, u32[]{:S(2)}) collective-permute-start(bf16[256,512]{1,0:T(8,128)(2,1)} %slice.64), channel_id=1, source_target_pairs={{0,32},{32,64},{64,96},{96,0},{1,33},{33,65},{65,97},{97,1},{2,34}... | collective-permute-start | bytes 786440 | tf_op jit(solution)/shard_map/ppermute | solution.py:93
  64.8 4.6 %collective-permute-start.8 = (bf16[256,512]{1,0:T(8,128)(2,1)}, bf16[256,512]{1,0:T(8,128)(2,1)}, u32[]{:S(2)}, u32[]{:S(2)}) collective-permute-start(bf16[256,512]{1,0:T(8,128)(2,1)} %slice.65), channel_id=1, source_target_pairs={{0,96},{32,0},{64,32},{96,64},{1,97},{33,1},{65,33},{97,65},{2,98}... | collective-permute-start | bytes 786440 | tf_op jit(solution)/shard_map/ppermute | solution.py:93
  69.5 2.3 %collective-permute-done.6.refs_7_ = bf16[256,512]{1,0:T(8,128)(2,1)} collective-permute-done((bf16[256,512]{1,0:T(8,128)(2,1)}, bf16[256,512]{1,0:T(8,128)(2,1)}, u32[]{:S(2)}, u32[]{:S(2)}) %collective-permute-start.6) | collective-permute-done | bytes 262176 | tf_op jit(solution)/shard_map/ppermute | solution.py:93
  77.2 2.4 %products_other.1 = bf16[1152,256]{1,0:T(8,128)(2,1)S(1)} custom-call(s32[3]{0:T(128)S(1)} %pad_add_fusion.position, bf16[528,512]{1,0:T(8,128)(2,1)S(1)} %pad_maximum_fusion.refs_0_, bf16[528,512]{1,0:T(8,128)(2,1)S(1)} %copy-done.2, bf16[256,512]{1,0:T(8,128)(2,1)} %collective-permute-done.1.refs_2_, bf16[272,512]{1,0:T(8,128)(2,1)S(1)} %collective-permute-done.3.refs_3_, ...), custom_call_target="tpu_custom_call" | custom-call | flops 1073741824 | bytes 7340032 | tf_op jit(solution)/shard_map/products_other/pallas_call | solution.py:143
  79.6 9.7 %collective-permute-start.9 = (bf16[1152,256]{1,0:T(8,128)(2,1)S(1)}, bf16[1152,256]{1,0:T(8,128)(2,1)S(1)}, u32[]{:S(2)}, u32[]{:S(2)}) collective-permute-start(bf16[1152,256]{1,0:T(8,128)(2,1)S(1)} %products_other.1), channel_id=1, source_target_pairs={{0,16},{16,0},{1,17},{17,1},{2,18},{18,2},{3,19},{19,3},{4,20},{20... | collective-permute-start | bytes 1769480 | tf_op jit(solution)/shard_map/ppermute | solution.py:88
  89.3 2.4 %products_own.1 = f32[1024,256]{1,0:T(8,128)S(1)} custom-call(s32[3]{0:T(128)S(1)} %pad_add_fusion.position, bf16[528,512]{1,0:T(8,128)(2,1)S(1)} %pad_maximum_fusion.refs_0_, bf16[528,512]{1,0:T(8,128)(2,1)S(1)} %copy-done.2, bf16[256,512]{1,0:T(8,128)(2,1)} %collective-permute-done.1.refs_2_, bf16[272,512]{1,0:T(8,128)(2,1)S(1)} %collective-permute-done.3.refs_3_, ...), custom_call_target="tpu_custom_call" | custom-call | flops 1073741824 | bytes 7340032 | tf_op jit(solution)/shard_map/products_own/pallas_call | solution.py:143
  92.8 14.0 %all-to-all-start.2 = ((bf16[8,128,256]{2,1,0:T(8,128)(2,1)}), bf16[8,128,256]{2,1,0:T(8,128)(2,1)S(1)}, u32[]{:S(2)}, u32[]{:S(2)}) async-start(bf16[8,128,256]{2,1,0:T(8,128)(2,1)} %bitcast.5), calls=%async_computation.2 | async-start | bytes 1048576 | tf_op jit(solution)/shard_map/all_to_all | solution.py:206
  108.4 16.3 %all-to-all-done.2 = bf16[8,128,256]{2,1,0:T(8,128)(2,1)S(1)} async-done(((bf16[8,128,256]{2,1,0:T(8,128)(2,1)}), bf16[8,128,256]{2,1,0:T(8,128)(2,1)S(1)}, u32[]{:S(2)}, u32[]{:S(2)}) %all-to-all-start.2) | async-done | bytes 524320 | tf_op jit(solution)/shard_map/all_to_all | solution.py:206
  125.6 3.4 %all-to-all-start.3 = ((bf16[4,128,256]{2,1,0:T(8,128)(2,1)}), bf16[4,128,256]{2,1,0:T(8,128)(2,1)S(1)}, u32[]{:S(2)}, u32[]{:S(2)}) async-start(bf16[4,128,256]{2,1,0:T(8,128)(2,1)} %broadcast_in_dim.13), calls=%async_computation.3 | async-start | bytes 524288 | tf_op jit(solution)/shard_map/all_to_all | solution.py:208
  129.8 6.5 %all-to-all-done.3 = bf16[4,128,256]{2,1,0:T(8,128)(2,1)S(1)} async-done(((bf16[4,128,256]{2,1,0:T(8,128)(2,1)}), bf16[4,128,256]{2,1,0:T(8,128)(2,1)S(1)}, u32[]{:S(2)}, u32[]{:S(2)}) %all-to-all-start.3) | async-done | bytes 262176 | tf_op jit(solution)/shard_map/all_to_all | solution.py:208
  138.4 13.9 %all-to-all-start.4 = ((bf16[128,2,128]{2,1,0:T(2,128)(2,1)}), bf16[128,2,128]{2,1,0:T(2,128)(2,1)S(1)}, u32[]{:S(2)}, u32[]{:S(2)}) async-start(bf16[128,2,128]{2,1,0:T(2,128)(2,1)} %reshape.141), calls=%async_computation.4 | async-start | bytes 131072 | tf_op jit(solution)/shard_map/all_to_all | solution.py:214
  152.7 13.9 %all-to-all-done.4 = bf16[128,2,128]{2,1,0:T(2,128)(2,1)S(1)} async-done(((bf16[128,2,128]{2,1,0:T(2,128)(2,1)}), bf16[128,2,128]{2,1,0:T(2,128)(2,1)S(1)}, u32[]{:S(2)}, u32[]{:S(2)}) %all-to-all-start.4) | async-done | bytes 65568 | tf_op jit(solution)/shard_map/all_to_all | solution.py:214
  (82 shorter events, 22.4 us)
Async XLA Ops:
  0.6 106.9 %copy-start = (bf16[1,8192]{1,0:T(2,128)(2,1)S(1)}, bf16[1,8192]{1,0:T(2,128)(2,1)}, u32[]{:S(2)}) copy-start(bf16[1,8192]{1,0:T(2,128)(2,1)} %param.16) | copy-start | bytes 49156
  2.4 10.4 %all-to-all-start = ((bf16[4,64,512]{2,1,0:T(8,128)(2,1)}), bf16[4,64,512]{2,1,0:T(8,128)(2,1)S(1)}, u32[]{:S(2)}, u32[]{:S(2)}) async-start(bf16[4,64,512]{2,1,0:T(8,128)(2,1)} %pad_maximum_fusion.1), calls=%async_computation | async-start | bytes 524288 | tf_op jit(solution)/shard_map/all_to_all | solution.py:187
  14.4 58.6 %all-to-all-start.1 = ((bf16[8,4,64,512]{3,2,1,0:T(8,128)(2,1)}), bf16[8,4,64,512]{3,2,1,0:T(8,128)(2,1)S(1)}, u32[]{:S(2)}, u32[]{:S(2)}) async-start(bf16[8,4,64,512]{3,2,1,0:T(8,128)(2,1)} %broadcast_in_dim.12), calls=%async_computation.1 | async-start | bytes 4194304 | tf_op jit(solution)/shard_map/all_to_all | solution.py:190
  21.3 20.8 %collective-permute-start.4 = (bf16[512,512]{1,0:T(8,128)(2,1)}, bf16[512,512]{1,0:T(8,128)(2,1)S(1)}, u32[]{:S(2)}, u32[]{:S(2)}) collective-permute-start(bf16[512,512]{1,0:T(8,128)(2,1)} %get-tuple-element.8), channel_id=1, source_target_pairs={{0,8},{8,0},{1,9},{9,1},{2,10},{10,2},{3,11},{11,3},{4,12},{12,4},... | collective-permute-start | bytes 1572872 | tf_op jit(solution)/shard_map/ppermute | solution.py:88
  31.9 16.7 %collective-permute-start.2 = (bf16[528,512]{1,0:T(8,128)(2,1)S(1)}, bf16[528,512]{1,0:T(8,128)(2,1)S(1)}, u32[]{:S(2)}, u32[]{:S(2)}) collective-permute-start(bf16[528,512]{1,0:T(8,128)(2,1)S(1)} %pad_maximum_fusion.refs_0_), channel_id=1, source_target_pairs={{0,96},{32,0},{64,32},{96,64},{1,97},{33,1},{65,33},{97,65},{2,98}... | collective-permute-start | bytes 1622024 | tf_op jit(solution)/shard_map/ppermute | solution.py:93
  34.7 16.5 %collective-permute-start = (bf16[528,512]{1,0:T(8,128)(2,1)S(1)}, bf16[528,512]{1,0:T(8,128)(2,1)S(1)}, u32[]{:S(2)}, u32[]{:S(2)}) collective-permute-start(bf16[528,512]{1,0:T(8,128)(2,1)S(1)} %pad_maximum_fusion.refs_0_), channel_id=1, source_target_pairs={{0,32},{32,64},{64,96},{96,0},{1,33},{33,65},{65,97},{97,1},{2,34}... | collective-permute-start | bytes 1622024 | tf_op jit(solution)/shard_map/ppermute | solution.py:93
  42.1 21.9 %copy-start.7 = (bf16[512,512]{1,0:T(8,128)(2,1)}, bf16[512,512]{1,0:T(8,128)(2,1)S(1)}, u32[]{:S(2)}) copy-start(bf16[512,512]{1,0:T(8,128)(2,1)S(1)} %collective-permute-done.4.refs_5_) | copy-start | bytes 1572868
  42.1 17.8 %collective-permute-start.5 = (bf16[512,512]{1,0:T(8,128)(2,1)S(1)}, bf16[512,512]{1,0:T(8,128)(2,1)S(1)}, u32[]{:S(2)}, u32[]{:S(2)}) collective-permute-start(bf16[512,512]{1,0:T(8,128)(2,1)S(1)} %collective-permute-done.4.refs_5_), channel_id=1, source_target_pairs={{0,32},{32,64},{64,96},{96,0},{1,33},{33,65},{65,97},{97,1},{2,34}... | collective-permute-start | bytes 1572872 | tf_op jit(solution)/shard_map/ppermute | solution.py:93
  44.3 18.9 %collective-permute-start.7 = (bf16[512,512]{1,0:T(8,128)(2,1)S(1)}, bf16[512,512]{1,0:T(8,128)(2,1)S(1)}, u32[]{:S(2)}, u32[]{:S(2)}) collective-permute-start(bf16[512,512]{1,0:T(8,128)(2,1)S(1)} %collective-permute-done.4.refs_5_), channel_id=1, source_target_pairs={{0,96},{32,0},{64,32},{96,64},{1,97},{33,1},{65,33},{97,65},{2,98}... | collective-permute-start | bytes 1572872 | tf_op jit(solution)/shard_map/ppermute | solution.py:93
  49.3 20.2 %collective-permute-start.3 = (bf16[272,512]{1,0:T(8,128)(2,1)}, bf16[272,512]{1,0:T(8,128)(2,1)S(1)}, u32[]{:S(2)}, u32[]{:S(2)}) collective-permute-start(bf16[272,512]{1,0:T(8,128)(2,1)} %slice.63), channel_id=1, source_target_pairs={{0,96},{32,0},{64,32},{96,64},{1,97},{33,1},{65,33},{97,65},{2,98}... | collective-permute-start | bytes 835592 | tf_op jit(solution)/shard_map/ppermute | solution.py:93
  52.8 16.7 %collective-permute-start.1 = (bf16[256,512]{1,0:T(8,128)(2,1)}, bf16[256,512]{1,0:T(8,128)(2,1)}, u32[]{:S(2)}, u32[]{:S(2)}) collective-permute-start(bf16[256,512]{1,0:T(8,128)(2,1)} %slice.62), channel_id=1, source_target_pairs={{0,32},{32,64},{64,96},{96,0},{1,33},{33,65},{65,97},{97,1},{2,34}... | collective-permute-start | bytes 786440 | tf_op jit(solution)/shard_map/ppermute | solution.py:93
  61.3 10.4 %collective-permute-start.6 = (bf16[256,512]{1,0:T(8,128)(2,1)}, bf16[256,512]{1,0:T(8,128)(2,1)}, u32[]{:S(2)}, u32[]{:S(2)}) collective-permute-start(bf16[256,512]{1,0:T(8,128)(2,1)} %slice.64), channel_id=1, source_target_pairs={{0,32},{32,64},{64,96},{96,0},{1,33},{33,65},{65,97},{97,1},{2,34}... | collective-permute-start | bytes 786440 | tf_op jit(solution)/shard_map/ppermute | solution.py:93
  64.8 8.2 %collective-permute-start.8 = (bf16[256,512]{1,0:T(8,128)(2,1)}, bf16[256,512]{1,0:T(8,128)(2,1)}, u32[]{:S(2)}, u32[]{:S(2)}) collective-permute-start(bf16[256,512]{1,0:T(8,128)(2,1)} %slice.65), channel_id=1, source_target_pairs={{0,96},{32,0},{64,32},{96,64},{1,97},{33,1},{65,33},{97,65},{2,98}... | collective-permute-start | bytes 786440 | tf_op jit(solution)/shard_map/ppermute | solution.py:93
  79.6 12.2 %copy-start.9 = (bf16[1152,256]{1,0:T(8,128)(2,1)}, bf16[1152,256]{1,0:T(8,128)(2,1)S(1)}, u32[]{:S(2)}) copy-start(bf16[1152,256]{1,0:T(8,128)(2,1)S(1)} %products_other.1) | copy-start | bytes 1769476
  79.6 12.2 %collective-permute-start.9 = (bf16[1152,256]{1,0:T(8,128)(2,1)S(1)}, bf16[1152,256]{1,0:T(8,128)(2,1)S(1)}, u32[]{:S(2)}, u32[]{:S(2)}) collective-permute-start(bf16[1152,256]{1,0:T(8,128)(2,1)S(1)} %products_other.1), channel_id=1, source_target_pairs={{0,16},{16,0},{1,17},{17,1},{2,18},{18,2},{3,19},{19,3},{4,20},{20... | collective-permute-start | bytes 1769480 | tf_op jit(solution)/shard_map/ppermute | solution.py:88
  91.7 15.0 %copy-start.16 = (bf16[1,128,1024]{2,1,0:T(8,128)(2,1)S(1)}, bf16[1,128,1024]{2,1,0:T(8,128)(2,1)}, u32[]{:S(2)}) copy-start(bf16[1,128,1024]{2,1,0:T(8,128)(2,1)} %param.17) | copy-start | bytes 786436
  92.8 14.7 %copy-start.17 = (bf16[1,128,1024]{2,1,0:T(8,128)(2,1)S(1)}, bf16[1,128,1024]{2,1,0:T(8,128)(2,1)}, u32[]{:S(2)}) copy-start(bf16[1,128,1024]{2,1,0:T(8,128)(2,1)} %param.18) | copy-start | bytes 786436
  92.8 32.0 %all-to-all-start.2 = ((bf16[8,128,256]{2,1,0:T(8,128)(2,1)}), bf16[8,128,256]{2,1,0:T(8,128)(2,1)S(1)}, u32[]{:S(2)}, u32[]{:S(2)}) async-start(bf16[8,128,256]{2,1,0:T(8,128)(2,1)} %bitcast.5), calls=%async_computation.2 | async-start | bytes 1048576 | tf_op jit(solution)/shard_map/all_to_all | solution.py:206
  108.4 27.9 %copy-start.13 = (f32[512,256]{1,0:T(8,128)S(1)}, f32[512,256]{1,0:T(8,128)}, u32[]{:S(2)}) copy-start(f32[512,256]{1,0:T(8,128)} %param.12) | copy-start | bytes 1572868
  108.4 27.9 %copy-start.14 = (bf16[512,256]{1,0:T(8,128)(2,1)S(1)}, bf16[512,256]{1,0:T(8,128)(2,1)}, u32[]{:S(2)}) copy-start(bf16[512,256]{1,0:T(8,128)(2,1)} %param.14) | copy-start | bytes 786436
  108.4 27.9 %copy-start.15 = (bf16[512,256]{1,0:T(8,128)(2,1)S(1)}, bf16[512,256]{1,0:T(8,128)(2,1)}, u32[]{:S(2)}) copy-start(bf16[512,256]{1,0:T(8,128)(2,1)} %param.13) | copy-start | bytes 786436
  125.6 10.7 %all-to-all-start.3 = ((bf16[4,128,256]{2,1,0:T(8,128)(2,1)}), bf16[4,128,256]{2,1,0:T(8,128)(2,1)S(1)}, u32[]{:S(2)}, u32[]{:S(2)}) async-start(bf16[4,128,256]{2,1,0:T(8,128)(2,1)} %broadcast_in_dim.13), calls=%async_computation.3 | async-start | bytes 524288 | tf_op jit(solution)/shard_map/all_to_all | solution.py:208
  137.6 30.2 %copy-start.10 = (f32[512,256]{1,0:T(8,128)}, f32[512,256]{1,0:T(8,128)S(1)}, u32[]{:S(2)}) copy-start(f32[512,256]{1,0:T(8,128)S(1)} %get-tuple-element.15) | copy-start | bytes 1572868
  138.4 28.1 %all-to-all-start.4 = ((bf16[128,2,128]{2,1,0:T(2,128)(2,1)}), bf16[128,2,128]{2,1,0:T(2,128)(2,1)S(1)}, u32[]{:S(2)}, u32[]{:S(2)}) async-start(bf16[128,2,128]{2,1,0:T(2,128)(2,1)} %reshape.141), calls=%async_computation.4 | async-start | bytes 131072 | tf_op jit(solution)/shard_map/all_to_all | solution.py:214
  (10 other events, 15.1 us)

commit v9 on v7

--- a/solution.py
+++ b/solution.py
@@ -93,8 +93,10 @@
     return lax.ppermute(array, axis, [(i, (i + by) % count) for i in range(count)])
 
 
-def from_behind(array, axis):
-    return [array] + [shifted(array, axis, by) for by in range(1, lax.axis_size(axis))]
+def around(array, axis, way):
+    behind, ahead = shifted(array, axis, 1), shifted(array, axis, -1)
+    across = shifted(behind if way == 1 else ahead, axis, way)
+    return [array, behind, across, ahead]
 
 
 def same_kernel(array, out):
@@ -108,7 +110,7 @@
         in_specs=[pl.BlockSpec(memory_space=pl.ANY)],
         out_specs=pl.BlockSpec(memory_space=pl.ANY),
         input_output_aliases={0: 0},
-        cost_estimate=pl.CostEstimate(flops=50 * 10**9, bytes_accessed=0, transcendentals=0),
+        cost_estimate=pl.CostEstimate(flops=24 * 10**9, bytes_accessed=0, transcendentals=0),
         name="held",
     )(array)
 
@@ -197,10 +199,7 @@
     piece, kept = lax.optimization_barrier((piece, kept))
     y_count = lax.axis_size("y")
     grads_all = lax.all_to_all(jnp.broadcast_to(piece[None], (y_count, *piece.shape)), "y", 0, 0)
-    behind = shifted(kept, "x", 1)
-    kept, received = lax.optimization_barrier((kept, held(received)))
-    inputs = [kept, behind, shifted(kept, "x", 2), shifted(kept, "x", 3)]
-    inputs += from_behind(received, "x")
+    inputs = around(kept, "x", 1) + around(held(received), "x", -1)
 
     sent = products(True, inputs, grads_all, block_width)
     sent_back = swap_over(sent, "core")

time: 168 us -> 161 us (0.958)
  waiting for transfers between devices: 77.7 us -> 69.5 us
    ppermute x6, waiting for transfers between devices: 34.2 us -> 22.6 us  [shifted(): lax.ppermute(array, axis, [(i, (i + by) % count) for i in range(count)])]
    all_to_all x1, waiting for transfers between devices: 0.9 us -> 10.2 us  [local(): lax.all_to_all(jnp.broadcast_to(piece[None], (y_count, *piece.shape)), 'y...]
    all_to_all x1, waiting for transfers between devices: 5.89 us -> 0.01 us  [local(): piece = lax.all_to_all(columns, 'x', 0, 0, tiled=True)]
where the time goes in v9:
time: 161 us; the launch traced here: 160 us
  starting transfers between devices  70.6 us (44%)
  waiting for transfers between devices  69.5 us (43%)
  local copies, waits for them, and re-layouts  6.47 us (4%)
  Pallas kernels  6.29 us (4%)
  other arithmetic  4.36 us (3%)
  between operations  1.62 us (1%)
    ppermute x6, waiting for transfers between devices, shifted(): lax.ppermute(array, axis, [(i, (i + by) % count) for i in range(count)])  22.6 us
    ppermute x6, starting transfers between devices, shifted(): lax.ppermute(array, axis, [(i, (i + by) % count) for i in range(count)])  18.3 us
    all_to_all x1, waiting for transfers between devices, local(): lax.all_to_all(over_x, ('zhi', 'side'), 0, 0, tiled=True)  16.3 us
    all_to_all x1, starting transfers between devices, local(): fresh_terms = lax.all_to_all(partial_fresh, REP + TP, 0, 0, tiled=True)  14.1 us
    all_to_all x1, waiting for transfers between devices, local(): fresh_terms = lax.all_to_all(partial_fresh, REP + TP, 0, 0, tiled=True)  13.9 us
    ppermute x2, starting transfers between devices, swap_over(): return lax.ppermute(array, axis, [(0, 1), (1, 0)])  13.5 us
    all_to_all x1, waiting for transfers between devices, local(): lax.all_to_all(jnp.broadcast_to(piece[None], (y_count, *piece.shape)), 'y...  10.2 us
    all_to_all x1, starting transfers between devices, local(): lax.all_to_all(over_x, ('zhi', 'side'), 0, 0, tiled=True)  9.67 us
  transfers between devices with their start and end apart: 13, of which 7 were waited for; matrix products, arithmetic and copies ran while one was open for 3% of the time, Pallas kernels for 2%

profile of v9, /device:TPU:1, one launch (start us, length us, event | category | flops | bytes accessed | tf_op | source)
XLA Modules:
  0.0 159.7 jit_solution(14022144743941313621)
XLA Ops:
  2.4 4.8 %all-to-all-start = ((bf16[4,64,512]{2,1,0:T(8,128)(2,1)}), bf16[4,64,512]{2,1,0:T(8,128)(2,1)S(1)}, u32[]{:S(2)}, u32[]{:S(2)}) async-start(bf16[4,64,512]{2,1,0:T(8,128)(2,1)} %pad_maximum_fusion.1), calls=%async_computation | async-start | bytes 524288 | tf_op jit(solution)/shard_map/all_to_all | solution.py:198
  8.2 10.6 %collective-permute-start.3 = (bf16[512,512]{1,0:T(8,128)(2,1)}, bf16[512,512]{1,0:T(8,128)(2,1)}, u32[]{:S(2)}, u32[]{:S(2)}) collective-permute-start(bf16[512,512]{1,0:T(8,128)(2,1)} %get-tuple-element.8), channel_id=1, source_target_pairs={{0,8},{8,0},{1,9},{9,1},{2,10},{10,2},{3,11},{11,3},{4,12},{12,4},... | collective-permute-start | bytes 1572872 | tf_op jit(solution)/shard_map/ppermute | solution.py:88
  18.9 1.6 broadcast_in_dim.12
  20.4 6.8 %all-to-all-start.1 = ((bf16[8,4,64,512]{3,2,1,0:T(8,128)(2,1)}), bf16[8,4,64,512]{3,2,1,0:T(8,128)(2,1)S(1)}, u32[]{:S(2)}, u32[]{:S(2)}) async-start(bf16[8,4,64,512]{3,2,1,0:T(8,128)(2,1)} %broadcast_in_dim.12), calls=%async_computation.1 | async-start | bytes 4194304 | tf_op jit(solution)/shard_map/all_to_all | solution.py:201
  27.2 3.4 %collective-permute-start = (bf16[528,512]{1,0:T(8,128)(2,1)S(1)}, bf16[528,512]{1,0:T(8,128)(2,1)S(1)}, u32[]{:S(2)}, u32[]{:S(2)}) collective-permute-start(bf16[528,512]{1,0:T(8,128)(2,1)S(1)} %pad_maximum_fusion.refs_0_), channel_id=1, source_target_pairs={{0,32},{32,64},{64,96},{96,0},{1,33},{33,65},{65,97},{97,1},{2,34}... | collective-permute-start | bytes 1622024 | tf_op jit(solution)/shard_map/ppermute | solution.py:93
  30.6 3.2 %collective-permute-start.5 = (bf16[512,512]{1,0:T(8,128)(2,1)}, bf16[512,512]{1,0:T(8,128)(2,1)}, u32[]{:S(2)}, u32[]{:S(2)}) collective-permute-start(bf16[512,512]{1,0:T(8,128)(2,1)} %held.1.refs_4_), channel_id=1, source_target_pairs={{0,96},{32,0},{64,32},{96,64},{1,97},{33,1},{65,33},{97,65},{2,98}... | collective-permute-start | bytes 1572872 | tf_op jit(solution)/shard_map/ppermute | solution.py:93
  33.8 3.3 %collective-permute-start.2 = (bf16[528,512]{1,0:T(8,128)(2,1)S(1)}, bf16[528,512]{1,0:T(8,128)(2,1)}, u32[]{:S(2)}, u32[]{:S(2)}) collective-permute-start(bf16[528,512]{1,0:T(8,128)(2,1)S(1)} %pad_maximum_fusion.refs_0_), channel_id=1, source_target_pairs={{0,96},{32,0},{64,32},{96,64},{1,97},{33,1},{65,33},{97,65},{2,98}... | collective-permute-start | bytes 1622024 | tf_op jit(solution)/shard_map/ppermute | solution.py:93
  37.1 5.5 %collective-permute-done.refs_1_ = bf16[528,512]{1,0:T(8,128)(2,1)S(1)} collective-permute-done((bf16[528,512]{1,0:T(8,128)(2,1)S(1)}, bf16[528,512]{1,0:T(8,128)(2,1)S(1)}, u32[]{:S(2)}, u32[]{:S(2)}) %collective-permute-start) | collective-permute-done | bytes 540704 | tf_op jit(solution)/shard_map/ppermute | solution.py:93
  42.6 2.0 %collective-permute-start.1 = (bf16[528,512]{1,0:T(8,128)(2,1)S(1)}, bf16[528,512]{1,0:T(8,128)(2,1)}, u32[]{:S(2)}, u32[]{:S(2)}) collective-permute-start(bf16[528,512]{1,0:T(8,128)(2,1)S(1)} %collective-permute-done.refs_1_), channel_id=1, source_target_pairs={{0,32},{32,64},{64,96},{96,0},{1,33},{33,65},{65,97},{97,1},{2,34}... | collective-permute-start | bytes 1622024 | tf_op jit(solution)/shard_map/ppermute | solution.py:93
  44.6 3.1 %collective-permute-start.4 = (bf16[512,512]{1,0:T(8,128)(2,1)}, bf16[512,512]{1,0:T(8,128)(2,1)}, u32[]{:S(2)}, u32[]{:S(2)}) collective-permute-start(bf16[512,512]{1,0:T(8,128)(2,1)} %held.1.refs_4_), channel_id=1, source_target_pairs={{0,32},{32,64},{64,96},{96,0},{1,33},{33,65},{65,97},{97,1},{2,34}... | collective-permute-start | bytes 1572872 | tf_op jit(solution)/shard_map/ppermute | solution.py:93
  47.7 3.4 %collective-permute-start.6 = (bf16[512,512]{1,0:T(8,128)(2,1)}, bf16[512,512]{1,0:T(8,128)(2,1)}, u32[]{:S(2)}, u32[]{:S(2)}) collective-permute-start(bf16[512,512]{1,0:T(8,128)(2,1)} %collective-permute-done.5.refs_7_), channel_id=1, source_target_pairs={{0,96},{32,0},{64,32},{96,64},{1,97},{33,1},{65,33},{97,65},{2,98}... | collective-permute-start | bytes 1572872 | tf_op jit(solution)/shard_map/ppermute | solution.py:93
  51.2 4.6 %collective-permute-done.2.refs_3_ = bf16[528,512]{1,0:T(8,128)(2,1)} collective-permute-done((bf16[528,512]{1,0:T(8,128)(2,1)S(1)}, bf16[528,512]{1,0:T(8,128)(2,1)}, u32[]{:S(2)}, u32[]{:S(2)}) %collective-permute-start.2) | collective-permute-done | bytes 540704 | tf_op jit(solution)/shard_map/ppermute | solution.py:93
  55.8 12.6 %collective-permute-done.4.refs_5_ = bf16[512,512]{1,0:T(8,128)(2,1)} collective-permute-done((bf16[512,512]{1,0:T(8,128)(2,1)}, bf16[512,512]{1,0:T(8,128)(2,1)}, u32[]{:S(2)}, u32[]{:S(2)}) %collective-permute-start.4) | collective-permute-done | bytes 524320 | tf_op jit(solution)/shard_map/ppermute | solution.py:93
  68.4 10.2 %all-to-all-done.1.refs_8_ = bf16[8,4,64,512]{3,2,1,0:T(8,128)(2,1)S(1)} async-done(((bf16[8,4,64,512]{3,2,1,0:T(8,128)(2,1)}), bf16[8,4,64,512]{3,2,1,0:T(8,128)(2,1)S(1)}, u32[]{:S(2)}, u32[]{:S(2)}) %all-to-all-start.1) | async-done | bytes 2097184 | tf_op jit(solution)/shard_map/all_to_all | solution.py:201
  78.5 3.1 %products_other.1 = bf16[1152,256]{1,0:T(8,128)(2,1)S(1)} custom-call(s32[3]{0:T(128)S(1)} %pad_add_fusion.position, bf16[528,512]{1,0:T(8,128)(2,1)S(1)} %pad_maximum_fusion.refs_0_, bf16[528,512]{1,0:T(8,128)(2,1)S(1)} %collective-permute-done.refs_1_, bf16[528,512]{1,0:T(8,128)(2,1)} %collective-permute-done.1.refs_2_, ...), custom_call_target="tpu_custom_call" | custom-call | flops 1073741824 | bytes 7340032 | tf_op jit(solution)/shard_map/products_other/pallas_call | solution.py:154
  81.7 2.9 %collective-permute-start.7 = (bf16[1152,256]{1,0:T(8,128)(2,1)S(1)}, bf16[1152,256]{1,0:T(8,128)(2,1)S(1)}, u32[]{:S(2)}, u32[]{:S(2)}) collective-permute-start(bf16[1152,256]{1,0:T(8,128)(2,1)S(1)} %products_other.1), channel_id=1, source_target_pairs={{0,16},{16,0},{1,17},{17,1},{2,18},{18,2},{3,19},{19,3},{4,20},{20... | collective-permute-start | bytes 1769480 | tf_op jit(solution)/shard_map/ppermute | solution.py:88
  84.6 3.2 %products_own.1 = f32[1024,256]{1,0:T(8,128)S(1)} custom-call(s32[3]{0:T(128)S(1)} %pad_add_fusion.position, bf16[528,512]{1,0:T(8,128)(2,1)S(1)} %pad_maximum_fusion.refs_0_, bf16[528,512]{1,0:T(8,128)(2,1)S(1)} %collective-permute-done.refs_1_, bf16[528,512]{1,0:T(8,128)(2,1)} %collective-permute-done.1.refs_2_, ...), custom_call_target="tpu_custom_call" | custom-call | flops 1073741824 | bytes 7340032 | tf_op jit(solution)/shard_map/products_own/pallas_call | solution.py:154
  88.8 9.7 %all-to-all-start.2 = ((bf16[8,128,256]{2,1,0:T(8,128)(2,1)}), bf16[8,128,256]{2,1,0:T(8,128)(2,1)S(1)}, u32[]{:S(2)}, u32[]{:S(2)}) async-start(bf16[8,128,256]{2,1,0:T(8,128)(2,1)} %bitcast.5), calls=%async_computation.2 | async-start | bytes 1048576 | tf_op jit(solution)/shard_map/all_to_all | solution.py:217
  100.1 16.3 %all-to-all-done.2 = bf16[8,128,256]{2,1,0:T(8,128)(2,1)S(1)} async-done(((bf16[8,128,256]{2,1,0:T(8,128)(2,1)}), bf16[8,128,256]{2,1,0:T(8,128)(2,1)S(1)}, u32[]{:S(2)}, u32[]{:S(2)}) %all-to-all-start.2) | async-done | bytes 524320 | tf_op jit(solution)/shard_map/all_to_all | solution.py:217
  117.3 3.4 %all-to-all-start.3 = ((bf16[4,128,256]{2,1,0:T(8,128)(2,1)}), bf16[4,128,256]{2,1,0:T(8,128)(2,1)S(1)}, u32[]{:S(2)}, u32[]{:S(2)}) async-start(bf16[4,128,256]{2,1,0:T(8,128)(2,1)} %broadcast_in_dim.13), calls=%async_computation.3 | async-start | bytes 524288 | tf_op jit(solution)/shard_map/all_to_all | solution.py:219
  121.5 6.5 %all-to-all-done.3 = bf16[4,128,256]{2,1,0:T(8,128)(2,1)S(1)} async-done(((bf16[4,128,256]{2,1,0:T(8,128)(2,1)}), bf16[4,128,256]{2,1,0:T(8,128)(2,1)S(1)}, u32[]{:S(2)}, u32[]{:S(2)}) %all-to-all-start.3) | async-done | bytes 262176 | tf_op jit(solution)/shard_map/all_to_all | solution.py:219
  128.0 1.3 fusion.5
  130.2 14.1 %all-to-all-start.4 = ((bf16[128,2,128]{2,1,0:T(2,128)(2,1)}), bf16[128,2,128]{2,1,0:T(2,128)(2,1)S(1)}, u32[]{:S(2)}, u32[]{:S(2)}) async-start(bf16[128,2,128]{2,1,0:T(2,128)(2,1)} %reshape.141), calls=%async_computation.4 | async-start | bytes 131072 | tf_op jit(solution)/shard_map/all_to_all | solution.py:225
  144.5 13.9 %all-to-all-done.4 = bf16[128,2,128]{2,1,0:T(2,128)(2,1)S(1)} async-done(((bf16[128,2,128]{2,1,0:T(2,128)(2,1)}), bf16[128,2,128]{2,1,0:T(2,128)(2,1)S(1)}, u32[]{:S(2)}, u32[]{:S(2)}) %all-to-all-start.4) | async-done | bytes 65568 | tf_op jit(solution)/shard_map/all_to_all | solution.py:225
  (59 shorter events, 8.8 us)
Async XLA Ops:
  0.6 98.6 %copy-start = (bf16[1,8192]{1,0:T(2,128)(2,1)S(1)}, bf16[1,8192]{1,0:T(2,128)(2,1)}, u32[]{:S(2)}) copy-start(bf16[1,8192]{1,0:T(2,128)(2,1)} %param.16) | copy-start | bytes 49156
  0.6 6.6 %copy-start.3 = (bf16[1,1024,512]{2,1,0:T(8,128)(2,1)S(1)}, bf16[1,1024,512]{2,1,0:T(8,128)(2,1)}, u32[]{:S(2)}) copy-start(bf16[1,1024,512]{2,1,0:T(8,128)(2,1)} %param.10) | copy-start | bytes 3145732
  2.4 16.4 %all-to-all-start = ((bf16[4,64,512]{2,1,0:T(8,128)(2,1)}), bf16[4,64,512]{2,1,0:T(8,128)(2,1)S(1)}, u32[]{:S(2)}, u32[]{:S(2)}) async-start(bf16[4,64,512]{2,1,0:T(8,128)(2,1)} %pad_maximum_fusion.1), calls=%async_computation | async-start | bytes 524288 | tf_op jit(solution)/shard_map/all_to_all | solution.py:198
  7.3 11.5 %copy-start.10 = (bf16[16,512]{1,0:T(8,128)(2,1)S(1)}, bf16[16,512]{1,0:T(8,128)(2,1)}, u32[]{:S(2)}) copy-start(bf16[16,512]{1,0:T(8,128)(2,1)} %param.15) | copy-start | bytes 49156
  8.2 22.5 %collective-permute-start.3 = (bf16[512,512]{1,0:T(8,128)(2,1)}, bf16[512,512]{1,0:T(8,128)(2,1)}, u32[]{:S(2)}, u32[]{:S(2)}) collective-permute-start(bf16[512,512]{1,0:T(8,128)(2,1)} %get-tuple-element.8), channel_id=1, source_target_pairs={{0,8},{8,0},{1,9},{9,1},{2,10},{10,2},{3,11},{11,3},{4,12},{12,4},... | collective-permute-start | bytes 1572872 | tf_op jit(solution)/shard_map/ppermute | solution.py:88
  20.4 58.1 %all-to-all-start.1 = ((bf16[8,4,64,512]{3,2,1,0:T(8,128)(2,1)}), bf16[8,4,64,512]{3,2,1,0:T(8,128)(2,1)S(1)}, u32[]{:S(2)}, u32[]{:S(2)}) async-start(bf16[8,4,64,512]{3,2,1,0:T(8,128)(2,1)} %broadcast_in_dim.12), calls=%async_computation.1 | async-start | bytes 4194304 | tf_op jit(solution)/shard_map/all_to_all | solution.py:201
  27.2 15.4 %collective-permute-start = (bf16[528,512]{1,0:T(8,128)(2,1)S(1)}, bf16[528,512]{1,0:T(8,128)(2,1)S(1)}, u32[]{:S(2)}, u32[]{:S(2)}) collective-permute-start(bf16[528,512]{1,0:T(8,128)(2,1)S(1)} %pad_maximum_fusion.refs_0_), channel_id=1, source_target_pairs={{0,32},{32,64},{64,96},{96,0},{1,33},{33,65},{65,97},{97,1},{2,34}... | collective-permute-start | bytes 1622024 | tf_op jit(solution)/shard_map/ppermute | solution.py:93
  30.6 17.0 %collective-permute-start.5 = (bf16[512,512]{1,0:T(8,128)(2,1)}, bf16[512,512]{1,0:T(8,128)(2,1)}, u32[]{:S(2)}, u32[]{:S(2)}) collective-permute-start(bf16[512,512]{1,0:T(8,128)(2,1)} %held.1.refs_4_), channel_id=1, source_target_pairs={{0,96},{32,0},{64,32},{96,64},{1,97},{33,1},{65,33},{97,65},{2,98}... | collective-permute-start | bytes 1572872 | tf_op jit(solution)/shard_map/ppermute | solution.py:93
  33.8 21.9 %collective-permute-start.2 = (bf16[528,512]{1,0:T(8,128)(2,1)S(1)}, bf16[528,512]{1,0:T(8,128)(2,1)}, u32[]{:S(2)}, u32[]{:S(2)}) collective-permute-start(bf16[528,512]{1,0:T(8,128)(2,1)S(1)} %pad_maximum_fusion.refs_0_), channel_id=1, source_target_pairs={{0,96},{32,0},{64,32},{96,64},{1,97},{33,1},{65,33},{97,65},{2,98}... | collective-permute-start | bytes 1622024 | tf_op jit(solution)/shard_map/ppermute | solution.py:93
  42.6 25.8 %collective-permute-start.1 = (bf16[528,512]{1,0:T(8,128)(2,1)S(1)}, bf16[528,512]{1,0:T(8,128)(2,1)}, u32[]{:S(2)}, u32[]{:S(2)}) collective-permute-start(bf16[528,512]{1,0:T(8,128)(2,1)S(1)} %collective-permute-done.refs_1_), channel_id=1, source_target_pairs={{0,32},{32,64},{64,96},{96,0},{1,33},{33,65},{65,97},{97,1},{2,34}... | collective-permute-start | bytes 1622024 | tf_op jit(solution)/shard_map/ppermute | solution.py:93
  44.6 23.8 %collective-permute-start.4 = (bf16[512,512]{1,0:T(8,128)(2,1)}, bf16[512,512]{1,0:T(8,128)(2,1)}, u32[]{:S(2)}, u32[]{:S(2)}) collective-permute-start(bf16[512,512]{1,0:T(8,128)(2,1)} %held.1.refs_4_), channel_id=1, source_target_pairs={{0,32},{32,64},{64,96},{96,0},{1,33},{33,65},{65,97},{97,1},{2,34}... | collective-permute-start | bytes 1572872 | tf_op jit(solution)/shard_map/ppermute | solution.py:93
  47.7 20.7 %collective-permute-start.6 = (bf16[512,512]{1,0:T(8,128)(2,1)}, bf16[512,512]{1,0:T(8,128)(2,1)}, u32[]{:S(2)}, u32[]{:S(2)}) collective-permute-start(bf16[512,512]{1,0:T(8,128)(2,1)} %collective-permute-done.5.refs_7_), channel_id=1, source_target_pairs={{0,96},{32,0},{64,32},{96,64},{1,97},{33,1},{65,33},{97,65},{2,98}... | collective-permute-start | bytes 1572872 | tf_op jit(solution)/shard_map/ppermute | solution.py:93
  81.7 6.0 %copy-start.1 = (bf16[1152,256]{1,0:T(8,128)(2,1)}, bf16[1152,256]{1,0:T(8,128)(2,1)S(1)}, u32[]{:S(2)}) copy-start(bf16[1152,256]{1,0:T(8,128)(2,1)S(1)} %products_other.1) | copy-start | bytes 1769476
  81.7 6.1 %collective-permute-start.7 = (bf16[1152,256]{1,0:T(8,128)(2,1)S(1)}, bf16[1152,256]{1,0:T(8,128)(2,1)S(1)}, u32[]{:S(2)}, u32[]{:S(2)}) collective-permute-start(bf16[1152,256]{1,0:T(8,128)(2,1)S(1)} %products_other.1), channel_id=1, source_target_pairs={{0,16},{16,0},{1,17},{17,1},{2,18},{18,2},{3,19},{19,3},{4,20},{20... | collective-permute-start | bytes 1769480 | tf_op jit(solution)/shard_map/ppermute | solution.py:88
  87.7 10.7 %copy-start.8 = (bf16[1,128,1024]{2,1,0:T(8,128)(2,1)S(1)}, bf16[1,128,1024]{2,1,0:T(8,128)(2,1)}, u32[]{:S(2)}) copy-start(bf16[1,128,1024]{2,1,0:T(8,128)(2,1)} %param.17) | copy-start | bytes 786436
  87.8 1.0 copy-start.4
  88.8 10.4 %copy-start.9 = (bf16[1,128,1024]{2,1,0:T(8,128)(2,1)S(1)}, bf16[1,128,1024]{2,1,0:T(8,128)(2,1)}, u32[]{:S(2)}) copy-start(bf16[1,128,1024]{2,1,0:T(8,128)(2,1)} %param.18) | copy-start | bytes 786436
  88.8 27.7 %all-to-all-start.2 = ((bf16[8,128,256]{2,1,0:T(8,128)(2,1)}), bf16[8,128,256]{2,1,0:T(8,128)(2,1)S(1)}, u32[]{:S(2)}, u32[]{:S(2)}) async-start(bf16[8,128,256]{2,1,0:T(8,128)(2,1)} %bitcast.5), calls=%async_computation.2 | async-start | bytes 1048576 | tf_op jit(solution)/shard_map/all_to_all | solution.py:217
  100.1 27.9 %copy-start.5 = (f32[512,256]{1,0:T(8,128)S(1)}, f32[512,256]{1,0:T(8,128)}, u32[]{:S(2)}) copy-start(f32[512,256]{1,0:T(8,128)} %param.12) | copy-start | bytes 1572868
  100.1 27.9 %copy-start.6 = (bf16[512,256]{1,0:T(8,128)(2,1)S(1)}, bf16[512,256]{1,0:T(8,128)(2,1)}, u32[]{:S(2)}) copy-start(bf16[512,256]{1,0:T(8,128)(2,1)} %param.14) | copy-start | bytes 786436
  100.1 27.9 %copy-start.7 = (bf16[512,256]{1,0:T(8,128)(2,1)S(1)}, bf16[512,256]{1,0:T(8,128)(2,1)}, u32[]{:S(2)}) copy-start(bf16[512,256]{1,0:T(8,128)(2,1)} %param.13) | copy-start | bytes 786436
  117.3 10.7 %all-to-all-start.3 = ((bf16[4,128,256]{2,1,0:T(8,128)(2,1)}), bf16[4,128,256]{2,1,0:T(8,128)(2,1)S(1)}, u32[]{:S(2)}, u32[]{:S(2)}) async-start(bf16[4,128,256]{2,1,0:T(8,128)(2,1)} %broadcast_in_dim.13), calls=%async_computation.3 | async-start | bytes 524288 | tf_op jit(solution)/shard_map/all_to_all | solution.py:219
  129.3 30.4 %copy-start.2 = (f32[512,256]{1,0:T(8,128)}, f32[512,256]{1,0:T(8,128)S(1)}, u32[]{:S(2)}) copy-start(f32[512,256]{1,0:T(8,128)S(1)} %get-tuple-element.15) | copy-start | bytes 1572868
  130.2 28.3 %all-to-all-start.4 = ((bf16[128,2,128]{2,1,0:T(2,128)(2,1)}), bf16[128,2,128]{2,1,0:T(2,128)(2,1)S(1)}, u32[]{:S(2)}, u32[]{:S(2)}) async-start(bf16[128,2,128]{2,1,0:T(2,128)(2,1)} %reshape.141), calls=%async_computation.4 | async-start | bytes 131072 | tf_op jit(solution)/shard_map/all_to_all | solution.py:225

commit v10 on v9

--- a/solution.py
+++ b/solution.py
@@ -121,39 +121,42 @@
     y_count, x_count, rows, _ = grads.shape
     half_rows = y_count * rows
     feature_count = inputs[0].shape[1]
-    width = out.shape[1]
+    _, width, lanes = out.shape
+    parts = feature_count // lanes
     column = 1 - core if for_other else core
     columns = pl.ds(pl.multiple_of(column * width, width), width)
     sources = [lax.rem(along - behind + x_count, x_count) for behind in range(x_count)]
-    right = jnp.concatenate(
+    grads_rows = jnp.concatenate(
         [grads[y, source, :, columns] for source in sources for y in range(y_count)]
     )
     for blocks, place in ((inputs[:x_count], half), (inputs[x_count:], 1 - half)):
-        left = jnp.concatenate([block[:half_rows, :] for block in blocks])
-        target = pl.ds(pl.multiple_of(place * feature_count, feature_count), feature_count)
-        out[target, :] = lax.dot_general(
-            left, right, (((0,), (0,)), ((), ())), preferred_element_type=jnp.float32
+        inputs_rows = jnp.concatenate([block[:half_rows, :] for block in blocks])
+        product = lax.dot_general(
+            grads_rows,
+            inputs_rows,
+            (((0,), (0,)), ((), ())),
+            preferred_element_type=jnp.float32,
         ).astype(out.dtype)
+        for part in range(parts):
+            out[place * parts + part] = product[:, part * lanes : (part + 1) * lanes]
     if for_other:
         decode_rows = inputs[0].shape[0] - half_rows
-        for part in range(feature_count // width):
+        for part in range(parts):
             for block, source in zip(inputs[:x_count], sources):
-                start = 2 * feature_count + (part * x_count + source) * decode_rows
+                start = (part * x_count + source) * decode_rows
                 target = pl.ds(pl.multiple_of(start, decode_rows), decode_rows)
-                out[target, :] = block[half_rows:, part * width : (part + 1) * width]
-
-
-def products(for_other, inputs, grads, width):
+                out[2 * parts, target, :] = block[half_rows:, part * lanes : (part + 1) * lanes]
+
+
+def products(for_other, inputs, grads, width, lanes):
     feature_count = inputs[0].shape[1]
     position = jnp.stack([lax.axis_index(axis) for axis in ("zhi", "x", "core")]).astype(jnp.int32)
     y_count, x_count, rows, _ = grads.shape
-    extra = 0
-    if for_other:
-        extra = (inputs[0].shape[0] - y_count * rows) * x_count * feature_count // width
+    blocks = 2 * feature_count // lanes + for_other
     dtype = jnp.bfloat16 if for_other else jnp.float32
     return pl.pallas_call(
         functools.partial(product_kernel, for_other),
-        out_shape=jax.ShapeDtypeStruct((2 * feature_count + extra, width), dtype),
+        out_shape=jax.ShapeDtypeStruct((blocks, width, lanes), dtype),
         in_specs=[pl.BlockSpec(memory_space=pltpu.SMEM)]
         + [pl.BlockSpec(memory_space=pltpu.VMEM)] * (len(inputs) + 1),
         out_specs=pl.BlockSpec(memory_space=pltpu.VMEM),
@@ -199,25 +202,26 @@
     piece, kept = lax.optimization_barrier((piece, kept))
     y_count = lax.axis_size("y")
     grads_all = lax.all_to_all(jnp.broadcast_to(piece[None], (y_count, *piece.shape)), "y", 0, 0)
-    inputs = around(kept, "x", 1) + around(held(received), "x", -1)
-
-    sent = products(True, inputs, grads_all, block_width)
+    behind, ahead = shifted(kept, "x", 1), shifted(kept, "x", -1)
+    received = held(received)
+    ahead, received = lax.optimization_barrier((ahead, received))
+    inputs = [kept, behind, shifted(behind, "x", 1), ahead] + around(received, "x", -1)
+
+    sent = products(True, inputs, grads_all, block_width, quarter)
     sent_back = swap_over(sent, "core")
-    kept_sum = products(False, inputs, grads_all, block_width)
-    over_rep = (kept_sum + sent_back[: 2 * feature_count].astype(jnp.float32)).astype(jnp.bfloat16)
-    over_x = over_rep.reshape(2 * side_count, quarter, block_width)
+    kept_sum = products(False, inputs, grads_all, block_width, quarter)
+    over_rep = (kept_sum + sent_back[:-1].astype(jnp.float32)).astype(jnp.bfloat16)
     decode_of_core = [
-        jnp.concatenate(jnp.split(array[2 * feature_count :], feature_count // block_width), axis=1)
+        jnp.concatenate(jnp.split(array[-1], side_count), axis=1).reshape(x_count, -1, feature_count)
         for array in (sent, sent_back)
     ]
-    decode_of_core = [array.reshape(x_count, -1, feature_count) for array in decode_of_core]
     decode_rows = jnp.where(
         core == 0, jnp.stack(decode_of_core, 1), jnp.stack(decode_of_core[::-1], 1)
     ).reshape(-1, feature_count)
-    own_quarter = summed(lax.all_to_all(over_x, ("zhi", "side"), 0, 0, tiled=True))
-    spread = jnp.broadcast_to(own_quarter[None], (side_count, quarter, block_width))
+    own_quarter = summed(lax.all_to_all(over_rep, ("zhi", "side"), 0, 0, tiled=True))
+    spread = jnp.broadcast_to(own_quarter[None], (side_count, *own_quarter.shape))
     gradient = lax.all_to_all(spread, "side", 0, 0, tiled=True)
-    gradient = gradient.reshape(feature_count, block_width).astype(jnp.float32)
+    gradient = gradient.transpose(0, 2, 1).reshape(feature_count, block_width).astype(jnp.float32)
     master_new, first_new, second_new = adamw(kv_master, first_moment, second_moment, gradient)
     rounded_weights = master_new.astype(jnp.bfloat16)
     partial_fresh = jnp.dot(decode_rows, rounded_weights, preferred_element_type=jnp.float32)

time: 161 us -> 155 us (0.963)
  starting transfers between devices: 70.6 us -> 66.8 us
  waiting for transfers between devices: 69.5 us -> 66.9 us
    all_to_all x1, starting transfers between devices: 9.67 us -> 4.42 us  [local(): lax.all_to_all(over_rep, ('zhi', 'side'), 0, 0, tiled=True)]
    all_to_all x1, waiting for transfers between devices: 10.2 us -> 6.21 us  [local(): lax.all_to_all(jnp.broadcast_to(piece[None], (y_count, *piece.shape)), 'y...]
    ppermute x6, starting transfers between devices: 18.3 us -> 21 us  [shifted(): lax.ppermute(array, axis, [(i, (i + by) % count) for i in range(count)])]
where the time goes in v10:
time: 155 us; the launch traced here: 154 us
  waiting for transfers between devices  66.9 us (43%)
  starting transfers between devices  66.8 us (43%)
  local copies, waits for them, and re-layouts  7.31 us (5%)
  Pallas kernels  6.28 us (4%)
  other arithmetic  4.32 us (3%)
  between operations  1.62 us (1%)
    ppermute x6, waiting for transfers between devices, shifted(): lax.ppermute(array, axis, [(i, (i + by) % count) for i in range(count)])  24 us
    ppermute x6, starting transfers between devices, shifted(): lax.ppermute(array, axis, [(i, (i + by) % count) for i in range(count)])  21 us
    all_to_all x1, waiting for transfers between devices, local(): lax.all_to_all(over_rep, ('zhi', 'side'), 0, 0, tiled=True)  17.1 us
    all_to_all x1, waiting for transfers between devices, local(): fresh_terms = lax.all_to_all(partial_fresh, REP + TP, 0, 0, tiled=True)  13.9 us
    ppermute x2, starting transfers between devices, swap_over(): return lax.ppermute(array, axis, [(0, 1), (1, 0)])  13.5 us
    all_to_all x1, starting transfers between devices, local(): fresh_terms = lax.all_to_all(partial_fresh, REP + TP, 0, 0, tiled=True)  12.9 us
    all_to_all x1, starting transfers between devices, local(): lax.all_to_all(jnp.broadcast_to(piece[None], (y_count, *piece.shape)), 'y...  6.82 us
    pallas_call x2, Pallas kernels, products(): pl.pallas_call(functools.partial(product_kernel, for_other), out_shape=ja...  6.28 us
  transfers between devices with their start and end apart: 13, of which 7 were waited for; matrix products, arithmetic and copies ran while one was open for 3% of the time, Pallas kernels for 2%

profile of v10, /device:TPU:1, one launch (start us, length us, event | category | flops | bytes accessed | tf_op | source)
XLA Modules:
  0.0 154.1 jit_solution(2911233406131782107)
XLA Ops:
  2.4 4.8 %all-to-all-start = ((bf16[4,64,512]{2,1,0:T(8,128)(2,1)}), bf16[4,64,512]{2,1,0:T(8,128)(2,1)S(1)}, u32[]{:S(2)}, u32[]{:S(2)}) async-start(bf16[4,64,512]{2,1,0:T(8,128)(2,1)} %pad_maximum_fusion.1), calls=%async_computation | async-start | bytes 524288 | tf_op jit(solution)/shard_map/all_to_all | solution.py:201
  8.2 10.6 %collective-permute-start.3 = (bf16[512,512]{1,0:T(8,128)(2,1)}, bf16[512,512]{1,0:T(8,128)(2,1)}, u32[]{:S(2)}, u32[]{:S(2)}) collective-permute-start(bf16[512,512]{1,0:T(8,128)(2,1)} %get-tuple-element.12), channel_id=1, source_target_pairs={{0,8},{8,0},{1,9},{9,1},{2,10},{10,2},{3,11},{11,3},{4,12},{12,4},... | collective-permute-start | bytes 1572872 | tf_op jit(solution)/shard_map/ppermute | solution.py:88
  18.9 1.6 %broadcast_in_dim.12 = bf16[8,4,64,512]{3,2,1,0:T(8,128)(2,1)} broadcast(bf16[4,64,512]{2,1,0:T(8,128)(2,1)S(1)} %all-to-all-done), dimensions={1,2,3} | broadcast | bytes 2359296 | tf_op jit(solution)/shard_map/broadcast_in_dim | solution.py:204
  20.4 6.8 %all-to-all-start.1 = ((bf16[8,4,64,512]{3,2,1,0:T(8,128)(2,1)}), bf16[8,4,64,512]{3,2,1,0:T(8,128)(2,1)S(1)}, u32[]{:S(2)}, u32[]{:S(2)}) async-start(bf16[8,4,64,512]{3,2,1,0:T(8,128)(2,1)} %broadcast_in_dim.12), calls=%async_computation.1 | async-start | bytes 4194304 | tf_op jit(solution)/shard_map/all_to_all | solution.py:204
  27.2 4.6 %collective-permute-start.2 = (bf16[528,512]{1,0:T(8,128)(2,1)S(1)}, bf16[528,512]{1,0:T(8,128)(2,1)S(1)}, u32[]{:S(2)}, u32[]{:S(2)}) collective-permute-start(bf16[528,512]{1,0:T(8,128)(2,1)S(1)} %pad_maximum_fusion.refs_0_), channel_id=1, source_target_pairs={{0,96},{32,0},{64,32},{96,64},{1,97},{33,1},{65,33},{97,65},{2,98}... | collective-permute-start | bytes 1622024 | tf_op jit(solution)/shard_map/ppermute | solution.py:93
  31.8 1.9 %collective-permute-start = (bf16[528,512]{1,0:T(8,128)(2,1)S(1)}, bf16[528,512]{1,0:T(8,128)(2,1)}, u32[]{:S(2)}, u32[]{:S(2)}) collective-permute-start(bf16[528,512]{1,0:T(8,128)(2,1)S(1)} %pad_maximum_fusion.refs_0_), channel_id=1, source_target_pairs={{0,32},{32,64},{64,96},{96,0},{1,33},{33,65},{65,97},{97,1},{2,34}... | collective-permute-start | bytes 1622024 | tf_op jit(solution)/shard_map/ppermute | solution.py:93
  33.8 7.8 %collective-permute-done.2.refs_3_ = bf16[528,512]{1,0:T(8,128)(2,1)S(1)} collective-permute-done((bf16[528,512]{1,0:T(8,128)(2,1)S(1)}, bf16[528,512]{1,0:T(8,128)(2,1)S(1)}, u32[]{:S(2)}, u32[]{:S(2)}) %collective-permute-start.2) | collective-permute-done | bytes 540704 | tf_op jit(solution)/shard_map/ppermute | solution.py:93
  41.6 5.3 %collective-permute-start.5 = (bf16[512,512]{1,0:T(8,128)(2,1)}, bf16[512,512]{1,0:T(8,128)(2,1)}, u32[]{:S(2)}, u32[]{:S(2)}) collective-permute-start(bf16[512,512]{1,0:T(8,128)(2,1)} %held.1.refs_4_), channel_id=1, source_target_pairs={{0,96},{32,0},{64,32},{96,64},{1,97},{33,1},{65,33},{97,65},{2,98}... | collective-permute-start | bytes 1572872 | tf_op jit(solution)/shard_map/ppermute | solution.py:93
  46.9 1.9 %collective-permute-start.1 = (bf16[528,512]{1,0:T(8,128)(2,1)}, bf16[528,512]{1,0:T(8,128)(2,1)}, u32[]{:S(2)}, u32[]{:S(2)}) collective-permute-start(bf16[528,512]{1,0:T(8,128)(2,1)} %collective-permute-done.refs_1_), channel_id=1, source_target_pairs={{0,32},{32,64},{64,96},{96,0},{1,33},{33,65},{65,97},{97,1},{2,34}... | collective-permute-start | bytes 1622024 | tf_op jit(solution)/shard_map/ppermute | solution.py:93
  48.8 1.9 %collective-permute-start.4 = (bf16[512,512]{1,0:T(8,128)(2,1)}, bf16[512,512]{1,0:T(8,128)(2,1)}, u32[]{:S(2)}, u32[]{:S(2)}) collective-permute-start(bf16[512,512]{1,0:T(8,128)(2,1)} %held.1.refs_4_), channel_id=1, source_target_pairs={{0,32},{32,64},{64,96},{96,0},{1,33},{33,65},{65,97},{97,1},{2,34}... | collective-permute-start | bytes 1572872 | tf_op jit(solution)/shard_map/ppermute | solution.py:93
  50.8 4.9 %collective-permute-done.5.refs_7_ = bf16[512,512]{1,0:T(8,128)(2,1)} collective-permute-done((bf16[512,512]{1,0:T(8,128)(2,1)}, bf16[512,512]{1,0:T(8,128)(2,1)}, u32[]{:S(2)}, u32[]{:S(2)}) %collective-permute-start.5) | collective-permute-done | bytes 524320 | tf_op jit(solution)/shard_map/ppermute | solution.py:93
  55.7 5.3 %collective-permute-start.6 = (bf16[512,512]{1,0:T(8,128)(2,1)}, bf16[512,512]{1,0:T(8,128)(2,1)}, u32[]{:S(2)}, u32[]{:S(2)}) collective-permute-start(bf16[512,512]{1,0:T(8,128)(2,1)} %collective-permute-done.5.refs_7_), channel_id=1, source_target_pairs={{0,96},{32,0},{64,32},{96,64},{1,97},{33,1},{65,33},{97,65},{2,98}... | collective-permute-start | bytes 1572872 | tf_op jit(solution)/shard_map/ppermute | solution.py:93
  61.1 11.2 %collective-permute-done.4.refs_5_ = bf16[512,512]{1,0:T(8,128)(2,1)} collective-permute-done((bf16[512,512]{1,0:T(8,128)(2,1)}, bf16[512,512]{1,0:T(8,128)(2,1)}, u32[]{:S(2)}, u32[]{:S(2)}) %collective-permute-start.4) | collective-permute-done | bytes 524320 | tf_op jit(solution)/shard_map/ppermute | solution.py:93
  72.3 6.2 %all-to-all-done.1.refs_8_ = bf16[8,4,64,512]{3,2,1,0:T(8,128)(2,1)S(1)} async-done(((bf16[8,4,64,512]{3,2,1,0:T(8,128)(2,1)}), bf16[8,4,64,512]{3,2,1,0:T(8,128)(2,1)S(1)}, u32[]{:S(2)}, u32[]{:S(2)}) %all-to-all-start.1) | async-done | bytes 2097184 | tf_op jit(solution)/shard_map/all_to_all | solution.py:204
  78.5 3.1 %products_other.1 = bf16[9,256,128]{2,1,0:T(8,128)(2,1)S(1)} custom-call(s32[3]{0:T(128)S(1)} %pad_add_fusion.position, bf16[528,512]{1,0:T(8,128)(2,1)S(1)} %pad_maximum_fusion.refs_0_, bf16[528,512]{1,0:T(8,128)(2,1)} %collective-permute-done.refs_1_, bf16[528,512]{1,0:T(8,128)(2,1)} %collective-permute-done.1.refs_2_, ...), custom_call_target="tpu_custom_call" | custom-call | flops 1073741824 | bytes 7340032 | tf_op jit(solution)/shard_map/products_other/pallas_call | solution.py:157
  81.7 2.9 %collective-permute-start.7 = (bf16[9,256,128]{2,1,0:T(8,128)(2,1)S(1)}, bf16[9,256,128]{2,1,0:T(8,128)(2,1)S(1)}, u32[]{:S(2)}, u32[]{:S(2)}) collective-permute-start(bf16[9,256,128]{2,1,0:T(8,128)(2,1)S(1)} %products_other.1), channel_id=1, source_target_pairs={{0,16},{16,0},{1,17},{17,1},{2,18},{18,2},{3,19},{19,3},{4,20},{20... | collective-permute-start | bytes 1769480 | tf_op jit(solution)/shard_map/ppermute | solution.py:88
  84.6 3.1 %products_own.1 = f32[8,256,128]{2,1,0:T(8,128)S(1)} custom-call(s32[3]{0:T(128)S(1)} %pad_add_fusion.position, bf16[528,512]{1,0:T(8,128)(2,1)S(1)} %pad_maximum_fusion.refs_0_, bf16[528,512]{1,0:T(8,128)(2,1)} %collective-permute-done.refs_1_, bf16[528,512]{1,0:T(8,128)(2,1)} %collective-permute-done.1.refs_2_, ...), custom_call_target="tpu_custom_call" | custom-call | flops 1073741824 | bytes 7340032 | tf_op jit(solution)/shard_map/products_own/pallas_call | solution.py:157
  89.5 4.4 %all-to-all-start.2 = ((bf16[8,256,128]{2,1,0:T(8,128)(2,1)}), bf16[8,256,128]{2,1,0:T(8,128)(2,1)S(1)}, u32[]{:S(2)}, u32[]{:S(2)}) async-start(bf16[8,256,128]{2,1,0:T(8,128)(2,1)} %add_convert_fusion), calls=%async_computation.2 | async-start | bytes 1048576 | tf_op jit(solution)/shard_map/all_to_all | solution.py:221
  94.8 17.1 %all-to-all-done.2 = bf16[8,256,128]{2,1,0:T(8,128)(2,1)S(1)} async-done(((bf16[8,256,128]{2,1,0:T(8,128)(2,1)}), bf16[8,256,128]{2,1,0:T(8,128)(2,1)S(1)}, u32[]{:S(2)}, u32[]{:S(2)}) %all-to-all-start.2) | async-done | bytes 524320 | tf_op jit(solution)/shard_map/all_to_all | solution.py:221
  112.9 3.4 %all-to-all-start.3 = ((bf16[4,256,128]{1,2,0:T(8,128)(2,1)}), bf16[4,256,128]{1,2,0:T(8,128)(2,1)S(1)}, u32[]{:S(2)}, u32[]{:S(2)}) async-start(bf16[4,256,128]{1,2,0:T(8,128)(2,1)} %broadcast_in_dim.13), calls=%async_computation.3 | async-start | bytes 524288 | tf_op jit(solution)/shard_map/all_to_all | solution.py:223
  117.9 5.7 %all-to-all-done.3 = bf16[4,256,128]{1,2,0:T(8,128)(2,1)S(1)} async-done(((bf16[4,256,128]{1,2,0:T(8,128)(2,1)}), bf16[4,256,128]{1,2,0:T(8,128)(2,1)S(1)}, u32[]{:S(2)}, u32[]{:S(2)}) %all-to-all-start.3) | async-done | bytes 262176 | tf_op jit(solution)/shard_map/all_to_all | solution.py:223
  123.6 1.3 fusion.5
  125.7 12.9 %all-to-all-start.4 = ((bf16[128,2,128]{2,1,0:T(2,128)(2,1)}), bf16[128,2,128]{2,1,0:T(2,128)(2,1)S(1)}, u32[]{:S(2)}, u32[]{:S(2)}) async-start(bf16[128,2,128]{2,1,0:T(2,128)(2,1)} %reshape.161), calls=%async_computation.4 | async-start | bytes 131072 | tf_op jit(solution)/shard_map/all_to_all | solution.py:229
  138.9 13.9 %all-to-all-done.4 = bf16[128,2,128]{2,1,0:T(2,128)(2,1)S(1)} async-done(((bf16[128,2,128]{2,1,0:T(2,128)(2,1)}), bf16[128,2,128]{2,1,0:T(2,128)(2,1)S(1)}, u32[]{:S(2)}, u32[]{:S(2)}) %all-to-all-start.4) | async-done | bytes 65568 | tf_op jit(solution)/shard_map/all_to_all | solution.py:229
  (58 shorter events, 9.6 us)
Async XLA Ops:
  0.6 94.1 %copy-start = (bf16[1,8192]{1,0:T(2,128)(2,1)S(1)}, bf16[1,8192]{1,0:T(2,128)(2,1)}, u32[]{:S(2)}) copy-start(bf16[1,8192]{1,0:T(2,128)(2,1)} %param.16) | copy-start | bytes 49156
  0.6 6.6 %copy-start.3 = (bf16[1,1024,512]{2,1,0:T(8,128)(2,1)S(1)}, bf16[1,1024,512]{2,1,0:T(8,128)(2,1)}, u32[]{:S(2)}) copy-start(bf16[1,1024,512]{2,1,0:T(8,128)(2,1)} %param.10) | copy-start | bytes 3145732
  2.4 16.4 %all-to-all-start = ((bf16[4,64,512]{2,1,0:T(8,128)(2,1)}), bf16[4,64,512]{2,1,0:T(8,128)(2,1)S(1)}, u32[]{:S(2)}, u32[]{:S(2)}) async-start(bf16[4,64,512]{2,1,0:T(8,128)(2,1)} %pad_maximum_fusion.1), calls=%async_computation | async-start | bytes 524288 | tf_op jit(solution)/shard_map/all_to_all | solution.py:201
  7.3 11.5 %copy-start.10 = (bf16[16,512]{1,0:T(8,128)(2,1)S(1)}, bf16[16,512]{1,0:T(8,128)(2,1)}, u32[]{:S(2)}) copy-start(bf16[16,512]{1,0:T(8,128)(2,1)} %param.15) | copy-start | bytes 49156
  8.2 25.6 %collective-permute-start.3 = (bf16[512,512]{1,0:T(8,128)(2,1)}, bf16[512,512]{1,0:T(8,128)(2,1)}, u32[]{:S(2)}, u32[]{:S(2)}) collective-permute-start(bf16[512,512]{1,0:T(8,128)(2,1)} %get-tuple-element.12), channel_id=1, source_target_pairs={{0,8},{8,0},{1,9},{9,1},{2,10},{10,2},{3,11},{11,3},{4,12},{12,4},... | collective-permute-start | bytes 1572872 | tf_op jit(solution)/shard_map/ppermute | solution.py:88
  20.4 58.1 %all-to-all-start.1 = ((bf16[8,4,64,512]{3,2,1,0:T(8,128)(2,1)}), bf16[8,4,64,512]{3,2,1,0:T(8,128)(2,1)S(1)}, u32[]{:S(2)}, u32[]{:S(2)}) async-start(bf16[8,4,64,512]{3,2,1,0:T(8,128)(2,1)} %broadcast_in_dim.12), calls=%async_computation.1 | async-start | bytes 4194304 | tf_op jit(solution)/shard_map/all_to_all | solution.py:204
  27.2 14.3 %collective-permute-start.2 = (bf16[528,512]{1,0:T(8,128)(2,1)S(1)}, bf16[528,512]{1,0:T(8,128)(2,1)S(1)}, u32[]{:S(2)}, u32[]{:S(2)}) collective-permute-start(bf16[528,512]{1,0:T(8,128)(2,1)S(1)} %pad_maximum_fusion.refs_0_), channel_id=1, source_target_pairs={{0,96},{32,0},{64,32},{96,64},{1,97},{33,1},{65,33},{97,65},{2,98}... | collective-permute-start | bytes 1622024 | tf_op jit(solution)/shard_map/ppermute | solution.py:93
  31.8 15.1 %collective-permute-start = (bf16[528,512]{1,0:T(8,128)(2,1)S(1)}, bf16[528,512]{1,0:T(8,128)(2,1)}, u32[]{:S(2)}, u32[]{:S(2)}) collective-permute-start(bf16[528,512]{1,0:T(8,128)(2,1)S(1)} %pad_maximum_fusion.refs_0_), channel_id=1, source_target_pairs={{0,32},{32,64},{64,96},{96,0},{1,33},{33,65},{65,97},{97,1},{2,34}... | collective-permute-start | bytes 1622024 | tf_op jit(solution)/shard_map/ppermute | solution.py:93
  41.6 14.1 %collective-permute-start.5 = (bf16[512,512]{1,0:T(8,128)(2,1)}, bf16[512,512]{1,0:T(8,128)(2,1)}, u32[]{:S(2)}, u32[]{:S(2)}) collective-permute-start(bf16[512,512]{1,0:T(8,128)(2,1)} %held.1.refs_4_), channel_id=1, source_target_pairs={{0,96},{32,0},{64,32},{96,64},{1,97},{33,1},{65,33},{97,65},{2,98}... | collective-permute-start | bytes 1572872 | tf_op jit(solution)/shard_map/ppermute | solution.py:93
  46.9 25.4 %collective-permute-start.1 = (bf16[528,512]{1,0:T(8,128)(2,1)}, bf16[528,512]{1,0:T(8,128)(2,1)}, u32[]{:S(2)}, u32[]{:S(2)}) collective-permute-start(bf16[528,512]{1,0:T(8,128)(2,1)} %collective-permute-done.refs_1_), channel_id=1, source_target_pairs={{0,32},{32,64},{64,96},{96,0},{1,33},{33,65},{65,97},{97,1},{2,34}... | collective-permute-start | bytes 1622024 | tf_op jit(solution)/shard_map/ppermute | solution.py:93
  48.8 23.5 %collective-permute-start.4 = (bf16[512,512]{1,0:T(8,128)(2,1)}, bf16[512,512]{1,0:T(8,128)(2,1)}, u32[]{:S(2)}, u32[]{:S(2)}) collective-permute-start(bf16[512,512]{1,0:T(8,128)(2,1)} %held.1.refs_4_), channel_id=1, source_target_pairs={{0,32},{32,64},{64,96},{96,0},{1,33},{33,65},{65,97},{97,1},{2,34}... | collective-permute-start | bytes 1572872 | tf_op jit(solution)/shard_map/ppermute | solution.py:93
  55.7 16.7 %collective-permute-start.6 = (bf16[512,512]{1,0:T(8,128)(2,1)}, bf16[512,512]{1,0:T(8,128)(2,1)}, u32[]{:S(2)}, u32[]{:S(2)}) collective-permute-start(bf16[512,512]{1,0:T(8,128)(2,1)} %collective-permute-done.5.refs_7_), channel_id=1, source_target_pairs={{0,96},{32,0},{64,32},{96,64},{1,97},{33,1},{65,33},{97,65},{2,98}... | collective-permute-start | bytes 1572872 | tf_op jit(solution)/shard_map/ppermute | solution.py:93
  81.7 6.0 %copy-start.1 = (bf16[9,256,128]{2,1,0:T(8,128)(2,1)}, bf16[9,256,128]{2,1,0:T(8,128)(2,1)S(1)}, u32[]{:S(2)}) copy-start(bf16[9,256,128]{2,1,0:T(8,128)(2,1)S(1)} %products_other.1) | copy-start | bytes 1769476
  81.7 6.1 %collective-permute-start.7 = (bf16[9,256,128]{2,1,0:T(8,128)(2,1)S(1)}, bf16[9,256,128]{2,1,0:T(8,128)(2,1)S(1)}, u32[]{:S(2)}, u32[]{:S(2)}) collective-permute-start(bf16[9,256,128]{2,1,0:T(8,128)(2,1)S(1)} %products_other.1), channel_id=1, source_target_pairs={{0,16},{16,0},{1,17},{17,1},{2,18},{18,2},{3,19},{19,3},{4,20},{20... | collective-permute-start | bytes 1769480 | tf_op jit(solution)/shard_map/ppermute | solution.py:88
  87.7 6.2 %copy-start.8 = (bf16[1,128,1024]{2,1,0:T(8,128)(2,1)S(1)}, bf16[1,128,1024]{2,1,0:T(8,128)(2,1)}, u32[]{:S(2)}) copy-start(bf16[1,128,1024]{2,1,0:T(8,128)(2,1)} %param.17) | copy-start | bytes 786436
  87.8 0.8 copy-start.4
  89.5 5.1 %copy-start.9 = (bf16[1,128,1024]{2,1,0:T(8,128)(2,1)S(1)}, bf16[1,128,1024]{2,1,0:T(8,128)(2,1)}, u32[]{:S(2)}) copy-start(bf16[1,128,1024]{2,1,0:T(8,128)(2,1)} %param.18) | copy-start | bytes 786436
  89.5 22.4 %all-to-all-start.2 = ((bf16[8,256,128]{2,1,0:T(8,128)(2,1)}), bf16[8,256,128]{2,1,0:T(8,128)(2,1)S(1)}, u32[]{:S(2)}, u32[]{:S(2)}) async-start(bf16[8,256,128]{2,1,0:T(8,128)(2,1)} %add_convert_fusion), calls=%async_computation.2 | async-start | bytes 1048576 | tf_op jit(solution)/shard_map/all_to_all | solution.py:221
  94.7 28.9 %copy-start.5 = (f32[512,256]{1,0:T(8,128)S(1)}, f32[512,256]{1,0:T(8,128)}, u32[]{:S(2)}) copy-start(f32[512,256]{1,0:T(8,128)} %param.12) | copy-start | bytes 1572868
  94.7 28.9 %copy-start.6 = (bf16[512,256]{1,0:T(8,128)(2,1)S(1)}, bf16[512,256]{1,0:T(8,128)(2,1)}, u32[]{:S(2)}) copy-start(bf16[512,256]{1,0:T(8,128)(2,1)} %param.14) | copy-start | bytes 786436
  94.7 28.9 %copy-start.7 = (bf16[512,256]{1,0:T(8,128)(2,1)S(1)}, bf16[512,256]{1,0:T(8,128)(2,1)}, u32[]{:S(2)}) copy-start(bf16[512,256]{1,0:T(8,128)(2,1)} %param.13) | copy-start | bytes 786436
  112.9 10.7 %all-to-all-start.3 = ((bf16[4,256,128]{1,2,0:T(8,128)(2,1)}), bf16[4,256,128]{1,2,0:T(8,128)(2,1)S(1)}, u32[]{:S(2)}, u32[]{:S(2)}) async-start(bf16[4,256,128]{1,2,0:T(8,128)(2,1)} %broadcast_in_dim.13), calls=%async_computation.3 | async-start | bytes 524288 | tf_op jit(solution)/shard_map/all_to_all | solution.py:223
  124.9 29.3 %copy-start.2 = (f32[512,256]{1,0:T(8,128)}, f32[512,256]{1,0:T(8,128)S(1)}, u32[]{:S(2)}) copy-start(f32[512,256]{1,0:T(8,128)S(1)} %get-tuple-element.23) | copy-start | bytes 1572868
  125.7 27.1 %all-to-all-start.4 = ((bf16[128,2,128]{2,1,0:T(2,128)(2,1)}), bf16[128,2,128]{2,1,0:T(2,128)(2,1)S(1)}, u32[]{:S(2)}, u32[]{:S(2)}) async-start(bf16[128,2,128]{2,1,0:T(2,128)(2,1)} %reshape.161), calls=%async_computation.4 | async-start | bytes 131072 | tf_op jit(solution)/shard_map/all_to_all | solution.py:229

commit v11 on v10

--- a/solution.py
+++ b/solution.py
@@ -97,6 +97,86 @@
     behind, ahead = shifted(array, axis, 1), shifted(array, axis, -1)
     across = shifted(behind if way == 1 else ahead, axis, way)
     return [array, behind, across, ahead]
+
+
+VMEM = pl.BlockSpec(memory_space=pltpu.VMEM)
+SMALL_KERNEL = pltpu.CompilerParams(vmem_limit_bytes=16 * 2**20)
+
+
+def columns_kernel(grads, out):
+    width = out.shape[2]
+    for i in range(out.shape[0]):
+        out[i] = grads[:, i * width : (i + 1) * width]
+
+
+def columns_by_x(grads, x_count):
+    shape = (x_count, grads.shape[0], grads.shape[1] // x_count)
+    return pl.pallas_call(
+        columns_kernel,
+        out_shape=jax.ShapeDtypeStruct(shape, grads.dtype),
+        in_specs=[VMEM],
+        out_specs=VMEM,
+        compiler_params=SMALL_KERNEL,
+        name="columns",
+    )(grads)
+
+
+def copies_kernel(array, out, sems):
+    copies = [
+        pltpu.make_async_copy(array, out.at[i], sems.at[i]) for i in range(out.shape[0])
+    ]
+    for copy in copies:
+        copy.start()
+    for copy in copies:
+        copy.wait()
+
+
+def copies_of(array, count):
+    return pl.pallas_call(
+        copies_kernel,
+        out_shape=jax.ShapeDtypeStruct((count, *array.shape), array.dtype),
+        in_specs=[VMEM],
+        out_specs=pl.BlockSpec(memory_space=pl.ANY),
+        scratch_shapes=[pltpu.SemaphoreType.DMA((count,))],
+        compiler_params=SMALL_KERNEL,
+        name="copies",
+    )(array)
+
+
+def total_kernel(kept, received, out):
+    out[...] = (kept[...] + received[: out.shape[0]].astype(jnp.float32)).astype(out.dtype)
+
+
+def total_of(kept, received):
+    return pl.pallas_call(
+        total_kernel,
+        out_shape=jax.ShapeDtypeStruct(kept.shape, received.dtype),
+        in_specs=[VMEM, VMEM],
+        out_specs=VMEM,
+        compiler_params=SMALL_KERNEL,
+        name="total",
+    )(kept, received)
+
+
+def quarters_kernel(terms, out):
+    total = terms[0].astype(jnp.float32)
+    for i in range(1, terms.shape[0]):
+        total = total + terms[i].astype(jnp.float32)
+    total = total.T.astype(out.dtype)
+    for i in range(out.shape[0]):
+        out[i] = total
+
+
+def quarters_of(terms, count):
+    _, width, lanes = terms.shape
+    return pl.pallas_call(
+        quarters_kernel,
+        out_shape=jax.ShapeDtypeStruct((count, lanes, width), terms.dtype),
+        in_specs=[VMEM],
+        out_specs=VMEM,
+        compiler_params=SMALL_KERNEL,
+        name="quarters",
+    )(terms)
 
 
 def same_kernel(array, out):
@@ -170,10 +250,6 @@
     )(position, *inputs, grads)
 
 
-def summed(terms):
-    return jnp.sum(terms.astype(jnp.float32), axis=0).astype(jnp.bfloat16)
-
-
 def local(
     learn_inputs,
     learn_grads,
@@ -196,12 +272,11 @@
     received = swap_over(jnp.where(half == 0, row_halves[1], row_halves[0]), "zhi")
     kept = jnp.concatenate([jnp.where(half == 0, row_halves[0], row_halves[1]), decode_inputs])
 
-    width = 2 * block_width
-    columns = jnp.stack([learn_grads[0, :, i * width : (i + 1) * width] for i in range(x_count)])
+    columns = columns_by_x(learn_grads[0], x_count)
     piece = lax.all_to_all(columns, "x", 0, 0, tiled=True)
     piece, kept = lax.optimization_barrier((piece, kept))
     y_count = lax.axis_size("y")
-    grads_all = lax.all_to_all(jnp.broadcast_to(piece[None], (y_count, *piece.shape)), "y", 0, 0)
+    grads_all = lax.all_to_all(copies_of(piece, y_count), "y", 0, 0)
     behind, ahead = shifted(kept, "x", 1), shifted(kept, "x", -1)
     received = held(received)
     ahead, received = lax.optimization_barrier((ahead, received))
@@ -210,7 +285,7 @@
     sent = products(True, inputs, grads_all, block_width, quarter)
     sent_back = swap_over(sent, "core")
     kept_sum = products(False, inputs, grads_all, block_width, quarter)
-    over_rep = (kept_sum + sent_back[:-1].astype(jnp.float32)).astype(jnp.bfloat16)
+    over_rep = total_of(kept_sum, sent_back)
     decode_of_core = [
         jnp.concatenate(jnp.split(array[-1], side_count), axis=1).reshape(x_count, -1, feature_count)
         for array in (sent, sent_back)
@@ -218,10 +293,9 @@
     decode_rows = jnp.where(
         core == 0, jnp.stack(decode_of_core, 1), jnp.stack(decode_of_core[::-1], 1)
     ).reshape(-1, feature_count)
-    own_quarter = summed(lax.all_to_all(over_rep, ("zhi", "side"), 0, 0, tiled=True))
-    spread = jnp.broadcast_to(own_quarter[None], (side_count, *own_quarter.shape))
-    gradient = lax.all_to_all(spread, "side", 0, 0, tiled=True)
-    gradient = gradient.transpose(0, 2, 1).reshape(feature_count, block_width).astype(jnp.float32)
+    terms = lax.all_to_all(over_rep, ("zhi", "side"), 0, 0, tiled=True)
+    gradient = lax.all_to_all(quarters_of(terms, side_count), "side", 0, 0, tiled=True)
+    gradient = gradient.reshape(feature_count, block_width).astype(jnp.float32)
     master_new, first_new, second_new = adamw(kv_master, first_moment, second_moment, gradient)
     rounded_weights = master_new.astype(jnp.bfloat16)
     partial_fresh = jnp.dot(decode_rows, rounded_weights, preferred_element_type=jnp.float32)

time: 155 us -> 155 us (level)
  Pallas kernels: 6.28 us -> 9 us
  other arithmetic: 4.32 us -> 2.63 us
    pallas_call x0 -> x4, Pallas kernels: none -> 2.73 us  [the longest x1 0.93 us: total_of(): pl.pallas_call(total_kernel, out_shape=jax.ShapeDtypeStruct(kept.shape, r...]
    broadcast_in_dim x2 -> x0, local copies, waits for them, and re-layouts: 2.29 us -> none  [the longest x1 1.57 us: local(): jnp.broadcast_to(piece[None], (y_count, *piece.shape))]
    unnamed x25 -> x29, local copies, waits for them, and re-layouts: 0.98 us -> 3.26 us
  transfers between devices with their start and end apart: 13 -> 13, of which waited for: 7 -> 7; matrix products, arithmetic and copies ran while one was open for 3% -> 2% of each run, Pallas kernels for 2% -> 2%
where the time goes in v11:
time: 155 us; the launch traced here: 154 us
  waiting for transfers between devices  66.9 us (43%)
  starting transfers between devices  66.8 us (43%)
  Pallas kernels  9 us (6%)
  local copies, waits for them, and re-layouts  6.13 us (4%)
  other arithmetic  2.63 us (2%)
  between operations  1.62 us (1%)
    ppermute x6, waiting for transfers between devices, shifted(): lax.ppermute(array, axis, [(i, (i + by) % count) for i in range(count)])  24 us
    ppermute x6, starting transfers between devices, shifted(): lax.ppermute(array, axis, [(i, (i + by) % count) for i in range(count)])  21 us
    all_to_all x1, waiting for transfers between devices, local(): terms = lax.all_to_all(over_rep, ('zhi', 'side'), 0, 0, tiled=True)  17.1 us
    all_to_all x1, waiting for transfers between devices, local(): fresh_terms = lax.all_to_all(partial_fresh, REP + TP, 0, 0, tiled=True)  13.9 us
    ppermute x2, starting transfers between devices, swap_over(): return lax.ppermute(array, axis, [(0, 1), (1, 0)])  13.5 us
    all_to_all x1, starting transfers between devices, local(): fresh_terms = lax.all_to_all(partial_fresh, REP + TP, 0, 0, tiled=True)  12.9 us
    all_to_all x1, starting transfers between devices, local(): grads_all = lax.all_to_all(copies_of(piece, y_count), 'y', 0, 0)  6.82 us
    pallas_call x2, Pallas kernels, products(): pl.pallas_call(functools.partial(product_kernel, for_other), out_shape=ja...  6.27 us
  transfers between devices with their start and end apart: 13, of which 7 were waited for; matrix products, arithmetic and copies ran while one was open for 2% of the time, Pallas kernels for 2%

profile of v11, /device:TPU:1, one launch (start us, length us, event | category | flops | bytes accessed | tf_op | source)
XLA Modules:
  0.0 154.0 jit_solution(4753837928544634684)
XLA Ops:
  2.3 4.8 %all-to-all-start = ((bf16[4,64,512]{2,1,0:T(8,128)(2,1)}), bf16[4,64,512]{2,1,0:T(8,128)(2,1)S(1)}, u32[]{:S(2)}, u32[]{:S(2)}) async-start(bf16[4,64,512]{2,1,0:T(8,128)(2,1)} %columns.1), calls=%async_computation | async-start | bytes 524288 | tf_op jit(solution)/shard_map/all_to_all | solution.py:276
  8.0 10.6 %collective-permute-start.3 = (bf16[512,512]{1,0:T(8,128)(2,1)}, bf16[512,512]{1,0:T(8,128)(2,1)}, u32[]{:S(2)}, u32[]{:S(2)}) collective-permute-start(bf16[512,512]{1,0:T(8,128)(2,1)} %get-tuple-element.12), channel_id=1, source_target_pairs={{0,8},{8,0},{1,9},{9,1},{2,10},{10,2},{3,11},{11,3},{4,12},{12,4},... | collective-permute-start | bytes 1572872 | tf_op jit(solution)/shard_map/ppermute | solution.py:88
  19.0 1.3 copy-done.1
  20.3 6.8 %all-to-all-start.1 = ((bf16[8,4,64,512]{3,2,1,0:T(8,128)(2,1)}), bf16[8,4,64,512]{3,2,1,0:T(8,128)(2,1)S(1)}, u32[]{:S(2)}, u32[]{:S(2)}) async-start(bf16[8,4,64,512]{3,2,1,0:T(8,128)(2,1)} %copy-done.1), calls=%async_computation.1 | async-start | bytes 4194304 | tf_op jit(solution)/shard_map/all_to_all | solution.py:279
  27.1 4.6 %collective-permute-start.2 = (bf16[528,512]{1,0:T(8,128)(2,1)S(1)}, bf16[528,512]{1,0:T(8,128)(2,1)S(1)}, u32[]{:S(2)}, u32[]{:S(2)}) collective-permute-start(bf16[528,512]{1,0:T(8,128)(2,1)S(1)} %pad_maximum_fusion.refs_0_), channel_id=1, source_target_pairs={{0,96},{32,0},{64,32},{96,64},{1,97},{33,1},{65,33},{97,65},{2,98}... | collective-permute-start | bytes 1622024 | tf_op jit(solution)/shard_map/ppermute | solution.py:93
  31.7 1.9 %collective-permute-start = (bf16[528,512]{1,0:T(8,128)(2,1)S(1)}, bf16[528,512]{1,0:T(8,128)(2,1)}, u32[]{:S(2)}, u32[]{:S(2)}) collective-permute-start(bf16[528,512]{1,0:T(8,128)(2,1)S(1)} %pad_maximum_fusion.refs_0_), channel_id=1, source_target_pairs={{0,32},{32,64},{64,96},{96,0},{1,33},{33,65},{65,97},{97,1},{2,34}... | collective-permute-start | bytes 1622024 | tf_op jit(solution)/shard_map/ppermute | solution.py:93
  33.7 7.8 %collective-permute-done.2.refs_3_ = bf16[528,512]{1,0:T(8,128)(2,1)S(1)} collective-permute-done((bf16[528,512]{1,0:T(8,128)(2,1)S(1)}, bf16[528,512]{1,0:T(8,128)(2,1)S(1)}, u32[]{:S(2)}, u32[]{:S(2)}) %collective-permute-start.2) | collective-permute-done | bytes 540704 | tf_op jit(solution)/shard_map/ppermute | solution.py:93
  41.5 5.3 %collective-permute-start.5 = (bf16[512,512]{1,0:T(8,128)(2,1)}, bf16[512,512]{1,0:T(8,128)(2,1)}, u32[]{:S(2)}, u32[]{:S(2)}) collective-permute-start(bf16[512,512]{1,0:T(8,128)(2,1)} %held.1.refs_4_), channel_id=1, source_target_pairs={{0,96},{32,0},{64,32},{96,64},{1,97},{33,1},{65,33},{97,65},{2,98}... | collective-permute-start | bytes 1572872 | tf_op jit(solution)/shard_map/ppermute | solution.py:93
  46.8 1.9 %collective-permute-start.1 = (bf16[528,512]{1,0:T(8,128)(2,1)}, bf16[528,512]{1,0:T(8,128)(2,1)}, u32[]{:S(2)}, u32[]{:S(2)}) collective-permute-start(bf16[528,512]{1,0:T(8,128)(2,1)} %collective-permute-done.refs_1_), channel_id=1, source_target_pairs={{0,32},{32,64},{64,96},{96,0},{1,33},{33,65},{65,97},{97,1},{2,34}... | collective-permute-start | bytes 1622024 | tf_op jit(solution)/shard_map/ppermute | solution.py:93
  48.7 1.9 %collective-permute-start.4 = (bf16[512,512]{1,0:T(8,128)(2,1)}, bf16[512,512]{1,0:T(8,128)(2,1)}, u32[]{:S(2)}, u32[]{:S(2)}) collective-permute-start(bf16[512,512]{1,0:T(8,128)(2,1)} %held.1.refs_4_), channel_id=1, source_target_pairs={{0,32},{32,64},{64,96},{96,0},{1,33},{33,65},{65,97},{97,1},{2,34}... | collective-permute-start | bytes 1572872 | tf_op jit(solution)/shard_map/ppermute | solution.py:93
  50.6 4.9 %collective-permute-done.5.refs_7_ = bf16[512,512]{1,0:T(8,128)(2,1)} collective-permute-done((bf16[512,512]{1,0:T(8,128)(2,1)}, bf16[512,512]{1,0:T(8,128)(2,1)}, u32[]{:S(2)}, u32[]{:S(2)}) %collective-permute-start.5) | collective-permute-done | bytes 524320 | tf_op jit(solution)/shard_map/ppermute | solution.py:93
  55.6 5.3 %collective-permute-start.6 = (bf16[512,512]{1,0:T(8,128)(2,1)}, bf16[512,512]{1,0:T(8,128)(2,1)}, u32[]{:S(2)}, u32[]{:S(2)}) collective-permute-start(bf16[512,512]{1,0:T(8,128)(2,1)} %collective-permute-done.5.refs_7_), channel_id=1, source_target_pairs={{0,96},{32,0},{64,32},{96,64},{1,97},{33,1},{65,33},{97,65},{2,98}... | collective-permute-start | bytes 1572872 | tf_op jit(solution)/shard_map/ppermute | solution.py:93
  61.0 11.2 %collective-permute-done.4.refs_5_ = bf16[512,512]{1,0:T(8,128)(2,1)} collective-permute-done((bf16[512,512]{1,0:T(8,128)(2,1)}, bf16[512,512]{1,0:T(8,128)(2,1)}, u32[]{:S(2)}, u32[]{:S(2)}) %collective-permute-start.4) | collective-permute-done | bytes 524320 | tf_op jit(solution)/shard_map/ppermute | solution.py:93
  72.2 6.2 %all-to-all-done.1.refs_8_ = bf16[8,4,64,512]{3,2,1,0:T(8,128)(2,1)S(1)} async-done(((bf16[8,4,64,512]{3,2,1,0:T(8,128)(2,1)}), bf16[8,4,64,512]{3,2,1,0:T(8,128)(2,1)S(1)}, u32[]{:S(2)}, u32[]{:S(2)}) %all-to-all-start.1) | async-done | bytes 2097184 | tf_op jit(solution)/shard_map/all_to_all | solution.py:279
  78.4 3.1 %products_other.1 = bf16[9,256,128]{2,1,0:T(8,128)(2,1)S(1)} custom-call(s32[3]{0:T(128)S(1)} %pad_add_fusion.position, bf16[528,512]{1,0:T(8,128)(2,1)S(1)} %pad_maximum_fusion.refs_0_, bf16[528,512]{1,0:T(8,128)(2,1)} %collective-permute-done.refs_1_, bf16[528,512]{1,0:T(8,128)(2,1)} %collective-permute-done.1.refs_2_, ...), custom_call_target="tpu_custom_call" | custom-call | flops 1073741824 | bytes 7340032 | tf_op jit(solution)/shard_map/products_other/pallas_call | solution.py:237
  81.6 2.9 %collective-permute-start.7 = (bf16[9,256,128]{2,1,0:T(8,128)(2,1)S(1)}, bf16[9,256,128]{2,1,0:T(8,128)(2,1)S(1)}, u32[]{:S(2)}, u32[]{:S(2)}) collective-permute-start(bf16[9,256,128]{2,1,0:T(8,128)(2,1)S(1)} %products_other.1), channel_id=1, source_target_pairs={{0,16},{16,0},{1,17},{17,1},{2,18},{18,2},{3,19},{19,3},{4,20},{20... | collective-permute-start | bytes 1769480 | tf_op jit(solution)/shard_map/ppermute | solution.py:88
  84.5 3.1 %products_own.1.kept = f32[8,256,128]{2,1,0:T(8,128)S(1)} custom-call(s32[3]{0:T(128)S(1)} %pad_add_fusion.position, bf16[528,512]{1,0:T(8,128)(2,1)S(1)} %pad_maximum_fusion.refs_0_, bf16[528,512]{1,0:T(8,128)(2,1)} %collective-permute-done.refs_1_, bf16[528,512]{1,0:T(8,128)(2,1)} %collective-permute-done.1.refs_2_, ...), custom_call_target="tpu_custom_call" | custom-call | flops 1073741824 | bytes 7340032 | tf_op jit(solution)/shard_map/products_own/pallas_call | solution.py:237
  89.4 4.4 %all-to-all-start.2 = ((bf16[8,256,128]{2,1,0:T(8,128)(2,1)}), bf16[8,256,128]{2,1,0:T(8,128)(2,1)S(1)}, u32[]{:S(2)}, u32[]{:S(2)}) async-start(bf16[8,256,128]{2,1,0:T(8,128)(2,1)} %total.1), calls=%async_computation.2 | async-start | bytes 1048576 | tf_op jit(solution)/shard_map/all_to_all | solution.py:296
  94.8 17.1 %all-to-all-done.2.terms = bf16[8,256,128]{2,1,0:T(8,128)(2,1)S(1)} async-done(((bf16[8,256,128]{2,1,0:T(8,128)(2,1)}), bf16[8,256,128]{2,1,0:T(8,128)(2,1)S(1)}, u32[]{:S(2)}, u32[]{:S(2)}) %all-to-all-start.2) | async-done | bytes 524320 | tf_op jit(solution)/shard_map/all_to_all | solution.py:296
  112.7 3.4 %all-to-all-start.3 = ((bf16[4,128,256]{2,1,0:T(8,128)(2,1)}), bf16[4,128,256]{2,1,0:T(8,128)(2,1)S(1)}, u32[]{:S(2)}, u32[]{:S(2)}) async-start(bf16[4,128,256]{2,1,0:T(8,128)(2,1)} %quarters.1), calls=%async_computation.3 | async-start | bytes 524288 | tf_op jit(solution)/shard_map/all_to_all | solution.py:297
  117.7 5.7 %all-to-all-done.3 = bf16[4,128,256]{2,1,0:T(8,128)(2,1)S(1)} async-done(((bf16[4,128,256]{2,1,0:T(8,128)(2,1)}), bf16[4,128,256]{2,1,0:T(8,128)(2,1)S(1)}, u32[]{:S(2)}, u32[]{:S(2)}) %all-to-all-start.3) | async-done | bytes 262176 | tf_op jit(solution)/shard_map/all_to_all | solution.py:297
  123.4 1.3 fusion.5
  125.6 12.9 %all-to-all-start.4 = ((bf16[128,2,128]{2,1,0:T(2,128)(2,1)}), bf16[128,2,128]{2,1,0:T(2,128)(2,1)S(1)}, u32[]{:S(2)}, u32[]{:S(2)}) async-start(bf16[128,2,128]{2,1,0:T(2,128)(2,1)} %reshape.159), calls=%async_computation.4 | async-start | bytes 131072 | tf_op jit(solution)/shard_map/all_to_all | solution.py:303
  138.8 13.9 %all-to-all-done.4 = bf16[128,2,128]{2,1,0:T(2,128)(2,1)S(1)} async-done(((bf16[128,2,128]{2,1,0:T(2,128)(2,1)}), bf16[128,2,128]{2,1,0:T(2,128)(2,1)S(1)}, u32[]{:S(2)}, u32[]{:S(2)}) %all-to-all-start.4) | async-done | bytes 65568 | tf_op jit(solution)/shard_map/all_to_all | solution.py:303
  (59 shorter events, 9.7 us)
Async XLA Ops:
  0.6 94.0 %copy-start = (bf16[1,8192]{1,0:T(2,128)(2,1)S(1)}, bf16[1,8192]{1,0:T(2,128)(2,1)}, u32[]{:S(2)}) copy-start(bf16[1,8192]{1,0:T(2,128)(2,1)} %param.16) | copy-start | bytes 49156
  1.6 5.6 %copy-start.6 = (bf16[1,1024,512]{2,1,0:T(8,128)(2,1)S(1)}, bf16[1,1024,512]{2,1,0:T(8,128)(2,1)}, u32[]{:S(2)}) copy-start(bf16[1,1024,512]{2,1,0:T(8,128)(2,1)} %param.10) | copy-start | bytes 3145732
  2.3 16.4 %all-to-all-start = ((bf16[4,64,512]{2,1,0:T(8,128)(2,1)}), bf16[4,64,512]{2,1,0:T(8,128)(2,1)S(1)}, u32[]{:S(2)}, u32[]{:S(2)}) async-start(bf16[4,64,512]{2,1,0:T(8,128)(2,1)} %columns.1), calls=%async_computation | async-start | bytes 524288 | tf_op jit(solution)/shard_map/all_to_all | solution.py:276
  7.2 11.5 %copy-start.12 = (bf16[16,512]{1,0:T(8,128)(2,1)S(1)}, bf16[16,512]{1,0:T(8,128)(2,1)}, u32[]{:S(2)}) copy-start(bf16[16,512]{1,0:T(8,128)(2,1)} %param.15) | copy-start | bytes 49156
  8.0 25.6 %collective-permute-start.3 = (bf16[512,512]{1,0:T(8,128)(2,1)}, bf16[512,512]{1,0:T(8,128)(2,1)}, u32[]{:S(2)}, u32[]{:S(2)}) collective-permute-start(bf16[512,512]{1,0:T(8,128)(2,1)} %get-tuple-element.12), channel_id=1, source_target_pairs={{0,8},{8,0},{1,9},{9,1},{2,10},{10,2},{3,11},{11,3},{4,12},{12,4},... | collective-permute-start | bytes 1572872 | tf_op jit(solution)/shard_map/ppermute | solution.py:88
  19.0 1.3 copy-start.1
  20.3 58.1 %all-to-all-start.1 = ((bf16[8,4,64,512]{3,2,1,0:T(8,128)(2,1)}), bf16[8,4,64,512]{3,2,1,0:T(8,128)(2,1)S(1)}, u32[]{:S(2)}, u32[]{:S(2)}) async-start(bf16[8,4,64,512]{3,2,1,0:T(8,128)(2,1)} %copy-done.1), calls=%async_computation.1 | async-start | bytes 4194304 | tf_op jit(solution)/shard_map/all_to_all | solution.py:279
  27.1 14.3 %collective-permute-start.2 = (bf16[528,512]{1,0:T(8,128)(2,1)S(1)}, bf16[528,512]{1,0:T(8,128)(2,1)S(1)}, u32[]{:S(2)}, u32[]{:S(2)}) collective-permute-start(bf16[528,512]{1,0:T(8,128)(2,1)S(1)} %pad_maximum_fusion.refs_0_), channel_id=1, source_target_pairs={{0,96},{32,0},{64,32},{96,64},{1,97},{33,1},{65,33},{97,65},{2,98}... | collective-permute-start | bytes 1622024 | tf_op jit(solution)/shard_map/ppermute | solution.py:93
  31.7 15.1 %collective-permute-start = (bf16[528,512]{1,0:T(8,128)(2,1)S(1)}, bf16[528,512]{1,0:T(8,128)(2,1)}, u32[]{:S(2)}, u32[]{:S(2)}) collective-permute-start(bf16[528,512]{1,0:T(8,128)(2,1)S(1)} %pad_maximum_fusion.refs_0_), channel_id=1, source_target_pairs={{0,32},{32,64},{64,96},{96,0},{1,33},{33,65},{65,97},{97,1},{2,34}... | collective-permute-start | bytes 1622024 | tf_op jit(solution)/shard_map/ppermute | solution.py:93
  41.5 14.1 %collective-permute-start.5 = (bf16[512,512]{1,0:T(8,128)(2,1)}, bf16[512,512]{1,0:T(8,128)(2,1)}, u32[]{:S(2)}, u32[]{:S(2)}) collective-permute-start(bf16[512,512]{1,0:T(8,128)(2,1)} %held.1.refs_4_), channel_id=1, source_target_pairs={{0,96},{32,0},{64,32},{96,64},{1,97},{33,1},{65,33},{97,65},{2,98}... | collective-permute-start | bytes 1572872 | tf_op jit(solution)/shard_map/ppermute | solution.py:93
  46.8 25.4 %collective-permute-start.1 = (bf16[528,512]{1,0:T(8,128)(2,1)}, bf16[528,512]{1,0:T(8,128)(2,1)}, u32[]{:S(2)}, u32[]{:S(2)}) collective-permute-start(bf16[528,512]{1,0:T(8,128)(2,1)} %collective-permute-done.refs_1_), channel_id=1, source_target_pairs={{0,32},{32,64},{64,96},{96,0},{1,33},{33,65},{65,97},{97,1},{2,34}... | collective-permute-start | bytes 1622024 | tf_op jit(solution)/shard_map/ppermute | solution.py:93
  48.7 23.5 %collective-permute-start.4 = (bf16[512,512]{1,0:T(8,128)(2,1)}, bf16[512,512]{1,0:T(8,128)(2,1)}, u32[]{:S(2)}, u32[]{:S(2)}) collective-permute-start(bf16[512,512]{1,0:T(8,128)(2,1)} %held.1.refs_4_), channel_id=1, source_target_pairs={{0,32},{32,64},{64,96},{96,0},{1,33},{33,65},{65,97},{97,1},{2,34}... | collective-permute-start | bytes 1572872 | tf_op jit(solution)/shard_map/ppermute | solution.py:93
  55.6 16.7 %collective-permute-start.6 = (bf16[512,512]{1,0:T(8,128)(2,1)}, bf16[512,512]{1,0:T(8,128)(2,1)}, u32[]{:S(2)}, u32[]{:S(2)}) collective-permute-start(bf16[512,512]{1,0:T(8,128)(2,1)} %collective-permute-done.5.refs_7_), channel_id=1, source_target_pairs={{0,96},{32,0},{64,32},{96,64},{1,97},{33,1},{65,33},{97,65},{2,98}... | collective-permute-start | bytes 1572872 | tf_op jit(solution)/shard_map/ppermute | solution.py:93
  81.6 6.0 %copy-start.3 = (bf16[9,256,128]{2,1,0:T(8,128)(2,1)}, bf16[9,256,128]{2,1,0:T(8,128)(2,1)S(1)}, u32[]{:S(2)}) copy-start(bf16[9,256,128]{2,1,0:T(8,128)(2,1)S(1)} %products_other.1) | copy-start | bytes 1769476
  81.6 6.1 %collective-permute-start.7 = (bf16[9,256,128]{2,1,0:T(8,128)(2,1)S(1)}, bf16[9,256,128]{2,1,0:T(8,128)(2,1)S(1)}, u32[]{:S(2)}, u32[]{:S(2)}) collective-permute-start(bf16[9,256,128]{2,1,0:T(8,128)(2,1)S(1)} %products_other.1), channel_id=1, source_target_pairs={{0,16},{16,0},{1,17},{17,1},{2,18},{18,2},{3,19},{19,3},{4,20},{20... | collective-permute-start | bytes 1769480 | tf_op jit(solution)/shard_map/ppermute | solution.py:88
  87.6 6.2 %copy-start.10 = (bf16[1,128,1024]{2,1,0:T(8,128)(2,1)S(1)}, bf16[1,128,1024]{2,1,0:T(8,128)(2,1)}, u32[]{:S(2)}) copy-start(bf16[1,128,1024]{2,1,0:T(8,128)(2,1)} %param.17) | copy-start | bytes 786436
  89.4 5.2 %copy-start.11 = (bf16[1,128,1024]{2,1,0:T(8,128)(2,1)S(1)}, bf16[1,128,1024]{2,1,0:T(8,128)(2,1)}, u32[]{:S(2)}) copy-start(bf16[1,128,1024]{2,1,0:T(8,128)(2,1)} %param.18) | copy-start | bytes 786436
  89.4 22.5 %all-to-all-start.2 = ((bf16[8,256,128]{2,1,0:T(8,128)(2,1)}), bf16[8,256,128]{2,1,0:T(8,128)(2,1)S(1)}, u32[]{:S(2)}, u32[]{:S(2)}) async-start(bf16[8,256,128]{2,1,0:T(8,128)(2,1)} %total.1), calls=%async_computation.2 | async-start | bytes 1048576 | tf_op jit(solution)/shard_map/all_to_all | solution.py:296
  94.6 28.8 %copy-start.7 = (f32[512,256]{1,0:T(8,128)S(1)}, f32[512,256]{1,0:T(8,128)}, u32[]{:S(2)}) copy-start(f32[512,256]{1,0:T(8,128)} %param.12) | copy-start | bytes 1572868
  94.6 28.8 %copy-start.8 = (bf16[512,256]{1,0:T(8,128)(2,1)S(1)}, bf16[512,256]{1,0:T(8,128)(2,1)}, u32[]{:S(2)}) copy-start(bf16[512,256]{1,0:T(8,128)(2,1)} %param.14) | copy-start | bytes 786436
  94.6 28.8 %copy-start.9 = (bf16[512,256]{1,0:T(8,128)(2,1)S(1)}, bf16[512,256]{1,0:T(8,128)(2,1)}, u32[]{:S(2)}) copy-start(bf16[512,256]{1,0:T(8,128)(2,1)} %param.13) | copy-start | bytes 786436
  112.7 10.7 %all-to-all-start.3 = ((bf16[4,128,256]{2,1,0:T(8,128)(2,1)}), bf16[4,128,256]{2,1,0:T(8,128)(2,1)S(1)}, u32[]{:S(2)}, u32[]{:S(2)}) async-start(bf16[4,128,256]{2,1,0:T(8,128)(2,1)} %quarters.1), calls=%async_computation.3 | async-start | bytes 524288 | tf_op jit(solution)/shard_map/all_to_all | solution.py:297
  124.8 29.2 %copy-start.5 = (f32[512,256]{1,0:T(8,128)}, f32[512,256]{1,0:T(8,128)S(1)}, u32[]{:S(2)}) copy-start(f32[512,256]{1,0:T(8,128)S(1)} %get-tuple-element.23) | copy-start | bytes 1572868
  125.6 27.1 %all-to-all-start.4 = ((bf16[128,2,128]{2,1,0:T(2,128)(2,1)}), bf16[128,2,128]{2,1,0:T(2,128)(2,1)S(1)}, u32[]{:S(2)}, u32[]{:S(2)}) async-start(bf16[128,2,128]{2,1,0:T(2,128)(2,1)} %reshape.159), calls=%async_computation.4 | async-start | bytes 131072 | tf_op jit(solution)/shard_map/all_to_all | solution.py:303
  (2 other events, 1.8 us)

commit v12 on v11

--- a/solution.py
+++ b/solution.py
@@ -100,13 +100,21 @@
 
 
 VMEM = pl.BlockSpec(memory_space=pltpu.VMEM)
+HBM = pl.BlockSpec(memory_space=pltpu.HBM)
 SMALL_KERNEL = pltpu.CompilerParams(vmem_limit_bytes=16 * 2**20)
-
-
-def columns_kernel(grads, out):
+HBM_KERNEL = pltpu.CompilerParams(vmem_limit_bytes=60 * 2**20)
+
+
+def columns_kernel(grads, out, sems):
     width = out.shape[2]
-    for i in range(out.shape[0]):
-        out[i] = grads[:, i * width : (i + 1) * width]
+    copies = [
+        pltpu.make_async_copy(grads.at[:, pl.ds(i * width, width)], out.at[i], sems.at[i])
+        for i in range(out.shape[0])
+    ]
+    for copy in copies:
+        copy.start()
+    for copy in copies:
+        copy.wait()
 
 
 def columns_by_x(grads, x_count):
@@ -114,9 +122,10 @@
     return pl.pallas_call(
         columns_kernel,
         out_shape=jax.ShapeDtypeStruct(shape, grads.dtype),
-        in_specs=[VMEM],
-        out_specs=VMEM,
-        compiler_params=SMALL_KERNEL,
+        in_specs=[HBM],
+        out_specs=HBM,
+        scratch_shapes=[pltpu.SemaphoreType.DMA((x_count,))],
+        compiler_params=HBM_KERNEL,
         name="columns",
     )(grads)
 
@@ -136,15 +145,18 @@
         copies_kernel,
         out_shape=jax.ShapeDtypeStruct((count, *array.shape), array.dtype),
         in_specs=[VMEM],
-        out_specs=pl.BlockSpec(memory_space=pl.ANY),
+        out_specs=HBM,
         scratch_shapes=[pltpu.SemaphoreType.DMA((count,))],
-        compiler_params=SMALL_KERNEL,
+        compiler_params=HBM_KERNEL,
         name="copies",
     )(array)
 
 
-def total_kernel(kept, received, out):
-    out[...] = (kept[...] + received[: out.shape[0]].astype(jnp.float32)).astype(out.dtype)
+def total_kernel(kept, received, out, total, sem):
+    total[...] = (kept[...] + received[: total.shape[0]].astype(jnp.float32)).astype(total.dtype)
+    copy = pltpu.make_async_copy(total, out, sem)
+    copy.start()
+    copy.wait()
 
 
 def total_of(kept, received):
@@ -152,7 +164,8 @@
         total_kernel,
         out_shape=jax.ShapeDtypeStruct(kept.shape, received.dtype),
         in_specs=[VMEM, VMEM],
-        out_specs=VMEM,
+        out_specs=HBM,
+        scratch_shapes=[pltpu.VMEM(kept.shape, received.dtype), pltpu.SemaphoreType.DMA],
         compiler_params=SMALL_KERNEL,
         name="total",
     )(kept, received)
@@ -190,7 +203,7 @@
         in_specs=[pl.BlockSpec(memory_space=pl.ANY)],
         out_specs=pl.BlockSpec(memory_space=pl.ANY),
         input_output_aliases={0: 0},
-        cost_estimate=pl.CostEstimate(flops=24 * 10**9, bytes_accessed=0, transcendentals=0),
+        cost_estimate=pl.CostEstimate(flops=26 * 10**9, bytes_accessed=0, transcendentals=0),
         name="held",
     )(array)
 

time: 155 us -> 165 us (1.065)
  Pallas kernels: 9 us -> 19.4 us
  waiting for transfers between devices: 66.9 us -> 75.2 us
  starting transfers between devices: 66.8 us -> 59.1 us
    pallas_call x1, Pallas kernels: 0.72 us -> 9.08 us  [columns_by_x(): pl.pallas_call(columns_kernel, out_shape=jax.ShapeDtypeStruct(shape, grad...]
    all_to_all x1, waiting for transfers between devices: 0.01 us -> 5.49 us  [local(): piece = lax.all_to_all(columns, 'x', 0, 0, tiled=True)]
    all_to_all x1, starting transfers between devices: 12.9 us -> 7.75 us  [local(): fresh_terms = lax.all_to_all(partial_fresh, REP + TP, 0, 0, tiled=True)]
    all_to_all x1, waiting for transfers between devices: 6.21 us -> 9.77 us  [local(): grads_all = lax.all_to_all(copies_of(piece, y_count), 'y', 0, 0)]
    ppermute x6, starting transfers between devices: 21 us -> 18.5 us  [shifted(): lax.ppermute(array, axis, [(i, (i + by) % count) for i in range(count)])]
    pallas_call x1, Pallas kernels: 0.23 us -> 2.34 us  [copies_of(): pl.pallas_call(copies_kernel, out_shape=jax.ShapeDtypeStruct((count, *arr...]
  transfers between devices with their start and end apart: 13 -> 13, of which waited for: 7 -> 8; matrix products, arithmetic and copies ran while one was open for 2% -> 1% of each run, Pallas kernels for 2% -> 9%
where the time goes in v12:
time: 165 us
  waiting for transfers between devices  75.2 us (46%)
  starting transfers between devices  59.1 us (36%)
  Pallas kernels  19.4 us (12%)
  local copies, waits for them, and re-layouts  4.57 us (3%)
  other arithmetic  3.83 us (2%)
    ppermute x6, waiting for transfers between devices, shifted(): lax.ppermute(array, axis, [(i, (i + by) % count) for i in range(count)])  23.2 us
    ppermute x6, starting transfers between devices, shifted(): lax.ppermute(array, axis, [(i, (i + by) % count) for i in range(count)])  18.5 us
    all_to_all x1, waiting for transfers between devices, local(): terms = lax.all_to_all(over_rep, ('zhi', 'side'), 0, 0, tiled=True)  17.1 us
    all_to_all x1, waiting for transfers between devices, local(): fresh_terms = lax.all_to_all(partial_fresh, REP + TP, 0, 0, tiled=True)  13.9 us
    ppermute x2, starting transfers between devices, swap_over(): return lax.ppermute(array, axis, [(0, 1), (1, 0)])  13.9 us
    all_to_all x1, waiting for transfers between devices, local(): grads_all = lax.all_to_all(copies_of(piece, y_count), 'y', 0, 0)  9.77 us
    pallas_call x1, Pallas kernels, columns_by_x(): pl.pallas_call(columns_kernel, out_shape=jax.ShapeDtypeStruct(shape, grad...  9.08 us
    all_to_all x1, starting transfers between devices, local(): fresh_terms = lax.all_to_all(partial_fresh, REP + TP, 0, 0, tiled=True)  7.75 us
  transfers between devices with their start and end apart: 13, of which 8 were waited for; matrix products, arithmetic and copies ran while one was open for 1% of the time, Pallas kernels for 9%

profile of v12, /device:TPU:1, one launch (start us, length us, event | category | flops | bytes accessed | tf_op | source)
XLA Modules:
  0.0 164.6 jit_solution(11482860571305308139)
XLA Ops:
  0.7 2.1 %select_bitcast_fusion = (bf16[512,512]{1,0:T(8,128)(2,1)}, bf16[512,512]{1,0:T(8,128)(2,1)S(1)}) fusion(pred[]{:T(512)S(6)} %eq.7, bf16[1,1024,512]{2,1,0:T(8,128)(2,1)} %param.10), kind=kLoop, calls=%fused_computation.12 | loop fusion | flops 524288 | bytes 2097153 | tf_op jit(solution)/shard_map/jit(_where)/select_n | solution.py:285
  2.7 11.5 %collective-permute-start.3 = (bf16[512,512]{1,0:T(8,128)(2,1)}, bf16[512,512]{1,0:T(8,128)(2,1)}, u32[]{:S(2)}, u32[]{:S(2)}) collective-permute-start(bf16[512,512]{1,0:T(8,128)(2,1)} %get-tuple-element.12), channel_id=1, source_target_pairs={{0,8},{8,0},{1,9},{9,1},{2,10},{10,2},{3,11},{11,3},{4,12},{12,4},... | collective-permute-start | bytes 1572872 | tf_op jit(solution)/shard_map/ppermute | solution.py:88
  14.2 9.1 %columns.1 = bf16[4,64,512]{2,1,0:T(8,128)(2,1)} custom-call(bf16[64,2048]{1,0:T(8,128)(2,1)} %bitcast.65), custom_call_target="tpu_custom_call" | custom-call | tf_op jit(solution)/shard_map/columns/pallas_call | solution.py:122
  23.3 4.0 %all-to-all-start = ((bf16[4,64,512]{2,1,0:T(8,128)(2,1)}), bf16[4,64,512]{2,1,0:T(8,128)(2,1)S(1)}, u32[]{:S(2)}, u32[]{:S(2)}) async-start(bf16[4,64,512]{2,1,0:T(8,128)(2,1)} %columns.1), calls=%async_computation | async-start | bytes 524288 | tf_op jit(solution)/shard_map/all_to_all | solution.py:289
  27.4 5.5 %all-to-all-done.array = bf16[4,64,512]{2,1,0:T(8,128)(2,1)S(1)} async-done(((bf16[4,64,512]{2,1,0:T(8,128)(2,1)}), bf16[4,64,512]{2,1,0:T(8,128)(2,1)S(1)}, u32[]{:S(2)}, u32[]{:S(2)}) %all-to-all-start) | async-done | bytes 262176 | tf_op jit(solution)/shard_map/all_to_all | solution.py:289
  33.5 2.3 %copies.1 = bf16[8,4,64,512]{3,2,1,0:T(8,128)(2,1)} custom-call(bf16[4,64,512]{2,1,0:T(8,128)(2,1)} %copy-done.4), custom_call_target="tpu_custom_call" | custom-call | tf_op jit(solution)/shard_map/copies/pallas_call | solution.py:144
  35.9 6.8 %all-to-all-start.1 = ((bf16[8,4,64,512]{3,2,1,0:T(8,128)(2,1)}), bf16[8,4,64,512]{3,2,1,0:T(8,128)(2,1)S(1)}, u32[]{:S(2)}, u32[]{:S(2)}) async-start(bf16[8,4,64,512]{3,2,1,0:T(8,128)(2,1)} %copies.1), calls=%async_computation.1 | async-start | bytes 4194304 | tf_op jit(solution)/shard_map/all_to_all | solution.py:292
  42.7 2.9 %collective-permute-start.2 = (bf16[528,512]{1,0:T(8,128)(2,1)S(1)}, bf16[528,512]{1,0:T(8,128)(2,1)S(1)}, u32[]{:S(2)}, u32[]{:S(2)}) collective-permute-start(bf16[528,512]{1,0:T(8,128)(2,1)S(1)} %pad_maximum_fusion.refs_0_), channel_id=1, source_target_pairs={{0,96},{32,0},{64,32},{96,64},{1,97},{33,1},{65,33},{97,65},{2,98}... | collective-permute-start | bytes 1622024 | tf_op jit(solution)/shard_map/ppermute | solution.py:93
  45.6 2.4 %collective-permute-start = (bf16[528,512]{1,0:T(8,128)(2,1)S(1)}, bf16[528,512]{1,0:T(8,128)(2,1)}, u32[]{:S(2)}, u32[]{:S(2)}) collective-permute-start(bf16[528,512]{1,0:T(8,128)(2,1)S(1)} %pad_maximum_fusion.refs_0_), channel_id=1, source_target_pairs={{0,32},{32,64},{64,96},{96,0},{1,33},{33,65},{65,97},{97,1},{2,34}... | collective-permute-start | bytes 1622024 | tf_op jit(solution)/shard_map/ppermute | solution.py:93
  48.0 7.8 %collective-permute-done.2.refs_3_ = bf16[528,512]{1,0:T(8,128)(2,1)S(1)} collective-permute-done((bf16[528,512]{1,0:T(8,128)(2,1)S(1)}, bf16[528,512]{1,0:T(8,128)(2,1)S(1)}, u32[]{:S(2)}, u32[]{:S(2)}) %collective-permute-start.2) | collective-permute-done | bytes 540704 | tf_op jit(solution)/shard_map/ppermute | solution.py:93
  55.8 4.1 %collective-permute-start.5 = (bf16[512,512]{1,0:T(8,128)(2,1)}, bf16[512,512]{1,0:T(8,128)(2,1)}, u32[]{:S(2)}, u32[]{:S(2)}) collective-permute-start(bf16[512,512]{1,0:T(8,128)(2,1)} %held.1.refs_4_), channel_id=1, source_target_pairs={{0,96},{32,0},{64,32},{96,64},{1,97},{33,1},{65,33},{97,65},{2,98}... | collective-permute-start | bytes 1572872 | tf_op jit(solution)/shard_map/ppermute | solution.py:93
  63.8 4.2 %collective-permute-done.5.refs_7_ = bf16[512,512]{1,0:T(8,128)(2,1)} collective-permute-done((bf16[512,512]{1,0:T(8,128)(2,1)}, bf16[512,512]{1,0:T(8,128)(2,1)}, u32[]{:S(2)}, u32[]{:S(2)}) %collective-permute-start.5) | collective-permute-done | bytes 524320 | tf_op jit(solution)/shard_map/ppermute | solution.py:93
  68.0 5.3 %collective-permute-start.6 = (bf16[512,512]{1,0:T(8,128)(2,1)}, bf16[512,512]{1,0:T(8,128)(2,1)}, u32[]{:S(2)}, u32[]{:S(2)}) collective-permute-start(bf16[512,512]{1,0:T(8,128)(2,1)} %collective-permute-done.5.refs_7_), channel_id=1, source_target_pairs={{0,96},{32,0},{64,32},{96,64},{1,97},{33,1},{65,33},{97,65},{2,98}... | collective-permute-start | bytes 1572872 | tf_op jit(solution)/shard_map/ppermute | solution.py:93
  73.4 11.2 %collective-permute-done.4.refs_5_ = bf16[512,512]{1,0:T(8,128)(2,1)} collective-permute-done((bf16[512,512]{1,0:T(8,128)(2,1)}, bf16[512,512]{1,0:T(8,128)(2,1)}, u32[]{:S(2)}, u32[]{:S(2)}) %collective-permute-start.4) | collective-permute-done | bytes 524320 | tf_op jit(solution)/shard_map/ppermute | solution.py:93
  84.6 9.8 %all-to-all-done.1.refs_8_ = bf16[8,4,64,512]{3,2,1,0:T(8,128)(2,1)S(1)} async-done(((bf16[8,4,64,512]{3,2,1,0:T(8,128)(2,1)}), bf16[8,4,64,512]{3,2,1,0:T(8,128)(2,1)S(1)}, u32[]{:S(2)}, u32[]{:S(2)}) %all-to-all-start.1) | async-done | bytes 2097184 | tf_op jit(solution)/shard_map/all_to_all | solution.py:292
  94.4 3.1 %products_other.1 = bf16[9,256,128]{2,1,0:T(8,128)(2,1)S(1)} custom-call(s32[3]{0:T(128)S(1)} %pad_add_fusion.position, bf16[528,512]{1,0:T(8,128)(2,1)S(1)} %pad_maximum_fusion.refs_0_, bf16[528,512]{1,0:T(8,128)(2,1)} %collective-permute-done.refs_1_, bf16[528,512]{1,0:T(8,128)(2,1)} %collective-permute-done.1.refs_2_, ...), custom_call_target="tpu_custom_call" | custom-call | flops 1073741824 | bytes 7340032 | tf_op jit(solution)/shard_map/products_other/pallas_call | solution.py:250
  97.5 2.4 %collective-permute-start.7 = (bf16[9,256,128]{2,1,0:T(8,128)(2,1)S(1)}, bf16[9,256,128]{2,1,0:T(8,128)(2,1)S(1)}, u32[]{:S(2)}, u32[]{:S(2)}) collective-permute-start(bf16[9,256,128]{2,1,0:T(8,128)(2,1)S(1)} %products_other.1), channel_id=1, source_target_pairs={{0,16},{16,0},{1,17},{17,1},{2,18},{18,2},{3,19},{19,3},{4,20},{20... | collective-permute-start | bytes 1769480 | tf_op jit(solution)/shard_map/ppermute | solution.py:88
  100.0 3.1 %products_own.1.kept = f32[8,256,128]{2,1,0:T(8,128)S(1)} custom-call(s32[3]{0:T(128)S(1)} %pad_add_fusion.position, bf16[528,512]{1,0:T(8,128)(2,1)S(1)} %pad_maximum_fusion.refs_0_, bf16[528,512]{1,0:T(8,128)(2,1)} %collective-permute-done.refs_1_, bf16[528,512]{1,0:T(8,128)(2,1)} %collective-permute-done.1.refs_2_, ...), custom_call_target="tpu_custom_call" | custom-call | flops 1073741824 | bytes 7340032 | tf_op jit(solution)/shard_map/products_own/pallas_call | solution.py:250
  104.9 4.7 %all-to-all-start.2 = ((bf16[8,256,128]{2,1,0:T(8,128)(2,1)}), bf16[8,256,128]{2,1,0:T(8,128)(2,1)S(1)}, u32[]{:S(2)}, u32[]{:S(2)}) async-start(bf16[8,256,128]{2,1,0:T(8,128)(2,1)} %total.1), calls=%async_computation.2 | async-start | bytes 1048576 | tf_op jit(solution)/shard_map/all_to_all | solution.py:309
  110.5 17.1 %all-to-all-done.2.terms = bf16[8,256,128]{2,1,0:T(8,128)(2,1)S(1)} async-done(((bf16[8,256,128]{2,1,0:T(8,128)(2,1)}), bf16[8,256,128]{2,1,0:T(8,128)(2,1)S(1)}, u32[]{:S(2)}, u32[]{:S(2)}) %all-to-all-start.2) | async-done | bytes 524320 | tf_op jit(solution)/shard_map/all_to_all | solution.py:309
  128.4 3.4 %all-to-all-start.3 = ((bf16[4,128,256]{2,1,0:T(8,128)(2,1)}), bf16[4,128,256]{2,1,0:T(8,128)(2,1)S(1)}, u32[]{:S(2)}, u32[]{:S(2)}) async-start(bf16[4,128,256]{2,1,0:T(8,128)(2,1)} %quarters.1), calls=%async_computation.3 | async-start | bytes 524288 | tf_op jit(solution)/shard_map/all_to_all | solution.py:310
  133.4 5.7 %all-to-all-done.3 = bf16[4,128,256]{2,1,0:T(8,128)(2,1)S(1)} async-done(((bf16[4,128,256]{2,1,0:T(8,128)(2,1)}), bf16[4,128,256]{2,1,0:T(8,128)(2,1)S(1)}, u32[]{:S(2)}, u32[]{:S(2)}) %all-to-all-start.3) | async-done | bytes 262176 | tf_op jit(solution)/shard_map/all_to_all | solution.py:310
  141.3 7.7 %all-to-all-start.4 = ((bf16[128,2,128]{2,1,0:T(2,128)(2,1)}), bf16[128,2,128]{2,1,0:T(2,128)(2,1)S(1)}, u32[]{:S(2)}, u32[]{:S(2)}) async-start(bf16[128,2,128]{2,1,0:T(2,128)(2,1)} %reshape.159), calls=%async_computation.4 | async-start | bytes 131072 | tf_op jit(solution)/shard_map/all_to_all | solution.py:316
  149.4 13.9 %all-to-all-done.4 = bf16[128,2,128]{2,1,0:T(2,128)(2,1)S(1)} async-done(((bf16[128,2,128]{2,1,0:T(2,128)(2,1)}), bf16[128,2,128]{2,1,0:T(2,128)(2,1)S(1)}, u32[]{:S(2)}, u32[]{:S(2)}) %all-to-all-start.4) | async-done | bytes 65568 | tf_op jit(solution)/shard_map/all_to_all | solution.py:316
  (55 shorter events, 12.8 us)
Async XLA Ops:
  0.6 109.7 %copy-start = (bf16[1,8192]{1,0:T(2,128)(2,1)S(1)}, bf16[1,8192]{1,0:T(2,128)(2,1)}, u32[]{:S(2)}) copy-start(bf16[1,8192]{1,0:T(2,128)(2,1)} %param.16) | copy-start | bytes 49156
  0.7 26.7 %copy-start.10 = (bf16[16,512]{1,0:T(8,128)(2,1)S(1)}, bf16[16,512]{1,0:T(8,128)(2,1)}, u32[]{:S(2)}) copy-start(bf16[16,512]{1,0:T(8,128)(2,1)} %param.15) | copy-start | bytes 49156
  2.7 45.3 %collective-permute-start.3 = (bf16[512,512]{1,0:T(8,128)(2,1)}, bf16[512,512]{1,0:T(8,128)(2,1)}, u32[]{:S(2)}, u32[]{:S(2)}) collective-permute-start(bf16[512,512]{1,0:T(8,128)(2,1)} %get-tuple-element.12), channel_id=1, source_target_pairs={{0,8},{8,0},{1,9},{9,1},{2,10},{10,2},{3,11},{11,3},{4,12},{12,4},... | collective-permute-start | bytes 1572872 | tf_op jit(solution)/shard_map/ppermute | solution.py:88
  23.3 9.6 %all-to-all-start = ((bf16[4,64,512]{2,1,0:T(8,128)(2,1)}), bf16[4,64,512]{2,1,0:T(8,128)(2,1)S(1)}, u32[]{:S(2)}, u32[]{:S(2)}) async-start(bf16[4,64,512]{2,1,0:T(8,128)(2,1)} %columns.1), calls=%async_computation | async-start | bytes 524288 | tf_op jit(solution)/shard_map/all_to_all | solution.py:289
  32.8 0.7 copy-start.4
  35.9 58.5 %all-to-all-start.1 = ((bf16[8,4,64,512]{3,2,1,0:T(8,128)(2,1)}), bf16[8,4,64,512]{3,2,1,0:T(8,128)(2,1)S(1)}, u32[]{:S(2)}, u32[]{:S(2)}) async-start(bf16[8,4,64,512]{3,2,1,0:T(8,128)(2,1)} %copies.1), calls=%async_computation.1 | async-start | bytes 4194304 | tf_op jit(solution)/shard_map/all_to_all | solution.py:292
  42.7 13.1 %collective-permute-start.2 = (bf16[528,512]{1,0:T(8,128)(2,1)S(1)}, bf16[528,512]{1,0:T(8,128)(2,1)S(1)}, u32[]{:S(2)}, u32[]{:S(2)}) collective-permute-start(bf16[528,512]{1,0:T(8,128)(2,1)S(1)} %pad_maximum_fusion.refs_0_), channel_id=1, source_target_pairs={{0,96},{32,0},{64,32},{96,64},{1,97},{33,1},{65,33},{97,65},{2,98}... | collective-permute-start | bytes 1622024 | tf_op jit(solution)/shard_map/ppermute | solution.py:93
  45.6 14.3 %collective-permute-start = (bf16[528,512]{1,0:T(8,128)(2,1)S(1)}, bf16[528,512]{1,0:T(8,128)(2,1)}, u32[]{:S(2)}, u32[]{:S(2)}) collective-permute-start(bf16[528,512]{1,0:T(8,128)(2,1)S(1)} %pad_maximum_fusion.refs_0_), channel_id=1, source_target_pairs={{0,32},{32,64},{64,96},{96,0},{1,33},{33,65},{65,97},{97,1},{2,34}... | collective-permute-start | bytes 1622024 | tf_op jit(solution)/shard_map/ppermute | solution.py:93
  55.8 12.2 %collective-permute-start.5 = (bf16[512,512]{1,0:T(8,128)(2,1)}, bf16[512,512]{1,0:T(8,128)(2,1)}, u32[]{:S(2)}, u32[]{:S(2)}) collective-permute-start(bf16[512,512]{1,0:T(8,128)(2,1)} %held.1.refs_4_), channel_id=1, source_target_pairs={{0,96},{32,0},{64,32},{96,64},{1,97},{33,1},{65,33},{97,65},{2,98}... | collective-permute-start | bytes 1572872 | tf_op jit(solution)/shard_map/ppermute | solution.py:93
  59.9 24.7 %collective-permute-start.1 = (bf16[528,512]{1,0:T(8,128)(2,1)}, bf16[528,512]{1,0:T(8,128)(2,1)}, u32[]{:S(2)}, u32[]{:S(2)}) collective-permute-start(bf16[528,512]{1,0:T(8,128)(2,1)} %collective-permute-done.refs_1_), channel_id=1, source_target_pairs={{0,32},{32,64},{64,96},{96,0},{1,33},{33,65},{65,97},{97,1},{2,34}... | collective-permute-start | bytes 1622024 | tf_op jit(solution)/shard_map/ppermute | solution.py:93
  61.9 22.7 %collective-permute-start.4 = (bf16[512,512]{1,0:T(8,128)(2,1)}, bf16[512,512]{1,0:T(8,128)(2,1)}, u32[]{:S(2)}, u32[]{:S(2)}) collective-permute-start(bf16[512,512]{1,0:T(8,128)(2,1)} %held.1.refs_4_), channel_id=1, source_target_pairs={{0,32},{32,64},{64,96},{96,0},{1,33},{33,65},{65,97},{97,1},{2,34}... | collective-permute-start | bytes 1572872 | tf_op jit(solution)/shard_map/ppermute | solution.py:93
  68.0 16.7 %collective-permute-start.6 = (bf16[512,512]{1,0:T(8,128)(2,1)}, bf16[512,512]{1,0:T(8,128)(2,1)}, u32[]{:S(2)}, u32[]{:S(2)}) collective-permute-start(bf16[512,512]{1,0:T(8,128)(2,1)} %collective-permute-done.5.refs_7_), channel_id=1, source_target_pairs={{0,96},{32,0},{64,32},{96,64},{1,97},{33,1},{65,33},{97,65},{2,98}... | collective-permute-start | bytes 1572872 | tf_op jit(solution)/shard_map/ppermute | solution.py:93
  97.5 5.6 %copy-start.2 = (bf16[9,256,128]{2,1,0:T(8,128)(2,1)}, bf16[9,256,128]{2,1,0:T(8,128)(2,1)S(1)}, u32[]{:S(2)}) copy-start(bf16[9,256,128]{2,1,0:T(8,128)(2,1)S(1)} %products_other.1) | copy-start | bytes 1769476
  97.5 5.6 %collective-permute-start.7 = (bf16[9,256,128]{2,1,0:T(8,128)(2,1)S(1)}, bf16[9,256,128]{2,1,0:T(8,128)(2,1)S(1)}, u32[]{:S(2)}, u32[]{:S(2)}) collective-permute-start(bf16[9,256,128]{2,1,0:T(8,128)(2,1)S(1)} %products_other.1), channel_id=1, source_target_pairs={{0,16},{16,0},{1,17},{17,1},{2,18},{18,2},{3,19},{19,3},{4,20},{20... | collective-permute-start | bytes 1769480 | tf_op jit(solution)/shard_map/ppermute | solution.py:88
  103.1 6.4 %copy-start.8 = (bf16[1,128,1024]{2,1,0:T(8,128)(2,1)S(1)}, bf16[1,128,1024]{2,1,0:T(8,128)(2,1)}, u32[]{:S(2)}) copy-start(bf16[1,128,1024]{2,1,0:T(8,128)(2,1)} %param.17) | copy-start | bytes 786436
  104.1 0.8 copy-start.1
  104.9 5.4 %copy-start.9 = (bf16[1,128,1024]{2,1,0:T(8,128)(2,1)S(1)}, bf16[1,128,1024]{2,1,0:T(8,128)(2,1)}, u32[]{:S(2)}) copy-start(bf16[1,128,1024]{2,1,0:T(8,128)(2,1)} %param.18) | copy-start | bytes 786436
  104.9 22.7 %all-to-all-start.2 = ((bf16[8,256,128]{2,1,0:T(8,128)(2,1)}), bf16[8,256,128]{2,1,0:T(8,128)(2,1)S(1)}, u32[]{:S(2)}, u32[]{:S(2)}) async-start(bf16[8,256,128]{2,1,0:T(8,128)(2,1)} %total.1), calls=%async_computation.2 | async-start | bytes 1048576 | tf_op jit(solution)/shard_map/all_to_all | solution.py:309
  110.3 28.8 %copy-start.5 = (f32[512,256]{1,0:T(8,128)S(1)}, f32[512,256]{1,0:T(8,128)}, u32[]{:S(2)}) copy-start(f32[512,256]{1,0:T(8,128)} %param.12) | copy-start | bytes 1572868
  110.4 28.8 %copy-start.6 = (bf16[512,256]{1,0:T(8,128)(2,1)S(1)}, bf16[512,256]{1,0:T(8,128)(2,1)}, u32[]{:S(2)}) copy-start(bf16[512,256]{1,0:T(8,128)(2,1)} %param.14) | copy-start | bytes 786436
  110.4 28.8 %copy-start.7 = (bf16[512,256]{1,0:T(8,128)(2,1)S(1)}, bf16[512,256]{1,0:T(8,128)(2,1)}, u32[]{:S(2)}) copy-start(bf16[512,256]{1,0:T(8,128)(2,1)} %param.13) | copy-start | bytes 786436
  128.4 10.7 %all-to-all-start.3 = ((bf16[4,128,256]{2,1,0:T(8,128)(2,1)}), bf16[4,128,256]{2,1,0:T(8,128)(2,1)S(1)}, u32[]{:S(2)}, u32[]{:S(2)}) async-start(bf16[4,128,256]{2,1,0:T(8,128)(2,1)} %quarters.1), calls=%async_computation.3 | async-start | bytes 524288 | tf_op jit(solution)/shard_map/all_to_all | solution.py:310
  140.5 24.1 %copy-start.3 = (f32[512,256]{1,0:T(8,128)}, f32[512,256]{1,0:T(8,128)S(1)}, u32[]{:S(2)}) copy-start(f32[512,256]{1,0:T(8,128)S(1)} %get-tuple-element.23) | copy-start | bytes 1572868
  141.3 22.0 %all-to-all-start.4 = ((bf16[128,2,128]{2,1,0:T(2,128)(2,1)}), bf16[128,2,128]{2,1,0:T(2,128)(2,1)S(1)}, u32[]{:S(2)}, u32[]{:S(2)}) async-start(bf16[128,2,128]{2,1,0:T(2,128)(2,1)} %reshape.159), calls=%async_computation.4 | async-start | bytes 131072 | tf_op jit(solution)/shard_map/all_to_all | solution.py:316

commit v13 on v11

--- a/solution.py
+++ b/solution.py
@@ -100,6 +100,7 @@
 
 
 VMEM = pl.BlockSpec(memory_space=pltpu.VMEM)
+HBM = pl.BlockSpec(memory_space=pltpu.HBM)
 SMALL_KERNEL = pltpu.CompilerParams(vmem_limit_bytes=16 * 2**20)
 
 
@@ -121,30 +122,11 @@
     )(grads)
 
 
-def copies_kernel(array, out, sems):
-    copies = [
-        pltpu.make_async_copy(array, out.at[i], sems.at[i]) for i in range(out.shape[0])
-    ]
-    for copy in copies:
-        copy.start()
-    for copy in copies:
-        copy.wait()
-
-
-def copies_of(array, count):
-    return pl.pallas_call(
-        copies_kernel,
-        out_shape=jax.ShapeDtypeStruct((count, *array.shape), array.dtype),
-        in_specs=[VMEM],
-        out_specs=pl.BlockSpec(memory_space=pl.ANY),
-        scratch_shapes=[pltpu.SemaphoreType.DMA((count,))],
-        compiler_params=SMALL_KERNEL,
-        name="copies",
-    )(array)
-
-
-def total_kernel(kept, received, out):
-    out[...] = (kept[...] + received[: out.shape[0]].astype(jnp.float32)).astype(out.dtype)
+def total_kernel(kept, received, out, total, sem):
+    total[...] = (kept[...] + received[: total.shape[0]].astype(jnp.float32)).astype(total.dtype)
+    copy = pltpu.make_async_copy(total, out, sem)
+    copy.start()
+    copy.wait()
 
 
 def total_of(kept, received):
@@ -152,7 +134,8 @@
         total_kernel,
         out_shape=jax.ShapeDtypeStruct(kept.shape, received.dtype),
         in_specs=[VMEM, VMEM],
-        out_specs=VMEM,
+        out_specs=HBM,
+        scratch_shapes=[pltpu.VMEM(kept.shape, received.dtype), pltpu.SemaphoreType.DMA],
         compiler_params=SMALL_KERNEL,
         name="total",
     )(kept, received)
@@ -190,7 +173,7 @@
         in_specs=[pl.BlockSpec(memory_space=pl.ANY)],
         out_specs=pl.BlockSpec(memory_space=pl.ANY),
         input_output_aliases={0: 0},
-        cost_estimate=pl.CostEstimate(flops=24 * 10**9, bytes_accessed=0, transcendentals=0),
+        cost_estimate=pl.CostEstimate(flops=26 * 10**9, bytes_accessed=0, transcendentals=0),
         name="held",
     )(array)
 
@@ -276,7 +259,8 @@
     piece = lax.all_to_all(columns, "x", 0, 0, tiled=True)
     piece, kept = lax.optimization_barrier((piece, kept))
     y_count = lax.axis_size("y")
-    grads_all = lax.all_to_all(copies_of(piece, y_count), "y", 0, 0)
+    copies = jnp.broadcast_to(piece[None], (y_count, *piece.shape))
+    grads_all = lax.all_to_all(copies, "y", 0, 0)
     behind, ahead = shifted(kept, "x", 1), shifted(kept, "x", -1)
     received = held(received)
     ahead, received = lax.optimization_barrier((ahead, received))

time: 155 us -> 156 us (level)
  waiting for transfers between devices: 66.9 us -> 76.1 us
  starting transfers between devices: 66.8 us -> 58.3 us
    all_to_all x1, waiting for transfers between devices: 0.01 us -> 5.89 us  [local(): piece = lax.all_to_all(columns, 'x', 0, 0, tiled=True)]
    all_to_all x1, starting transfers between devices: 12.9 us -> 7.75 us  [local(): fresh_terms = lax.all_to_all(partial_fresh, REP + TP, 0, 0, tiled=True)]
    all_to_all x1, waiting for transfers between devices: 6.21 us -> 9.3 us  [local(): grads_all = lax.all_to_all(copies, 'y', 0, 0)]
    ppermute x6, starting transfers between devices: 21 us -> 18 us  [shifted(): lax.ppermute(array, axis, [(i, (i + by) % count) for i in range(count)])]
    unnamed x29 -> x25, local copies, waits for them, and re-layouts: 3.26 us -> 0.99 us
    broadcast_in_dim x0 -> x1, local copies, waits for them, and re-layouts: none -> 1.56 us  [local(): copies = jnp.broadcast_to(piece[None], (y_count, *piece.shape))]
  transfers between devices with their start and end apart: 13 -> 13, of which waited for: 7 -> 8; matrix products, arithmetic and copies ran while one was open for 2% -> 2% of each run, Pallas kernels for 2% -> 2%
where the time goes in v13:
time: 156 us; the launch traced here: 155 us
  waiting for transfers between devices  76.1 us (49%)
  starting transfers between devices  58.3 us (37%)
  Pallas kernels  8.73 us (6%)
  local copies, waits for them, and re-layouts  5.43 us (3%)
  other arithmetic  3.87 us (2%)
  between operations  1.62 us (1%)
    ppermute x6, waiting for transfers between devices, shifted(): lax.ppermute(array, axis, [(i, (i + by) % count) for i in range(count)])  24.2 us
    ppermute x6, starting transfers between devices, shifted(): lax.ppermute(array, axis, [(i, (i + by) % count) for i in range(count)])  18 us
    all_to_all x1, waiting for transfers between devices, local(): terms = lax.all_to_all(over_rep, ('zhi', 'side'), 0, 0, tiled=True)  17.1 us
    all_to_all x1, waiting for transfers between devices, local(): fresh_terms = lax.all_to_all(partial_fresh, REP + TP, 0, 0, tiled=True)  13.9 us
    ppermute x2, starting transfers between devices, swap_over(): return lax.ppermute(array, axis, [(0, 1), (1, 0)])  13.9 us
    all_to_all x1, waiting for transfers between devices, local(): grads_all = lax.all_to_all(copies, 'y', 0, 0)  9.3 us
    all_to_all x1, starting transfers between devices, local(): fresh_terms = lax.all_to_all(partial_fresh, REP + TP, 0, 0, tiled=True)  7.75 us
    all_to_all x1, starting transfers between devices, local(): grads_all = lax.all_to_all(copies, 'y', 0, 0)  6.82 us
  transfers between devices with their start and end apart: 13, of which 8 were waited for; matrix products, arithmetic and copies ran while one was open for 2% of the time, Pallas kernels for 2%

profile of v13, /device:TPU:1, one launch (start us, length us, event | category | flops | bytes accessed | tf_op | source)
XLA Modules:
  0.0 155.0 jit_solution(658157097984779291)
XLA Ops:
  0.7 2.1 %select_bitcast_fusion = (bf16[512,512]{1,0:T(8,128)(2,1)}, bf16[512,512]{1,0:T(8,128)(2,1)S(1)}) fusion(pred[]{:T(512)S(6)} %eq.7, bf16[1,1024,512]{2,1,0:T(8,128)(2,1)} %param.10), kind=kLoop, calls=%fused_computation.12 | loop fusion | flops 524288 | bytes 2097153 | tf_op jit(solution)/shard_map/jit(_where)/select_n | solution.py:255
  2.8 11.5 %collective-permute-start.3 = (bf16[512,512]{1,0:T(8,128)(2,1)}, bf16[512,512]{1,0:T(8,128)(2,1)}, u32[]{:S(2)}, u32[]{:S(2)}) collective-permute-start(bf16[512,512]{1,0:T(8,128)(2,1)} %get-tuple-element.12), channel_id=1, source_target_pairs={{0,8},{8,0},{1,9},{9,1},{2,10},{10,2},{3,11},{11,3},{4,12},{12,4},... | collective-permute-start | bytes 1572872 | tf_op jit(solution)/shard_map/ppermute | solution.py:88
  15.0 4.0 %all-to-all-start = ((bf16[4,64,512]{2,1,0:T(8,128)(2,1)}), bf16[4,64,512]{2,1,0:T(8,128)(2,1)S(1)}, u32[]{:S(2)}, u32[]{:S(2)}) async-start(bf16[4,64,512]{2,1,0:T(8,128)(2,1)} %columns.1), calls=%async_computation | async-start | bytes 524288 | tf_op jit(solution)/shard_map/all_to_all | solution.py:259
  19.0 5.9 %all-to-all-done = bf16[4,64,512]{2,1,0:T(8,128)(2,1)S(1)} async-done(((bf16[4,64,512]{2,1,0:T(8,128)(2,1)}), bf16[4,64,512]{2,1,0:T(8,128)(2,1)S(1)}, u32[]{:S(2)}, u32[]{:S(2)}) %all-to-all-start) | async-done | bytes 262176 | tf_op jit(solution)/shard_map/all_to_all | solution.py:259
  26.5 6.8 %all-to-all-start.1 = ((bf16[8,4,64,512]{3,2,1,0:T(8,128)(2,1)}), bf16[8,4,64,512]{3,2,1,0:T(8,128)(2,1)S(1)}, u32[]{:S(2)}, u32[]{:S(2)}) async-start(bf16[8,4,64,512]{3,2,1,0:T(8,128)(2,1)} %broadcast_in_dim.10), calls=%async_computation.1 | async-start | bytes 4194304 | tf_op jit(solution)/shard_map/all_to_all | solution.py:263
  33.3 2.8 %collective-permute-start.2 = (bf16[528,512]{1,0:T(8,128)(2,1)S(1)}, bf16[528,512]{1,0:T(8,128)(2,1)S(1)}, u32[]{:S(2)}, u32[]{:S(2)}) collective-permute-start(bf16[528,512]{1,0:T(8,128)(2,1)S(1)} %pad_maximum_fusion.refs_0_), channel_id=1, source_target_pairs={{0,96},{32,0},{64,32},{96,64},{1,97},{33,1},{65,33},{97,65},{2,98}... | collective-permute-start | bytes 1622024 | tf_op jit(solution)/shard_map/ppermute | solution.py:93
  36.1 2.5 %collective-permute-start = (bf16[528,512]{1,0:T(8,128)(2,1)S(1)}, bf16[528,512]{1,0:T(8,128)(2,1)}, u32[]{:S(2)}, u32[]{:S(2)}) collective-permute-start(bf16[528,512]{1,0:T(8,128)(2,1)S(1)} %pad_maximum_fusion.refs_0_), channel_id=1, source_target_pairs={{0,32},{32,64},{64,96},{96,0},{1,33},{33,65},{65,97},{97,1},{2,34}... | collective-permute-start | bytes 1622024 | tf_op jit(solution)/shard_map/ppermute | solution.py:93
  38.6 8.2 %collective-permute-done.2.refs_3_ = bf16[528,512]{1,0:T(8,128)(2,1)S(1)} collective-permute-done((bf16[528,512]{1,0:T(8,128)(2,1)S(1)}, bf16[528,512]{1,0:T(8,128)(2,1)S(1)}, u32[]{:S(2)}, u32[]{:S(2)}) %collective-permute-start.2) | collective-permute-done | bytes 540704 | tf_op jit(solution)/shard_map/ppermute | solution.py:93
  46.8 3.9 %collective-permute-start.5 = (bf16[512,512]{1,0:T(8,128)(2,1)}, bf16[512,512]{1,0:T(8,128)(2,1)}, u32[]{:S(2)}, u32[]{:S(2)}) collective-permute-start(bf16[512,512]{1,0:T(8,128)(2,1)} %held.1.refs_4_), channel_id=1, source_target_pairs={{0,96},{32,0},{64,32},{96,64},{1,97},{33,1},{65,33},{97,65},{2,98}... | collective-permute-start | bytes 1572872 | tf_op jit(solution)/shard_map/ppermute | solution.py:93
  50.7 1.9 %collective-permute-start.1 = (bf16[528,512]{1,0:T(8,128)(2,1)}, bf16[528,512]{1,0:T(8,128)(2,1)}, u32[]{:S(2)}, u32[]{:S(2)}) collective-permute-start(bf16[528,512]{1,0:T(8,128)(2,1)} %collective-permute-done.refs_1_), channel_id=1, source_target_pairs={{0,32},{32,64},{64,96},{96,0},{1,33},{33,65},{65,97},{97,1},{2,34}... | collective-permute-start | bytes 1622024 | tf_op jit(solution)/shard_map/ppermute | solution.py:93
  52.6 1.9 %collective-permute-start.4 = (bf16[512,512]{1,0:T(8,128)(2,1)}, bf16[512,512]{1,0:T(8,128)(2,1)}, u32[]{:S(2)}, u32[]{:S(2)}) collective-permute-start(bf16[512,512]{1,0:T(8,128)(2,1)} %held.1.refs_4_), channel_id=1, source_target_pairs={{0,32},{32,64},{64,96},{96,0},{1,33},{33,65},{65,97},{97,1},{2,34}... | collective-permute-start | bytes 1572872 | tf_op jit(solution)/shard_map/ppermute | solution.py:93
  54.6 4.8 %collective-permute-done.5.refs_7_ = bf16[512,512]{1,0:T(8,128)(2,1)} collective-permute-done((bf16[512,512]{1,0:T(8,128)(2,1)}, bf16[512,512]{1,0:T(8,128)(2,1)}, u32[]{:S(2)}, u32[]{:S(2)}) %collective-permute-start.5) | collective-permute-done | bytes 524320 | tf_op jit(solution)/shard_map/ppermute | solution.py:93
  59.3 5.0 %collective-permute-start.6 = (bf16[512,512]{1,0:T(8,128)(2,1)}, bf16[512,512]{1,0:T(8,128)(2,1)}, u32[]{:S(2)}, u32[]{:S(2)}) collective-permute-start(bf16[512,512]{1,0:T(8,128)(2,1)} %collective-permute-done.5.refs_7_), channel_id=1, source_target_pairs={{0,96},{32,0},{64,32},{96,64},{1,97},{33,1},{65,33},{97,65},{2,98}... | collective-permute-start | bytes 1572872 | tf_op jit(solution)/shard_map/ppermute | solution.py:93
  64.4 11.2 %collective-permute-done.4.refs_5_ = bf16[512,512]{1,0:T(8,128)(2,1)} collective-permute-done((bf16[512,512]{1,0:T(8,128)(2,1)}, bf16[512,512]{1,0:T(8,128)(2,1)}, u32[]{:S(2)}, u32[]{:S(2)}) %collective-permute-start.4) | collective-permute-done | bytes 524320 | tf_op jit(solution)/shard_map/ppermute | solution.py:93
  75.7 9.3 %all-to-all-done.1.refs_8_ = bf16[8,4,64,512]{3,2,1,0:T(8,128)(2,1)S(1)} async-done(((bf16[8,4,64,512]{3,2,1,0:T(8,128)(2,1)}), bf16[8,4,64,512]{3,2,1,0:T(8,128)(2,1)S(1)}, u32[]{:S(2)}, u32[]{:S(2)}) %all-to-all-start.1) | async-done | bytes 2097184 | tf_op jit(solution)/shard_map/all_to_all | solution.py:263
  85.0 3.1 %products_other.1 = bf16[9,256,128]{2,1,0:T(8,128)(2,1)S(1)} custom-call(s32[3]{0:T(128)S(1)} %pad_add_fusion.position, bf16[528,512]{1,0:T(8,128)(2,1)S(1)} %pad_maximum_fusion.refs_0_, bf16[528,512]{1,0:T(8,128)(2,1)} %collective-permute-done.refs_1_, bf16[528,512]{1,0:T(8,128)(2,1)} %collective-permute-done.1.refs_2_, ...), custom_call_target="tpu_custom_call" | custom-call | flops 1073741824 | bytes 7340032 | tf_op jit(solution)/shard_map/products_other/pallas_call | solution.py:220
  88.1 2.5 %collective-permute-start.7 = (bf16[9,256,128]{2,1,0:T(8,128)(2,1)S(1)}, bf16[9,256,128]{2,1,0:T(8,128)(2,1)S(1)}, u32[]{:S(2)}, u32[]{:S(2)}) collective-permute-start(bf16[9,256,128]{2,1,0:T(8,128)(2,1)S(1)} %products_other.1), channel_id=1, source_target_pairs={{0,16},{16,0},{1,17},{17,1},{2,18},{18,2},{3,19},{19,3},{4,20},{20... | collective-permute-start | bytes 1769480 | tf_op jit(solution)/shard_map/ppermute | solution.py:88
  90.6 3.1 %products_own.1.kept = f32[8,256,128]{2,1,0:T(8,128)S(1)} custom-call(s32[3]{0:T(128)S(1)} %pad_add_fusion.position, bf16[528,512]{1,0:T(8,128)(2,1)S(1)} %pad_maximum_fusion.refs_0_, bf16[528,512]{1,0:T(8,128)(2,1)} %collective-permute-done.refs_1_, bf16[528,512]{1,0:T(8,128)(2,1)} %collective-permute-done.1.refs_2_, ...), custom_call_target="tpu_custom_call" | custom-call | flops 1073741824 | bytes 7340032 | tf_op jit(solution)/shard_map/products_own/pallas_call | solution.py:220
  95.5 4.4 %all-to-all-start.2 = ((bf16[8,256,128]{2,1,0:T(8,128)(2,1)}), bf16[8,256,128]{2,1,0:T(8,128)(2,1)S(1)}, u32[]{:S(2)}, u32[]{:S(2)}) async-start(bf16[8,256,128]{2,1,0:T(8,128)(2,1)} %total.1), calls=%async_computation.2 | async-start | bytes 1048576 | tf_op jit(solution)/shard_map/all_to_all | solution.py:280
  100.9 17.1 %all-to-all-done.2.terms = bf16[8,256,128]{2,1,0:T(8,128)(2,1)S(1)} async-done(((bf16[8,256,128]{2,1,0:T(8,128)(2,1)}), bf16[8,256,128]{2,1,0:T(8,128)(2,1)S(1)}, u32[]{:S(2)}, u32[]{:S(2)}) %all-to-all-start.2) | async-done | bytes 524320 | tf_op jit(solution)/shard_map/all_to_all | solution.py:280
  118.8 3.4 %all-to-all-start.3 = ((bf16[4,128,256]{2,1,0:T(8,128)(2,1)}), bf16[4,128,256]{2,1,0:T(8,128)(2,1)S(1)}, u32[]{:S(2)}, u32[]{:S(2)}) async-start(bf16[4,128,256]{2,1,0:T(8,128)(2,1)} %quarters.1), calls=%async_computation.3 | async-start | bytes 524288 | tf_op jit(solution)/shard_map/all_to_all | solution.py:281
  123.8 5.7 %all-to-all-done.3 = bf16[4,128,256]{2,1,0:T(8,128)(2,1)S(1)} async-done(((bf16[4,128,256]{2,1,0:T(8,128)(2,1)}), bf16[4,128,256]{2,1,0:T(8,128)(2,1)S(1)}, u32[]{:S(2)}, u32[]{:S(2)}) %all-to-all-start.3) | async-done | bytes 262176 | tf_op jit(solution)/shard_map/all_to_all | solution.py:281
  131.7 7.8 %all-to-all-start.4 = ((bf16[128,2,128]{2,1,0:T(2,128)(2,1)}), bf16[128,2,128]{2,1,0:T(2,128)(2,1)S(1)}, u32[]{:S(2)}, u32[]{:S(2)}) async-start(bf16[128,2,128]{2,1,0:T(2,128)(2,1)} %reshape.160), calls=%async_computation.4 | async-start | bytes 131072 | tf_op jit(solution)/shard_map/all_to_all | solution.py:287
  139.7 13.9 %all-to-all-done.4 = bf16[128,2,128]{2,1,0:T(2,128)(2,1)S(1)} async-done(((bf16[128,2,128]{2,1,0:T(2,128)(2,1)}), bf16[128,2,128]{2,1,0:T(2,128)(2,1)S(1)}, u32[]{:S(2)}, u32[]{:S(2)}) %all-to-all-start.4) | async-done | bytes 65568 | tf_op jit(solution)/shard_map/all_to_all | solution.py:287
  (55 shorter events, 10.5 us)
Async XLA Ops:
  0.6 100.1 %copy-start = (bf16[1,8192]{1,0:T(2,128)(2,1)S(1)}, bf16[1,8192]{1,0:T(2,128)(2,1)}, u32[]{:S(2)}) copy-start(bf16[1,8192]{1,0:T(2,128)(2,1)} %param.16) | copy-start | bytes 49156
  0.6 13.6 %copy-start.3 = (bf16[1,64,2048]{2,1,0:T(8,128)(2,1)S(1)}, bf16[1,64,2048]{2,1,0:T(8,128)(2,1)}, u32[]{:S(2)}) copy-start(bf16[1,64,2048]{2,1,0:T(8,128)(2,1)} %param.11) | copy-start | bytes 786436
  0.7 18.3 %copy-start.10 = (bf16[16,512]{1,0:T(8,128)(2,1)S(1)}, bf16[16,512]{1,0:T(8,128)(2,1)}, u32[]{:S(2)}) copy-start(bf16[16,512]{1,0:T(8,128)(2,1)} %param.15) | copy-start | bytes 49156
  2.8 35.8 %collective-permute-start.3 = (bf16[512,512]{1,0:T(8,128)(2,1)}, bf16[512,512]{1,0:T(8,128)(2,1)}, u32[]{:S(2)}, u32[]{:S(2)}) collective-permute-start(bf16[512,512]{1,0:T(8,128)(2,1)} %get-tuple-element.12), channel_id=1, source_target_pairs={{0,8},{8,0},{1,9},{9,1},{2,10},{10,2},{3,11},{11,3},{4,12},{12,4},... | collective-permute-start | bytes 1572872 | tf_op jit(solution)/shard_map/ppermute | solution.py:88
  15.0 9.9 %all-to-all-start = ((bf16[4,64,512]{2,1,0:T(8,128)(2,1)}), bf16[4,64,512]{2,1,0:T(8,128)(2,1)S(1)}, u32[]{:S(2)}, u32[]{:S(2)}) async-start(bf16[4,64,512]{2,1,0:T(8,128)(2,1)} %columns.1), calls=%async_computation | async-start | bytes 524288 | tf_op jit(solution)/shard_map/all_to_all | solution.py:259
  26.5 58.5 %all-to-all-start.1 = ((bf16[8,4,64,512]{3,2,1,0:T(8,128)(2,1)}), bf16[8,4,64,512]{3,2,1,0:T(8,128)(2,1)S(1)}, u32[]{:S(2)}, u32[]{:S(2)}) async-start(bf16[8,4,64,512]{3,2,1,0:T(8,128)(2,1)} %broadcast_in_dim.10), calls=%async_computation.1 | async-start | bytes 4194304 | tf_op jit(solution)/shard_map/all_to_all | solution.py:263
  33.3 13.5 %collective-permute-start.2 = (bf16[528,512]{1,0:T(8,128)(2,1)S(1)}, bf16[528,512]{1,0:T(8,128)(2,1)S(1)}, u32[]{:S(2)}, u32[]{:S(2)}) collective-permute-start(bf16[528,512]{1,0:T(8,128)(2,1)S(1)} %pad_maximum_fusion.refs_0_), channel_id=1, source_target_pairs={{0,96},{32,0},{64,32},{96,64},{1,97},{33,1},{65,33},{97,65},{2,98}... | collective-permute-start | bytes 1622024 | tf_op jit(solution)/shard_map/ppermute | solution.py:93
  36.1 14.6 %collective-permute-start = (bf16[528,512]{1,0:T(8,128)(2,1)S(1)}, bf16[528,512]{1,0:T(8,128)(2,1)}, u32[]{:S(2)}, u32[]{:S(2)}) collective-permute-start(bf16[528,512]{1,0:T(8,128)(2,1)S(1)} %pad_maximum_fusion.refs_0_), channel_id=1, source_target_pairs={{0,32},{32,64},{64,96},{96,0},{1,33},{33,65},{65,97},{97,1},{2,34}... | collective-permute-start | bytes 1622024 | tf_op jit(solution)/shard_map/ppermute | solution.py:93
  46.8 12.5 %collective-permute-start.5 = (bf16[512,512]{1,0:T(8,128)(2,1)}, bf16[512,512]{1,0:T(8,128)(2,1)}, u32[]{:S(2)}, u32[]{:S(2)}) collective-permute-start(bf16[512,512]{1,0:T(8,128)(2,1)} %held.1.refs_4_), channel_id=1, source_target_pairs={{0,96},{32,0},{64,32},{96,64},{1,97},{33,1},{65,33},{97,65},{2,98}... | collective-permute-start | bytes 1572872 | tf_op jit(solution)/shard_map/ppermute | solution.py:93
  50.7 25.0 %collective-permute-start.1 = (bf16[528,512]{1,0:T(8,128)(2,1)}, bf16[528,512]{1,0:T(8,128)(2,1)}, u32[]{:S(2)}, u32[]{:S(2)}) collective-permute-start(bf16[528,512]{1,0:T(8,128)(2,1)} %collective-permute-done.refs_1_), channel_id=1, source_target_pairs={{0,32},{32,64},{64,96},{96,0},{1,33},{33,65},{65,97},{97,1},{2,34}... | collective-permute-start | bytes 1622024 | tf_op jit(solution)/shard_map/ppermute | solution.py:93
  52.6 23.0 %collective-permute-start.4 = (bf16[512,512]{1,0:T(8,128)(2,1)}, bf16[512,512]{1,0:T(8,128)(2,1)}, u32[]{:S(2)}, u32[]{:S(2)}) collective-permute-start(bf16[512,512]{1,0:T(8,128)(2,1)} %held.1.refs_4_), channel_id=1, source_target_pairs={{0,32},{32,64},{64,96},{96,0},{1,33},{33,65},{65,97},{97,1},{2,34}... | collective-permute-start | bytes 1572872 | tf_op jit(solution)/shard_map/ppermute | solution.py:93
  59.3 16.3 %collective-permute-start.6 = (bf16[512,512]{1,0:T(8,128)(2,1)}, bf16[512,512]{1,0:T(8,128)(2,1)}, u32[]{:S(2)}, u32[]{:S(2)}) collective-permute-start(bf16[512,512]{1,0:T(8,128)(2,1)} %collective-permute-done.5.refs_7_), channel_id=1, source_target_pairs={{0,96},{32,0},{64,32},{96,64},{1,97},{33,1},{65,33},{97,65},{2,98}... | collective-permute-start | bytes 1572872 | tf_op jit(solution)/shard_map/ppermute | solution.py:93
  88.1 5.6 %copy-start.2 = (bf16[9,256,128]{2,1,0:T(8,128)(2,1)}, bf16[9,256,128]{2,1,0:T(8,128)(2,1)S(1)}, u32[]{:S(2)}) copy-start(bf16[9,256,128]{2,1,0:T(8,128)(2,1)S(1)} %products_other.1) | copy-start | bytes 1769476
  88.1 5.6 %collective-permute-start.7 = (bf16[9,256,128]{2,1,0:T(8,128)(2,1)S(1)}, bf16[9,256,128]{2,1,0:T(8,128)(2,1)S(1)}, u32[]{:S(2)}, u32[]{:S(2)}) collective-permute-start(bf16[9,256,128]{2,1,0:T(8,128)(2,1)S(1)} %products_other.1), channel_id=1, source_target_pairs={{0,16},{16,0},{1,17},{17,1},{2,18},{18,2},{3,19},{19,3},{4,20},{20... | collective-permute-start | bytes 1769480 | tf_op jit(solution)/shard_map/ppermute | solution.py:88
  93.7 6.2 %copy-start.8 = (bf16[1,128,1024]{2,1,0:T(8,128)(2,1)S(1)}, bf16[1,128,1024]{2,1,0:T(8,128)(2,1)}, u32[]{:S(2)}) copy-start(bf16[1,128,1024]{2,1,0:T(8,128)(2,1)} %param.17) | copy-start | bytes 786436
  94.7 0.8 copy-start.1
  95.5 5.1 %copy-start.9 = (bf16[1,128,1024]{2,1,0:T(8,128)(2,1)S(1)}, bf16[1,128,1024]{2,1,0:T(8,128)(2,1)}, u32[]{:S(2)}) copy-start(bf16[1,128,1024]{2,1,0:T(8,128)(2,1)} %param.18) | copy-start | bytes 786436
  95.5 22.4 %all-to-all-start.2 = ((bf16[8,256,128]{2,1,0:T(8,128)(2,1)}), bf16[8,256,128]{2,1,0:T(8,128)(2,1)S(1)}, u32[]{:S(2)}, u32[]{:S(2)}) async-start(bf16[8,256,128]{2,1,0:T(8,128)(2,1)} %total.1), calls=%async_computation.2 | async-start | bytes 1048576 | tf_op jit(solution)/shard_map/all_to_all | solution.py:280
  100.7 28.8 %copy-start.5 = (f32[512,256]{1,0:T(8,128)S(1)}, f32[512,256]{1,0:T(8,128)}, u32[]{:S(2)}) copy-start(f32[512,256]{1,0:T(8,128)} %param.12) | copy-start | bytes 1572868
  100.7 28.8 %copy-start.6 = (bf16[512,256]{1,0:T(8,128)(2,1)S(1)}, bf16[512,256]{1,0:T(8,128)(2,1)}, u32[]{:S(2)}) copy-start(bf16[512,256]{1,0:T(8,128)(2,1)} %param.14) | copy-start | bytes 786436
  100.7 28.8 %copy-start.7 = (bf16[512,256]{1,0:T(8,128)(2,1)S(1)}, bf16[512,256]{1,0:T(8,128)(2,1)}, u32[]{:S(2)}) copy-start(bf16[512,256]{1,0:T(8,128)(2,1)} %param.13) | copy-start | bytes 786436
  118.8 10.7 %all-to-all-start.3 = ((bf16[4,128,256]{2,1,0:T(8,128)(2,1)}), bf16[4,128,256]{2,1,0:T(8,128)(2,1)S(1)}, u32[]{:S(2)}, u32[]{:S(2)}) async-start(bf16[4,128,256]{2,1,0:T(8,128)(2,1)} %quarters.1), calls=%async_computation.3 | async-start | bytes 524288 | tf_op jit(solution)/shard_map/all_to_all | solution.py:281
  130.8 24.1 %copy-start.4 = (f32[512,256]{1,0:T(8,128)}, f32[512,256]{1,0:T(8,128)S(1)}, u32[]{:S(2)}) copy-start(f32[512,256]{1,0:T(8,128)S(1)} %get-tuple-element.23) | copy-start | bytes 1572868
  131.7 22.0 %all-to-all-start.4 = ((bf16[128,2,128]{2,1,0:T(2,128)(2,1)}), bf16[128,2,128]{2,1,0:T(2,128)(2,1)S(1)}, u32[]{:S(2)}, u32[]{:S(2)}) async-start(bf16[128,2,128]{2,1,0:T(2,128)(2,1)} %reshape.160), calls=%async_computation.4 | async-start | bytes 131072 | tf_op jit(solution)/shard_map/all_to_all | solution.py:287

commit v14 on v13

--- a/solution.py
+++ b/solution.py
@@ -122,19 +122,24 @@
     )(grads)
 
 
-def total_kernel(kept, received, out, total, sem):
-    total[...] = (kept[...] + received[: total.shape[0]].astype(jnp.float32)).astype(total.dtype)
+def total_kernel(kept, received, out, decode, total, sem):
+    blocks = total.shape[0]
+    total[...] = (kept[...] + received[:blocks].astype(jnp.float32)).astype(total.dtype)
     copy = pltpu.make_async_copy(total, out, sem)
     copy.start()
+    decode[...] = received[blocks]
     copy.wait()
 
 
 def total_of(kept, received):
     return pl.pallas_call(
         total_kernel,
-        out_shape=jax.ShapeDtypeStruct(kept.shape, received.dtype),
+        out_shape=[
+            jax.ShapeDtypeStruct(kept.shape, received.dtype),
+            jax.ShapeDtypeStruct(received.shape[1:], received.dtype),
+        ],
         in_specs=[VMEM, VMEM],
-        out_specs=HBM,
+        out_specs=[HBM, VMEM],
         scratch_shapes=[pltpu.VMEM(kept.shape, received.dtype), pltpu.SemaphoreType.DMA],
         compiler_params=SMALL_KERNEL,
         name="total",
@@ -173,13 +178,16 @@
         in_specs=[pl.BlockSpec(memory_space=pl.ANY)],
         out_specs=pl.BlockSpec(memory_space=pl.ANY),
         input_output_aliases={0: 0},
-        cost_estimate=pl.CostEstimate(flops=26 * 10**9, bytes_accessed=0, transcendentals=0),
+        cost_estimate=pl.CostEstimate(flops=24 * 10**9, bytes_accessed=0, transcendentals=0),
         name="held",
     )(array)
 
 
 def product_kernel(for_other, position, *refs):
-    *inputs, grads, out = refs
+    if for_other:
+        *inputs, grads, out = refs
+    else:
+        *inputs, grads, out, decode = refs
     half, along, core = position[0], position[1], position[2]
     y_count, x_count, rows, _ = grads.shape
     half_rows = y_count * rows
@@ -202,13 +210,16 @@
         ).astype(out.dtype)
         for part in range(parts):
             out[place * parts + part] = product[:, part * lanes : (part + 1) * lanes]
-    if for_other:
-        decode_rows = inputs[0].shape[0] - half_rows
-        for part in range(parts):
-            for block, source in zip(inputs[:x_count], sources):
-                start = (part * x_count + source) * decode_rows
-                target = pl.ds(pl.multiple_of(start, decode_rows), decode_rows)
-                out[2 * parts, target, :] = block[half_rows:, part * lanes : (part + 1) * lanes]
+    decode_rows = inputs[0].shape[0] - half_rows
+    for part in range(parts):
+        for block, source in zip(inputs[:x_count], sources):
+            start = (part * x_count + source) * decode_rows
+            target = pl.ds(pl.multiple_of(start, decode_rows), decode_rows)
+            rows_of_part = block[half_rows:, part * lanes : (part + 1) * lanes]
+            if for_other:
+                out[2 * parts, target, :] = rows_of_part
+            else:
+                decode[target, :] = rows_of_part
 
 
 def products(for_other, inputs, grads, width, lanes):
@@ -217,12 +228,15 @@
     y_count, x_count, rows, _ = grads.shape
     blocks = 2 * feature_count // lanes + for_other
     dtype = jnp.bfloat16 if for_other else jnp.float32
+    out_shape = [jax.ShapeDtypeStruct((blocks, width, lanes), dtype)]
+    if not for_other:
+        out_shape.append(jax.ShapeDtypeStruct((width, lanes), jnp.bfloat16))
     return pl.pallas_call(
         functools.partial(product_kernel, for_other),
-        out_shape=jax.ShapeDtypeStruct((blocks, width, lanes), dtype),
+        out_shape=out_shape,
         in_specs=[pl.BlockSpec(memory_space=pltpu.SMEM)]
         + [pl.BlockSpec(memory_space=pltpu.VMEM)] * (len(inputs) + 1),
-        out_specs=pl.BlockSpec(memory_space=pltpu.VMEM),
+        out_specs=[VMEM] * len(out_shape),
         compiler_params=pltpu.CompilerParams(vmem_limit_bytes=32 * 2**20),
         cost_estimate=pl.CostEstimate(
             flops=4 * feature_count * y_count * x_count * rows * width,
@@ -266,13 +280,13 @@
     ahead, received = lax.optimization_barrier((ahead, received))
     inputs = [kept, behind, shifted(behind, "x", 1), ahead] + around(received, "x", -1)
 
-    sent = products(True, inputs, grads_all, block_width, quarter)
+    (sent,) = products(True, inputs, grads_all, block_width, quarter)
     sent_back = swap_over(sent, "core")
-    kept_sum = products(False, inputs, grads_all, block_width, quarter)
-    over_rep = total_of(kept_sum, sent_back)
+    kept_sum, decode_own = products(False, inputs, grads_all, block_width, quarter)
+    over_rep, decode_other = total_of(kept_sum, sent_back)
     decode_of_core = [
-        jnp.concatenate(jnp.split(array[-1], side_count), axis=1).reshape(x_count, -1, feature_count)
-        for array in (sent, sent_back)
+        jnp.concatenate(jnp.split(array, side_count), axis=1).reshape(x_count, -1, feature_count)
+        for array in (decode_own, decode_other)
     ]
     decode_rows = jnp.where(
         core == 0, jnp.stack(decode_of_core, 1), jnp.stack(decode_of_core[::-1], 1)

time: 156 us -> 154 us (0.987)
  starting transfers between devices: 58.3 us -> 66.8 us
  waiting for transfers between devices: 76.1 us -> 68.4 us
    all_to_all x1, waiting for transfers between devices: 5.89 us -> 0.01 us  [local(): piece = lax.all_to_all(columns, 'x', 0, 0, tiled=True)]
    all_to_all x1, starting transfers between devices: 7.75 us -> 12.9 us  [local(): fresh_terms = lax.all_to_all(partial_fresh, REP + TP, 0, 0, tiled=True)]
    all_to_all x1, waiting for transfers between devices: 9.3 us -> 6.21 us  [local(): grads_all = lax.all_to_all(copies, 'y', 0, 0)]
    ppermute x6, starting transfers between devices: 18 us -> 21 us  [shifted(): lax.ppermute(array, axis, [(i, (i + by) % count) for i in range(count)])]
  transfers between devices with their start and end apart: 13 -> 13, of which waited for: 8 -> 7; matrix products, arithmetic and copies ran while one was open for 2% -> 2% of each run, Pallas kernels for 2% -> 2%
where the time goes in v14:
time: 154 us; the launch traced here: 153 us
  waiting for transfers between devices  68.4 us (44%)
  starting transfers between devices  66.8 us (43%)
  Pallas kernels  8.73 us (6%)
  local copies, waits for them, and re-layouts  4.02 us (3%)
  other arithmetic  2.65 us (2%)
  between operations  1.63 us (1%)
    ppermute x6, waiting for transfers between devices, shifted(): lax.ppermute(array, axis, [(i, (i + by) % count) for i in range(count)])  24 us
    ppermute x6, starting transfers between devices, shifted(): lax.ppermute(array, axis, [(i, (i + by) % count) for i in range(count)])  21 us
    all_to_all x1, waiting for transfers between devices, local(): terms = lax.all_to_all(over_rep, ('zhi', 'side'), 0, 0, tiled=True)  17.1 us
    all_to_all x1, waiting for transfers between devices, local(): fresh_terms = lax.all_to_all(partial_fresh, REP + TP, 0, 0, tiled=True)  13.9 us
    ppermute x2, starting transfers between devices, swap_over(): return lax.ppermute(array, axis, [(0, 1), (1, 0)])  13.5 us
    all_to_all x1, starting transfers between devices, local(): fresh_terms = lax.all_to_all(partial_fresh, REP + TP, 0, 0, tiled=True)  12.9 us
    all_to_all x1, waiting for transfers between devices, local(): lax.all_to_all(quarters_of(terms, side_count), 'side', 0, 0, tiled=True)  7.24 us
    all_to_all x1, starting transfers between devices, local(): grads_all = lax.all_to_all(copies, 'y', 0, 0)  6.82 us
  transfers between devices with their start and end apart: 13, of which 7 were waited for; matrix products, arithmetic and copies ran while one was open for 2% of the time, Pallas kernels for 2%

profile of v14, /device:TPU:1, one launch (start us, length us, event | category | flops | bytes accessed | tf_op | source)
XLA Modules:
  0.0 153.1 jit_solution(2673501130050476030)
XLA Ops:
  2.3 4.8 %all-to-all-start = ((bf16[4,64,512]{2,1,0:T(8,128)(2,1)}), bf16[4,64,512]{2,1,0:T(8,128)(2,1)S(1)}, u32[]{:S(2)}, u32[]{:S(2)}) async-start(bf16[4,64,512]{2,1,0:T(8,128)(2,1)} %columns.1), calls=%async_computation | async-start | bytes 524288 | tf_op jit(solution)/shard_map/all_to_all | solution.py:273
  8.0 10.6 %collective-permute-start.3 = (bf16[512,512]{1,0:T(8,128)(2,1)}, bf16[512,512]{1,0:T(8,128)(2,1)}, u32[]{:S(2)}, u32[]{:S(2)}) collective-permute-start(bf16[512,512]{1,0:T(8,128)(2,1)} %get-tuple-element.20), channel_id=1, source_target_pairs={{0,8},{8,0},{1,9},{9,1},{2,10},{10,2},{3,11},{11,3},{4,12},{12,4},... | collective-permute-start | bytes 1572872 | tf_op jit(solution)/shard_map/ppermute | solution.py:88
  18.7 1.6 %broadcast_in_dim.10 = bf16[8,4,64,512]{3,2,1,0:T(8,128)(2,1)} broadcast(bf16[4,64,512]{2,1,0:T(8,128)(2,1)S(1)} %all-to-all-done), dimensions={1,2,3} | broadcast | bytes 2359296 | tf_op jit(solution)/shard_map/broadcast_in_dim | solution.py:276
  20.3 6.8 %all-to-all-start.1 = ((bf16[8,4,64,512]{3,2,1,0:T(8,128)(2,1)}), bf16[8,4,64,512]{3,2,1,0:T(8,128)(2,1)S(1)}, u32[]{:S(2)}, u32[]{:S(2)}) async-start(bf16[8,4,64,512]{3,2,1,0:T(8,128)(2,1)} %broadcast_in_dim.10), calls=%async_computation.1 | async-start | bytes 4194304 | tf_op jit(solution)/shard_map/all_to_all | solution.py:277
  27.1 4.6 %collective-permute-start.2 = (bf16[528,512]{1,0:T(8,128)(2,1)S(1)}, bf16[528,512]{1,0:T(8,128)(2,1)S(1)}, u32[]{:S(2)}, u32[]{:S(2)}) collective-permute-start(bf16[528,512]{1,0:T(8,128)(2,1)S(1)} %pad_maximum_fusion.refs_0_), channel_id=1, source_target_pairs={{0,96},{32,0},{64,32},{96,64},{1,97},{33,1},{65,33},{97,65},{2,98}... | collective-permute-start | bytes 1622024 | tf_op jit(solution)/shard_map/ppermute | solution.py:93
  31.7 1.9 %collective-permute-start = (bf16[528,512]{1,0:T(8,128)(2,1)S(1)}, bf16[528,512]{1,0:T(8,128)(2,1)}, u32[]{:S(2)}, u32[]{:S(2)}) collective-permute-start(bf16[528,512]{1,0:T(8,128)(2,1)S(1)} %pad_maximum_fusion.refs_0_), channel_id=1, source_target_pairs={{0,32},{32,64},{64,96},{96,0},{1,33},{33,65},{65,97},{97,1},{2,34}... | collective-permute-start | bytes 1622024 | tf_op jit(solution)/shard_map/ppermute | solution.py:93
  33.7 7.8 %collective-permute-done.2.refs_3_ = bf16[528,512]{1,0:T(8,128)(2,1)S(1)} collective-permute-done((bf16[528,512]{1,0:T(8,128)(2,1)S(1)}, bf16[528,512]{1,0:T(8,128)(2,1)S(1)}, u32[]{:S(2)}, u32[]{:S(2)}) %collective-permute-start.2) | collective-permute-done | bytes 540704 | tf_op jit(solution)/shard_map/ppermute | solution.py:93
  41.5 5.3 %collective-permute-start.5 = (bf16[512,512]{1,0:T(8,128)(2,1)}, bf16[512,512]{1,0:T(8,128)(2,1)}, u32[]{:S(2)}, u32[]{:S(2)}) collective-permute-start(bf16[512,512]{1,0:T(8,128)(2,1)} %held.1.refs_4_), channel_id=1, source_target_pairs={{0,96},{32,0},{64,32},{96,64},{1,97},{33,1},{65,33},{97,65},{2,98}... | collective-permute-start | bytes 1572872 | tf_op jit(solution)/shard_map/ppermute | solution.py:93
  46.8 1.9 %collective-permute-start.1 = (bf16[528,512]{1,0:T(8,128)(2,1)}, bf16[528,512]{1,0:T(8,128)(2,1)}, u32[]{:S(2)}, u32[]{:S(2)}) collective-permute-start(bf16[528,512]{1,0:T(8,128)(2,1)} %collective-permute-done.refs_1_), channel_id=1, source_target_pairs={{0,32},{32,64},{64,96},{96,0},{1,33},{33,65},{65,97},{97,1},{2,34}... | collective-permute-start | bytes 1622024 | tf_op jit(solution)/shard_map/ppermute | solution.py:93
  48.7 1.9 %collective-permute-start.4 = (bf16[512,512]{1,0:T(8,128)(2,1)}, bf16[512,512]{1,0:T(8,128)(2,1)}, u32[]{:S(2)}, u32[]{:S(2)}) collective-permute-start(bf16[512,512]{1,0:T(8,128)(2,1)} %held.1.refs_4_), channel_id=1, source_target_pairs={{0,32},{32,64},{64,96},{96,0},{1,33},{33,65},{65,97},{97,1},{2,34}... | collective-permute-start | bytes 1572872 | tf_op jit(solution)/shard_map/ppermute | solution.py:93
  50.6 4.9 %collective-permute-done.5.refs_7_ = bf16[512,512]{1,0:T(8,128)(2,1)} collective-permute-done((bf16[512,512]{1,0:T(8,128)(2,1)}, bf16[512,512]{1,0:T(8,128)(2,1)}, u32[]{:S(2)}, u32[]{:S(2)}) %collective-permute-start.5) | collective-permute-done | bytes 524320 | tf_op jit(solution)/shard_map/ppermute | solution.py:93
  55.6 5.3 %collective-permute-start.6 = (bf16[512,512]{1,0:T(8,128)(2,1)}, bf16[512,512]{1,0:T(8,128)(2,1)}, u32[]{:S(2)}, u32[]{:S(2)}) collective-permute-start(bf16[512,512]{1,0:T(8,128)(2,1)} %collective-permute-done.5.refs_7_), channel_id=1, source_target_pairs={{0,96},{32,0},{64,32},{96,64},{1,97},{33,1},{65,33},{97,65},{2,98}... | collective-permute-start | bytes 1572872 | tf_op jit(solution)/shard_map/ppermute | solution.py:93
  61.0 11.2 %collective-permute-done.4.refs_5_ = bf16[512,512]{1,0:T(8,128)(2,1)} collective-permute-done((bf16[512,512]{1,0:T(8,128)(2,1)}, bf16[512,512]{1,0:T(8,128)(2,1)}, u32[]{:S(2)}, u32[]{:S(2)}) %collective-permute-start.4) | collective-permute-done | bytes 524320 | tf_op jit(solution)/shard_map/ppermute | solution.py:93
  72.2 6.2 %all-to-all-done.1.refs_8_ = bf16[8,4,64,512]{3,2,1,0:T(8,128)(2,1)S(1)} async-done(((bf16[8,4,64,512]{3,2,1,0:T(8,128)(2,1)}), bf16[8,4,64,512]{3,2,1,0:T(8,128)(2,1)S(1)}, u32[]{:S(2)}, u32[]{:S(2)}) %all-to-all-start.1) | async-done | bytes 2097184 | tf_op jit(solution)/shard_map/all_to_all | solution.py:277
  78.4 3.1 %products_other.1 = bf16[9,256,128]{2,1,0:T(8,128)(2,1)S(1)} custom-call(s32[3]{0:T(128)S(1)} %pad_add_fusion.position, bf16[528,512]{1,0:T(8,128)(2,1)S(1)} %pad_maximum_fusion.refs_0_, bf16[528,512]{1,0:T(8,128)(2,1)} %collective-permute-done.refs_1_, bf16[528,512]{1,0:T(8,128)(2,1)} %collective-permute-done.1.refs_2_, ...), custom_call_target="tpu_custom_call" | custom-call | flops 1073741824 | bytes 7340032 | tf_op jit(solution)/shard_map/products_other/pallas_call | solution.py:234
  81.6 2.9 %collective-permute-start.7 = (bf16[9,256,128]{2,1,0:T(8,128)(2,1)S(1)}, bf16[9,256,128]{2,1,0:T(8,128)(2,1)S(1)}, u32[]{:S(2)}, u32[]{:S(2)}) collective-permute-start(bf16[9,256,128]{2,1,0:T(8,128)(2,1)S(1)} %products_other.1), channel_id=1, source_target_pairs={{0,16},{16,0},{1,17},{17,1},{2,18},{18,2},{3,19},{19,3},{4,20},{20... | collective-permute-start | bytes 1769480 | tf_op jit(solution)/shard_map/ppermute | solution.py:88
  84.5 3.1 %products_own.1 = (f32[8,256,128]{2,1,0:T(8,128)S(1)}, bf16[256,128]{1,0:T(8,128)(2,1)S(1)}) custom-call(s32[3]{0:T(128)S(1)} %pad_add_fusion.position, bf16[528,512]{1,0:T(8,128)(2,1)S(1)} %pad_maximum_fusion.refs_0_, bf16[528,512]{1,0:T(8,128)(2,1)} %collective-permute-done.refs_1_, bf16[528,512]{1,0:T(8,128)(2,1)} %collective-permute-done.1.refs_2_, ...), custom_call_target="tpu_custom_call" | custom-call | flops 1073741824 | bytes 7340032 | tf_op jit(solution)/shard_map/products_own/pallas_call | solution.py:234
  88.5 4.4 %all-to-all-start.2 = ((bf16[8,256,128]{2,1,0:T(8,128)(2,1)}), bf16[8,256,128]{2,1,0:T(8,128)(2,1)S(1)}, u32[]{:S(2)}, u32[]{:S(2)}) async-start(bf16[8,256,128]{2,1,0:T(8,128)(2,1)} %get-tuple-element.17), calls=%async_computation.2 | async-start | bytes 1048576 | tf_op jit(solution)/shard_map/all_to_all | solution.py:294
  93.9 17.1 %all-to-all-done.2.terms = bf16[8,256,128]{2,1,0:T(8,128)(2,1)S(1)} async-done(((bf16[8,256,128]{2,1,0:T(8,128)(2,1)}), bf16[8,256,128]{2,1,0:T(8,128)(2,1)S(1)}, u32[]{:S(2)}, u32[]{:S(2)}) %all-to-all-start.2) | async-done | bytes 524320 | tf_op jit(solution)/shard_map/all_to_all | solution.py:294
  111.8 3.4 %all-to-all-start.3 = ((bf16[4,128,256]{2,1,0:T(8,128)(2,1)}), bf16[4,128,256]{2,1,0:T(8,128)(2,1)S(1)}, u32[]{:S(2)}, u32[]{:S(2)}) async-start(bf16[4,128,256]{2,1,0:T(8,128)(2,1)} %quarters.1), calls=%async_computation.3 | async-start | bytes 524288 | tf_op jit(solution)/shard_map/all_to_all | solution.py:295
  115.3 7.2 %all-to-all-done.3 = bf16[4,128,256]{2,1,0:T(8,128)(2,1)S(1)} async-done(((bf16[4,128,256]{2,1,0:T(8,128)(2,1)}), bf16[4,128,256]{2,1,0:T(8,128)(2,1)S(1)}, u32[]{:S(2)}, u32[]{:S(2)}) %all-to-all-start.3) | async-done | bytes 262176 | tf_op jit(solution)/shard_map/all_to_all | solution.py:295
  122.6 1.3 fusion.5
  124.7 12.9 %all-to-all-start.4 = ((bf16[128,2,128]{2,1,0:T(2,128)(2,1)}), bf16[128,2,128]{2,1,0:T(2,128)(2,1)S(1)}, u32[]{:S(2)}, u32[]{:S(2)}) async-start(bf16[128,2,128]{2,1,0:T(2,128)(2,1)} %reshape.136), calls=%async_computation.4 | async-start | bytes 131072 | tf_op jit(solution)/shard_map/all_to_all | solution.py:301
  137.9 13.9 %all-to-all-done.4 = bf16[128,2,128]{2,1,0:T(2,128)(2,1)S(1)} async-done(((bf16[128,2,128]{2,1,0:T(2,128)(2,1)}), bf16[128,2,128]{2,1,0:T(2,128)(2,1)S(1)}, u32[]{:S(2)}, u32[]{:S(2)}) %all-to-all-start.4) | async-done | bytes 65568 | tf_op jit(solution)/shard_map/all_to_all | solution.py:301
  (55 shorter events, 7.1 us)
Async XLA Ops:
  0.6 93.1 %copy-start = (bf16[1,8192]{1,0:T(2,128)(2,1)S(1)}, bf16[1,8192]{1,0:T(2,128)(2,1)}, u32[]{:S(2)}) copy-start(bf16[1,8192]{1,0:T(2,128)(2,1)} %param.16) | copy-start | bytes 49156
  0.6 1.0 copy-start.1
  1.6 5.6 %copy-start.3 = (bf16[1,1024,512]{2,1,0:T(8,128)(2,1)S(1)}, bf16[1,1024,512]{2,1,0:T(8,128)(2,1)}, u32[]{:S(2)}) copy-start(bf16[1,1024,512]{2,1,0:T(8,128)(2,1)} %param.10) | copy-start | bytes 3145732
  2.3 16.4 %all-to-all-start = ((bf16[4,64,512]{2,1,0:T(8,128)(2,1)}), bf16[4,64,512]{2,1,0:T(8,128)(2,1)S(1)}, u32[]{:S(2)}, u32[]{:S(2)}) async-start(bf16[4,64,512]{2,1,0:T(8,128)(2,1)} %columns.1), calls=%async_computation | async-start | bytes 524288 | tf_op jit(solution)/shard_map/all_to_all | solution.py:273
  7.2 11.5 %copy-start.9 = (bf16[16,512]{1,0:T(8,128)(2,1)S(1)}, bf16[16,512]{1,0:T(8,128)(2,1)}, u32[]{:S(2)}) copy-start(bf16[16,512]{1,0:T(8,128)(2,1)} %param.15) | copy-start | bytes 49156
  8.0 25.6 %collective-permute-start.3 = (bf16[512,512]{1,0:T(8,128)(2,1)}, bf16[512,512]{1,0:T(8,128)(2,1)}, u32[]{:S(2)}, u32[]{:S(2)}) collective-permute-start(bf16[512,512]{1,0:T(8,128)(2,1)} %get-tuple-element.20), channel_id=1, source_target_pairs={{0,8},{8,0},{1,9},{9,1},{2,10},{10,2},{3,11},{11,3},{4,12},{12,4},... | collective-permute-start | bytes 1572872 | tf_op jit(solution)/shard_map/ppermute | solution.py:88
  20.3 58.1 %all-to-all-start.1 = ((bf16[8,4,64,512]{3,2,1,0:T(8,128)(2,1)}), bf16[8,4,64,512]{3,2,1,0:T(8,128)(2,1)S(1)}, u32[]{:S(2)}, u32[]{:S(2)}) async-start(bf16[8,4,64,512]{3,2,1,0:T(8,128)(2,1)} %broadcast_in_dim.10), calls=%async_computation.1 | async-start | bytes 4194304 | tf_op jit(solution)/shard_map/all_to_all | solution.py:277
  27.1 14.3 %collective-permute-start.2 = (bf16[528,512]{1,0:T(8,128)(2,1)S(1)}, bf16[528,512]{1,0:T(8,128)(2,1)S(1)}, u32[]{:S(2)}, u32[]{:S(2)}) collective-permute-start(bf16[528,512]{1,0:T(8,128)(2,1)S(1)} %pad_maximum_fusion.refs_0_), channel_id=1, source_target_pairs={{0,96},{32,0},{64,32},{96,64},{1,97},{33,1},{65,33},{97,65},{2,98}... | collective-permute-start | bytes 1622024 | tf_op jit(solution)/shard_map/ppermute | solution.py:93
  31.7 15.1 %collective-permute-start = (bf16[528,512]{1,0:T(8,128)(2,1)S(1)}, bf16[528,512]{1,0:T(8,128)(2,1)}, u32[]{:S(2)}, u32[]{:S(2)}) collective-permute-start(bf16[528,512]{1,0:T(8,128)(2,1)S(1)} %pad_maximum_fusion.refs_0_), channel_id=1, source_target_pairs={{0,32},{32,64},{64,96},{96,0},{1,33},{33,65},{65,97},{97,1},{2,34}... | collective-permute-start | bytes 1622024 | tf_op jit(solution)/shard_map/ppermute | solution.py:93
  41.5 14.1 %collective-permute-start.5 = (bf16[512,512]{1,0:T(8,128)(2,1)}, bf16[512,512]{1,0:T(8,128)(2,1)}, u32[]{:S(2)}, u32[]{:S(2)}) collective-permute-start(bf16[512,512]{1,0:T(8,128)(2,1)} %held.1.refs_4_), channel_id=1, source_target_pairs={{0,96},{32,0},{64,32},{96,64},{1,97},{33,1},{65,33},{97,65},{2,98}... | collective-permute-start | bytes 1572872 | tf_op jit(solution)/shard_map/ppermute | solution.py:93
  46.8 25.4 %collective-permute-start.1 = (bf16[528,512]{1,0:T(8,128)(2,1)}, bf16[528,512]{1,0:T(8,128)(2,1)}, u32[]{:S(2)}, u32[]{:S(2)}) collective-permute-start(bf16[528,512]{1,0:T(8,128)(2,1)} %collective-permute-done.refs_1_), channel_id=1, source_target_pairs={{0,32},{32,64},{64,96},{96,0},{1,33},{33,65},{65,97},{97,1},{2,34}... | collective-permute-start | bytes 1622024 | tf_op jit(solution)/shard_map/ppermute | solution.py:93
  48.7 23.5 %collective-permute-start.4 = (bf16[512,512]{1,0:T(8,128)(2,1)}, bf16[512,512]{1,0:T(8,128)(2,1)}, u32[]{:S(2)}, u32[]{:S(2)}) collective-permute-start(bf16[512,512]{1,0:T(8,128)(2,1)} %held.1.refs_4_), channel_id=1, source_target_pairs={{0,32},{32,64},{64,96},{96,0},{1,33},{33,65},{65,97},{97,1},{2,34}... | collective-permute-start | bytes 1572872 | tf_op jit(solution)/shard_map/ppermute | solution.py:93
  55.6 16.7 %collective-permute-start.6 = (bf16[512,512]{1,0:T(8,128)(2,1)}, bf16[512,512]{1,0:T(8,128)(2,1)}, u32[]{:S(2)}, u32[]{:S(2)}) collective-permute-start(bf16[512,512]{1,0:T(8,128)(2,1)} %collective-permute-done.5.refs_7_), channel_id=1, source_target_pairs={{0,96},{32,0},{64,32},{96,64},{1,97},{33,1},{65,33},{97,65},{2,98}... | collective-permute-start | bytes 1572872 | tf_op jit(solution)/shard_map/ppermute | solution.py:93
  81.6 6.0 %collective-permute-start.7 = (bf16[9,256,128]{2,1,0:T(8,128)(2,1)S(1)}, bf16[9,256,128]{2,1,0:T(8,128)(2,1)S(1)}, u32[]{:S(2)}, u32[]{:S(2)}) collective-permute-start(bf16[9,256,128]{2,1,0:T(8,128)(2,1)S(1)} %products_other.1), channel_id=1, source_target_pairs={{0,16},{16,0},{1,17},{17,1},{2,18},{18,2},{3,19},{19,3},{4,20},{20... | collective-permute-start | bytes 1769480 | tf_op jit(solution)/shard_map/ppermute | solution.py:88
  87.6 5.4 %copy-start.7 = (bf16[1,128,1024]{2,1,0:T(8,128)(2,1)S(1)}, bf16[1,128,1024]{2,1,0:T(8,128)(2,1)}, u32[]{:S(2)}) copy-start(bf16[1,128,1024]{2,1,0:T(8,128)(2,1)} %param.17) | copy-start | bytes 786436
  88.5 5.2 %copy-start.8 = (bf16[1,128,1024]{2,1,0:T(8,128)(2,1)S(1)}, bf16[1,128,1024]{2,1,0:T(8,128)(2,1)}, u32[]{:S(2)}) copy-start(bf16[1,128,1024]{2,1,0:T(8,128)(2,1)} %param.18) | copy-start | bytes 786436
  88.5 22.5 %all-to-all-start.2 = ((bf16[8,256,128]{2,1,0:T(8,128)(2,1)}), bf16[8,256,128]{2,1,0:T(8,128)(2,1)S(1)}, u32[]{:S(2)}, u32[]{:S(2)}) async-start(bf16[8,256,128]{2,1,0:T(8,128)(2,1)} %get-tuple-element.17), calls=%async_computation.2 | async-start | bytes 1048576 | tf_op jit(solution)/shard_map/all_to_all | solution.py:294
  93.8 28.8 %copy-start.4 = (f32[512,256]{1,0:T(8,128)S(1)}, f32[512,256]{1,0:T(8,128)}, u32[]{:S(2)}) copy-start(f32[512,256]{1,0:T(8,128)} %param.12) | copy-start | bytes 1572868
  93.8 28.8 %copy-start.5 = (bf16[512,256]{1,0:T(8,128)(2,1)S(1)}, bf16[512,256]{1,0:T(8,128)(2,1)}, u32[]{:S(2)}) copy-start(bf16[512,256]{1,0:T(8,128)(2,1)} %param.14) | copy-start | bytes 786436
  93.8 28.8 %copy-start.6 = (bf16[512,256]{1,0:T(8,128)(2,1)S(1)}, bf16[512,256]{1,0:T(8,128)(2,1)}, u32[]{:S(2)}) copy-start(bf16[512,256]{1,0:T(8,128)(2,1)} %param.13) | copy-start | bytes 786436
  111.8 10.7 %all-to-all-start.3 = ((bf16[4,128,256]{2,1,0:T(8,128)(2,1)}), bf16[4,128,256]{2,1,0:T(8,128)(2,1)S(1)}, u32[]{:S(2)}, u32[]{:S(2)}) async-start(bf16[4,128,256]{2,1,0:T(8,128)(2,1)} %quarters.1), calls=%async_computation.3 | async-start | bytes 524288 | tf_op jit(solution)/shard_map/all_to_all | solution.py:295
  123.9 29.2 %copy-start.2 = (f32[512,256]{1,0:T(8,128)}, f32[512,256]{1,0:T(8,128)S(1)}, u32[]{:S(2)}) copy-start(f32[512,256]{1,0:T(8,128)S(1)} %get-tuple-element.23) | copy-start | bytes 1572868
  124.7 27.1 %all-to-all-start.4 = ((bf16[128,2,128]{2,1,0:T(2,128)(2,1)}), bf16[128,2,128]{2,1,0:T(2,128)(2,1)S(1)}, u32[]{:S(2)}, u32[]{:S(2)}) async-start(bf16[128,2,128]{2,1,0:T(2,128)(2,1)} %reshape.136), calls=%async_computation.4 | async-start | bytes 131072 | tf_op jit(solution)/shard_map/all_to_all | solution.py:301
